TPU v7x, 32 devices: a whole 2x2x4 slice. The times are simulated.
32 devices in a mesh: row: 8 (over y, x, core), col: 4 (over z).
Axes of the slice: x: 2, y: 2, z: 4, core: 2. Of those that a mesh axis runs over, the one named last changes fastest.
Arguments:
- hidden_img: bfloat16 [4096, 2432], P('row', 'col'), may hold values from -75 to 75
- hidden_txt: bfloat16 [768, 2432], P('row', 'col'), may hold values from -75 to 75
- text_len: int32 [4], replicated, may hold values from 1 to 154, as said below
- step_index: int32 [4], replicated, may hold values from 0 to 27
- latent: float32 [4096, 64], P('row'), may hold values from -6 to 6
- cond: float32 [4, 2432], P(None, 'row'), may hold values from -6 to 6
- mod_weight: bfloat16 [2432, 7, 2432], P('row', None, 'col'), may hold values from -0.125 to 0.125
- qkv_weight: bfloat16 [2432, 3, 2048], P('row', None, 'col'), may hold values from -0.125 to 0.125
- kv_text_weight: bfloat16 [2432, 2, 2048], P('row', None, 'col'), may hold values from -0.125 to 0.125
- q_gain: float32 [64], replicated, may hold values from 0.5 to 6
- k_gain: float32 [2, 64], replicated, may hold values from 0.5 to 6
- out_weight: bfloat16 [2048, 2432], P('row', 'col'), may hold values from -6 to 6
- final_weight: bfloat16 [2432, 64], P('row'), may hold values from -0.125 to 0.125
Outputs:
- velocity: float32 [4096, 64], P('row')
- latent_next: float32 [4096, 64], P('row')
Inputs may be any that keep to these rules, and one draw needn't show every extreme that they name: `text_len`: some request has exactly 154 text tokens in every draw.
All inputs are finite; a program needn't handle non-finite values.
Results may differ from a plain program's by a relative error of at most 0.015.
The roundings to bfloat16 on the way count: a program that leaves them out, or rounds other values in their place, can miss the bound.
Values may be sent and summed in bfloat16 or wider, within the bound.
No kernel may reach another device: no remote copies, remote signals or barrier semaphores. Data moves between devices by JAX's collectives and lax.ppermute only.
A program may use at most 64 MiB of HBM per device.

v0:
```python
import jax
import jax.numpy as jnp
from jax import lax
from jax.sharding import PartitionSpec as P

STEPS = 28


EPS_NORM = 1e-06


def partner_2(block, axis, distance):
    count = lax.axis_size(axis)
    route = []
    for low in range(count):
        high = low | 1 << distance
        if high != low and high < count:
            route += [(low, high), (high, low)]
    return lax.ppermute(block, axis, route)


def modulate_full(values, offset, stretch):
    average = jnp.mean(values, axis=1, keepdims=True)
    mean_square = jnp.mean(values * values, axis=1, keepdims=True)
    normed = (values - average) * lax.rsqrt(mean_square - average * average + EPS_NORM)
    return (normed * (1.0 + stretch) + offset).astype(jnp.bfloat16)


def head_norm(values, gain_row):
    mean_square = jnp.mean(values * values, axis=-1, keepdims=True)
    return (values * lax.rsqrt(mean_square + EPS_NORM) * gain_row).astype(jnp.bfloat16)


def sigma_of(step_now):
    remain = 1.0 - step_now.astype(jnp.float32) / STEPS
    return 3.0 * remain / (1.0 + 2.0 * remain)


def per_device(
    hidden_img,
    hidden_txt,
    text_len,
    step_index,
    latent,
    cond,
    mod_weight,
    qkv_weight,
    kv_text_weight,
    q_gain,
    k_gain,
    out_weight,
    final_weight,
):
    row_pos = lax.axis_index("row")
    request = row_pos // 2
    lower_half = row_pos % 2 == 0
    img_rows, width_part = hidden_img.shape
    txt_rows = hidden_txt.shape[0]
    head_dim = q_gain.shape[0]
    qkv_cols = qkv_weight.shape[2]
    heads_here = qkv_cols // head_dim
    activated = jax.nn.silu(cond).astype(jnp.bfloat16)
    mod_local = mod_weight.reshape(mod_weight.shape[0], 7 * width_part)
    mod_terms = jnp.dot(activated, mod_local, preferred_element_type=jnp.float32).reshape(
        activated.shape[0], 7, width_part
    )
    mod_all = lax.psum(mod_terms, "row")
    mod_own = lax.dynamic_index_in_dim(mod_all, request, 0, keepdims=False)
    mod_full = lax.all_gather(mod_own, "col", axis=1, tiled=True)
    img_full, txt_full = (
        lax.all_gather(hidden_img, "col", axis=1, tiled=True),
        lax.all_gather(hidden_txt, "col", axis=1, tiled=True),
    )
    img_ready = modulate_full(img_full.astype(jnp.float32), mod_full[0], mod_full[1])
    txt_ready = modulate_full(txt_full.astype(jnp.float32), mod_full[3], mod_full[4])
    qkv_flat = qkv_weight.reshape(qkv_weight.shape[0], 3 * qkv_cols)
    kv_flat = kv_text_weight.reshape(kv_text_weight.shape[0], 2 * qkv_cols)
    img_proj = jnp.dot(
        img_ready,
        lax.all_gather(qkv_flat, "row", axis=0, tiled=True),
        preferred_element_type=jnp.float32,
    )
    txt_proj = jnp.dot(
        txt_ready,
        lax.all_gather(kv_flat, "row", axis=0, tiled=True),
        preferred_element_type=jnp.float32,
    )
    img_proj = img_proj.reshape(img_rows, 3, heads_here, head_dim)
    txt_proj = txt_proj.reshape(txt_rows, 2, heads_here, head_dim)
    queries = head_norm(img_proj[:, 0], q_gain)
    img_keys = head_norm(img_proj[:, 1], k_gain[0])
    img_values = img_proj[:, 2].astype(jnp.bfloat16)
    txt_keys = head_norm(txt_proj[:, 0], k_gain[1])
    txt_values = txt_proj[:, 1].astype(jnp.bfloat16)
    length = lax.dynamic_index_in_dim(text_len, request, 0, keepdims=False)
    scaling = head_dim ** (-0.5)
    partner = partner_2((img_keys, img_values, txt_keys, txt_values), "row", 0)

    def ordered(own_part, peer_part):
        return jnp.concatenate(
            [
                jnp.where(lower_half, own_part, peer_part),
                jnp.where(lower_half, peer_part, own_part),
            ],
            axis=0,
        )

    all_keys = jnp.concatenate(
        [ordered(img_keys, partner[0]), ordered(txt_keys, partner[2])], axis=0
    )
    all_values = jnp.concatenate(
        [ordered(img_values, partner[1]), ordered(txt_values, partner[3])], axis=0
    )
    key_valid = jnp.concatenate(
        [jnp.ones((2 * img_rows,), dtype=bool), jnp.arange(2 * txt_rows) < length]
    )

    def attend(head_ops):
        q_head, k_head, v_head = head_ops
        scores = jnp.dot(q_head, k_head.T, preferred_element_type=jnp.float32) * scaling
        scores = jnp.where(key_valid[None, :], scores, -jnp.inf)
        row_max = jnp.max(scores, axis=1, keepdims=True)
        weights = jnp.exp(scores - row_max)
        probabilities = (weights / jnp.sum(weights, axis=1, keepdims=True)).astype(jnp.bfloat16)
        return jnp.dot(probabilities, v_head, preferred_element_type=jnp.float32).astype(
            jnp.bfloat16
        )

    attended = lax.map(
        attend,
        (jnp.moveaxis(queries, 1, 0), jnp.moveaxis(all_keys, 1, 0), jnp.moveaxis(all_values, 1, 0)),
    )
    attended = jnp.moveaxis(attended, 0, 1).reshape(img_rows, qkv_cols)
    full_heads = lax.all_gather(attended, "col", axis=1, tiled=True)
    projected = jnp.dot(
        full_heads,
        lax.all_gather(out_weight, "row", axis=0, tiled=True),
        preferred_element_type=jnp.float32,
    )
    updated = (hidden_img.astype(jnp.float32) + mod_own[2] * projected).astype(jnp.bfloat16)
    head_full = lax.all_gather(final_weight, "row", axis=0, tiled=True)
    residual = lax.all_gather(updated, "col", axis=1, tiled=True)
    head_in = modulate_full(residual.astype(jnp.float32), mod_full[5], mod_full[6])
    velocity = jnp.dot(head_in, head_full, preferred_element_type=jnp.float32)
    step_now = lax.dynamic_index_in_dim(step_index, request, 0, keepdims=False)
    sigma_step = sigma_of(step_now + 1) - sigma_of(step_now)
    latent_next = latent + sigma_step * velocity
    return (velocity, latent_next)


def solution(mesh):
    in_specs = (
        P("row", "col"),
        P("row", "col"),
        P(),
        P(),
        P("row", None),
        P(None, "row"),
        P("row", None, "col"),
        P("row", None, "col"),
        P("row", None, "col"),
        P(),
        P(),
        P("row", "col"),
        P("row", None),
    )
    out_specs = (P("row", None), P("row", None))
    return jax.shard_map(
        per_device, mesh=mesh, in_specs=in_specs, out_specs=out_specs, check_vma=False
    )
```

profile of v0, /device:TPU:0, one launch (start us, length us, event | category | flops | bytes accessed | tf_op | source)
XLA Modules:
  0.0 332.9 jit_solution(2651646647328075157)
XLA Ops:
  8.0 2.4 copy.41
  10.4 3.7 %reshape.128 = bf16[304,4256]{1,0:T(8,128)(2,1)} reshape(bf16[304,7,608]{2,1,0:T(8,128)(2,1)S(1)} %copy.41) | data formatting | bytes 5175296 | tf_op jit(solution)/shard_map/reshape | solution.py:63
  14.1 6.1 %dot_general.26 = bf16[7,608,304]{1,0,2:T(8,128)(2,1)S(1)} reshape(bf16[4256,304]{0,1:T(8,128)(2,1)} %bitcast.101) | data formatting | bytes 5175296 | tf_op jit(solution)/shard_map/dot_general | solution.py:64
  20.3 1.3 fusion.24
  21.6 0.5 all-gather.10.cloned.1.call-update
  22.2 2.1 copy.58
  24.3 1.0 copy.57
  25.4 0.7 all-gather.18.cloned.1.call-update
  26.2 21.7 %all-gather.1 = bf16[4,608,96]{1,2,0:T(8,128)(2,1)S(1)} all-gather(bf16[1,608,96]{1,2,0:T(8,128)(2,1)S(1)} %bitcast.118), channel_id=1, replica_groups=mesh['row'=8,'col'=4] {'col'}, dimensions={0}, use_global_device_ids=true | all-gather | bytes 583680 | tf_op jit(solution)/shard_map/all_gather | solution.py:72
  48.4 0.5 reshape.168
  49.0 0.6 dynamic_slice.23
  49.6 0.6 iota_compare_fusion
  50.3 23.7 %all-reduce.3.cloned.1.call-done = f32[4,7,608]{2,0,1:T(4,128)} async-done(((f32[4,7,608]{2,0,1:T(4,128)}), f32[4,7,608]{2,0,1:T(4,128)}) %all-reduce.3.cloned.1.call-update) | async-done | bytes 68112 | tf_op jit(solution)/shard_map/psum | solution.py:67
  74.0 0.9 constant_dynamic-slice_fusion
  75.1 26.8 %all-gather = f32[1,7,2432]{1,0,2:T(1,128)S(1)} all-gather(f32[1,7,608]{1,0,2:T(1,128)S(1)} %copy.43), channel_id=2, replica_groups=mesh['row'=8,'col'=4] {'col'}, dimensions={2}, use_global_device_ids=true | all-gather | bytes 85120 | tf_op jit(solution)/shard_map/all_gather | solution.py:69
  101.9 43.0 %fusion.38 = (f32[2432]{0:T(1024)S(1)}, f32[2432]{0:T(1024)S(1)}, f32[2432]{0:T(1024)S(1)}, f32[2432]{0:T(1024)S(1)}, f32[2432]{0:T(1024)S(1)}, /*index=5*/f32[2432]{0:T(1024)}) fusion(f32[1,7,2432]{1,0,2:T(1,128)S(1)} %all-gather), kind=kLoop, calls=%fused_computation.52 | loop fusion | flops 7296 | bytes 116736 | tf_op jit(solution)/shard_map/add | solution.py:26
  144.9 2.4 convert_reduce_fusion.1
  147.4 4.5 %fusion.42 = f32[96,1024]{0,1:T(8,128)S(1)} fusion(bf16[2432,1024]{1,0:T(8,128)(2,1)} %all-gather.14.cloned.1.call-done, f32[2432,96]{0,1:T(8,128)S(1)} %reshape.168, f32[2432]{0:T(1024)S(1)} %get-tuple-element.61, f32[96]{0:T(128)S(1)} %get-tuple-element.96, f32[96]{0:T(128)S(1)} %get-tuple-element.95, f32[2432]{0:T(1024)S(1)} %get-tuple-element.60), kind=kOutput, calls=%fused_computation.69 | convolution fusion | flops 479318016 | bytes 6328064 | tf_op jit(solution)/shard_map/dot_general | solution.py:83
  152.0 0.5 collective-permute-start.1
  152.7 0.8 collective-permute-done.1
  153.4 0.8 broadcast_select_fusion.6
  154.2 23.8 %all-gather.12.cloned.1.call-done = bf16[2432,1536]{1,0:T(8,128)(2,1)} async-done(((bf16[304,1536]{1,0:T(8,128)(2,1)}), bf16[2432,1536]{1,0:T(8,128)(2,1)}) %all-gather.12.cloned.1.call-update) | async-done | bytes 7471120 | tf_op jit(solution)/shard_map/all_gather | solution.py:80
  178.0 8.7 %fusion.26 = f32[512,1536]{0,1:T(8,128)S(1)} fusion(bf16[2432,1536]{1,0:T(8,128)(2,1)} %all-gather.12.cloned.1.call-done, bf16[512,2432]{0,1:T(8,128)(2,1)} %all-gather.10.cloned.1.call-done, f32[2432]{0:T(1024)S(1)} %get-tuple-element.62, f32[2432]{0:T(1024)S(1)} %get-tuple-element.63, f32[512]{0:T(512)S(1)} %get-tuple-element.92, ...), kind=kOutput, calls=%fused_computation.35 | convolution fusion | flops 3832676352 | bytes 13130752 | tf_op jit(solution)/shard_map/dot_general | solution.py:78
  186.9 0.3 multiply_reduce_fusion
  187.2 0.3 collective-permute-start.2
  187.5 0.5 multiply_convert_fusion
  188.0 0.3 collective-permute-start
  188.3 0.8 collective-permute-done.2
  189.3 2.0 concatenate.11
  191.3 1.1 broadcast_select_fusion.2
  192.4 2.2 concatenate.10
  194.6 24.6 %while.10 = (s32[]{:T(128)}, bf16[8,512,64]{1,2,0:T(8,128)(2,1)}, pred[1216]{0:T(1024)(128)(4,1)S(1)}, bf16[8,512,64]{1,2,0:T(8,128)(2,1)S(1)}, bf16[8,1216,64]{...) while((s32[]{:T(128)}, bf16[8,512,64]{1,2,0:T(8,128)(2,1)}, ...), condition=%wide.region_11.12_spmd, body=%wide.region_8.11_spmd.sunk | while | flops 164396032 | bytes 7944269 | solution.py:129
  194.6 0.6 fusion.64
  195.2 0.4 fusion.65
  195.6 2.1 fusion.66
  197.7 0.5 fusion.64
  198.3 0.4 fusion.65
  198.7 2.1 fusion.66
  200.8 0.6 fusion.64
  201.4 0.4 fusion.65
  201.8 2.1 fusion.66
  203.9 0.5 fusion.64
  204.4 0.4 fusion.65
  204.8 2.1 fusion.66
  206.9 0.6 fusion.64
  207.5 0.4 fusion.65
  207.9 2.1 fusion.66
  210.0 0.5 fusion.64
  210.6 0.4 fusion.65
  211.0 2.1 fusion.66
  213.1 0.5 fusion.64
  213.6 0.4 fusion.65
  214.0 2.1 fusion.66
  216.1 0.5 fusion.64
  216.7 0.4 fusion.65
  217.1 2.1 fusion.66
  219.5 0.7 dynamic-slice_reduce_fusion
  220.3 44.7 %all-gather.16.cloned.1.call-done = bf16[512,2048]{0,1:T(8,128)(2,1)} async-done(((bf16[512,512]{0,1:T(8,128)(2,1)}), bf16[512,2048]{0,1:T(8,128)(2,1)}) %all-gather.16.cloned.1.call-update) | async-done | bytes 2097168 | tf_op jit(solution)/shard_map/all_gather | solution.py:134
  265.0 4.6 %fusion.35 = bf16[512,608]{0,1:T(8,128)(2,1)} fusion(bf16[2048,608]{0,1:T(8,128)(2,1)} %all-gather.18.cloned.1.call-done, bf16[512,2048]{0,1:T(8,128)(2,1)} %all-gather.16.cloned.1.call-done, bf16[512,608]{0,1:T(8,128)(2,1)S(1)} %copy-done.2, f32[608]{0:T(1024)S(1)} %dynamic-slice_reduce_fusion), kind=kOutput, calls=%fused_computation.43 | convolution fusion | flops 1276313600 | bytes 5835136 | tf_op jit(solution)/shard_map/dot_general | solution.py:135
  269.7 0.6 dynamic_slice.24
  271.6 9.5 %all-gather.2 = bf16[8,304,64]{1,2,0:T(8,128)(2,1)S(1)} all-gather(bf16[1,304,64]{1,2,0:T(8,128)(2,1)S(1)} %bitcast.119), channel_id=1, replica_groups=mesh['row'=8,'col'=4] {'row'}, dimensions={0}, use_global_device_ids=true | all-gather | bytes 350208 | tf_op jit(solution)/shard_map/all_gather | solution.py:141
  281.8 39.3 %all-gather.20.cloned.1.call-done = bf16[512,2432]{0,1:T(8,128)(2,1)} async-done(((bf16[512,608]{0,1:T(8,128)(2,1)}), bf16[512,2432]{0,1:T(8,128)(2,1)}) %all-gather.20.cloned.1.call-update) | async-done | bytes 2490384 | tf_op jit(solution)/shard_map/all_gather | solution.py:142
  321.1 2.6 convert_reduce_fusion
  323.7 1.8 multiply_add_fusion
  (62 shorter events, 2.6 us)
Async XLA Ops:
  8.0 66.0 %all-reduce.3.cloned.1.call-start = ((), (), s32[]{:S(2)}) async-start(), calls=%async_computation | async-start | bytes 143360 | tf_op jit(solution)/shard_map/psum | solution.py:67
  14.1 6.1 %copy-start.6 = (f32[4,304]{1,0:T(4,128)S(1)}, f32[4,304]{1,0:T(4,128)}, u32[]{:S(2)}) copy-start(f32[4,304]{1,0:T(4,128)} %param.20) | copy-start | bytes 14596
  21.5 2.8 copy-start.1
  21.5 123.4 %all-gather.10.cloned.1.call-start = ((), (), s32[]{:S(2)}) async-start(), calls=%async_computation.1 | async-start | bytes 3112960 | tf_op jit(solution)/shard_map/all_gather | solution.py:71
  22.1 125.2 %all-gather.14.cloned.1.call-start = ((), (), s32[]{:S(2)}) async-start(), calls=%async_computation.3 | async-start | bytes 5603328 | tf_op jit(solution)/shard_map/all_gather | solution.py:85
  22.2 4.0 %copy-start.3 = (bf16[96,608]{1,0:T(8,128)(2,1)S(1)}, bf16[96,608]{1,0:T(8,128)(2,1)}, u32[]{:S(2)}) copy-start(bf16[96,608]{1,0:T(8,128)(2,1)} %param.16) | copy-start | bytes 350212
  24.3 153.8 %all-gather.12.cloned.1.call-start = ((), (), s32[]{:S(2)}) async-start(), calls=%async_computation.2 | async-start | bytes 8404992 | tf_op jit(solution)/shard_map/all_gather | solution.py:80
  25.4 194.9 %all-gather.18.cloned.1.call-start = ((), (), s32[]{:S(2)}) async-start(), calls=%async_computation.5 | async-start | bytes 2801664 | tf_op jit(solution)/shard_map/all_gather | solution.py:137
  26.1 238.9 %all-gather.16.cloned.1.call-start = ((), (), s32[]{:S(2)}) async-start(), calls=%async_computation.4 | async-start | bytes 2621440 | tf_op jit(solution)/shard_map/all_gather | solution.py:134
  47.9 1.1 copy-start.7
  47.9 1.1 copy-start.10
  152.0 1.4 collective-permute-start.1
  152.5 35.8 %collective-permute-start.3 = (bf16[96,8,64]{0,2,1:T(8,128)(2,1)S(1)}, bf16[96,8,64]{0,2,1:T(8,128)(2,1)S(1)}, u32[]{:S(2)}, u32[]{:S(2)}) collective-permute-start(bf16[96,8,64]{0,2,1:T(8,128)(2,1)S(1)} %fusion.48), channel_id=1, source_target_pairs={{0,4},{4,0},{8,12},{12,8},{16,20},{20,16},{24,28},{28,24},{1,5},{5... | collective-permute-start | bytes 294920 | tf_op jit(solution)/shard_map/ppermute | solution.py:19
  186.8 0.7 copy-start.8
  187.2 2.0 collective-permute-start.2
  188.0 3.3 collective-permute-start
  194.6 70.4 %copy-start.2 = (bf16[512,608]{0,1:T(8,128)(2,1)S(1)}, bf16[512,608]{0,1:T(8,128)(2,1)}, u32[]{:S(2)}) copy-start(bf16[512,608]{0,1:T(8,128)(2,1)} %param.15) | copy-start | bytes 1867780
  219.2 101.8 %all-gather.20.cloned.1.call-start = ((), (), s32[]{:S(2)}) async-start(), calls=%async_computation.6 | async-start | bytes 3112960 | tf_op jit(solution)/shard_map/all_gather | solution.py:142
  220.2 49.4 %copy-start.11 = (s32[4]{0:T(128)S(1)}, s32[4]{0:T(128)}, u32[]{:S(2)}) copy-start(s32[4]{0:T(128)} %param.18) | copy-start | bytes 52
  220.2 51.3 %copy-start.4 = (bf16[304,64]{0,1:T(8,128)(2,1)S(1)}, bf16[304,64]{0,1:T(8,128)(2,1)}, u32[]{:S(2)}) copy-start(bf16[304,64]{0,1:T(8,128)(2,1)} %param.27) | copy-start | bytes 116740
  269.6 54.0 %copy-start.5 = (f32[2432]{0:T(1024)S(1)}, f32[2432]{0:T(1024)}, u32[]{:S(2)}) copy-start(f32[2432]{0:T(1024)} %get-tuple-element.64) | copy-start | bytes 29188
  269.6 54.0 %copy-start.9 = (f32[512,64]{0,1:T(8,128)S(1)}, f32[512,64]{0,1:T(8,128)}, u32[]{:S(2)}) copy-start(f32[512,64]{0,1:T(8,128)} %param.19) | copy-start | bytes 393220
  321.1 2.6 copy-start
Sparse Core Ops, SparseCore 0:
  21.7 52.3 all-reduce.2
Sparse Core Ops, SparseCore 1:
  23.6 59.9 all-gather.9
  85.3 40.6 all-gather.13
  127.7 50.3 all-gather.11
  179.9 29.7 all-gather.17
  219.3 45.6 all-gather.15
  269.7 51.3 all-gather.19
where the time goes:
time: 334 us; the launch traced here: 333 us
  waiting for transfers between devices  134 us (40%)
  blocking collectives  58.1 us (17%)
  other arithmetic  55.3 us (17%)
  matrix products  42.2 us (13%)
  local copies, waits for them, and re-layouts  23.9 us (7%)
  between operations  17.3 us (5%)
    all_gather x1, waiting for transfers between devices, per_device(): full_heads = lax.all_gather(attended, 'col', axis=1, tiled=True)  44.7 us
    add x1, other arithmetic, modulate_full(): return (normed * (1.0 + stretch) + offset).astype(jnp.bfloat16)  43 us
    all_gather x1, waiting for transfers between devices, per_device(): residual = lax.all_gather(updated, 'col', axis=1, tiled=True)  39.3 us
    all_gather x1, blocking collectives, per_device(): mod_full = lax.all_gather(mod_own, 'col', axis=1, tiled=True)  26.8 us
    all_gather x1, waiting for transfers between devices, per_device(): lax.all_gather(qkv_flat, 'row', axis=0, tiled=True)  23.8 us
    psum x1, waiting for transfers between devices, per_device(): mod_all = lax.psum(mod_terms, 'row')  23.7 us
    all_gather x1, blocking collectives, per_device(): lax.all_gather(hidden_txt, 'col', axis=1, tiled=True)  21.7 us
    dot_general x8, matrix products, attend(): jnp.dot(probabilities, v_head, preferred_element_type=jnp.float32)  16.9 us
  transfers between devices with their start and end apart: 11, of which 6 were waited for; matrix products, arithmetic and copies ran while one was open for 30% of the time, Pallas kernels for 0%

commit v1 on v0

v1 whole, which is shorter than its diff:
```python
import functools

import jax
import jax.numpy as jnp
from jax import lax
from jax.experimental import pallas as pl
from jax.experimental.pallas import tpu as pltpu
from jax.sharding import PartitionSpec as P

STEPS = 28
EPS_NORM = 1e-06
F32 = jnp.float32
BF16 = jnp.bfloat16
VMEM_LIMIT = 48 * 1024 * 1024
ANY = pl.BlockSpec(memory_space=pl.ANY)
VMEM = pl.BlockSpec(memory_space=pltpu.VMEM)
SMEM = pl.BlockSpec(memory_space=pltpu.SMEM)


def swap(block, axis, mask):
    count = lax.axis_size(axis)
    return lax.ppermute(block, axis, [(i, i ^ mask) for i in range(count)])


def shift(block, axis, step):
    count = lax.axis_size(axis)
    route = [(i, i + step) for i in range(count) if 0 <= i + step < count]
    return lax.ppermute(block, axis, route)


def line_gather(block, axis):
    held = {0: block}
    for step in range(1, lax.axis_size(axis)):
        held[-step] = shift(held[1 - step], axis, 1)
        held[step] = shift(held[step - 1], axis, -1)
    return held


def doubling_gather(block, axis, masks):
    held = {0: block}
    for mask in masks:
        for known in list(held):
            held[known | mask] = swap(held[known], axis, mask)
    return held


def in_line(held, axis):
    offsets, count = sorted(held), lax.axis_size(axis)
    rows = held[0].shape[0]
    if rows % 16 == 0:
        return [held[k] for k in offsets], offsets, count
    joined = jnp.concatenate([held[k] for k in offsets], axis=0)
    first = (count - 1 - lax.axis_index(axis)) * rows
    return [lax.dynamic_slice_in_dim(joined, first, count * rows, 0)], [None], 1


def in_order(held, axis):
    masks, count = sorted(held), lax.axis_size(axis)
    rows = held[0].shape[0]
    if rows % 16 == 0:
        return [held[k] for k in masks], masks
    joined = jnp.stack([held[k] for k in masks])
    order = jnp.bitwise_xor(jnp.arange(count), lax.axis_index(axis))
    return [joined[order].reshape((count * rows,) + joined.shape[2:])], [None]


def cost(flops, touched, exps=0):
    return pl.CostEstimate(flops=flops, bytes_accessed=touched, transcendentals=exps)


def call(kernel, outs, in_specs, scratch, estimate, out_specs=None):
    if out_specs is None:
        out_specs = jax.tree.map(lambda _: VMEM, outs)
    return pl.pallas_call(
        kernel,
        out_shape=outs,
        in_specs=in_specs,
        out_specs=out_specs,
        scratch_shapes=scratch,
        cost_estimate=estimate,
        compiler_params=pltpu.CompilerParams(vmem_limit_bytes=VMEM_LIMIT),
    )


def line_copies(refs, offsets, place, count, target, sems, act):
    for n, (ref, offset) in enumerate(zip(refs, offsets)):
        owner = 0 if offset is None else place + offset

        @pl.when((owner >= 0) & (owner < count))
        def _():
            copy = pltpu.make_async_copy(ref, target(owner), sems.at[n])
            getattr(copy, act)()


def mod_kernel(cond_ref, w_ref, out_ref):
    values = cond_ref[...]
    activated = (values * (1.0 / (1.0 + jnp.exp(-values)))).astype(BF16)
    for group in range(w_ref.shape[0]):
        out_ref[:, group, :] = jnp.dot(activated, w_ref[group], preferred_element_type=F32)


def norm_kernel(offsets, count, img, place_ref, mod_ref, *refs):
    blocks = refs[: len(offsets)]
    out_ref, x_ref, sems = refs[len(offsets) :]
    width, tokens = blocks[0].shape
    place = place_ref[1]
    target = lambda owner: x_ref.at[pl.ds(pl.multiple_of(owner * width, 16), width)]
    line_copies(blocks, offsets, place, count, target, sems, "start")
    line_copies(blocks, offsets, place, count, target, sems, "wait")
    rows = 16
    total = width * count

    def gather_stats(i, carry):
        part = x_ref[pl.ds(pl.multiple_of(i * rows, rows), rows)].astype(F32)
        sums, squares = carry
        for r in range(0, rows, 8):
            piece = part[r : r + 8]
            sums += piece
            squares += piece * piece
        return sums, squares

    zero = jnp.zeros((8, tokens), F32)
    sums, squares = lax.fori_loop(0, total // rows, gather_stats, (zero, zero), unroll=4)
    average = jnp.sum(sums, axis=0, keepdims=True) / total
    mean_square = jnp.sum(squares, axis=0, keepdims=True) / total
    inverse = lax.rsqrt(mean_square - average * average + EPS_NORM)
    shape = (rows, tokens)
    average = jnp.broadcast_to(average, shape)
    inverse = jnp.broadcast_to(inverse, shape)

    for owner in range(count):
        slot = 0 if count == 1 else jnp.bitwise_xor(owner, place)

        def normalise(i, _):
            at = pl.multiple_of(i * rows, rows)
            mod = mod_ref[slot, pl.ds(at, rows), :]
            here = pl.ds(pl.multiple_of(owner * width + i * rows, rows), rows)
            normed = (x_ref[here].astype(F32) - average) * inverse
            out_ref[here, :img] = (normed[:, :img] * mod[:, 1:2] + mod[:, 0:1]).astype(BF16)
            out_ref[here, img:] = (normed[:, img:] * mod[:, 4:5] + mod[:, 3:4]).astype(BF16)
            return 0

        lax.fori_loop(0, width // rows, normalise, 0, unroll=2)


def project_kernel(masks, img, head, place_ref, q_gain_ref, k_gain_ref, x_ref, *refs):
    blocks = refs[: len(masks)]
    q_ref, kv_ref, w_ref, sems = refs[len(masks) :]
    depth = blocks[0].shape[0]
    half = q_ref.shape[0]
    place = place_ref[0]
    copies = []
    for n, (ref, mask) in enumerate(zip(blocks, masks)):
        owner = 0 if mask is None else jnp.bitwise_xor(place, mask)
        copies.append(
            pltpu.make_async_copy(
                ref, w_ref.at[pl.ds(pl.multiple_of(owner * depth, 16), depth)], sems.at[n]
            )
        )
    for copy in copies:
        copy.start()
    for copy in copies:
        copy.wait()

    def product(part, low, high):
        return lax.dot_general(
            w_ref[:, part * half : (part + 1) * half],
            x_ref[:, low:high],
            (((0,), (0,)), ((), ())),
            preferred_element_type=F32,
        )

    def head_norm(values, gain):
        cols = values.shape[1]
        split = values.reshape(half // head, head, cols)
        mean_square = jnp.mean(split * split, axis=1, keepdims=True)
        normed = split * lax.rsqrt(mean_square + EPS_NORM) * gain[None]
        return normed.reshape(half, cols)

    tokens = x_ref.shape[1]
    scaling = head ** (-0.5)
    queries = head_norm(product(0, 0, img), q_gain_ref[...]).astype(BF16)
    q_ref[...] = (queries.astype(F32) * scaling).astype(BF16)
    kv_ref[:half, :img] = head_norm(product(1, 0, img), k_gain_ref[:, 0:1]).astype(BF16)
    kv_ref[half:, :img] = product(2, 0, img).astype(BF16)
    kv_ref[:half, img:] = head_norm(product(3, img, tokens), k_gain_ref[:, 1:2]).astype(BF16)
    kv_ref[half:, img:] = product(4, img, tokens).astype(BF16)


def attend_kernel(img, head, place_ref, q_ref, own_ref, peer_ref, out_ref, k_ref, v_ref):
    half, queries = q_ref.shape
    txt = own_ref.shape[1] - img
    room = (txt + 127) // 128 * 128
    side = lax.rem(place_ref[0], 2)
    length = place_ref[2]
    keys = 2 * img + 2 * room
    k_ref[:, 2 * img :] = jnp.zeros((half, 2 * room), BF16)
    v_ref[:, 2 * img :] = jnp.zeros((half, 2 * room), BF16)
    for n, ref in enumerate((own_ref, peer_ref)):
        at, tail = n * img, 2 * img + n * room
        k_ref[:, at : at + img] = ref[:half, :img]
        v_ref[:, at : at + img] = ref[half:, :img]
        k_ref[:, tail : tail + txt] = ref[:half, img:]
        v_ref[:, tail : tail + txt] = ref[half:, img:]
    slot = lax.broadcasted_iota(jnp.int32, (2 * room, 1), 0)
    second = (slot >= room).astype(jnp.int32)
    inside = slot - second * room
    owner = jnp.where(second == 1, 1 - side, side)
    allowed = (inside < txt) & (owner * txt + inside < length)
    step = 256 if queries % 256 == 0 else queries

    def one(i, _):
        at = pl.multiple_of(i * head, head)
        for low in range(0, queries, step):
            scores = lax.dot_general(
                k_ref[pl.ds(at, head)],
                q_ref[pl.ds(at, head), low : low + step],
                (((0,), (0,)), ((), ())),
                preferred_element_type=F32,
            )
            tail = jnp.where(allowed, scores[2 * img :], -1e30)
            scores = jnp.concatenate([scores[: 2 * img], tail], axis=0)
            weights = jnp.exp(scores - jnp.max(scores, axis=0, keepdims=True))
            inverse = 1.0 / jnp.sum(weights, axis=0, keepdims=True)
            mixed = jnp.dot(
                v_ref[pl.ds(at, head)], weights.astype(BF16), preferred_element_type=F32
            )
            out_ref[pl.ds(at, head), low : low + step] = (mixed * inverse).astype(BF16)
        return 0

    lax.fori_loop(0, half // head, one, 0)


def output_kernel(
    offsets, count, masks, place_ref, gate_ref, out_mod_ref, x_ref, *refs
):
    n_lines = len(offsets)
    firsts, refs = refs[:n_lines], refs[n_lines:]
    seconds, refs = refs[:n_lines], refs[n_lines:]
    weights, refs = refs[: len(masks)], refs[len(masks) :]
    out_ref, a_ref, w_ref, sems_a, sems_b, sems_w = refs
    width, tokens = x_ref.shape
    half = firsts[0].shape[0]
    place = place_ref[0]
    col = place_ref[1]
    copies = []
    for n, (ref, mask) in enumerate(zip(weights, masks)):
        owner = jnp.bitwise_xor(place, mask)
        copies.append(pltpu.make_async_copy(ref, w_ref.at[owner], sems_w.at[n]))
    for copy in copies:
        copy.start()
    lines = ((firsts, 0, sems_a), (seconds, 1, sems_b))
    for act in ("start", "wait"):
        for blocks, n, sems in lines:
            target = lambda owner, n=n: a_ref.at[
                pl.ds(pl.multiple_of((2 * owner + n) * half, half), half)
            ]
            line_copies(blocks, offsets, col, count, target, sems, act)
    for copy in copies:
        copy.wait()
    depth = w_ref.shape[2]
    blocks = w_ref.shape[0]

    projected = jnp.zeros((width, tokens), F32)
    for n in range(blocks):
        projected += jnp.dot(
            w_ref[n, :width], a_ref[n * depth : (n + 1) * depth], preferred_element_type=F32
        )
    updated = (x_ref[...].astype(F32) + gate_ref[...] * projected).astype(BF16)
    wide = updated.astype(F32)
    sums = jnp.sum(wide, axis=0, keepdims=True)
    squares = jnp.sum(wide * wide, axis=0, keepdims=True)

    per_col = blocks // count
    slab = width // per_col
    patch = out_ref.shape[0] - 8
    result = jnp.zeros((patch, tokens), F32)
    gains = jnp.zeros((patch, 1), F32)
    shifts = jnp.zeros((patch, 1), F32)
    for n in range(per_col):
        owner = col * per_col + n
        pieces = [
            w_ref[owner, width + k * patch : width + (k + 1) * patch]
            for k in range((w_ref.shape[1] - width) // patch)
        ]
        for k, piece in enumerate(pieces):
            low, high = k * depth, min((k + 1) * depth, slab)
            if low >= high:
                continue
            linear = piece[:, : high - low].astype(F32)
            gained = linear * (1.0 + out_mod_ref[n, 1:2, low:high])
            shifts += jnp.sum(linear * out_mod_ref[n, 0:1, low:high], axis=1, keepdims=True)
            gains += jnp.sum(gained, axis=1, keepdims=True)
            part = updated[n * slab + low : n * slab + high]
            for _ in range(3):
                term = gained.astype(BF16)
                result += jnp.dot(term, part, preferred_element_type=F32)
                gained = gained - term.astype(F32)
    out_ref[:patch, :tokens] = result
    row = lax.broadcasted_iota(jnp.int32, (8, tokens), 0)
    out_ref[patch:, :tokens] = jnp.where(row == 0, sums, jnp.where(row == 1, squares, 0.0))
    lane = lax.broadcasted_iota(jnp.int32, (patch, 128), 1)
    out_ref[:patch, tokens:] = jnp.where(lane == 0, gains, jnp.where(lane == 1, shifts, 0.0))
    out_ref[patch:, tokens:] = jnp.zeros((8, 128), F32)


def sigma_of(step_now):
    remain = 1.0 - step_now.astype(F32) / STEPS
    return 3.0 * remain / (1.0 + 2.0 * remain)


def per_device(
    hidden_img,
    hidden_txt,
    text_len,
    step_index,
    latent,
    cond,
    mod_weight,
    qkv_weight,
    kv_text_weight,
    q_gain,
    k_gain,
    out_weight,
    final_weight,
):
    row_count, col_count = lax.axis_size("row"), lax.axis_size("col")
    row_pos, col_pos = lax.axis_index("row"), lax.axis_index("col")
    request = row_pos // 2
    requests = cond.shape[0]
    img, width = hidden_img.shape
    txt = hidden_txt.shape[0]
    tokens = img + txt
    head = q_gain.shape[0]
    part_cols = qkv_weight.shape[2]
    half = part_cols // 2
    full_width = width * col_count
    length = lax.dynamic_index_in_dim(text_len, request, 0, keepdims=False)
    place = jnp.stack([row_pos, col_pos, length]).astype(jnp.int32)

    chip_masks = [1 << bit for bit in range(1, row_count.bit_length() - 1)]
    gathered = []
    packed = []
    for n in range(2):
        cols = slice(n * half, (n + 1) * half)
        packed.append(
            jnp.concatenate(
                [qkv_weight[:, k, cols] for k in range(3)]
                + [kv_text_weight[:, k, cols] for k in range(2)],
                axis=1,
            )
        )
    x_own = jnp.concatenate([hidden_img.T, hidden_txt.T], axis=1)
    x_blocks = line_gather(x_own, "col")
    for n in range(2):
        order = chip_masks[::-1] if n == 0 else chip_masks
        gathered.append(doubling_gather(packed[n], "row", order + [1]))

    mod_part = call(
        mod_kernel,
        jax.ShapeDtypeStruct((requests, 7, width), F32),
        [VMEM, VMEM],
        [],
        cost(2 * requests * cond.shape[1] * 7 * width, mod_weight.size * 2),
    )(cond, jnp.moveaxis(mod_weight, 1, 0))
    mask = row_count // 2
    while mask > 1:
        bit = (row_pos // mask) % 2
        pair = mod_part.reshape((2, mod_part.shape[0] // 2) + mod_part.shape[1:])
        keep = lax.dynamic_index_in_dim(pair, bit, 0, keepdims=False)
        give = lax.dynamic_index_in_dim(pair, 1 - bit, 0, keepdims=False)
        mod_part = keep + swap(give, "row", mask)
        mask //= 2
    mod_part = mod_part[0]
    mod_own = mod_part + swap(mod_part, "row", 1)
    norm_mod = mod_own[:5] + jnp.array([0.0, 1.0, 0.0, 0.0, 1.0], F32)[:, None]
    norm_mod = norm_mod[None]
    mask = 1
    while mask < col_count:
        norm_mod = jnp.concatenate([norm_mod, swap(norm_mod, "col", mask)], axis=0)
        mask *= 2
    norm_mod = jnp.swapaxes(norm_mod, 1, 2)

    x_blocks, offsets, count = in_line(x_blocks, "col")
    if count == 1:
        norm_mod = norm_mod[jnp.bitwise_xor(jnp.arange(col_count), col_pos)]
        norm_mod = norm_mod.reshape(1, full_width, 5)
    ready = call(
        functools.partial(norm_kernel, offsets, count, img),
        jax.ShapeDtypeStruct((full_width, tokens), BF16),
        [SMEM, VMEM] + [ANY] * len(offsets),
        [pltpu.VMEM((full_width, tokens), BF16), pltpu.SemaphoreType.DMA((len(offsets),))],
        cost(12 * full_width * tokens, 4 * full_width * tokens),
    )(place, norm_mod, *x_blocks)

    attended = []
    for n in range(2):
        blocks, masks = in_order(gathered[n], "row")
        queries, pair = call(
            functools.partial(project_kernel, masks, img, head),
            (
                jax.ShapeDtypeStruct((half, img), BF16),
                jax.ShapeDtypeStruct((2 * half, tokens), BF16),
            ),
            [SMEM, VMEM, VMEM, VMEM] + [ANY] * len(masks),
            [pltpu.VMEM((full_width, 5 * half), BF16), pltpu.SemaphoreType.DMA((len(masks),))],
            cost(2 * full_width * half * (3 * img + 2 * txt), 10 * full_width * half),
            (VMEM, VMEM),
        )(place, q_gain[:, None], k_gain.T, ready, *blocks)
        peer = swap(pair, "row", 1)
        keys = 2 * img + 2 * ((txt + 127) // 128 * 128)
        attended.append(
            call(
                functools.partial(attend_kernel, img, head),
                jax.ShapeDtypeStruct((half, img), BF16),
                [SMEM, VMEM, VMEM, VMEM],
                [pltpu.VMEM((half, keys), BF16)] * 2,
                cost(4 * half * keys * img, 8 * half * keys, keys * img * half // head),
            )(place, queries, pair, peer)
        )

    head_depth, patch = final_weight.shape
    depth = out_weight.shape[0]
    folds = -(-head_depth // depth)
    tail = jnp.pad(final_weight.T, ((0, 0), (0, folds * depth - head_depth)))
    tail = jnp.swapaxes(tail.reshape(patch, folds, depth), 0, 1).reshape(folds * patch, depth)
    out_packed = jnp.concatenate([out_weight.T, tail], axis=0)
    out_blocks = doubling_gather(out_packed, "row", [1] + chip_masks)
    masks = sorted(out_blocks)
    offsets = list(range(1 - col_count, col_count))
    lines = [line_gather(block, "col") for block in attended]
    per_col = row_count // col_count
    out_mod = mod_own[5:7].reshape(2, per_col, width // per_col).swapaxes(0, 1)
    partial_sum = call(
        functools.partial(output_kernel, offsets, col_count, masks),
        jax.ShapeDtypeStruct((patch + 8, img + 128), F32),
        [SMEM, VMEM, VMEM, VMEM] + [ANY] * (2 * len(offsets) + len(masks)),
        [
            pltpu.VMEM((part_cols * col_count, img), BF16),
            pltpu.VMEM((row_count,) + out_packed.shape, BF16),
            pltpu.SemaphoreType.DMA((len(offsets),)),
            pltpu.SemaphoreType.DMA((len(offsets),)),
            pltpu.SemaphoreType.DMA((len(masks),)),
        ],
        cost(2 * part_cols * col_count * width * img, 8 * part_cols * col_count * width),
    )(
        place,
        mod_own[2][:, None],
        out_mod,
        hidden_img.T,
        *[line[k] for line in lines for k in offsets],
        *[out_blocks[k] for k in masks],
    )
    mask = 1
    while mask < col_count:
        partial_sum = partial_sum + swap(partial_sum, "col", mask)
        mask *= 2
    average = partial_sum[patch : patch + 1, :img] / full_width
    mean_square = partial_sum[patch + 1 : patch + 2, :img] / full_width
    inverse = lax.rsqrt(mean_square - average * average + EPS_NORM)
    gains = partial_sum[:patch, img : img + 1]
    shifts = partial_sum[:patch, img + 1 : img + 2]
    velocity = inverse * (partial_sum[:patch, :img] - average * gains) + shifts
    step_now = lax.dynamic_index_in_dim(step_index, request, 0, keepdims=False)
    sigma_step = sigma_of(step_now + 1) - sigma_of(step_now)
    latent_next = latent.T + sigma_step * velocity
    return (velocity.T, latent_next.T)


def solution(mesh):
    in_specs = (
        P("row", "col"),
        P("row", "col"),
        P(),
        P(),
        P("row", None),
        P(None, "row"),
        P("row", None, "col"),
        P("row", None, "col"),
        P("row", None, "col"),
        P(),
        P(),
        P("row", "col"),
        P("row", None),
    )
    out_specs = (P("row", None), P("row", None))
    return jax.shard_map(
        per_device, mesh=mesh, in_specs=in_specs, out_specs=out_specs, check_vma=False
    )
```

time: 334 us -> 250 us (0.75)
  starting transfers between devices: 1.8 us -> 75 us
  blocking collectives: 58.1 us -> 0 us
  waiting for transfers between devices: 134 us -> 76.7 us
  Pallas kernels: 0 us -> 49.6 us
  other arithmetic: 55.3 us -> 7.74 us
  matrix products: 42.2 us -> 0 us
  between operations: 17.3 us -> 2.82 us
  local copies, waits for them, and re-layouts: 23.9 us -> 36.9 us
    all_gather x6 -> x0, waiting for transfers between devices: 108 us -> none  [the longest x1 44.7 us: per_device(): full_heads = lax.all_gather(attended, 'col', axis=1, tiled=True)]
    ppermute x4 -> x48, waiting for transfers between devices: 1.57 us -> 76.7 us  [the longest x30 63.4 us: swap(): return lax.ppermute(block, axis, [(i, i ^ mask) for i in range(count)])]
    ppermute x4 -> x48, starting transfers between devices: 1.28 us -> 75 us  [the longest x18 53.9 us: shift(): return lax.ppermute(block, axis, route)]
    all_gather x3 -> x0, blocking collectives: 58.1 us -> none  [the longest x1 26.8 us: per_device(): mod_full = lax.all_gather(mod_own, 'col', axis=1, tiled=True)]
    pallas_call x0 -> x7, Pallas kernels: none -> 49.6 us  [the longest x2 16.2 us: per_device(): call(functools.partial(project_kernel, masks, img, head), (jax.ShapeDtype...]
    dot_general x21 -> x0, matrix products: 42.2 us -> none  [the longest x8 16.9 us: attend(): jnp.dot(probabilities, v_head, preferred_element_type=jnp.float32)]
    add x1 -> x4, other arithmetic: 43 us -> 1.41 us  [the longest x1 1.33 us: per_device(): mod_part = keep + swap(give, 'row', mask)]
    psum x1 -> x0, waiting for transfers between devices: 23.7 us -> none  [per_device(): mod_all = lax.psum(mod_terms, 'row')]
  transfers between devices with their start and end apart: 11 -> 48, of which waited for: 6 -> 13; matrix products, arithmetic and copies ran while one was open for 30% -> 11% of each run, Pallas kernels for 0% -> 18%
where the time goes in v1:
time: 250 us; the launch traced here: 249 us
  waiting for transfers between devices  76.7 us (31%)
  starting transfers between devices  75 us (30%)
  Pallas kernels  49.6 us (20%)
  local copies, waits for them, and re-layouts  36.9 us (15%)
  other arithmetic  7.74 us (3%)
  between operations  2.82 us (1%)
    ppermute x30, waiting for transfers between devices, swap(): return lax.ppermute(block, axis, [(i, i ^ mask) for i in range(count)])  63.4 us
    ppermute x18, starting transfers between devices, shift(): return lax.ppermute(block, axis, route)  53.9 us
    ppermute x30, starting transfers between devices, swap(): return lax.ppermute(block, axis, [(i, i ^ mask) for i in range(count)])  21 us
    unnamed x86, local copies, waits for them, and re-layouts  19.3 us
    pallas_call x2, Pallas kernels, per_device(): call(functools.partial(project_kernel, masks, img, head), (jax.ShapeDtype...  16.2 us
    pallas_call x2, Pallas kernels, per_device(): call(functools.partial(attend_kernel, img, head), jax.ShapeDtypeStruct((h...  14.6 us
    ppermute x18, waiting for transfers between devices, shift(): return lax.ppermute(block, axis, route)  13.2 us
    pallas_call x1, Pallas kernels, per_device(): call(functools.partial(norm_kernel, offsets, count, img), jax.ShapeDtypeS...  12.8 us
  transfers between devices with their start and end apart: 48, of which 13 were waited for; matrix products, arithmetic and copies ran while one was open for 11% of the time, Pallas kernels for 18%

profile of v1, /device:TPU:0, one launch (start us, length us, event | category | flops | bytes accessed | tf_op | source)
XLA Modules:
  0.0 248.7 jit_solution(3355168569090375806)
XLA Ops:
  0.6 1.1 copy.92
  1.7 1.1 pad_maximum_fusion.refs_3_
  2.8 1.3 collective-permute-start.8
  4.1 6.4 %collective-permute-start.5 = (bf16[608,608]{1,0:T(8,128)(2,1)S(1)}, bf16[608,608]{1,0:T(8,128)(2,1)}, u32[]{:S(2)}, u32[]{:S(2)}) collective-permute-start(bf16[608,608]{1,0:T(8,128)(2,1)S(1)} %pad_maximum_fusion.refs_3_), channel_id=1, source_target_pairs={{0,1},{1,2},{2,3},{4,5},{5,6},{6,7},{8,9},{9,10},{10,11},{12,13},{... | collective-permute-start | bytes 2217992 | tf_op jit(solution)/shard_map/ppermute | solution.py:28
  10.6 1.8 copy-done
  12.9 2.0 collective-permute-start
  14.9 1.9 fusion.10
  16.9 1.0 bitcast_dynamic-update-slice_fusion.2
  17.9 1.1 copy.107
  19.0 1.1 copy.85
  20.1 1.3 bitcast_add_fusion
  22.3 1.5 collective-permute-start.1
  23.8 1.0 bitcast_dynamic-update-slice_fusion.1
  24.8 5.9 %collective-permute-done.1 = f32[1,7,608]{1,2,0:T(8,128)S(1)} collective-permute-done((f32[1,7,608]{1,2,0:T(8,128)}, f32[1,7,608]{1,2,0:T(8,128)S(1)}, u32[]{:S(2)}, u32[]{:S(2)}) %collective-permute-start.1) | collective-permute-done | bytes 17056 | tf_op jit(solution)/shard_map/ppermute | solution.py:22
  30.7 1.0 add_bitcast_fusion
  31.8 1.0 bitcast_dynamic-update-slice_fusion
  34.5 8.6 %collective-permute-done.3 = f32[1,5,608]{1,2,0:T(8,128)} collective-permute-done((f32[1,5,608]{1,2,0:T(8,128)S(1)}, f32[1,5,608]{1,2,0:T(8,128)}, u32[]{:S(2)}, u32[]{:S(2)}) %collective-permute-start.3) | collective-permute-done | bytes 12192 | tf_op jit(solution)/shard_map/ppermute | solution.py:22
  43.1 1.1 copy.90
  44.2 1.9 collective-permute-start.4
  47.1 1.6 collective-permute-start.26
  51.4 1.4 collective-permute-start.14
  53.4 14.1 %collective-permute-done.26.refs_2_ = bf16[304,1280]{1,0:T(8,128)(2,1)S(1)} collective-permute-done((bf16[304,1280]{1,0:T(8,128)(2,1)S(1)}, bf16[304,1280]{1,0:T(8,128)(2,1)S(1)}, u32[]{:S(2)}, u32[]{:S(2)}) %collective-permute-start.26) | collective-permute-done | bytes 778272 | tf_op jit(solution)/shard_map/ppermute | solution.py:22
  67.5 1.3 collective-permute-start.9
  70.7 4.5 %collective-permute-start.6 = (bf16[608,608]{1,0:T(8,128)(2,1)}, bf16[608,608]{1,0:T(8,128)(2,1)S(1)}, u32[]{:S(2)}, u32[]{:S(2)}) collective-permute-start(bf16[608,608]{1,0:T(8,128)(2,1)} %collective-permute-done.5.refs_2_), channel_id=1, source_target_pairs={{0,1},{1,2},{2,3},{4,5},{5,6},{6,7},{8,9},{9,10},{10,11},{12,13},{... | collective-permute-start | bytes 2217992 | tf_op jit(solution)/shard_map/ppermute | solution.py:28
  75.1 10.6 %collective-permute-done.14.refs_4_ = bf16[304,1280]{1,0:T(8,128)(2,1)} collective-permute-done((bf16[304,1280]{1,0:T(8,128)(2,1)S(1)}, bf16[304,1280]{1,0:T(8,128)(2,1)}, u32[]{:S(2)}, u32[]{:S(2)}) %collective-permute-start.14) | collective-permute-done | bytes 778272 | tf_op jit(solution)/shard_map/ppermute | solution.py:22
  88.6 1.3 collective-permute-start.10
  90.8 9.4 %collective-permute-done.30.refs_6_ = bf16[304,1280]{1,0:T(8,128)(2,1)} collective-permute-done((bf16[304,1280]{1,0:T(8,128)(2,1)S(1)}, bf16[304,1280]{1,0:T(8,128)(2,1)}, u32[]{:S(2)}, u32[]{:S(2)}) %collective-permute-start.30) | collective-permute-done | bytes 778272 | tf_op jit(solution)/shard_map/ppermute | solution.py:22
  100.1 2.5 %collective-permute-start.7 = (bf16[608,608]{1,0:T(8,128)(2,1)S(1)}, bf16[608,608]{1,0:T(8,128)(2,1)S(1)}, u32[]{:S(2)}, u32[]{:S(2)}) collective-permute-start(bf16[608,608]{1,0:T(8,128)(2,1)S(1)} %collective-permute-done.6.refs_1_), channel_id=1, source_target_pairs={{0,1},{1,2},{2,3},{4,5},{5,6},{6,7},{8,9},{9,10},{10,11},{12,13},{... | collective-permute-start | bytes 2217992 | tf_op jit(solution)/shard_map/ppermute | solution.py:28
  105.9 1.7 collective-permute-done.16.refs_6_
  107.6 1.8 collective-permute-done.10.refs_6_
  110.4 7.2 %collective-permute-done.7.refs_0_ = bf16[608,608]{1,0:T(8,128)(2,1)S(1)} collective-permute-done((bf16[608,608]{1,0:T(8,128)(2,1)S(1)}, bf16[608,608]{1,0:T(8,128)(2,1)S(1)}, u32[]{:S(2)}, u32[]{:S(2)}) %collective-permute-start.7) | collective-permute-done | bytes 739360 | tf_op jit(solution)/shard_map/ppermute | solution.py:28
  120.0 1.1 copy.91
  121.1 2.5 %maximum_bitcast_fusion.mod_ref = f32[4,608,5]{2,1,0:T(8,128)} fusion(f32[2,5,608]{1,2,0:T(8,128)} %copy.91, f32[1,5,608]{1,2,0:T(8,128)} %collective-permute-done.3, f32[1,5,608]{1,2,0:T(8,128)} %copy-done.26), kind=kLoop, calls=%fused_computation | loop fusion | flops 24320 | bytes 97280 | tf_op jit(solution)/shard_map/transpose | solution.py:382
  123.7 1.1 copy-done.18
  124.8 12.8 %shard_map.150.x_ref = bf16[2432,608]{1,0:T(8,128)(2,1)} custom-call(s32[3]{0:T(128)S(1)} %pad_add_fusion.place_ref, f32[4,608,5]{2,1,0:T(8,128)} %maximum_bitcast_fusion.mod_ref, bf16[608,608]{1,0:T(8,128)(2,1)S(1)} %copy-done.18, bf16[608,608]{1,0:T(8,128)(2,1)S(1)} %copy-done.14, bf16[608,608]{1,0:T(8,128)(2,1)} %collective-permute-done.5.refs_2_, ...), custom_call_target="tpu_custom_call" | custom-call | flops 17743872 | bytes 5914624 | tf_op jit(solution)/shard_map/pallas_call | solution.py:388
  137.7 8.4 %shard_map.153 = (bf16[256,512]{1,0:T(8,128)(2,1)S(1)}, bf16[512,608]{1,0:T(8,128)(2,1)S(1)}) custom-call(s32[3]{0:T(128)S(1)} %pad_add_fusion.place_ref, f32[64,1]{1,0:T(8,128)S(1)} %copy.95.q_gain_ref, f32[64,2]{1,0:T(8,128)S(1)} %bitcast.73, bf16[2432,608]{1,0:T(8,128)(2,1)} %shard_map.150.x_ref, bf16[304,1280]{1,0:T(8,128)(2,1)S(1)} %fusion.1.refs_0_, ...), custom_call_target="tpu_custom_call" | custom-call | flops 2151677952 | bytes 6225920 | tf_op jit(solution)/shard_map/pallas_call | solution.py:399
  146.2 1.1 copy.101
  147.9 7.8 %shard_map.151 = (bf16[256,512]{1,0:T(8,128)(2,1)S(1)}, bf16[512,608]{1,0:T(8,128)(2,1)S(1)}) custom-call(s32[3]{0:T(128)S(1)} %pad_add_fusion.place_ref, f32[64,1]{1,0:T(8,128)S(1)} %copy.95.q_gain_ref, f32[64,2]{1,0:T(8,128)S(1)} %bitcast.74, bf16[2432,608]{1,0:T(8,128)(2,1)} %shard_map.150.x_ref, bf16[304,1280]{1,0:T(8,128)(2,1)S(1)} %fusion.3.refs_0_, ...), custom_call_target="tpu_custom_call" | custom-call | flops 2151677952 | bytes 6225920 | tf_op jit(solution)/shard_map/pallas_call | solution.py:399
  155.7 1.1 copy.96
  158.5 1.5 collective-permute-start.41
  160.0 1.3 collective-permute-start.43
  161.3 1.4 copy.102.peer_ref
  163.7 7.3 %shard_map.154.refs_10_ = bf16[256,512]{1,0:T(8,128)(2,1)S(1)} custom-call(s32[3]{0:T(128)S(1)} %pad_add_fusion.place_ref, bf16[256,512]{1,0:T(8,128)(2,1)S(1)} %copy-done.21, bf16[512,608]{1,0:T(8,128)(2,1)S(1)} %get-tuple-element.9.own_ref, bf16[512,608]{1,0:T(8,128)(2,1)S(1)} %copy.102.peer_ref), custom_call_target="tpu_custom_call" | custom-call | flops 671088640 | bytes 2621440 | tf_op jit(solution)/shard_map/pallas_call | solution.py:413
  171.0 4.0 %collective-permute-start.33 = (bf16[256,512]{1,0:T(8,128)(2,1)S(1)}, bf16[256,512]{1,0:T(8,128)(2,1)S(1)}, u32[]{:S(2)}, u32[]{:S(2)}) collective-permute-start(bf16[256,512]{1,0:T(8,128)(2,1)S(1)} %shard_map.154.refs_10_), channel_id=1, source_target_pairs={{0,1},{1,2},{2,3},{4,5},{5,6},{6,7},{8,9},{9,10},{10,11},{12,13},{... | collective-permute-start | bytes 786440 | tf_op jit(solution)/shard_map/ppermute | solution.py:28
  175.0 1.4 copy.97.peer_ref
  177.3 7.3 %shard_map.152.refs_3_ = bf16[256,512]{1,0:T(8,128)(2,1)S(1)} custom-call(s32[3]{0:T(128)S(1)} %pad_add_fusion.place_ref, bf16[256,512]{1,0:T(8,128)(2,1)S(1)} %copy-done.23, bf16[512,608]{1,0:T(8,128)(2,1)S(1)} %get-tuple-element.7.own_ref, bf16[512,608]{1,0:T(8,128)(2,1)S(1)} %copy.97.peer_ref), custom_call_target="tpu_custom_call" | custom-call | flops 671088640 | bytes 2621440 | tf_op jit(solution)/shard_map/pallas_call | solution.py:413
  184.6 1.3 collective-permute-start.36
  185.9 4.6 %collective-permute-start.19 = (bf16[256,512]{1,0:T(8,128)(2,1)S(1)}, bf16[256,512]{1,0:T(8,128)(2,1)S(1)}, u32[]{:S(2)}, u32[]{:S(2)}) collective-permute-start(bf16[256,512]{1,0:T(8,128)(2,1)S(1)} %shard_map.152.refs_3_), channel_id=1, source_target_pairs={{0,1},{1,2},{2,3},{4,5},{5,6},{6,7},{8,9},{9,10},{10,11},{12,13},{... | collective-permute-start | bytes 786440 | tf_op jit(solution)/shard_map/ppermute | solution.py:28
  190.5 1.3 collective-permute-start.22
  192.6 4.6 %collective-permute-start.34 = (bf16[256,512]{1,0:T(8,128)(2,1)S(1)}, bf16[256,512]{1,0:T(8,128)(2,1)S(1)}, u32[]{:S(2)}, u32[]{:S(2)}) collective-permute-start(bf16[256,512]{1,0:T(8,128)(2,1)S(1)} %collective-permute-done.33.refs_9_), channel_id=1, source_target_pairs={{0,1},{1,2},{2,3},{4,5},{5,6},{6,7},{8,9},{9,10},{10,11},{12,13},{... | collective-permute-start | bytes 786440 | tf_op jit(solution)/shard_map/ppermute | solution.py:28
  197.2 1.3 collective-permute-start.37
  198.5 5.2 %collective-permute-start.20 = (bf16[256,512]{1,0:T(8,128)(2,1)S(1)}, bf16[256,512]{1,0:T(8,128)(2,1)}, u32[]{:S(2)}, u32[]{:S(2)}) collective-permute-start(bf16[256,512]{1,0:T(8,128)(2,1)S(1)} %collective-permute-done.19.refs_2_), channel_id=1, source_target_pairs={{0,1},{1,2},{2,3},{4,5},{5,6},{6,7},{8,9},{9,10},{10,11},{12,13},{... | collective-permute-start | bytes 786440 | tf_op jit(solution)/shard_map/ppermute | solution.py:28
  203.8 1.3 collective-permute-start.23
  205.1 1.4 collective-permute-start.45
  206.4 5.2 %collective-permute-start.35 = (bf16[256,512]{1,0:T(8,128)(2,1)S(1)}, bf16[256,512]{1,0:T(8,128)(2,1)}, u32[]{:S(2)}, u32[]{:S(2)}) collective-permute-start(bf16[256,512]{1,0:T(8,128)(2,1)S(1)} %collective-permute-done.34.refs_8_), channel_id=1, source_target_pairs={{0,1},{1,2},{2,3},{4,5},{5,6},{6,7},{8,9},{9,10},{10,11},{12,13},{... | collective-permute-start | bytes 786440 | tf_op jit(solution)/shard_map/ppermute | solution.py:28
  211.7 1.3 collective-permute-start.38
  213.0 5.3 %collective-permute-start.21 = (bf16[256,512]{1,0:T(8,128)(2,1)}, bf16[256,512]{1,0:T(8,128)(2,1)}, u32[]{:S(2)}, u32[]{:S(2)}) collective-permute-start(bf16[256,512]{1,0:T(8,128)(2,1)} %collective-permute-done.20.refs_1_), channel_id=1, source_target_pairs={{0,1},{1,2},{2,3},{4,5},{5,6},{6,7},{8,9},{9,10},{10,11},{12,13},{... | collective-permute-start | bytes 786440 | tf_op jit(solution)/shard_map/ppermute | solution.py:28
  218.2 1.3 collective-permute-start.24
  220.4 1.1 copy.87
  221.5 1.1 slice_bitcast_fusion.gate_ref
  222.7 4.1 %collective-permute-done.24.refs_6_ = bf16[256,512]{1,0:T(8,128)(2,1)} collective-permute-done((bf16[256,512]{1,0:T(8,128)(2,1)}, bf16[256,512]{1,0:T(8,128)(2,1)}, u32[]{:S(2)}, u32[]{:S(2)}) %collective-permute-start.24) | collective-permute-done | bytes 262176 | tf_op jit(solution)/shard_map/ppermute | solution.py:28
  226.8 5.5 %shard_map.155 = f32[72,640]{1,0:T(8,128)S(1)} custom-call(s32[3]{0:T(128)S(1)} %pad_add_fusion.place_ref, f32[608,1]{1,0:T(8,128)S(1)} %slice_bitcast_fusion.gate_ref, f32[2,2,304]{2,1,0:T(2,128)S(1)} %bitcast.75, bf16[608,512]{1,0:T(8,128)(2,1)} %bitcast.77, bf16[256,512]{1,0:T(8,128)(2,1)} %collective-permute-done.21.refs_0_, ...), custom_call_target="tpu_custom_call" | custom-call | flops 1275068416 | bytes 9961472 | tf_op jit(solution)/shard_map/pallas_call | solution.py:434
  232.4 7.2 %collective-permute-done.46 = f32[72,640]{1,0:T(8,128)S(1)} collective-permute-done((f32[72,640]{1,0:T(8,128)S(1)}, f32[72,640]{1,0:T(8,128)S(1)}, u32[]{:S(2)}, u32[]{:S(2)}) %collective-permute-start.46) | collective-permute-done | bytes 184352 | tf_op jit(solution)/shard_map/ppermute | solution.py:22
  242.5 5.1 %collective-permute-done.47 = f32[72,640]{1,0:T(8,128)S(1)} collective-permute-done((f32[72,640]{1,0:T(8,128)S(1)}, f32[72,640]{1,0:T(8,128)S(1)}, u32[]{:S(2)}, u32[]{:S(2)}) %collective-permute-start.47) | collective-permute-done | bytes 184352 | tf_op jit(solution)/shard_map/ppermute | solution.py:22
  (161 shorter events, 28.2 us)
Async XLA Ops:
  0.6 10.0 %copy-start.19 = (f32[4,304]{1,0:T(4,128)S(1)}, f32[4,304]{1,0:T(4,128)}, u32[]{:S(2)}) copy-start(f32[4,304]{1,0:T(4,128)} %cond_ref.1) | copy-start | bytes 14596
  2.8 48.5 %collective-permute-start.8 = (bf16[608,608]{1,0:T(8,128)(2,1)S(1)}, bf16[608,608]{1,0:T(8,128)(2,1)S(1)}, u32[]{:S(2)}, u32[]{:S(2)}) collective-permute-start(bf16[608,608]{1,0:T(8,128)(2,1)S(1)} %pad_maximum_fusion.refs_3_), channel_id=1, source_target_pairs={{1,0},{2,1},{3,2},{5,4},{6,5},{7,6},{9,8},{10,9},{11,10},{13,12},{... | collective-permute-start | bytes 2217992 | tf_op jit(solution)/shard_map/ppermute | solution.py:28
  4.1 48.6 %collective-permute-start.5 = (bf16[608,608]{1,0:T(8,128)(2,1)S(1)}, bf16[608,608]{1,0:T(8,128)(2,1)}, u32[]{:S(2)}, u32[]{:S(2)}) collective-permute-start(bf16[608,608]{1,0:T(8,128)(2,1)S(1)} %pad_maximum_fusion.refs_3_), channel_id=1, source_target_pairs={{0,1},{1,2},{2,3},{4,5},{5,6},{6,7},{8,9},{9,10},{10,11},{12,13},{... | collective-permute-start | bytes 2217992 | tf_op jit(solution)/shard_map/ppermute | solution.py:28
  12.9 6.1 %collective-permute-start = (f32[2,7,608]{2,0,1:T(2,128)S(1)}, f32[2,7,608]{2,0,1:T(2,128)S(1)}, u32[]{:S(2)}, u32[]{:S(2)}) collective-permute-start(f32[2,7,608]{2,0,1:T(2,128)S(1)} %bitcast.84), channel_id=1, source_target_pairs={{0,16},{4,20},{8,24},{12,28},{16,0},{20,4},{24,8},{28,12},{1,17},{... | collective-permute-start | bytes 102152 | tf_op jit(solution)/shard_map/ppermute | solution.py:22
  22.3 8.5 %collective-permute-start.1 = (f32[1,7,608]{1,2,0:T(8,128)}, f32[1,7,608]{1,2,0:T(8,128)S(1)}, u32[]{:S(2)}, u32[]{:S(2)}) collective-permute-start(f32[1,7,608]{1,2,0:T(8,128)} %constant_dynamic-slice_fusion), channel_id=1, source_target_pairs={{0,8},{4,12},{8,0},{12,4},{16,24},{20,28},{24,16},{28,20},{1,9},{5... | collective-permute-start | bytes 51080 | tf_op jit(solution)/shard_map/ppermute | solution.py:22
  24.8 8.7 %copy-start.36 = (f32[5]{0:T(128)S(1)}, f32[5]{0:T(128)}, u32[]{:S(2)}) copy-start(f32[5]{0:T(128)} %constant.103.clone) | copy-start | bytes 64
  31.7 1.7 collective-permute-start.2
  33.5 85.0 %copy-start.26 = (f32[1,5,608]{1,2,0:T(8,128)}, f32[1,5,608]{1,2,0:T(8,128)S(1)}, u32[]{:S(2)}) copy-start(f32[1,5,608]{1,2,0:T(8,128)S(1)} %fusion) | copy-start | bytes 36484
  33.5 9.6 %collective-permute-start.3 = (f32[1,5,608]{1,2,0:T(8,128)S(1)}, f32[1,5,608]{1,2,0:T(8,128)}, u32[]{:S(2)}, u32[]{:S(2)}) collective-permute-start(f32[1,5,608]{1,2,0:T(8,128)S(1)} %fusion), channel_id=1, source_target_pairs={{0,1},{1,0},{2,3},{3,2},{4,5},{5,4},{6,7},{7,6},{8,9},{9,8},{10,11... | collective-permute-start | bytes 36488 | tf_op jit(solution)/shard_map/ppermute | solution.py:22
  34.3 84.1 %copy-start.34 = (f32[2,64]{1,0:T(2,128)S(1)}, f32[2,64]{1,0:T(2,128)}, u32[]{:S(2)}) copy-start(f32[2,64]{1,0:T(2,128)} %param.24) | copy-start | bytes 1540
  34.3 84.2 %copy-start.35 = (f32[64]{0:T(128)S(1)}, f32[64]{0:T(128)}, u32[]{:S(2)}) copy-start(f32[64]{0:T(128)} %param.23) | copy-start | bytes 772
  34.4 84.3 %copy-start.33 = (bf16[304,64]{0,1:T(8,128)(2,1)S(1)}, bf16[304,64]{0,1:T(8,128)(2,1)}, u32[]{:S(2)}) copy-start(bf16[304,64]{0,1:T(8,128)(2,1)} %param.26) | copy-start | bytes 116740
  34.4 84.3 %copy-start.37 = (s32[4]{0:T(128)S(1)}, s32[4]{0:T(128)}, u32[]{:S(2)}) copy-start(s32[4]{0:T(128)} %param.16) | copy-start | bytes 52
  44.2 5.2 %collective-permute-start.4 = (f32[2,5,608]{2,0,1:T(2,128)S(1)}, f32[2,5,608]{2,0,1:T(2,128)S(1)}, u32[]{:S(2)}, u32[]{:S(2)}) collective-permute-start(f32[2,5,608]{2,0,1:T(2,128)S(1)} %pad_maximum_fusion.2), channel_id=1, source_target_pairs={{0,2},{1,3},{2,0},{3,1},{4,6},{5,7},{6,4},{7,5},{8,10},{9,11},{10,... | collective-permute-start | bytes 72968 | tf_op jit(solution)/shard_map/ppermute | solution.py:22
  47.1 20.4 %collective-permute-start.26 = (bf16[304,1280]{1,0:T(8,128)(2,1)S(1)}, bf16[304,1280]{1,0:T(8,128)(2,1)S(1)}, u32[]{:S(2)}, u32[]{:S(2)}) collective-permute-start(bf16[304,1280]{1,0:T(8,128)(2,1)S(1)} %fusion.1.refs_0_), channel_id=1, source_target_pairs={{0,8},{4,12},{8,0},{12,4},{16,24},{20,28},{24,16},{28,20},{1,9},{5... | collective-permute-start | bytes 2334728 | tf_op jit(solution)/shard_map/ppermute | solution.py:22
  48.7 20.3 %collective-permute-start.28 = (bf16[304,1280]{1,0:T(8,128)(2,1)S(1)}, bf16[304,1280]{1,0:T(8,128)(2,1)S(1)}, u32[]{:S(2)}, u32[]{:S(2)}) collective-permute-start(bf16[304,1280]{1,0:T(8,128)(2,1)S(1)} %fusion.1.refs_0_), channel_id=1, source_target_pairs={{0,16},{4,20},{8,24},{12,28},{16,0},{20,4},{24,8},{28,12},{1,17},{... | collective-permute-start | bytes 2334728 | tf_op jit(solution)/shard_map/ppermute | solution.py:22
  49.4 20.3 %collective-permute-start.25 = (bf16[304,1280]{1,0:T(8,128)(2,1)S(1)}, bf16[304,1280]{1,0:T(8,128)(2,1)S(1)}, u32[]{:S(2)}, u32[]{:S(2)}) collective-permute-start(bf16[304,1280]{1,0:T(8,128)(2,1)S(1)} %fusion.1.refs_0_), channel_id=1, source_target_pairs={{0,4},{4,0},{8,12},{12,8},{16,20},{20,16},{24,28},{28,24},{1,5},{5... | collective-permute-start | bytes 2334728 | tf_op jit(solution)/shard_map/ppermute | solution.py:22
  51.4 34.3 %collective-permute-start.14 = (bf16[304,1280]{1,0:T(8,128)(2,1)S(1)}, bf16[304,1280]{1,0:T(8,128)(2,1)}, u32[]{:S(2)}, u32[]{:S(2)}) collective-permute-start(bf16[304,1280]{1,0:T(8,128)(2,1)S(1)} %fusion.3.refs_0_), channel_id=1, source_target_pairs={{0,16},{4,20},{8,24},{12,28},{16,0},{20,4},{24,8},{28,12},{1,17},{... | collective-permute-start | bytes 2334728 | tf_op jit(solution)/shard_map/ppermute | solution.py:22
  52.8 33.9 %collective-permute-start.12 = (bf16[304,1280]{1,0:T(8,128)(2,1)S(1)}, bf16[304,1280]{1,0:T(8,128)(2,1)}, u32[]{:S(2)}, u32[]{:S(2)}) collective-permute-start(bf16[304,1280]{1,0:T(8,128)(2,1)S(1)} %fusion.3.refs_0_), channel_id=1, source_target_pairs={{0,8},{4,12},{8,0},{12,4},{16,24},{20,28},{24,16},{28,20},{1,9},{5... | collective-permute-start | bytes 2334728 | tf_op jit(solution)/shard_map/ppermute | solution.py:22
  67.5 20.6 %collective-permute-start.9 = (bf16[608,608]{1,0:T(8,128)(2,1)S(1)}, bf16[608,608]{1,0:T(8,128)(2,1)S(1)}, u32[]{:S(2)}, u32[]{:S(2)}) collective-permute-start(bf16[608,608]{1,0:T(8,128)(2,1)S(1)} %collective-permute-done.8.refs_4_), channel_id=1, source_target_pairs={{1,0},{2,1},{3,2},{5,4},{6,5},{7,6},{9,8},{10,9},{11,10},{13,12},{... | collective-permute-start | bytes 2217992 | tf_op jit(solution)/shard_map/ppermute | solution.py:28
  69.0 31.2 %collective-permute-start.30 = (bf16[304,1280]{1,0:T(8,128)(2,1)S(1)}, bf16[304,1280]{1,0:T(8,128)(2,1)}, u32[]{:S(2)}, u32[]{:S(2)}) collective-permute-start(bf16[304,1280]{1,0:T(8,128)(2,1)S(1)} %collective-permute-done.26.refs_2_), channel_id=1, source_target_pairs={{0,16},{4,20},{8,24},{12,28},{16,0},{20,4},{24,8},{28,12},{1,17},{... | collective-permute-start | bytes 2334728 | tf_op jit(solution)/shard_map/ppermute | solution.py:22
  70.7 17.9 %collective-permute-start.6 = (bf16[608,608]{1,0:T(8,128)(2,1)}, bf16[608,608]{1,0:T(8,128)(2,1)S(1)}, u32[]{:S(2)}, u32[]{:S(2)}) collective-permute-start(bf16[608,608]{1,0:T(8,128)(2,1)} %collective-permute-done.5.refs_2_), channel_id=1, source_target_pairs={{0,1},{1,2},{2,3},{4,5},{5,6},{6,7},{8,9},{9,10},{10,11},{12,13},{... | collective-permute-start | bytes 2217992 | tf_op jit(solution)/shard_map/ppermute | solution.py:28
  85.7 17.8 %collective-permute-start.27 = (bf16[304,1280]{1,0:T(8,128)(2,1)S(1)}, bf16[304,1280]{1,0:T(8,128)(2,1)S(1)}, u32[]{:S(2)}, u32[]{:S(2)}) collective-permute-start(bf16[304,1280]{1,0:T(8,128)(2,1)S(1)} %collective-permute-done.26.refs_2_), channel_id=1, source_target_pairs={{0,4},{4,0},{8,12},{12,8},{16,20},{20,16},{24,28},{28,24},{1,5},{5... | collective-permute-start | bytes 2334728 | tf_op jit(solution)/shard_map/ppermute | solution.py:22
  86.6 17.9 %collective-permute-start.29 = (bf16[304,1280]{1,0:T(8,128)(2,1)S(1)}, bf16[304,1280]{1,0:T(8,128)(2,1)S(1)}, u32[]{:S(2)}, u32[]{:S(2)}) collective-permute-start(bf16[304,1280]{1,0:T(8,128)(2,1)S(1)} %collective-permute-done.28.refs_4_), channel_id=1, source_target_pairs={{0,4},{4,0},{8,12},{12,8},{16,20},{20,16},{24,28},{28,24},{1,5},{5... | collective-permute-start | bytes 2334728 | tf_op jit(solution)/shard_map/ppermute | solution.py:22
  88.0 19.6 %collective-permute-start.16 = (bf16[304,1280]{1,0:T(8,128)(2,1)}, bf16[304,1280]{1,0:T(8,128)(2,1)}, u32[]{:S(2)}, u32[]{:S(2)}) collective-permute-start(bf16[304,1280]{1,0:T(8,128)(2,1)} %collective-permute-done.14.refs_4_), channel_id=1, source_target_pairs={{0,8},{4,12},{8,0},{12,4},{16,24},{20,28},{24,16},{28,20},{1,9},{5... | collective-permute-start | bytes 2334728 | tf_op jit(solution)/shard_map/ppermute | solution.py:22
  88.6 20.9 %collective-permute-start.10 = (bf16[608,608]{1,0:T(8,128)(2,1)S(1)}, bf16[608,608]{1,0:T(8,128)(2,1)S(1)}, u32[]{:S(2)}, u32[]{:S(2)}) collective-permute-start(bf16[608,608]{1,0:T(8,128)(2,1)S(1)} %collective-permute-done.9.refs_5_), channel_id=1, source_target_pairs={{1,0},{2,1},{3,2},{5,4},{6,5},{7,6},{9,8},{10,9},{11,10},{13,12},{... | collective-permute-start | bytes 2217992 | tf_op jit(solution)/shard_map/ppermute | solution.py:28
  100.1 17.4 %collective-permute-start.7 = (bf16[608,608]{1,0:T(8,128)(2,1)S(1)}, bf16[608,608]{1,0:T(8,128)(2,1)S(1)}, u32[]{:S(2)}, u32[]{:S(2)}) collective-permute-start(bf16[608,608]{1,0:T(8,128)(2,1)S(1)} %collective-permute-done.6.refs_1_), channel_id=1, source_target_pairs={{0,1},{1,2},{2,3},{4,5},{5,6},{6,7},{8,9},{9,10},{10,11},{12,13},{... | collective-permute-start | bytes 2217992 | tf_op jit(solution)/shard_map/ppermute | solution.py:28
  104.5 33.1 %collective-permute-start.31 = (bf16[304,1280]{1,0:T(8,128)(2,1)}, bf16[304,1280]{1,0:T(8,128)(2,1)}, u32[]{:S(2)}, u32[]{:S(2)}) collective-permute-start(bf16[304,1280]{1,0:T(8,128)(2,1)} %collective-permute-done.30.refs_6_), channel_id=1, source_target_pairs={{0,4},{4,0},{8,12},{12,8},{16,20},{20,16},{24,28},{28,24},{1,5},{5... | collective-permute-start | bytes 2334728 | tf_op jit(solution)/shard_map/ppermute | solution.py:22
  105.4 42.4 %collective-permute-start.11 = (bf16[304,1280]{1,0:T(8,128)(2,1)S(1)}, bf16[304,1280]{1,0:T(8,128)(2,1)}, u32[]{:S(2)}, u32[]{:S(2)}) collective-permute-start(bf16[304,1280]{1,0:T(8,128)(2,1)S(1)} %fusion.3.refs_0_), channel_id=1, source_target_pairs={{0,4},{4,0},{8,12},{12,8},{16,20},{20,16},{24,28},{28,24},{1,5},{5... | collective-permute-start | bytes 2334728 | tf_op jit(solution)/shard_map/ppermute | solution.py:22
  107.6 40.3 %collective-permute-start.15 = (bf16[304,1280]{1,0:T(8,128)(2,1)}, bf16[304,1280]{1,0:T(8,128)(2,1)}, u32[]{:S(2)}, u32[]{:S(2)}) collective-permute-start(bf16[304,1280]{1,0:T(8,128)(2,1)} %collective-permute-done.14.refs_4_), channel_id=1, source_target_pairs={{0,4},{4,0},{8,12},{12,8},{16,20},{20,16},{24,28},{28,24},{1,5},{5... | collective-permute-start | bytes 2334728 | tf_op jit(solution)/shard_map/ppermute | solution.py:22
  110.4 37.5 %collective-permute-start.13 = (bf16[304,1280]{1,0:T(8,128)(2,1)}, bf16[304,1280]{1,0:T(8,128)(2,1)}, u32[]{:S(2)}, u32[]{:S(2)}) collective-permute-start(bf16[304,1280]{1,0:T(8,128)(2,1)} %collective-permute-done.12.refs_2_), channel_id=1, source_target_pairs={{0,4},{4,0},{8,12},{12,8},{16,20},{20,16},{24,28},{28,24},{1,5},{5... | collective-permute-start | bytes 2334728 | tf_op jit(solution)/shard_map/ppermute | solution.py:22
  118.5 29.4 %collective-permute-start.17 = (bf16[304,1280]{1,0:T(8,128)(2,1)}, bf16[304,1280]{1,0:T(8,128)(2,1)}, u32[]{:S(2)}, u32[]{:S(2)}) collective-permute-start(bf16[304,1280]{1,0:T(8,128)(2,1)} %collective-permute-done.16.refs_6_), channel_id=1, source_target_pairs={{0,4},{4,0},{8,12},{12,8},{16,20},{20,16},{24,28},{28,24},{1,5},{5... | collective-permute-start | bytes 2334728 | tf_op jit(solution)/shard_map/ppermute | solution.py:22
  124.8 12.8 %copy-start.2 = (bf16[304,1280]{1,0:T(8,128)(2,1)S(1)}, bf16[304,1280]{1,0:T(8,128)(2,1)}, u32[]{:S(2)}) copy-start(bf16[304,1280]{1,0:T(8,128)(2,1)} %copy-done.1) | copy-start | bytes 2334724
  124.8 12.9 %copy-start.4 = (bf16[304,1280]{1,0:T(8,128)(2,1)S(1)}, bf16[304,1280]{1,0:T(8,128)(2,1)}, u32[]{:S(2)}) copy-start(bf16[304,1280]{1,0:T(8,128)(2,1)} %copy-done.3) | copy-start | bytes 2334724
  124.8 12.9 %copy-start.6 = (bf16[304,1280]{1,0:T(8,128)(2,1)S(1)}, bf16[304,1280]{1,0:T(8,128)(2,1)}, u32[]{:S(2)}) copy-start(bf16[304,1280]{1,0:T(8,128)(2,1)} %copy-done.5) | copy-start | bytes 2334724
  124.8 12.9 %copy-start.10 = (bf16[304,1280]{1,0:T(8,128)(2,1)S(1)}, bf16[304,1280]{1,0:T(8,128)(2,1)}, u32[]{:S(2)}) copy-start(bf16[304,1280]{1,0:T(8,128)(2,1)} %copy-done.9) | copy-start | bytes 2334724
  124.8 12.9 %copy-start.12 = (bf16[304,1280]{1,0:T(8,128)(2,1)S(1)}, bf16[304,1280]{1,0:T(8,128)(2,1)}, u32[]{:S(2)}) copy-start(bf16[304,1280]{1,0:T(8,128)(2,1)} %copy-done.11) | copy-start | bytes 2334724
  147.3 12.8 %collective-permute-start.32 = (bf16[512,608]{0,1:T(8,128)(2,1)}, bf16[512,608]{0,1:T(8,128)(2,1)}, u32[]{:S(2)}, u32[]{:S(2)}) collective-permute-start(bf16[512,608]{0,1:T(8,128)(2,1)} %copy.101), channel_id=1, source_target_pairs={{0,4},{4,0},{8,12},{12,8},{16,20},{20,16},{24,28},{28,24},{1,5},{5... | collective-permute-start | bytes 1867784 | tf_op jit(solution)/shard_map/ppermute | solution.py:22
  147.8 10.7 %collective-permute-start.39 = (bf16[736,256]{1,0:T(8,128)(2,1)S(1)}, bf16[736,256]{1,0:T(8,128)(2,1)S(1)}, u32[]{:S(2)}, u32[]{:S(2)}) collective-permute-start(bf16[736,256]{1,0:T(8,128)(2,1)S(1)} %pad_maximum_fusion.1.refs_14_), channel_id=1, source_target_pairs={{0,4},{4,0},{8,12},{12,8},{16,20},{20,16},{24,28},{28,24},{1,5},{5... | collective-permute-start | bytes 1130504 | tf_op jit(solution)/shard_map/ppermute | solution.py:22
  156.8 14.2 %collective-permute-start.18 = (bf16[512,608]{0,1:T(8,128)(2,1)}, bf16[512,608]{0,1:T(8,128)(2,1)}, u32[]{:S(2)}, u32[]{:S(2)}) collective-permute-start(bf16[512,608]{0,1:T(8,128)(2,1)} %copy.96), channel_id=1, source_target_pairs={{0,4},{4,0},{8,12},{12,8},{16,20},{20,16},{24,28},{28,24},{1,5},{5... | collective-permute-start | bytes 1867784 | tf_op jit(solution)/shard_map/ppermute | solution.py:22
  157.3 27.4 %collective-permute-start.40 = (bf16[736,256]{1,0:T(8,128)(2,1)S(1)}, bf16[736,256]{1,0:T(8,128)(2,1)S(1)}, u32[]{:S(2)}, u32[]{:S(2)}) collective-permute-start(bf16[736,256]{1,0:T(8,128)(2,1)S(1)} %pad_maximum_fusion.1.refs_14_), channel_id=1, source_target_pairs={{0,8},{4,12},{8,0},{12,4},{16,24},{20,28},{24,16},{28,20},{1,9},{5... | collective-permute-start | bytes 1130504 | tf_op jit(solution)/shard_map/ppermute | solution.py:22
  157.8 28.1 %collective-permute-start.42 = (bf16[736,256]{1,0:T(8,128)(2,1)S(1)}, bf16[736,256]{1,0:T(8,128)(2,1)}, u32[]{:S(2)}, u32[]{:S(2)}) collective-permute-start(bf16[736,256]{1,0:T(8,128)(2,1)S(1)} %pad_maximum_fusion.1.refs_14_), channel_id=1, source_target_pairs={{0,16},{4,20},{8,24},{12,28},{16,0},{20,4},{24,8},{28,12},{1,17},{... | collective-permute-start | bytes 1130504 | tf_op jit(solution)/shard_map/ppermute | solution.py:22
  158.5 32.0 %collective-permute-start.41 = (bf16[736,256]{1,0:T(8,128)(2,1)S(1)}, bf16[736,256]{1,0:T(8,128)(2,1)}, u32[]{:S(2)}, u32[]{:S(2)}) collective-permute-start(bf16[736,256]{1,0:T(8,128)(2,1)S(1)} %collective-permute-done.39.refs_15_), channel_id=1, source_target_pairs={{0,8},{4,12},{8,0},{12,4},{16,24},{20,28},{24,16},{28,20},{1,9},{5... | collective-permute-start | bytes 1130504 | tf_op jit(solution)/shard_map/ppermute | solution.py:22
  160.0 31.8 %collective-permute-start.43 = (bf16[736,256]{1,0:T(8,128)(2,1)S(1)}, bf16[736,256]{1,0:T(8,128)(2,1)}, u32[]{:S(2)}, u32[]{:S(2)}) collective-permute-start(bf16[736,256]{1,0:T(8,128)(2,1)S(1)} %collective-permute-done.39.refs_15_), channel_id=1, source_target_pairs={{0,16},{4,20},{8,24},{12,28},{16,0},{20,4},{24,8},{28,12},{1,17},{... | collective-permute-start | bytes 1130504 | tf_op jit(solution)/shard_map/ppermute | solution.py:22
  171.0 21.7 %collective-permute-start.33 = (bf16[256,512]{1,0:T(8,128)(2,1)S(1)}, bf16[256,512]{1,0:T(8,128)(2,1)S(1)}, u32[]{:S(2)}, u32[]{:S(2)}) collective-permute-start(bf16[256,512]{1,0:T(8,128)(2,1)S(1)} %shard_map.154.refs_10_), channel_id=1, source_target_pairs={{0,1},{1,2},{2,3},{4,5},{5,6},{6,7},{8,9},{9,10},{10,11},{12,13},{... | collective-permute-start | bytes 786440 | tf_op jit(solution)/shard_map/ppermute | solution.py:28
  177.3 42.2 %copy-start.25 = (f32[7,608]{0,1:T(8,128)S(1)}, f32[7,608]{0,1:T(8,128)}, u32[]{:S(2)}) copy-start(f32[7,608]{0,1:T(8,128)} %copy-done.24) | copy-start | bytes 51076
  184.6 12.6 %collective-permute-start.36 = (bf16[256,512]{1,0:T(8,128)(2,1)S(1)}, bf16[256,512]{1,0:T(8,128)(2,1)S(1)}, u32[]{:S(2)}, u32[]{:S(2)}) collective-permute-start(bf16[256,512]{1,0:T(8,128)(2,1)S(1)} %shard_map.154.refs_10_), channel_id=1, source_target_pairs={{1,0},{2,1},{3,2},{5,4},{6,5},{7,6},{9,8},{10,9},{11,10},{13,12},{... | collective-permute-start | bytes 786440 | tf_op jit(solution)/shard_map/ppermute | solution.py:28
  185.9 12.6 %collective-permute-start.19 = (bf16[256,512]{1,0:T(8,128)(2,1)S(1)}, bf16[256,512]{1,0:T(8,128)(2,1)S(1)}, u32[]{:S(2)}, u32[]{:S(2)}) collective-permute-start(bf16[256,512]{1,0:T(8,128)(2,1)S(1)} %shard_map.152.refs_3_), channel_id=1, source_target_pairs={{0,1},{1,2},{2,3},{4,5},{5,6},{6,7},{8,9},{9,10},{10,11},{12,13},{... | collective-permute-start | bytes 786440 | tf_op jit(solution)/shard_map/ppermute | solution.py:28
  190.5 13.2 %collective-permute-start.22 = (bf16[256,512]{1,0:T(8,128)(2,1)S(1)}, bf16[256,512]{1,0:T(8,128)(2,1)S(1)}, u32[]{:S(2)}, u32[]{:S(2)}) collective-permute-start(bf16[256,512]{1,0:T(8,128)(2,1)S(1)} %shard_map.152.refs_3_), channel_id=1, source_target_pairs={{1,0},{2,1},{3,2},{5,4},{6,5},{7,6},{9,8},{10,9},{11,10},{13,12},{... | collective-permute-start | bytes 786440 | tf_op jit(solution)/shard_map/ppermute | solution.py:28
  191.8 13.2 %collective-permute-start.44 = (bf16[736,256]{1,0:T(8,128)(2,1)S(1)}, bf16[736,256]{1,0:T(8,128)(2,1)S(1)}, u32[]{:S(2)}, u32[]{:S(2)}) collective-permute-start(bf16[736,256]{1,0:T(8,128)(2,1)S(1)} %collective-permute-done.40.refs_16_), channel_id=1, source_target_pairs={{0,16},{4,20},{8,24},{12,28},{16,0},{20,4},{24,8},{28,12},{1,17},{... | collective-permute-start | bytes 1130504 | tf_op jit(solution)/shard_map/ppermute | solution.py:22
  192.6 13.8 %collective-permute-start.34 = (bf16[256,512]{1,0:T(8,128)(2,1)S(1)}, bf16[256,512]{1,0:T(8,128)(2,1)S(1)}, u32[]{:S(2)}, u32[]{:S(2)}) collective-permute-start(bf16[256,512]{1,0:T(8,128)(2,1)S(1)} %collective-permute-done.33.refs_9_), channel_id=1, source_target_pairs={{0,1},{1,2},{2,3},{4,5},{5,6},{6,7},{8,9},{9,10},{10,11},{12,13},{... | collective-permute-start | bytes 786440 | tf_op jit(solution)/shard_map/ppermute | solution.py:28
  197.2 14.5 %collective-permute-start.37 = (bf16[256,512]{1,0:T(8,128)(2,1)S(1)}, bf16[256,512]{1,0:T(8,128)(2,1)S(1)}, u32[]{:S(2)}, u32[]{:S(2)}) collective-permute-start(bf16[256,512]{1,0:T(8,128)(2,1)S(1)} %collective-permute-done.36.refs_11_), channel_id=1, source_target_pairs={{1,0},{2,1},{3,2},{5,4},{6,5},{7,6},{9,8},{10,9},{11,10},{13,12},{... | collective-permute-start | bytes 786440 | tf_op jit(solution)/shard_map/ppermute | solution.py:28
  198.5 14.5 %collective-permute-start.20 = (bf16[256,512]{1,0:T(8,128)(2,1)S(1)}, bf16[256,512]{1,0:T(8,128)(2,1)}, u32[]{:S(2)}, u32[]{:S(2)}) collective-permute-start(bf16[256,512]{1,0:T(8,128)(2,1)S(1)} %collective-permute-done.19.refs_2_), channel_id=1, source_target_pairs={{0,1},{1,2},{2,3},{4,5},{5,6},{6,7},{8,9},{9,10},{10,11},{12,13},{... | collective-permute-start | bytes 786440 | tf_op jit(solution)/shard_map/ppermute | solution.py:28
  203.8 14.5 %collective-permute-start.23 = (bf16[256,512]{1,0:T(8,128)(2,1)S(1)}, bf16[256,512]{1,0:T(8,128)(2,1)}, u32[]{:S(2)}, u32[]{:S(2)}) collective-permute-start(bf16[256,512]{1,0:T(8,128)(2,1)S(1)} %collective-permute-done.22.refs_4_), channel_id=1, source_target_pairs={{1,0},{2,1},{3,2},{5,4},{6,5},{7,6},{9,8},{10,9},{11,10},{13,12},{... | collective-permute-start | bytes 786440 | tf_op jit(solution)/shard_map/ppermute | solution.py:28
  205.1 15.3 %copy-start.30 = (bf16[736,256]{1,0:T(8,128)(2,1)}, bf16[736,256]{1,0:T(8,128)(2,1)S(1)}, u32[]{:S(2)}) copy-start(bf16[736,256]{1,0:T(8,128)(2,1)S(1)} %collective-permute-done.44.refs_20_) | copy-start | bytes 1130500
  205.1 17.6 %collective-permute-start.45 = (bf16[736,256]{1,0:T(8,128)(2,1)}, bf16[736,256]{1,0:T(8,128)(2,1)}, u32[]{:S(2)}, u32[]{:S(2)}) collective-permute-start(bf16[736,256]{1,0:T(8,128)(2,1)} %collective-permute-done.41.refs_17_), channel_id=1, source_target_pairs={{0,16},{4,20},{8,24},{12,28},{16,0},{20,4},{24,8},{28,12},{1,17},{... | collective-permute-start | bytes 1130504 | tf_op jit(solution)/shard_map/ppermute | solution.py:22
  206.4 16.2 %collective-permute-start.35 = (bf16[256,512]{1,0:T(8,128)(2,1)S(1)}, bf16[256,512]{1,0:T(8,128)(2,1)}, u32[]{:S(2)}, u32[]{:S(2)}) collective-permute-start(bf16[256,512]{1,0:T(8,128)(2,1)S(1)} %collective-permute-done.34.refs_8_), channel_id=1, source_target_pairs={{0,1},{1,2},{2,3},{4,5},{5,6},{6,7},{8,9},{9,10},{10,11},{12,13},{... | collective-permute-start | bytes 786440 | tf_op jit(solution)/shard_map/ppermute | solution.py:28
  211.7 11.0 %collective-permute-start.38 = (bf16[256,512]{1,0:T(8,128)(2,1)S(1)}, bf16[256,512]{1,0:T(8,128)(2,1)}, u32[]{:S(2)}, u32[]{:S(2)}) collective-permute-start(bf16[256,512]{1,0:T(8,128)(2,1)S(1)} %collective-permute-done.37.refs_12_), channel_id=1, source_target_pairs={{1,0},{2,1},{3,2},{5,4},{6,5},{7,6},{9,8},{10,9},{11,10},{13,12},{... | collective-permute-start | bytes 786440 | tf_op jit(solution)/shard_map/ppermute | solution.py:28
  213.0 9.7 %collective-permute-start.21 = (bf16[256,512]{1,0:T(8,128)(2,1)}, bf16[256,512]{1,0:T(8,128)(2,1)}, u32[]{:S(2)}, u32[]{:S(2)}) collective-permute-start(bf16[256,512]{1,0:T(8,128)(2,1)} %collective-permute-done.20.refs_1_), channel_id=1, source_target_pairs={{0,1},{1,2},{2,3},{4,5},{5,6},{6,7},{8,9},{9,10},{10,11},{12,13},{... | collective-permute-start | bytes 786440 | tf_op jit(solution)/shard_map/ppermute | solution.py:28
  218.2 8.6 %collective-permute-start.24 = (bf16[256,512]{1,0:T(8,128)(2,1)}, bf16[256,512]{1,0:T(8,128)(2,1)}, u32[]{:S(2)}, u32[]{:S(2)}) collective-permute-start(bf16[256,512]{1,0:T(8,128)(2,1)} %collective-permute-done.23.refs_5_), channel_id=1, source_target_pairs={{1,0},{2,1},{3,2},{5,4},{6,5},{7,6},{9,8},{10,9},{11,10},{13,12},{... | collective-permute-start | bytes 786440 | tf_op jit(solution)/shard_map/ppermute | solution.py:28
  226.8 13.8 %copy-start.38 = (s32[4]{0:T(128)S(1)}, s32[4]{0:T(128)}, u32[]{:S(2)}) copy-start(s32[4]{0:T(128)} %param.17) | copy-start | bytes 52
  232.3 15.5 %copy-start.32 = (f32[512,64]{0,1:T(8,128)S(1)}, f32[512,64]{0,1:T(8,128)}, u32[]{:S(2)}) copy-start(f32[512,64]{0,1:T(8,128)} %param.18) | copy-start | bytes 393220
  232.3 7.3 %collective-permute-start.46 = (f32[72,640]{1,0:T(8,128)S(1)}, f32[72,640]{1,0:T(8,128)S(1)}, u32[]{:S(2)}, u32[]{:S(2)}) collective-permute-start(f32[72,640]{1,0:T(8,128)S(1)} %shard_map.155), channel_id=1, source_target_pairs={{0,1},{1,0},{2,3},{3,2},{4,5},{5,4},{6,7},{7,6},{8,9},{9,8},{10,11... | collective-permute-start | bytes 552968 | tf_op jit(solution)/shard_map/ppermute | solution.py:22
  239.7 7.9 %collective-permute-start.47 = (f32[72,640]{1,0:T(8,128)S(1)}, f32[72,640]{1,0:T(8,128)S(1)}, u32[]{:S(2)}, u32[]{:S(2)}) collective-permute-start(f32[72,640]{1,0:T(8,128)S(1)} %add.96), channel_id=1, source_target_pairs={{0,2},{1,3},{2,0},{3,1},{4,6},{5,7},{6,4},{7,5},{8,10},{9,11},{10,... | collective-permute-start | bytes 552968 | tf_op jit(solution)/shard_map/ppermute | solution.py:22
  (23 other events, 36.6 us)

commit v2 on v1

--- a/solution.py
+++ b/solution.py
@@ -11,7 +11,7 @@
 EPS_NORM = 1e-06
 F32 = jnp.float32
 BF16 = jnp.bfloat16
-VMEM_LIMIT = 48 * 1024 * 1024
+VMEM_LIMIT = 24 * 1024 * 1024
 ANY = pl.BlockSpec(memory_space=pl.ANY)
 VMEM = pl.BlockSpec(memory_space=pltpu.VMEM)
 SMEM = pl.BlockSpec(memory_space=pltpu.SMEM)
@@ -92,62 +92,75 @@
             getattr(copy, act)()
 
 
-def mod_kernel(cond_ref, w_ref, out_ref):
-    values = cond_ref[...]
+def mod_kernel(place_ref, cond_ref, w_ref, out_ref):
+    requests, groups, width = cond_ref.shape[0], w_ref.shape[0], w_ref.shape[2]
+    request = place_ref[0] // 2
+    values = jnp.concatenate(
+        [cond_ref[pl.ds(jnp.bitwise_xor(request, k), 1), :] for k in range(requests)], axis=0
+    )
     activated = (values * (1.0 / (1.0 + jnp.exp(-values)))).astype(BF16)
-    for group in range(w_ref.shape[0]):
-        out_ref[:, group, :] = jnp.dot(activated, w_ref[group], preferred_element_type=F32)
+    out_ref[...] = jnp.zeros(out_ref.shape, F32)
+    for group in range(groups):
+        out_ref[:, group, :width] = jnp.dot(
+            activated, w_ref[group], preferred_element_type=F32
+        )
+
+
+def pack_kernel(qkv_ref, kv_ref, first_ref, second_ref):
+    half = first_ref.shape[1] // 5
+    for n, out_ref in enumerate((first_ref, second_ref)):
+        low, high = n * half, (n + 1) * half
+        for k in range(3):
+            out_ref[:, k * half : (k + 1) * half] = qkv_ref[k, :, low:high]
+        for k in range(2):
+            out_ref[:, (3 + k) * half : (4 + k) * half] = kv_ref[:, k, low:high]
 
 
 def norm_kernel(offsets, count, img, place_ref, mod_ref, *refs):
     blocks = refs[: len(offsets)]
-    out_ref, x_ref, sems = refs[len(offsets) :]
+    out_ref, x_ref, average_ref, inverse_ref, sems = refs[len(offsets) :]
     width, tokens = blocks[0].shape
     place = place_ref[1]
     target = lambda owner: x_ref.at[pl.ds(pl.multiple_of(owner * width, 16), width)]
     line_copies(blocks, offsets, place, count, target, sems, "start")
     line_copies(blocks, offsets, place, count, target, sems, "wait")
-    rows = 16
     total = width * count
-
-    def gather_stats(i, carry):
-        part = x_ref[pl.ds(pl.multiple_of(i * rows, rows), rows)].astype(F32)
+    chunk = 128
+
+    def turn(i, carry):
+        at = pl.multiple_of(i * chunk, chunk)
+        part = x_ref[pl.ds(at, chunk)].T
+        out_ref[:, pl.ds(at, chunk)] = part
+        wide = part.astype(F32)
         sums, squares = carry
-        for r in range(0, rows, 8):
-            piece = part[r : r + 8]
-            sums += piece
-            squares += piece * piece
-        return sums, squares
-
-    zero = jnp.zeros((8, tokens), F32)
-    sums, squares = lax.fori_loop(0, total // rows, gather_stats, (zero, zero), unroll=4)
-    average = jnp.sum(sums, axis=0, keepdims=True) / total
-    mean_square = jnp.sum(squares, axis=0, keepdims=True) / total
+        return sums + wide, squares + wide * wide
+
+    zero = jnp.zeros((tokens, chunk), F32)
+    sums, squares = lax.fori_loop(0, total // chunk, turn, (zero, zero))
+    average = jnp.sum(sums, axis=1, keepdims=True) / total
+    mean_square = jnp.sum(squares, axis=1, keepdims=True) / total
     inverse = lax.rsqrt(mean_square - average * average + EPS_NORM)
-    shape = (rows, tokens)
-    average = jnp.broadcast_to(average, shape)
-    inverse = jnp.broadcast_to(inverse, shape)
-
-    for owner in range(count):
-        slot = 0 if count == 1 else jnp.bitwise_xor(owner, place)
-
-        def normalise(i, _):
-            at = pl.multiple_of(i * rows, rows)
-            mod = mod_ref[slot, pl.ds(at, rows), :]
-            here = pl.ds(pl.multiple_of(owner * width + i * rows, rows), rows)
-            normed = (x_ref[here].astype(F32) - average) * inverse
-            out_ref[here, :img] = (normed[:, :img] * mod[:, 1:2] + mod[:, 0:1]).astype(BF16)
-            out_ref[here, img:] = (normed[:, img:] * mod[:, 4:5] + mod[:, 3:4]).astype(BF16)
-            return 0
-
-        lax.fori_loop(0, width // rows, normalise, 0, unroll=2)
-
-
-def project_kernel(masks, img, head, place_ref, q_gain_ref, k_gain_ref, x_ref, *refs):
+    average_ref[...] = jnp.broadcast_to(average, (tokens, chunk))
+    inverse_ref[...] = jnp.broadcast_to(inverse, (tokens, chunk))
+
+    def normalise(i, _):
+        at = pl.multiple_of(i * chunk, chunk)
+        here = pl.ds(at, chunk)
+        for low, high, group in ((0, img, 0), (img, tokens, 3)):
+            normed = out_ref[low:high, here].astype(F32) - average_ref[low:high]
+            normed = normed * inverse_ref[low:high]
+            stretch = 1.0 + mod_ref[group + 1 : group + 2, here]
+            out_ref[low:high, here] = (normed * stretch + mod_ref[group : group + 1, here]).astype(BF16)
+        return 0
+
+    lax.fori_loop(0, total // chunk, normalise, 0)
+
+
+def project_kernel(masks, img, head, place_ref, gain_ref, x_ref, *refs):
     blocks = refs[: len(masks)]
     q_ref, kv_ref, w_ref, sems = refs[len(masks) :]
     depth = blocks[0].shape[0]
-    half = q_ref.shape[0]
+    half = q_ref.shape[1]
     place = place_ref[0]
     copies = []
     for n, (ref, mask) in enumerate(zip(blocks, masks)):
@@ -161,74 +174,72 @@
         copy.start()
     for copy in copies:
         copy.wait()
+    row = lax.broadcasted_iota(jnp.int32, (half, half), 0) // head
+    col = lax.broadcasted_iota(jnp.int32, (half, half), 1) // head
+    mean_of = jnp.where(row == col, 1.0 / head, 0.0).astype(BF16)
 
     def product(part, low, high):
-        return lax.dot_general(
+        return jnp.dot(
+            x_ref[low:high],
             w_ref[:, part * half : (part + 1) * half],
-            x_ref[:, low:high],
-            (((0,), (0,)), ((), ())),
             preferred_element_type=F32,
         )
 
     def head_norm(values, gain):
-        cols = values.shape[1]
-        split = values.reshape(half // head, head, cols)
-        mean_square = jnp.mean(split * split, axis=1, keepdims=True)
-        normed = split * lax.rsqrt(mean_square + EPS_NORM) * gain[None]
-        return normed.reshape(half, cols)
-
-    tokens = x_ref.shape[1]
+        square = values * values
+        mean_square = jnp.zeros_like(square)
+        for _ in range(3):
+            term = square.astype(BF16)
+            mean_square += jnp.dot(term, mean_of, preferred_element_type=F32)
+            square = square - term.astype(F32)
+        return (values * lax.rsqrt(mean_square + EPS_NORM) * gain).astype(BF16)
+
+    tokens = x_ref.shape[0]
     scaling = head ** (-0.5)
-    queries = head_norm(product(0, 0, img), q_gain_ref[...]).astype(BF16)
+    queries = head_norm(product(0, 0, img), gain_ref[0:1])
     q_ref[...] = (queries.astype(F32) * scaling).astype(BF16)
-    kv_ref[:half, :img] = head_norm(product(1, 0, img), k_gain_ref[:, 0:1]).astype(BF16)
-    kv_ref[half:, :img] = product(2, 0, img).astype(BF16)
-    kv_ref[:half, img:] = head_norm(product(3, img, tokens), k_gain_ref[:, 1:2]).astype(BF16)
-    kv_ref[half:, img:] = product(4, img, tokens).astype(BF16)
-
-
-def attend_kernel(img, head, place_ref, q_ref, own_ref, peer_ref, out_ref, k_ref, v_ref):
-    half, queries = q_ref.shape
-    txt = own_ref.shape[1] - img
-    room = (txt + 127) // 128 * 128
+    kv_ref[:img, :half] = head_norm(product(1, 0, img), gain_ref[1:2])
+    kv_ref[:img, half:] = product(2, 0, img).astype(BF16)
+    kv_ref[img:, :half] = head_norm(product(3, img, tokens), gain_ref[2:3])
+    kv_ref[img:, half:] = product(4, img, tokens).astype(BF16)
+
+
+def attend_kernel(img, txt, head, place_ref, q_ref, own_ref, peer_ref, out_ref):
+    queries, half = q_ref.shape
+    room = own_ref.shape[0] - img
     side = lax.rem(place_ref[0], 2)
     length = place_ref[2]
-    keys = 2 * img + 2 * room
-    k_ref[:, 2 * img :] = jnp.zeros((half, 2 * room), BF16)
-    v_ref[:, 2 * img :] = jnp.zeros((half, 2 * room), BF16)
-    for n, ref in enumerate((own_ref, peer_ref)):
-        at, tail = n * img, 2 * img + n * room
-        k_ref[:, at : at + img] = ref[:half, :img]
-        v_ref[:, at : at + img] = ref[half:, :img]
-        k_ref[:, tail : tail + txt] = ref[:half, img:]
-        v_ref[:, tail : tail + txt] = ref[half:, img:]
-    slot = lax.broadcasted_iota(jnp.int32, (2 * room, 1), 0)
-    second = (slot >= room).astype(jnp.int32)
-    inside = slot - second * room
-    owner = jnp.where(second == 1, 1 - side, side)
-    allowed = (inside < txt) & (owner * txt + inside < length)
+    slot = lax.broadcasted_iota(jnp.int32, (room, 1), 0)
+    parts = []
+    for ref, owner in ((own_ref, side), (peer_ref, 1 - side)):
+        allowed = (slot < txt) & (owner * txt + slot < length)
+        parts.append((ref[:, :half], ref[:, half:].T, allowed))
+    lane = lax.broadcasted_iota(jnp.int32, (1, half), 1) // head
     step = 256 if queries % 256 == 0 else queries
-
-    def one(i, _):
-        at = pl.multiple_of(i * head, head)
+    for k in range(half // head):
         for low in range(0, queries, step):
-            scores = lax.dot_general(
-                k_ref[pl.ds(at, head)],
-                q_ref[pl.ds(at, head), low : low + step],
-                (((0,), (0,)), ((), ())),
-                preferred_element_type=F32,
-            )
-            tail = jnp.where(allowed, scores[2 * img :], -1e30)
-            scores = jnp.concatenate([scores[: 2 * img], tail], axis=0)
-            weights = jnp.exp(scores - jnp.max(scores, axis=0, keepdims=True))
-            inverse = 1.0 / jnp.sum(weights, axis=0, keepdims=True)
-            mixed = jnp.dot(
-                v_ref[pl.ds(at, head)], weights.astype(BF16), preferred_element_type=F32
-            )
-            out_ref[pl.ds(at, head), low : low + step] = (mixed * inverse).astype(BF16)
-        return 0
-
-    lax.fori_loop(0, half // head, one, 0)
+            query = jnp.where(lane == k, q_ref[low : low + step], 0.0).astype(BF16)
+            scores, tops = [], []
+            for keys, _, allowed in parts:
+                score = lax.dot_general(
+                    keys, query, (((1,), (1,)), ((), ())), preferred_element_type=F32
+                )
+                tail = jnp.where(allowed, score[img:], -1e30)
+                scores += [score[:img], tail]
+            top = jnp.max(scores[0], axis=0, keepdims=True)
+            for score in scores[1:]:
+                top = jnp.maximum(top, jnp.max(score, axis=0, keepdims=True))
+            total = jnp.zeros_like(top)
+            mixed = jnp.zeros((head, step), F32)
+            for n, (_, values, _) in enumerate(parts):
+                weights = jnp.exp(jnp.concatenate(scores[2 * n : 2 * n + 2], axis=0) - top)
+                total += jnp.sum(weights, axis=0, keepdims=True)
+                mixed += jnp.dot(
+                    values[k * head : (k + 1) * head],
+                    weights.astype(BF16),
+                    preferred_element_type=F32,
+                )
+            out_ref[k * head : (k + 1) * head, low : low + step] = (mixed / total).astype(BF16)
 
 
 def output_kernel(
@@ -330,7 +341,6 @@
     requests = cond.shape[0]
     img, width = hidden_img.shape
     txt = hidden_txt.shape[0]
-    tokens = img + txt
     head = q_gain.shape[0]
     part_cols = qkv_weight.shape[2]
     half = part_cols // 2
@@ -338,84 +348,86 @@
     length = lax.dynamic_index_in_dim(text_len, request, 0, keepdims=False)
     place = jnp.stack([row_pos, col_pos, length]).astype(jnp.int32)
 
+    room = -(-txt // 128) * 128
+    tokens = img + room
+    x_own = jnp.concatenate(
+        [hidden_img.T, jnp.pad(hidden_txt.T, ((0, 0), (0, room - txt)))], axis=1
+    )
+    x_blocks = line_gather(x_own, "col")
     chip_masks = [1 << bit for bit in range(1, row_count.bit_length() - 1)]
+    packed = call(
+        pack_kernel,
+        (jax.ShapeDtypeStruct((qkv_weight.shape[0], 5 * half), BF16),) * 2,
+        [VMEM, VMEM],
+        [],
+        cost(0, 20 * qkv_weight.shape[0] * half),
+        (VMEM, VMEM),
+    )(jnp.moveaxis(qkv_weight, 1, 0), kv_text_weight)
     gathered = []
-    packed = []
-    for n in range(2):
-        cols = slice(n * half, (n + 1) * half)
-        packed.append(
-            jnp.concatenate(
-                [qkv_weight[:, k, cols] for k in range(3)]
-                + [kv_text_weight[:, k, cols] for k in range(2)],
-                axis=1,
-            )
-        )
-    x_own = jnp.concatenate([hidden_img.T, hidden_txt.T], axis=1)
-    x_blocks = line_gather(x_own, "col")
     for n in range(2):
         order = chip_masks[::-1] if n == 0 else chip_masks
         gathered.append(doubling_gather(packed[n], "row", order + [1]))
 
+    wide = -(-width // 128) * 128
     mod_part = call(
         mod_kernel,
-        jax.ShapeDtypeStruct((requests, 7, width), F32),
-        [VMEM, VMEM],
+        jax.ShapeDtypeStruct((requests, 8, wide), F32),
+        [SMEM, VMEM, VMEM],
         [],
         cost(2 * requests * cond.shape[1] * 7 * width, mod_weight.size * 2),
-    )(cond, jnp.moveaxis(mod_weight, 1, 0))
-    mask = row_count // 2
-    while mask > 1:
-        bit = (row_pos // mask) % 2
-        pair = mod_part.reshape((2, mod_part.shape[0] // 2) + mod_part.shape[1:])
-        keep = lax.dynamic_index_in_dim(pair, bit, 0, keepdims=False)
-        give = lax.dynamic_index_in_dim(pair, 1 - bit, 0, keepdims=False)
-        mod_part = keep + swap(give, "row", mask)
-        mask //= 2
-    mod_part = mod_part[0]
-    mod_own = mod_part + swap(mod_part, "row", 1)
-    norm_mod = mod_own[:5] + jnp.array([0.0, 1.0, 0.0, 0.0, 1.0], F32)[:, None]
-    norm_mod = norm_mod[None]
+    )(place, cond, jnp.moveaxis(mod_weight, 1, 0))
+    first = chip_masks[-1]
+    mod_part, gathered[0][first] = lax.optimization_barrier((mod_part, gathered[0][first]))
+    mod_own = mod_part[0]
+    for k in range(1, requests):
+        mod_own = mod_own + swap(mod_part[k], "row", 2 * k)
+    mod_own = mod_own + swap(mod_own, "row", 1)
+    norm_mod = lax.dynamic_update_slice_in_dim(
+        jnp.zeros((8, full_width), F32), mod_own[:, :width], col_pos * width, 1
+    )
     mask = 1
     while mask < col_count:
-        norm_mod = jnp.concatenate([norm_mod, swap(norm_mod, "col", mask)], axis=0)
+        norm_mod = norm_mod + swap(norm_mod, "col", mask)
         mask *= 2
-    norm_mod = jnp.swapaxes(norm_mod, 1, 2)
+    mod_own = mod_own[:, :width]
 
     x_blocks, offsets, count = in_line(x_blocks, "col")
-    if count == 1:
-        norm_mod = norm_mod[jnp.bitwise_xor(jnp.arange(col_count), col_pos)]
-        norm_mod = norm_mod.reshape(1, full_width, 5)
     ready = call(
         functools.partial(norm_kernel, offsets, count, img),
-        jax.ShapeDtypeStruct((full_width, tokens), BF16),
+        jax.ShapeDtypeStruct((tokens, full_width), BF16),
         [SMEM, VMEM] + [ANY] * len(offsets),
-        [pltpu.VMEM((full_width, tokens), BF16), pltpu.SemaphoreType.DMA((len(offsets),))],
+        [
+            pltpu.VMEM((full_width, tokens), BF16),
+            pltpu.VMEM((tokens, 128), F32),
+            pltpu.VMEM((tokens, 128), F32),
+            pltpu.SemaphoreType.DMA((len(offsets),)),
+        ],
         cost(12 * full_width * tokens, 4 * full_width * tokens),
     )(place, norm_mod, *x_blocks)
 
+    gains = jnp.tile(jnp.concatenate([q_gain[None], k_gain], axis=0), (1, half // head))
     attended = []
     for n in range(2):
         blocks, masks = in_order(gathered[n], "row")
         queries, pair = call(
             functools.partial(project_kernel, masks, img, head),
             (
-                jax.ShapeDtypeStruct((half, img), BF16),
-                jax.ShapeDtypeStruct((2 * half, tokens), BF16),
+                jax.ShapeDtypeStruct((img, half), BF16),
+                jax.ShapeDtypeStruct((tokens, 2 * half), BF16),
             ),
-            [SMEM, VMEM, VMEM, VMEM] + [ANY] * len(masks),
+            [SMEM, VMEM, VMEM] + [ANY] * len(masks),
             [pltpu.VMEM((full_width, 5 * half), BF16), pltpu.SemaphoreType.DMA((len(masks),))],
             cost(2 * full_width * half * (3 * img + 2 * txt), 10 * full_width * half),
             (VMEM, VMEM),
-        )(place, q_gain[:, None], k_gain.T, ready, *blocks)
+        )(place, gains, ready, *blocks)
         peer = swap(pair, "row", 1)
-        keys = 2 * img + 2 * ((txt + 127) // 128 * 128)
         attended.append(
             call(
-                functools.partial(attend_kernel, img, head),
+                functools.partial(attend_kernel, img, txt, head),
                 jax.ShapeDtypeStruct((half, img), BF16),
                 [SMEM, VMEM, VMEM, VMEM],
-                [pltpu.VMEM((half, keys), BF16)] * 2,
-                cost(4 * half * keys * img, 8 * half * keys, keys * img * half // head),
+                [],
+                cost(8 * half * tokens * img, 8 * half * tokens, 2 * tokens * img * half // head),
             )(place, queries, pair, peer)
         )
 

time: 250 us -> 229 us (0.916)
  local copies, waits for them, and re-layouts: 36.9 us -> 22.1 us
  starting transfers between devices: 75 us -> 86.1 us
  Pallas kernels: 49.6 us -> 42.7 us
  waiting for transfers between devices: 76.7 us -> 71 us
  other arithmetic: 7.74 us -> 2.95 us
    ppermute x30 -> x31, waiting for transfers between devices: 63.4 us -> 55.7 us  [swap(): return lax.ppermute(block, axis, [(i, i ^ mask) for i in range(count)])]
    ppermute x30 -> x31, starting transfers between devices: 21 us -> 28.5 us  [swap(): return lax.ppermute(block, axis, [(i, i ^ mask) for i in range(count)])]
    ppermute x5 -> x0, local copies, waits for them, and re-layouts: 6.02 us -> none  [swap(): return lax.ppermute(block, axis, [(i, i ^ mask) for i in range(count)])]
    pallas_call x1, Pallas kernels: 12.8 us -> 7.51 us  [per_device(): call(functools.partial(norm_kernel, offsets, count, img), jax.ShapeDtypeS...]
    ppermute x18, starting transfers between devices: 53.9 us -> 57.7 us  [shift(): return lax.ppermute(block, axis, route)]
    transpose x1 -> x0, other arithmetic: 2.54 us -> none  [per_device(): norm_mod = jnp.swapaxes(norm_mod, 1, 2)]
    pallas_call x3 -> x4, Pallas kernels: 15 us -> 14.1 us  [the longest x2 10.8 us: per_device(): call(functools.partial(attend_kernel, img, txt, head), jax.ShapeDtypeStru...]
    unnamed x86 -> x59, local copies, waits for them, and re-layouts: 19.3 us -> 18.9 us
  transfers between devices with their start and end apart: 48 -> 49, of which waited for: 13 -> 14; matrix products, arithmetic and copies ran while one was open for 11% -> 3% of each run, Pallas kernels for 18% -> 15%
where the time goes in v2:
time: 229 us; the launch traced here: 227 us
  starting transfers between devices  86.1 us (38%)
  waiting for transfers between devices  71 us (31%)
  Pallas kernels  42.7 us (19%)
  local copies, waits for them, and re-layouts  22.1 us (10%)
  other arithmetic  2.95 us (1%)
  between operations  2.56 us (1%)
    ppermute x18, starting transfers between devices, shift(): return lax.ppermute(block, axis, route)  57.7 us
    ppermute x31, waiting for transfers between devices, swap(): return lax.ppermute(block, axis, [(i, i ^ mask) for i in range(count)])  55.7 us
    ppermute x31, starting transfers between devices, swap(): return lax.ppermute(block, axis, [(i, i ^ mask) for i in range(count)])  28.5 us
    unnamed x59, local copies, waits for them, and re-layouts  18.9 us
    pallas_call x2, Pallas kernels, per_device(): call(functools.partial(project_kernel, masks, img, head), (jax.ShapeDtype...  15.9 us
    ppermute x18, waiting for transfers between devices, shift(): return lax.ppermute(block, axis, route)  15.3 us
    pallas_call x2, Pallas kernels, per_device(): call(functools.partial(attend_kernel, img, txt, head), jax.ShapeDtypeStru...  10.8 us
    pallas_call x1, Pallas kernels, per_device(): call(functools.partial(norm_kernel, offsets, count, img), jax.ShapeDtypeS...  7.51 us
  transfers between devices with their start and end apart: 49, of which 14 were waited for; matrix products, arithmetic and copies ran while one was open for 3% of the time, Pallas kernels for 15%

profile of v2, /device:TPU:0, one launch (start us, length us, event | category | flops | bytes accessed | tf_op | source)
XLA Modules:
  0.0 227.5 jit_solution(4898908156558287421)
XLA Ops:
  0.6 1.2 copy-done.2
  1.8 1.1 copy-done.9
  2.9 2.2 shard_map.141
  5.1 3.0 %collective-permute-start = (bf16[304,1280]{1,0:T(8,128)(2,1)}, bf16[304,1280]{1,0:T(8,128)(2,1)}, u32[]{:S(2)}, u32[]{:S(2)}) collective-permute-start(bf16[304,1280]{1,0:T(8,128)(2,1)} %get-tuple-element.10.refs_0_), channel_id=1, source_target_pairs={{0,16},{4,20},{8,24},{12,28},{16,0},{20,4},{24,8},{28,12},{1,17},{... | collective-permute-start | bytes 2334728 | tf_op jit(solution)/shard_map/ppermute | solution.py:22
  8.1 1.7 copy.18
  9.7 1.2 fusion.1.refs_3_
  11.0 1.3 collective-permute-start.10
  12.3 5.4 %collective-permute-start.7 = (bf16[608,640]{1,0:T(8,128)(2,1)S(1)}, bf16[608,640]{1,0:T(8,128)(2,1)}, u32[]{:S(2)}, u32[]{:S(2)}) collective-permute-start(bf16[608,640]{1,0:T(8,128)(2,1)S(1)} %fusion.1.refs_3_), channel_id=1, source_target_pairs={{0,1},{1,2},{2,3},{4,5},{5,6},{6,7},{8,9},{9,10},{10,11},{12,13},{... | collective-permute-start | bytes 2334728 | tf_op jit(solution)/shard_map/ppermute | solution.py:28
  17.7 1.5 collective-permute-start.27
  21.1 1.0 shard_map.140
  22.1 4.5 %collective-permute-done.refs_4_ = bf16[304,1280]{1,0:T(8,128)(2,1)} collective-permute-done((bf16[304,1280]{1,0:T(8,128)(2,1)}, bf16[304,1280]{1,0:T(8,128)(2,1)}, u32[]{:S(2)}, u32[]{:S(2)}) %collective-permute-start) | collective-permute-done | bytes 778272 | tf_op jit(solution)/shard_map/ppermute | solution.py:22
  26.6 5.2 %collective-permute-done.10.refs_4_ = bf16[608,640]{1,0:T(8,128)(2,1)} collective-permute-done((bf16[608,640]{1,0:T(8,128)(2,1)S(1)}, bf16[608,640]{1,0:T(8,128)(2,1)}, u32[]{:S(2)}, u32[]{:S(2)}) %collective-permute-start.10) | collective-permute-done | bytes 778272 | tf_op jit(solution)/shard_map/ppermute | solution.py:28
  31.8 1.5 collective-permute-start.1
  33.3 3.3 %collective-permute-done.1 = f32[8,640]{1,0:T(8,128)S(1)} collective-permute-done((f32[8,640]{1,0:T(8,128)S(1)}, f32[8,640]{1,0:T(8,128)S(1)}, u32[]{:S(2)}, u32[]{:S(2)}) %collective-permute-start.1) | collective-permute-done | bytes 20512 | tf_op jit(solution)/shard_map/ppermute | solution.py:22
  37.0 5.8 %collective-permute-done.2 = f32[8,640]{1,0:T(8,128)S(1)} collective-permute-done((f32[8,640]{1,0:T(8,128)S(1)}, f32[8,640]{1,0:T(8,128)S(1)}, u32[]{:S(2)}, u32[]{:S(2)}) %collective-permute-start.2) | collective-permute-done | bytes 20512 | tf_op jit(solution)/shard_map/ppermute | solution.py:22
  42.8 2.7 %collective-permute-start.3 = (f32[8,640]{1,0:T(8,128)S(1)}, f32[8,640]{1,0:T(8,128)S(1)}, u32[]{:S(2)}, u32[]{:S(2)}) collective-permute-start(f32[8,640]{1,0:T(8,128)S(1)} %get-tuple-element.25), channel_id=1, source_target_pairs={{0,24},{4,28},{8,16},{12,20},{16,8},{20,12},{24,0},{28,4},{1,25},{... | collective-permute-start | bytes 61448 | tf_op jit(solution)/shard_map/ppermute | solution.py:22
  45.4 2.0 collective-permute-done.3
  47.4 1.7 collective-permute-start.14
  49.3 1.3 collective-permute-start.11
  50.6 5.5 %collective-permute-start.8 = (bf16[608,640]{1,0:T(8,128)(2,1)}, bf16[608,640]{1,0:T(8,128)(2,1)}, u32[]{:S(2)}, u32[]{:S(2)}) collective-permute-start(bf16[608,640]{1,0:T(8,128)(2,1)} %collective-permute-done.7.refs_2_), channel_id=1, source_target_pairs={{0,1},{1,2},{2,3},{4,5},{5,6},{6,7},{8,9},{9,10},{10,11},{12,13},{... | collective-permute-start | bytes 2334728 | tf_op jit(solution)/shard_map/ppermute | solution.py:28
  56.0 1.5 collective-permute-start.31
  57.9 0.9 collective-permute-start.5
  58.9 15.1 %collective-permute-done.5 = f32[8,2432]{1,0:T(8,128)S(1)} collective-permute-done((f32[8,2432]{1,0:T(8,128)S(1)}, f32[8,2432]{1,0:T(8,128)S(1)}, u32[]{:S(2)}, u32[]{:S(2)}) %collective-permute-start.5) | collective-permute-done | bytes 77856 | tf_op jit(solution)/shard_map/ppermute | solution.py:22
  74.4 3.7 %collective-permute-start.6 = (f32[8,2432]{1,0:T(8,128)S(1)}, f32[8,2432]{1,0:T(8,128)S(1)}, u32[]{:S(2)}, u32[]{:S(2)}) collective-permute-start(f32[8,2432]{1,0:T(8,128)S(1)} %add.73), channel_id=1, source_target_pairs={{0,2},{1,3},{2,0},{3,1},{4,6},{5,7},{6,4},{7,5},{8,10},{9,11},{10,... | collective-permute-start | bytes 233480 | tf_op jit(solution)/shard_map/ppermute | solution.py:22
  78.1 3.0 %collective-permute-done.6 = f32[8,2432]{1,0:T(8,128)S(1)} collective-permute-done((f32[8,2432]{1,0:T(8,128)S(1)}, f32[8,2432]{1,0:T(8,128)S(1)}, u32[]{:S(2)}, u32[]{:S(2)}) %collective-permute-start.6) | collective-permute-done | bytes 77856 | tf_op jit(solution)/shard_map/ppermute | solution.py:22
  81.7 1.3 collective-permute-start.12
  83.0 5.0 %collective-permute-start.9 = (bf16[608,640]{1,0:T(8,128)(2,1)}, bf16[608,640]{1,0:T(8,128)(2,1)S(1)}, u32[]{:S(2)}, u32[]{:S(2)}) collective-permute-start(bf16[608,640]{1,0:T(8,128)(2,1)} %collective-permute-done.8.refs_1_), channel_id=1, source_target_pairs={{0,1},{1,2},{2,3},{4,5},{5,6},{6,7},{8,9},{9,10},{10,11},{12,13},{... | collective-permute-start | bytes 2334728 | tf_op jit(solution)/shard_map/ppermute | solution.py:28
  89.5 11.7 %collective-permute-done.17.refs_6_ = bf16[304,1280]{1,0:T(8,128)(2,1)} collective-permute-done((bf16[304,1280]{1,0:T(8,128)(2,1)}, bf16[304,1280]{1,0:T(8,128)(2,1)}, u32[]{:S(2)}, u32[]{:S(2)}) %collective-permute-start.17) | collective-permute-done | bytes 778272 | tf_op jit(solution)/shard_map/ppermute | solution.py:22
  101.2 2.7 %collective-permute-done.12.refs_6_ = bf16[608,640]{1,0:T(8,128)(2,1)S(1)} collective-permute-done((bf16[608,640]{1,0:T(8,128)(2,1)}, bf16[608,640]{1,0:T(8,128)(2,1)S(1)}, u32[]{:S(2)}, u32[]{:S(2)}) %collective-permute-start.12) | collective-permute-done | bytes 778272 | tf_op jit(solution)/shard_map/ppermute | solution.py:28
  105.2 0.9 copy-done.7
  107.2 1.1 copy-done.6
  108.3 1.1 copy-done.8
  109.4 7.5 %shard_map.142.x_ref = bf16[640,2432]{1,0:T(8,128)(2,1)S(1)} custom-call(s32[3]{0:T(128)S(1)} %pad_add_fusion.place_ref, f32[8,2432]{1,0:T(8,128)S(1)} %add.74.mod_ref, bf16[608,640]{1,0:T(8,128)(2,1)S(1)} %copy-done.8, bf16[608,640]{1,0:T(8,128)(2,1)} %collective-permute-done.8.refs_1_, bf16[608,640]{1,0:T(8,128)(2,1)} %collective-permute-done.7.refs_2_, ...), custom_call_target="tpu_custom_call" | custom-call | flops 18677760 | bytes 6225920 | tf_op jit(solution)/shard_map/pallas_call | solution.py:395
  117.0 7.8 %shard_map.145 = (bf16[512,256]{1,0:T(8,128)(2,1)S(1)}, bf16[640,512]{1,0:T(8,128)(2,1)S(1)}) custom-call(s32[3]{0:T(128)S(1)} %pad_add_fusion.place_ref, f32[3,256]{1,0:T(4,128)S(1)} %tile.10.gain_ref, bf16[640,2432]{1,0:T(8,128)(2,1)S(1)} %shard_map.142.x_ref, bf16[304,1280]{1,0:T(8,128)(2,1)} %get-tuple-element.15.refs_0_, ...), custom_call_target="tpu_custom_call" | custom-call | flops 2151677952 | bytes 6225920 | tf_op jit(solution)/shard_map/pallas_call | solution.py:412
  125.5 8.0 %shard_map.143 = (bf16[512,256]{1,0:T(8,128)(2,1)S(1)}, bf16[640,512]{1,0:T(8,128)(2,1)S(1)}) custom-call(s32[3]{0:T(128)S(1)} %pad_add_fusion.place_ref, f32[3,256]{1,0:T(4,128)S(1)} %tile.10.gain_ref, bf16[640,2432]{1,0:T(8,128)(2,1)S(1)} %shard_map.142.x_ref, bf16[304,1280]{1,0:T(8,128)(2,1)} %get-tuple-element.10.refs_0_, ...), custom_call_target="tpu_custom_call" | custom-call | flops 2151677952 | bytes 6225920 | tf_op jit(solution)/shard_map/pallas_call | solution.py:412
  134.0 1.5 collective-permute-start.41
  135.5 1.5 collective-permute-start.43
  138.1 5.4 %shard_map.146.refs_10_ = bf16[256,512]{1,0:T(8,128)(2,1)S(1)} custom-call(s32[3]{0:T(128)S(1)} %pad_add_fusion.place_ref, bf16[512,256]{1,0:T(8,128)(2,1)S(1)} %get-tuple-element.16.q_ref, bf16[640,512]{1,0:T(8,128)(2,1)S(1)} %get-tuple-element.17.own_ref, bf16[640,512]{1,0:T(8,128)(2,1)S(1)} %collective-permute-done.33.peer_ref), custom_call_target="tpu_custom_call" | custom-call | flops 671088640 | bytes 1310720 | tf_op jit(solution)/shard_map/pallas_call | solution.py:425
  143.5 4.6 %collective-permute-start.34 = (bf16[256,512]{1,0:T(8,128)(2,1)S(1)}, bf16[256,512]{1,0:T(8,128)(2,1)S(1)}, u32[]{:S(2)}, u32[]{:S(2)}) collective-permute-start(bf16[256,512]{1,0:T(8,128)(2,1)S(1)} %shard_map.146.refs_10_), channel_id=1, source_target_pairs={{0,1},{1,2},{2,3},{4,5},{5,6},{6,7},{8,9},{9,10},{10,11},{12,13},{... | collective-permute-start | bytes 786440 | tf_op jit(solution)/shard_map/ppermute | solution.py:28
  148.1 5.4 %shard_map.144.refs_3_ = bf16[256,512]{1,0:T(8,128)(2,1)S(1)} custom-call(s32[3]{0:T(128)S(1)} %pad_add_fusion.place_ref, bf16[512,256]{1,0:T(8,128)(2,1)S(1)} %get-tuple-element.13.q_ref, bf16[640,512]{1,0:T(8,128)(2,1)S(1)} %get-tuple-element.14.own_ref, bf16[640,512]{1,0:T(8,128)(2,1)S(1)} %collective-permute-done.19.peer_ref), custom_call_target="tpu_custom_call" | custom-call | flops 671088640 | bytes 1310720 | tf_op jit(solution)/shard_map/pallas_call | solution.py:425
  153.6 1.3 collective-permute-start.37
  154.9 4.6 %collective-permute-start.20 = (bf16[256,512]{1,0:T(8,128)(2,1)S(1)}, bf16[256,512]{1,0:T(8,128)(2,1)S(1)}, u32[]{:S(2)}, u32[]{:S(2)}) collective-permute-start(bf16[256,512]{1,0:T(8,128)(2,1)S(1)} %shard_map.144.refs_3_), channel_id=1, source_target_pairs={{0,1},{1,2},{2,3},{4,5},{5,6},{6,7},{8,9},{9,10},{10,11},{12,13},{... | collective-permute-start | bytes 786440 | tf_op jit(solution)/shard_map/ppermute | solution.py:28
  159.4 1.3 collective-permute-start.23
  161.5 1.5 collective-permute-start.45
  163.0 5.3 %collective-permute-start.35 = (bf16[256,512]{1,0:T(8,128)(2,1)S(1)}, bf16[256,512]{1,0:T(8,128)(2,1)}, u32[]{:S(2)}, u32[]{:S(2)}) collective-permute-start(bf16[256,512]{1,0:T(8,128)(2,1)S(1)} %collective-permute-done.34.refs_9_), channel_id=1, source_target_pairs={{0,1},{1,2},{2,3},{4,5},{5,6},{6,7},{8,9},{9,10},{10,11},{12,13},{... | collective-permute-start | bytes 786440 | tf_op jit(solution)/shard_map/ppermute | solution.py:28
  169.0 1.3 collective-permute-start.38
  170.9 5.2 %collective-permute-start.21 = (bf16[256,512]{1,0:T(8,128)(2,1)S(1)}, bf16[256,512]{1,0:T(8,128)(2,1)}, u32[]{:S(2)}, u32[]{:S(2)}) collective-permute-start(bf16[256,512]{1,0:T(8,128)(2,1)S(1)} %collective-permute-done.20.refs_2_), channel_id=1, source_target_pairs={{0,1},{1,2},{2,3},{4,5},{5,6},{6,7},{8,9},{9,10},{10,11},{12,13},{... | collective-permute-start | bytes 786440 | tf_op jit(solution)/shard_map/ppermute | solution.py:28
  176.9 1.3 collective-permute-start.24
  180.2 5.3 %collective-permute-start.36 = (bf16[256,512]{1,0:T(8,128)(2,1)}, bf16[256,512]{1,0:T(8,128)(2,1)}, u32[]{:S(2)}, u32[]{:S(2)}) collective-permute-start(bf16[256,512]{1,0:T(8,128)(2,1)} %collective-permute-done.35.refs_8_), channel_id=1, source_target_pairs={{0,1},{1,2},{2,3},{4,5},{5,6},{6,7},{8,9},{9,10},{10,11},{12,13},{... | collective-permute-start | bytes 786440 | tf_op jit(solution)/shard_map/ppermute | solution.py:28
  185.4 1.3 collective-permute-start.39
  186.7 5.3 %collective-permute-start.22 = (bf16[256,512]{1,0:T(8,128)(2,1)}, bf16[256,512]{1,0:T(8,128)(2,1)}, u32[]{:S(2)}, u32[]{:S(2)}) collective-permute-start(bf16[256,512]{1,0:T(8,128)(2,1)} %collective-permute-done.21.refs_1_), channel_id=1, source_target_pairs={{0,1},{1,2},{2,3},{4,5},{5,6},{6,7},{8,9},{9,10},{10,11},{12,13},{... | collective-permute-start | bytes 786440 | tf_op jit(solution)/shard_map/ppermute | solution.py:28
  192.0 1.3 collective-permute-start.25
  193.6 2.3 %collective-permute-done.39.refs_13_ = bf16[256,512]{1,0:T(8,128)(2,1)} collective-permute-done((bf16[256,512]{1,0:T(8,128)(2,1)}, bf16[256,512]{1,0:T(8,128)(2,1)}, u32[]{:S(2)}, u32[]{:S(2)}) %collective-permute-start.39) | collective-permute-done | bytes 262176 | tf_op jit(solution)/shard_map/ppermute | solution.py:28
  195.9 4.7 %collective-permute-done.25.refs_6_ = bf16[256,512]{1,0:T(8,128)(2,1)} collective-permute-done((bf16[256,512]{1,0:T(8,128)(2,1)}, bf16[256,512]{1,0:T(8,128)(2,1)}, u32[]{:S(2)}, u32[]{:S(2)}) %collective-permute-start.25) | collective-permute-done | bytes 262176 | tf_op jit(solution)/shard_map/ppermute | solution.py:28
  200.6 1.0 copy-done.11
  201.6 0.9 copy-done.13
  202.5 0.9 copy-done.15
  203.5 0.9 copy-done.17
  204.4 0.9 copy-done.19
  205.4 0.9 copy-done.21
  206.3 5.3 %shard_map.147 = f32[72,640]{1,0:T(8,128)S(1)} custom-call(s32[3]{0:T(128)S(1)} %pad_add_fusion.place_ref, f32[608,1]{1,0:T(8,128)S(1)} %copy.20.gate_ref, f32[2,2,304]{2,1,0:T(2,128)S(1)} %bitcast.49, bf16[608,512]{1,0:T(8,128)(2,1)S(1)} %bitcast.47, bf16[256,512]{1,0:T(8,128)(2,1)} %collective-permute-done.22.refs_0_, ...), custom_call_target="tpu_custom_call" | custom-call | flops 1275068416 | bytes 9961472 | tf_op jit(solution)/shard_map/pallas_call | solution.py:446
  212.0 6.2 %collective-permute-done.47 = f32[72,640]{1,0:T(8,128)S(1)} collective-permute-done((f32[72,640]{1,0:T(8,128)S(1)}, f32[72,640]{1,0:T(8,128)S(1)}, u32[]{:S(2)}, u32[]{:S(2)}) %collective-permute-start.47) | collective-permute-done | bytes 184352 | tf_op jit(solution)/shard_map/ppermute | solution.py:22
  218.2 2.2 collective-permute-start.48
  222.4 4.0 %collective-permute-done.48 = f32[72,640]{1,0:T(8,128)S(1)} collective-permute-done((f32[72,640]{1,0:T(8,128)S(1)}, f32[72,640]{1,0:T(8,128)S(1)}, u32[]{:S(2)}, u32[]{:S(2)}) %collective-permute-start.48) | collective-permute-done | bytes 184352 | tf_op jit(solution)/shard_map/ppermute | solution.py:22
  (129 shorter events, 16.8 us)
Async XLA Ops:
  0.6 1.2 copy-start.2
  1.8 1.1 copy-start.9
  2.9 16.8 %copy-start.27 = (s32[4]{0:T(128)S(1)}, s32[4]{0:T(128)}, u32[]{:S(2)}) copy-start(s32[4]{0:T(128)} %param.15) | copy-start | bytes 52
  2.9 18.1 %copy-start = (bf16[304,7,608]{2,0,1:T(8,128)(2,1)S(1)}, bf16[304,7,608]{2,0,1:T(8,128)(2,1)}, u32[]{:S(2)}) copy-start(bf16[304,7,608]{2,0,1:T(8,128)(2,1)} %param.19) | copy-start | bytes 7762948
  2.9 18.1 %copy-start.22 = (f32[4,304]{1,0:T(4,128)S(1)}, f32[4,304]{1,0:T(4,128)}, u32[]{:S(2)}) copy-start(f32[4,304]{1,0:T(4,128)} %cond_ref.1) | copy-start | bytes 14596
  5.1 21.5 %collective-permute-start = (bf16[304,1280]{1,0:T(8,128)(2,1)}, bf16[304,1280]{1,0:T(8,128)(2,1)}, u32[]{:S(2)}, u32[]{:S(2)}) collective-permute-start(bf16[304,1280]{1,0:T(8,128)(2,1)} %get-tuple-element.10.refs_0_), channel_id=1, source_target_pairs={{0,16},{4,20},{8,24},{12,28},{16,0},{20,4},{24,8},{28,12},{1,17},{... | collective-permute-start | bytes 2334728 | tf_op jit(solution)/shard_map/ppermute | solution.py:22
  11.0 20.8 %collective-permute-start.10 = (bf16[608,640]{1,0:T(8,128)(2,1)S(1)}, bf16[608,640]{1,0:T(8,128)(2,1)}, u32[]{:S(2)}, u32[]{:S(2)}) collective-permute-start(bf16[608,640]{1,0:T(8,128)(2,1)S(1)} %fusion.1.refs_3_), channel_id=1, source_target_pairs={{1,0},{2,1},{3,2},{5,4},{6,5},{7,6},{9,8},{10,9},{11,10},{13,12},{... | collective-permute-start | bytes 2334728 | tf_op jit(solution)/shard_map/ppermute | solution.py:28
  12.3 36.9 %collective-permute-start.7 = (bf16[608,640]{1,0:T(8,128)(2,1)S(1)}, bf16[608,640]{1,0:T(8,128)(2,1)}, u32[]{:S(2)}, u32[]{:S(2)}) collective-permute-start(bf16[608,640]{1,0:T(8,128)(2,1)S(1)} %fusion.1.refs_3_), channel_id=1, source_target_pairs={{0,1},{1,2},{2,3},{4,5},{5,6},{6,7},{8,9},{9,10},{10,11},{12,13},{... | collective-permute-start | bytes 2334728 | tf_op jit(solution)/shard_map/ppermute | solution.py:28
  17.7 31.5 %collective-permute-start.27 = (bf16[304,1280]{1,0:T(8,128)(2,1)}, bf16[304,1280]{1,0:T(8,128)(2,1)}, u32[]{:S(2)}, u32[]{:S(2)}) collective-permute-start(bf16[304,1280]{1,0:T(8,128)(2,1)} %get-tuple-element.15.refs_0_), channel_id=1, source_target_pairs={{0,8},{4,12},{8,0},{12,4},{16,24},{20,28},{24,16},{28,20},{1,9},{5... | collective-permute-start | bytes 2334728 | tf_op jit(solution)/shard_map/ppermute | solution.py:22
  19.2 31.3 %collective-permute-start.29 = (bf16[304,1280]{1,0:T(8,128)(2,1)}, bf16[304,1280]{1,0:T(8,128)(2,1)}, u32[]{:S(2)}, u32[]{:S(2)}) collective-permute-start(bf16[304,1280]{1,0:T(8,128)(2,1)} %get-tuple-element.15.refs_0_), channel_id=1, source_target_pairs={{0,16},{4,20},{8,24},{12,28},{16,0},{20,4},{24,8},{28,12},{1,17},{... | collective-permute-start | bytes 2334728 | tf_op jit(solution)/shard_map/ppermute | solution.py:22
  21.0 85.2 %copy-start.25 = (f32[2,64]{1,0:T(2,128)S(1)}, f32[2,64]{1,0:T(2,128)}, u32[]{:S(2)}) copy-start(f32[2,64]{1,0:T(2,128)} %param.23) | copy-start | bytes 1540
  21.0 85.2 %copy-start.26 = (f32[64]{0:T(128)S(1)}, f32[64]{0:T(128)}, u32[]{:S(2)}) copy-start(f32[64]{0:T(128)} %param.22) | copy-start | bytes 772
  26.6 31.4 %collective-permute-start.26 = (bf16[304,1280]{1,0:T(8,128)(2,1)}, bf16[304,1280]{1,0:T(8,128)(2,1)S(1)}, u32[]{:S(2)}, u32[]{:S(2)}) collective-permute-start(bf16[304,1280]{1,0:T(8,128)(2,1)} %get-tuple-element.15.refs_0_), channel_id=1, source_target_pairs={{0,4},{4,0},{8,12},{12,8},{16,20},{20,16},{24,28},{28,24},{1,5},{5... | collective-permute-start | bytes 2334728 | tf_op jit(solution)/shard_map/ppermute | solution.py:22
  31.8 4.8 %collective-permute-start.1 = (f32[8,640]{1,0:T(8,128)S(1)}, f32[8,640]{1,0:T(8,128)S(1)}, u32[]{:S(2)}, u32[]{:S(2)}) collective-permute-start(f32[8,640]{1,0:T(8,128)S(1)} %get-tuple-element.24), channel_id=1, source_target_pairs={{0,8},{4,12},{8,0},{12,4},{16,24},{20,28},{24,16},{28,20},{1,9},{5... | collective-permute-start | bytes 61448 | tf_op jit(solution)/shard_map/ppermute | solution.py:22
  36.6 6.1 %collective-permute-start.2 = (f32[8,640]{1,0:T(8,128)S(1)}, f32[8,640]{1,0:T(8,128)S(1)}, u32[]{:S(2)}, u32[]{:S(2)}) collective-permute-start(f32[8,640]{1,0:T(8,128)S(1)} %get-tuple-element.26), channel_id=1, source_target_pairs={{0,16},{4,20},{8,24},{12,28},{16,0},{20,4},{24,8},{28,12},{1,17},{... | collective-permute-start | bytes 61448 | tf_op jit(solution)/shard_map/ppermute | solution.py:22
  42.8 4.7 %collective-permute-start.3 = (f32[8,640]{1,0:T(8,128)S(1)}, f32[8,640]{1,0:T(8,128)S(1)}, u32[]{:S(2)}, u32[]{:S(2)}) collective-permute-start(f32[8,640]{1,0:T(8,128)S(1)} %get-tuple-element.25), channel_id=1, source_target_pairs={{0,24},{4,28},{8,16},{12,20},{16,8},{20,12},{24,0},{28,4},{1,25},{... | collective-permute-start | bytes 61448 | tf_op jit(solution)/shard_map/ppermute | solution.py:22
  47.4 26.9 %collective-permute-start.14 = (bf16[304,1280]{1,0:T(8,128)(2,1)}, bf16[304,1280]{1,0:T(8,128)(2,1)S(1)}, u32[]{:S(2)}, u32[]{:S(2)}) collective-permute-start(bf16[304,1280]{1,0:T(8,128)(2,1)} %get-tuple-element.10.refs_0_), channel_id=1, source_target_pairs={{0,8},{4,12},{8,0},{12,4},{16,24},{20,28},{24,16},{28,20},{1,9},{5... | collective-permute-start | bytes 2334728 | tf_op jit(solution)/shard_map/ppermute | solution.py:22
  49.2 6.9 %collective-permute-start.4 = (f32[8,640]{1,0:T(8,128)S(1)}, f32[8,640]{1,0:T(8,128)S(1)}, u32[]{:S(2)}, u32[]{:S(2)}) collective-permute-start(f32[8,640]{1,0:T(8,128)S(1)} %fusion.7), channel_id=1, source_target_pairs={{0,4},{4,0},{8,12},{12,8},{16,20},{20,16},{24,28},{28,24},{1,5},{5... | collective-permute-start | bytes 61448 | tf_op jit(solution)/shard_map/ppermute | solution.py:22
  49.3 31.9 %collective-permute-start.11 = (bf16[608,640]{1,0:T(8,128)(2,1)}, bf16[608,640]{1,0:T(8,128)(2,1)}, u32[]{:S(2)}, u32[]{:S(2)}) collective-permute-start(bf16[608,640]{1,0:T(8,128)(2,1)} %collective-permute-done.10.refs_4_), channel_id=1, source_target_pairs={{1,0},{2,1},{3,2},{5,4},{6,5},{7,6},{9,8},{10,9},{11,10},{13,12},{... | collective-permute-start | bytes 2334728 | tf_op jit(solution)/shard_map/ppermute | solution.py:28
  50.6 31.1 %collective-permute-start.8 = (bf16[608,640]{1,0:T(8,128)(2,1)}, bf16[608,640]{1,0:T(8,128)(2,1)}, u32[]{:S(2)}, u32[]{:S(2)}) collective-permute-start(bf16[608,640]{1,0:T(8,128)(2,1)} %collective-permute-done.7.refs_2_), channel_id=1, source_target_pairs={{0,1},{1,2},{2,3},{4,5},{5,6},{6,7},{8,9},{9,10},{10,11},{12,13},{... | collective-permute-start | bytes 2334728 | tf_op jit(solution)/shard_map/ppermute | solution.py:28
  56.0 26.9 %collective-permute-start.31 = (bf16[304,1280]{1,0:T(8,128)(2,1)}, bf16[304,1280]{1,0:T(8,128)(2,1)S(1)}, u32[]{:S(2)}, u32[]{:S(2)}) collective-permute-start(bf16[304,1280]{1,0:T(8,128)(2,1)} %collective-permute-done.27.refs_2_), channel_id=1, source_target_pairs={{0,16},{4,20},{8,24},{12,28},{16,0},{20,4},{24,8},{28,12},{1,17},{... | collective-permute-start | bytes 2334728 | tf_op jit(solution)/shard_map/ppermute | solution.py:22
  57.9 16.0 %collective-permute-start.5 = (f32[8,2432]{1,0:T(8,128)S(1)}, f32[8,2432]{1,0:T(8,128)S(1)}, u32[]{:S(2)}, u32[]{:S(2)}) collective-permute-start(f32[8,2432]{1,0:T(8,128)S(1)} %dynamic_update_slice.5), channel_id=1, source_target_pairs={{0,1},{1,0},{2,3},{3,2},{4,5},{5,4},{6,7},{7,6},{8,9},{9,8},{10,11... | collective-permute-start | bytes 233480 | tf_op jit(solution)/shard_map/ppermute | solution.py:22
  74.0 14.0 %collective-permute-start.28 = (bf16[304,1280]{1,0:T(8,128)(2,1)}, bf16[304,1280]{1,0:T(8,128)(2,1)}, u32[]{:S(2)}, u32[]{:S(2)}) collective-permute-start(bf16[304,1280]{1,0:T(8,128)(2,1)} %collective-permute-done.27.refs_2_), channel_id=1, source_target_pairs={{0,4},{4,0},{8,12},{12,8},{16,20},{20,16},{24,28},{28,24},{1,5},{5... | collective-permute-start | bytes 2334728 | tf_op jit(solution)/shard_map/ppermute | solution.py:22
  74.4 6.7 %collective-permute-start.6 = (f32[8,2432]{1,0:T(8,128)S(1)}, f32[8,2432]{1,0:T(8,128)S(1)}, u32[]{:S(2)}, u32[]{:S(2)}) collective-permute-start(f32[8,2432]{1,0:T(8,128)S(1)} %add.73), channel_id=1, source_target_pairs={{0,2},{1,3},{2,0},{3,1},{4,6},{5,7},{6,4},{7,5},{8,10},{9,11},{10,... | collective-permute-start | bytes 233480 | tf_op jit(solution)/shard_map/ppermute | solution.py:22
  81.1 7.0 %collective-permute-start.30 = (bf16[304,1280]{1,0:T(8,128)(2,1)}, bf16[304,1280]{1,0:T(8,128)(2,1)S(1)}, u32[]{:S(2)}, u32[]{:S(2)}) collective-permute-start(bf16[304,1280]{1,0:T(8,128)(2,1)} %collective-permute-done.29.refs_4_), channel_id=1, source_target_pairs={{0,4},{4,0},{8,12},{12,8},{16,20},{20,16},{24,28},{28,24},{1,5},{5... | collective-permute-start | bytes 2334728 | tf_op jit(solution)/shard_map/ppermute | solution.py:22
  81.1 20.1 %collective-permute-start.17 = (bf16[304,1280]{1,0:T(8,128)(2,1)}, bf16[304,1280]{1,0:T(8,128)(2,1)}, u32[]{:S(2)}, u32[]{:S(2)}) collective-permute-start(bf16[304,1280]{1,0:T(8,128)(2,1)} %collective-permute-done.refs_4_), channel_id=1, source_target_pairs={{0,8},{4,12},{8,0},{12,4},{16,24},{20,28},{24,16},{28,20},{1,9},{5... | collective-permute-start | bytes 2334728 | tf_op jit(solution)/shard_map/ppermute | solution.py:22
  81.7 22.3 %collective-permute-start.12 = (bf16[608,640]{1,0:T(8,128)(2,1)}, bf16[608,640]{1,0:T(8,128)(2,1)S(1)}, u32[]{:S(2)}, u32[]{:S(2)}) collective-permute-start(bf16[608,640]{1,0:T(8,128)(2,1)} %collective-permute-done.11.refs_5_), channel_id=1, source_target_pairs={{1,0},{2,1},{3,2},{5,4},{6,5},{7,6},{9,8},{10,9},{11,10},{13,12},{... | collective-permute-start | bytes 2334728 | tf_op jit(solution)/shard_map/ppermute | solution.py:28
  83.0 22.3 %collective-permute-start.9 = (bf16[608,640]{1,0:T(8,128)(2,1)}, bf16[608,640]{1,0:T(8,128)(2,1)S(1)}, u32[]{:S(2)}, u32[]{:S(2)}) collective-permute-start(bf16[608,640]{1,0:T(8,128)(2,1)} %collective-permute-done.8.refs_1_), channel_id=1, source_target_pairs={{0,1},{1,2},{2,3},{4,5},{5,6},{6,7},{8,9},{9,10},{10,11},{12,13},{... | collective-permute-start | bytes 2334728 | tf_op jit(solution)/shard_map/ppermute | solution.py:28
  88.0 29.0 %collective-permute-start.32 = (bf16[304,1280]{1,0:T(8,128)(2,1)S(1)}, bf16[304,1280]{1,0:T(8,128)(2,1)}, u32[]{:S(2)}, u32[]{:S(2)}) collective-permute-start(bf16[304,1280]{1,0:T(8,128)(2,1)S(1)} %collective-permute-done.31.refs_6_), channel_id=1, source_target_pairs={{0,4},{4,0},{8,12},{12,8},{16,20},{20,16},{24,28},{28,24},{1,5},{5... | collective-permute-start | bytes 2334728 | tf_op jit(solution)/shard_map/ppermute | solution.py:22
  89.0 36.3 %collective-permute-start.13 = (bf16[304,1280]{1,0:T(8,128)(2,1)}, bf16[304,1280]{1,0:T(8,128)(2,1)}, u32[]{:S(2)}, u32[]{:S(2)}) collective-permute-start(bf16[304,1280]{1,0:T(8,128)(2,1)} %get-tuple-element.10.refs_0_), channel_id=1, source_target_pairs={{0,4},{4,0},{8,12},{12,8},{16,20},{20,16},{24,28},{28,24},{1,5},{5... | collective-permute-start | bytes 2334728 | tf_op jit(solution)/shard_map/ppermute | solution.py:22
  101.2 24.3 %collective-permute-start.16 = (bf16[304,1280]{1,0:T(8,128)(2,1)}, bf16[304,1280]{1,0:T(8,128)(2,1)}, u32[]{:S(2)}, u32[]{:S(2)}) collective-permute-start(bf16[304,1280]{1,0:T(8,128)(2,1)} %collective-permute-done.refs_4_), channel_id=1, source_target_pairs={{0,4},{4,0},{8,12},{12,8},{16,20},{20,16},{24,28},{28,24},{1,5},{5... | collective-permute-start | bytes 2334728 | tf_op jit(solution)/shard_map/ppermute | solution.py:22
  104.8 20.7 %collective-permute-start.15 = (bf16[304,1280]{1,0:T(8,128)(2,1)S(1)}, bf16[304,1280]{1,0:T(8,128)(2,1)}, u32[]{:S(2)}, u32[]{:S(2)}) collective-permute-start(bf16[304,1280]{1,0:T(8,128)(2,1)S(1)} %collective-permute-done.14.refs_2_), channel_id=1, source_target_pairs={{0,4},{4,0},{8,12},{12,8},{16,20},{20,16},{24,28},{28,24},{1,5},{5... | collective-permute-start | bytes 2334728 | tf_op jit(solution)/shard_map/ppermute | solution.py:22
  106.1 19.4 %collective-permute-start.18 = (bf16[304,1280]{1,0:T(8,128)(2,1)}, bf16[304,1280]{1,0:T(8,128)(2,1)}, u32[]{:S(2)}, u32[]{:S(2)}) collective-permute-start(bf16[304,1280]{1,0:T(8,128)(2,1)} %collective-permute-done.17.refs_6_), channel_id=1, source_target_pairs={{0,4},{4,0},{8,12},{12,8},{16,20},{20,16},{24,28},{28,24},{1,5},{5... | collective-permute-start | bytes 2334728 | tf_op jit(solution)/shard_map/ppermute | solution.py:22
  107.2 1.1 copy-start.6
  108.3 1.1 copy-start.8
  109.4 7.5 %copy-start.4 = (bf16[304,1280]{1,0:T(8,128)(2,1)S(1)}, bf16[304,1280]{1,0:T(8,128)(2,1)}, u32[]{:S(2)}) copy-start(bf16[304,1280]{1,0:T(8,128)(2,1)} %copy-done.3) | copy-start | bytes 2334724
  117.0 8.3 %copy-start.23 = (bf16[256,608]{0,1:T(8,128)(2,1)S(1)}, bf16[256,608]{0,1:T(8,128)(2,1)}, u32[]{:S(2)}) copy-start(bf16[256,608]{0,1:T(8,128)(2,1)} %param.24) | copy-start | bytes 933892
  124.8 12.8 %collective-permute-start.33 = (bf16[640,512]{1,0:T(8,128)(2,1)S(1)}, bf16[640,512]{1,0:T(8,128)(2,1)S(1)}, u32[]{:S(2)}, u32[]{:S(2)}) collective-permute-start(bf16[640,512]{1,0:T(8,128)(2,1)S(1)} %get-tuple-element.17.own_ref), channel_id=1, source_target_pairs={{0,4},{4,0},{8,12},{12,8},{16,20},{20,16},{24,28},{28,24},{1,5},{5... | collective-permute-start | bytes 1966088 | tf_op jit(solution)/shard_map/ppermute | solution.py:22
  125.3 11.7 %collective-permute-start.40 = (bf16[736,256]{1,0:T(8,128)(2,1)S(1)}, bf16[736,256]{1,0:T(8,128)(2,1)S(1)}, u32[]{:S(2)}, u32[]{:S(2)}) collective-permute-start(bf16[736,256]{1,0:T(8,128)(2,1)S(1)} %pad_maximum_fusion.refs_14_), channel_id=1, source_target_pairs={{0,4},{4,0},{8,12},{12,8},{16,20},{20,16},{24,28},{28,24},{1,5},{5... | collective-permute-start | bytes 1130504 | tf_op jit(solution)/shard_map/ppermute | solution.py:22
  133.6 10.0 %collective-permute-start.19 = (bf16[640,512]{1,0:T(8,128)(2,1)S(1)}, bf16[640,512]{1,0:T(8,128)(2,1)S(1)}, u32[]{:S(2)}, u32[]{:S(2)}) collective-permute-start(bf16[640,512]{1,0:T(8,128)(2,1)S(1)} %get-tuple-element.14.own_ref), channel_id=1, source_target_pairs={{0,4},{4,0},{8,12},{12,8},{16,20},{20,16},{24,28},{28,24},{1,5},{5... | collective-permute-start | bytes 1966088 | tf_op jit(solution)/shard_map/ppermute | solution.py:22
  134.0 19.5 %collective-permute-start.41 = (bf16[736,256]{1,0:T(8,128)(2,1)S(1)}, bf16[736,256]{1,0:T(8,128)(2,1)S(1)}, u32[]{:S(2)}, u32[]{:S(2)}) collective-permute-start(bf16[736,256]{1,0:T(8,128)(2,1)S(1)} %pad_maximum_fusion.refs_14_), channel_id=1, source_target_pairs={{0,8},{4,12},{8,0},{12,4},{16,24},{20,28},{24,16},{28,20},{1,9},{5... | collective-permute-start | bytes 1130504 | tf_op jit(solution)/shard_map/ppermute | solution.py:22
  135.5 19.3 %collective-permute-start.43 = (bf16[736,256]{1,0:T(8,128)(2,1)S(1)}, bf16[736,256]{1,0:T(8,128)(2,1)S(1)}, u32[]{:S(2)}, u32[]{:S(2)}) collective-permute-start(bf16[736,256]{1,0:T(8,128)(2,1)S(1)} %pad_maximum_fusion.refs_14_), channel_id=1, source_target_pairs={{0,16},{4,20},{8,24},{12,28},{16,0},{20,4},{24,8},{28,12},{1,17},{... | collective-permute-start | bytes 1130504 | tf_op jit(solution)/shard_map/ppermute | solution.py:22
  137.1 22.4 %collective-permute-start.42 = (bf16[736,256]{1,0:T(8,128)(2,1)S(1)}, bf16[736,256]{1,0:T(8,128)(2,1)S(1)}, u32[]{:S(2)}, u32[]{:S(2)}) collective-permute-start(bf16[736,256]{1,0:T(8,128)(2,1)S(1)} %collective-permute-done.40.refs_15_), channel_id=1, source_target_pairs={{0,8},{4,12},{8,0},{12,4},{16,24},{20,28},{24,16},{28,20},{1,9},{5... | collective-permute-start | bytes 1130504 | tf_op jit(solution)/shard_map/ppermute | solution.py:22
  137.6 23.9 %collective-permute-start.44 = (bf16[736,256]{1,0:T(8,128)(2,1)S(1)}, bf16[736,256]{1,0:T(8,128)(2,1)S(1)}, u32[]{:S(2)}, u32[]{:S(2)}) collective-permute-start(bf16[736,256]{1,0:T(8,128)(2,1)S(1)} %collective-permute-done.40.refs_15_), channel_id=1, source_target_pairs={{0,16},{4,20},{8,24},{12,28},{16,0},{20,4},{24,8},{28,12},{1,17},{... | collective-permute-start | bytes 1130504 | tf_op jit(solution)/shard_map/ppermute | solution.py:22
  143.5 19.4 %collective-permute-start.34 = (bf16[256,512]{1,0:T(8,128)(2,1)S(1)}, bf16[256,512]{1,0:T(8,128)(2,1)S(1)}, u32[]{:S(2)}, u32[]{:S(2)}) collective-permute-start(bf16[256,512]{1,0:T(8,128)(2,1)S(1)} %shard_map.146.refs_10_), channel_id=1, source_target_pairs={{0,1},{1,2},{2,3},{4,5},{5,6},{6,7},{8,9},{9,10},{10,11},{12,13},{... | collective-permute-start | bytes 786440 | tf_op jit(solution)/shard_map/ppermute | solution.py:28
  148.1 52.4 %copy-start.1 = (bf16[512,608]{0,1:T(8,128)(2,1)S(1)}, bf16[512,608]{0,1:T(8,128)(2,1)}, u32[]{:S(2)}) copy-start(bf16[512,608]{0,1:T(8,128)(2,1)} %param.13) | copy-start | bytes 1867780
  153.6 15.4 %collective-permute-start.37 = (bf16[256,512]{1,0:T(8,128)(2,1)S(1)}, bf16[256,512]{1,0:T(8,128)(2,1)S(1)}, u32[]{:S(2)}, u32[]{:S(2)}) collective-permute-start(bf16[256,512]{1,0:T(8,128)(2,1)S(1)} %shard_map.146.refs_10_), channel_id=1, source_target_pairs={{1,0},{2,1},{3,2},{5,4},{6,5},{7,6},{9,8},{10,9},{11,10},{13,12},{... | collective-permute-start | bytes 786440 | tf_op jit(solution)/shard_map/ppermute | solution.py:28
  154.9 16.1 %collective-permute-start.20 = (bf16[256,512]{1,0:T(8,128)(2,1)S(1)}, bf16[256,512]{1,0:T(8,128)(2,1)S(1)}, u32[]{:S(2)}, u32[]{:S(2)}) collective-permute-start(bf16[256,512]{1,0:T(8,128)(2,1)S(1)} %shard_map.144.refs_3_), channel_id=1, source_target_pairs={{0,1},{1,2},{2,3},{4,5},{5,6},{6,7},{8,9},{9,10},{10,11},{12,13},{... | collective-permute-start | bytes 786440 | tf_op jit(solution)/shard_map/ppermute | solution.py:28
  159.4 17.5 %collective-permute-start.23 = (bf16[256,512]{1,0:T(8,128)(2,1)S(1)}, bf16[256,512]{1,0:T(8,128)(2,1)S(1)}, u32[]{:S(2)}, u32[]{:S(2)}) collective-permute-start(bf16[256,512]{1,0:T(8,128)(2,1)S(1)} %shard_map.144.refs_3_), channel_id=1, source_target_pairs={{1,0},{2,1},{3,2},{5,4},{6,5},{7,6},{9,8},{10,9},{11,10},{13,12},{... | collective-permute-start | bytes 786440 | tf_op jit(solution)/shard_map/ppermute | solution.py:28
  161.5 17.4 %collective-permute-start.45 = (bf16[736,256]{1,0:T(8,128)(2,1)S(1)}, bf16[736,256]{1,0:T(8,128)(2,1)S(1)}, u32[]{:S(2)}, u32[]{:S(2)}) collective-permute-start(bf16[736,256]{1,0:T(8,128)(2,1)S(1)} %collective-permute-done.41.refs_16_), channel_id=1, source_target_pairs={{0,16},{4,20},{8,24},{12,28},{16,0},{20,4},{24,8},{28,12},{1,17},{... | collective-permute-start | bytes 1130504 | tf_op jit(solution)/shard_map/ppermute | solution.py:22
  163.0 17.2 %collective-permute-start.35 = (bf16[256,512]{1,0:T(8,128)(2,1)S(1)}, bf16[256,512]{1,0:T(8,128)(2,1)}, u32[]{:S(2)}, u32[]{:S(2)}) collective-permute-start(bf16[256,512]{1,0:T(8,128)(2,1)S(1)} %collective-permute-done.34.refs_9_), channel_id=1, source_target_pairs={{0,1},{1,2},{2,3},{4,5},{5,6},{6,7},{8,9},{9,10},{10,11},{12,13},{... | collective-permute-start | bytes 786440 | tf_op jit(solution)/shard_map/ppermute | solution.py:28
  169.0 16.5 %collective-permute-start.38 = (bf16[256,512]{1,0:T(8,128)(2,1)S(1)}, bf16[256,512]{1,0:T(8,128)(2,1)}, u32[]{:S(2)}, u32[]{:S(2)}) collective-permute-start(bf16[256,512]{1,0:T(8,128)(2,1)S(1)} %collective-permute-done.37.refs_11_), channel_id=1, source_target_pairs={{1,0},{2,1},{3,2},{5,4},{6,5},{7,6},{9,8},{10,9},{11,10},{13,12},{... | collective-permute-start | bytes 786440 | tf_op jit(solution)/shard_map/ppermute | solution.py:28
  170.9 15.8 %collective-permute-start.21 = (bf16[256,512]{1,0:T(8,128)(2,1)S(1)}, bf16[256,512]{1,0:T(8,128)(2,1)}, u32[]{:S(2)}, u32[]{:S(2)}) collective-permute-start(bf16[256,512]{1,0:T(8,128)(2,1)S(1)} %collective-permute-done.20.refs_2_), channel_id=1, source_target_pairs={{0,1},{1,2},{2,3},{4,5},{5,6},{6,7},{8,9},{9,10},{10,11},{12,13},{... | collective-permute-start | bytes 786440 | tf_op jit(solution)/shard_map/ppermute | solution.py:28
  176.9 15.1 %collective-permute-start.24 = (bf16[256,512]{1,0:T(8,128)(2,1)S(1)}, bf16[256,512]{1,0:T(8,128)(2,1)}, u32[]{:S(2)}, u32[]{:S(2)}) collective-permute-start(bf16[256,512]{1,0:T(8,128)(2,1)S(1)} %collective-permute-done.23.refs_4_), channel_id=1, source_target_pairs={{1,0},{2,1},{3,2},{5,4},{6,5},{7,6},{9,8},{10,9},{11,10},{13,12},{... | collective-permute-start | bytes 786440 | tf_op jit(solution)/shard_map/ppermute | solution.py:28
  179.7 13.9 %collective-permute-start.46 = (bf16[736,256]{1,0:T(8,128)(2,1)S(1)}, bf16[736,256]{1,0:T(8,128)(2,1)}, u32[]{:S(2)}, u32[]{:S(2)}) collective-permute-start(bf16[736,256]{1,0:T(8,128)(2,1)S(1)} %collective-permute-done.42.refs_17_), channel_id=1, source_target_pairs={{0,16},{4,20},{8,24},{12,28},{16,0},{20,4},{24,8},{28,12},{1,17},{... | collective-permute-start | bytes 1130504 | tf_op jit(solution)/shard_map/ppermute | solution.py:22
  180.2 13.4 %collective-permute-start.36 = (bf16[256,512]{1,0:T(8,128)(2,1)}, bf16[256,512]{1,0:T(8,128)(2,1)}, u32[]{:S(2)}, u32[]{:S(2)}) collective-permute-start(bf16[256,512]{1,0:T(8,128)(2,1)} %collective-permute-done.35.refs_8_), channel_id=1, source_target_pairs={{0,1},{1,2},{2,3},{4,5},{5,6},{6,7},{8,9},{9,10},{10,11},{12,13},{... | collective-permute-start | bytes 786440 | tf_op jit(solution)/shard_map/ppermute | solution.py:28
  185.4 10.5 %collective-permute-start.39 = (bf16[256,512]{1,0:T(8,128)(2,1)}, bf16[256,512]{1,0:T(8,128)(2,1)}, u32[]{:S(2)}, u32[]{:S(2)}) collective-permute-start(bf16[256,512]{1,0:T(8,128)(2,1)} %collective-permute-done.38.refs_12_), channel_id=1, source_target_pairs={{1,0},{2,1},{3,2},{5,4},{6,5},{7,6},{9,8},{10,9},{11,10},{13,12},{... | collective-permute-start | bytes 786440 | tf_op jit(solution)/shard_map/ppermute | solution.py:28
  186.7 9.2 %collective-permute-start.22 = (bf16[256,512]{1,0:T(8,128)(2,1)}, bf16[256,512]{1,0:T(8,128)(2,1)}, u32[]{:S(2)}, u32[]{:S(2)}) collective-permute-start(bf16[256,512]{1,0:T(8,128)(2,1)} %collective-permute-done.21.refs_1_), channel_id=1, source_target_pairs={{0,1},{1,2},{2,3},{4,5},{5,6},{6,7},{8,9},{9,10},{10,11},{12,13},{... | collective-permute-start | bytes 786440 | tf_op jit(solution)/shard_map/ppermute | solution.py:28
  192.0 8.6 %collective-permute-start.25 = (bf16[256,512]{1,0:T(8,128)(2,1)}, bf16[256,512]{1,0:T(8,128)(2,1)}, u32[]{:S(2)}, u32[]{:S(2)}) collective-permute-start(bf16[256,512]{1,0:T(8,128)(2,1)} %collective-permute-done.24.refs_5_), channel_id=1, source_target_pairs={{1,0},{2,1},{3,2},{5,4},{6,5},{7,6},{9,8},{10,9},{11,10},{13,12},{... | collective-permute-start | bytes 786440 | tf_op jit(solution)/shard_map/ppermute | solution.py:28
  200.6 1.0 copy-start.11
  206.3 14.1 %copy-start.28 = (s32[4]{0:T(128)S(1)}, s32[4]{0:T(128)}, u32[]{:S(2)}) copy-start(s32[4]{0:T(128)} %param.16) | copy-start | bytes 52
  206.3 20.3 %copy-start.24 = (f32[512,64]{0,1:T(8,128)S(1)}, f32[512,64]{0,1:T(8,128)}, u32[]{:S(2)}) copy-start(f32[512,64]{0,1:T(8,128)} %param.17) | copy-start | bytes 393220
  211.6 6.6 %collective-permute-start.47 = (f32[72,640]{1,0:T(8,128)S(1)}, f32[72,640]{1,0:T(8,128)S(1)}, u32[]{:S(2)}, u32[]{:S(2)}) collective-permute-start(f32[72,640]{1,0:T(8,128)S(1)} %shard_map.147), channel_id=1, source_target_pairs={{0,1},{1,0},{2,3},{3,2},{4,5},{5,4},{6,7},{7,6},{8,9},{9,8},{10,11... | collective-permute-start | bytes 552968 | tf_op jit(solution)/shard_map/ppermute | solution.py:22
  218.2 8.2 %collective-permute-start.48 = (f32[72,640]{1,0:T(8,128)S(1)}, f32[72,640]{1,0:T(8,128)S(1)}, u32[]{:S(2)}, u32[]{:S(2)}) collective-permute-start(f32[72,640]{1,0:T(8,128)S(1)} %add.75), channel_id=1, source_target_pairs={{0,2},{1,3},{2,0},{3,1},{4,6},{5,7},{6,4},{7,5},{8,10},{9,11},{10,... | collective-permute-start | bytes 552968 | tf_op jit(solution)/shard_map/ppermute | solution.py:22
  (14 other events, 11.7 us)

commit v3 on v2

--- a/solution.py
+++ b/solution.py
@@ -11,7 +11,6 @@
 EPS_NORM = 1e-06
 F32 = jnp.float32
 BF16 = jnp.bfloat16
-VMEM_LIMIT = 24 * 1024 * 1024
 ANY = pl.BlockSpec(memory_space=pl.ANY)
 VMEM = pl.BlockSpec(memory_space=pltpu.VMEM)
 SMEM = pl.BlockSpec(memory_space=pltpu.SMEM)
@@ -29,11 +28,35 @@
 
 
 def line_gather(block, axis):
+    count = lax.axis_size(axis)
+    if count == 4:
+        send = lambda held, route: lax.ppermute(held, axis, route)
+        middle, outward = [(1, 2), (2, 1)], [(1, 0), (2, 3)]
+        pair = swap(block, axis, 1)
+        near = send(block, middle)
+        far = send(pair, middle)
+        inner = lambda p: (p == 1) | (p == 2)
+        outer = lambda p: (p == 0) | (p == 3)
+        other = lambda p: jnp.where(p < 2, 2, 1)
+        other_far = lambda p: jnp.where(p < 2, 3, 0)
+        always = lambda p: p >= 0
+        return [
+            (block, lambda p: p, always),
+            (pair, lambda p: jnp.bitwise_xor(p, 1), always),
+            (near, other, inner),
+            (send(near, outward), other, outer),
+            (far, other_far, inner),
+            (send(far, outward), other_far, outer),
+        ]
     held = {0: block}
-    for step in range(1, lax.axis_size(axis)):
+    for step in range(1, count):
         held[-step] = shift(held[1 - step], axis, 1)
         held[step] = shift(held[step - 1], axis, -1)
-    return held
+    result = []
+    for offset in sorted(held):
+        inside = lambda p, offset=offset: (p + offset >= 0) & (p + offset < count)
+        result.append((held[offset], lambda p, offset=offset: p + offset, inside))
+    return result
 
 
 def doubling_gather(block, axis, masks):
@@ -42,16 +65,6 @@
         for known in list(held):
             held[known | mask] = swap(held[known], axis, mask)
     return held
-
-
-def in_line(held, axis):
-    offsets, count = sorted(held), lax.axis_size(axis)
-    rows = held[0].shape[0]
-    if rows % 16 == 0:
-        return [held[k] for k in offsets], offsets, count
-    joined = jnp.concatenate([held[k] for k in offsets], axis=0)
-    first = (count - 1 - lax.axis_index(axis)) * rows
-    return [lax.dynamic_slice_in_dim(joined, first, count * rows, 0)], [None], 1
 
 
 def in_order(held, axis):
@@ -68,7 +81,7 @@
     return pl.CostEstimate(flops=flops, bytes_accessed=touched, transcendentals=exps)
 
 
-def call(kernel, outs, in_specs, scratch, estimate, out_specs=None):
+def call(kernel, outs, in_specs, scratch, estimate, out_specs=None, vmem=24):
     if out_specs is None:
         out_specs = jax.tree.map(lambda _: VMEM, outs)
     return pl.pallas_call(
@@ -78,17 +91,16 @@
         out_specs=out_specs,
         scratch_shapes=scratch,
         cost_estimate=estimate,
-        compiler_params=pltpu.CompilerParams(vmem_limit_bytes=VMEM_LIMIT),
+        compiler_params=pltpu.CompilerParams(vmem_limit_bytes=vmem * 1024 * 1024),
     )
 
 
-def line_copies(refs, offsets, place, count, target, sems, act):
-    for n, (ref, offset) in enumerate(zip(refs, offsets)):
-        owner = 0 if offset is None else place + offset
-
-        @pl.when((owner >= 0) & (owner < count))
+def line_copies(refs, routes, place, target, sems, act):
+    for n, (ref, (owner, held)) in enumerate(zip(refs, routes)):
+
+        @pl.when(held(place))
         def _():
-            copy = pltpu.make_async_copy(ref, target(owner), sems.at[n])
+            copy = pltpu.make_async_copy(ref, target(owner(place)), sems.at[n])
             getattr(copy, act)()
 
 
@@ -116,74 +128,95 @@
             out_ref[:, (3 + k) * half : (4 + k) * half] = kv_ref[:, k, low:high]
 
 
-def norm_kernel(offsets, count, img, place_ref, mod_ref, *refs):
-    blocks = refs[: len(offsets)]
-    out_ref, x_ref, average_ref, inverse_ref, sems = refs[len(offsets) :]
-    width, tokens = blocks[0].shape
-    place = place_ref[1]
-    target = lambda owner: x_ref.at[pl.ds(pl.multiple_of(owner * width, 16), width)]
-    line_copies(blocks, offsets, place, count, target, sems, "start")
-    line_copies(blocks, offsets, place, count, target, sems, "wait")
-    total = width * count
+def stats_kernel(img_ref, txt_ref, out_ref):
+    img = img_ref.shape[1]
+    txt = txt_ref.shape[0]
+    out_ref[...] = jnp.zeros(out_ref.shape, F32)
+    for values, low, high in (
+        (img_ref[...].astype(F32), 0, img),
+        (txt_ref[...].astype(F32).T, img, img + txt),
+    ):
+        out_ref[0:1, low:high] = jnp.sum(values, axis=0, keepdims=True)
+        out_ref[1:2, low:high] = jnp.sum(values * values, axis=0, keepdims=True)
+
+
+def norm_kernel(total, img_ref, txt_ref, stats_ref, mod_ref, *out_refs):
+    width, img = img_ref.shape
+    txt = txt_ref.shape[0]
+    stats = stats_ref[...] / total
+    row = lax.broadcasted_iota(jnp.int32, stats.shape, 0)
+    average = stats[0:1]
+    inverse = lax.rsqrt(stats[1:2] - average * average + EPS_NORM)
+    columns = jnp.where(row == 0, average, inverse).T
+    split = out_refs[0].shape[0]
     chunk = 128
-
-    def turn(i, carry):
-        at = pl.multiple_of(i * chunk, chunk)
-        part = x_ref[pl.ds(at, chunk)].T
-        out_ref[:, pl.ds(at, chunk)] = part
-        wide = part.astype(F32)
-        sums, squares = carry
-        return sums + wide, squares + wide * wide
-
-    zero = jnp.zeros((tokens, chunk), F32)
-    sums, squares = lax.fori_loop(0, total // chunk, turn, (zero, zero))
-    average = jnp.sum(sums, axis=1, keepdims=True) / total
-    mean_square = jnp.sum(squares, axis=1, keepdims=True) / total
-    inverse = lax.rsqrt(mean_square - average * average + EPS_NORM)
-    average_ref[...] = jnp.broadcast_to(average, (tokens, chunk))
-    inverse_ref[...] = jnp.broadcast_to(inverse, (tokens, chunk))
-
-    def normalise(i, _):
-        at = pl.multiple_of(i * chunk, chunk)
-        here = pl.ds(at, chunk)
-        for low, high, group in ((0, img, 0), (img, tokens, 3)):
-            normed = out_ref[low:high, here].astype(F32) - average_ref[low:high]
-            normed = normed * inverse_ref[low:high]
-            stretch = 1.0 + mod_ref[group + 1 : group + 2, here]
-            out_ref[low:high, here] = (normed * stretch + mod_ref[group : group + 1, here]).astype(BF16)
-        return 0
-
-    lax.fori_loop(0, total // chunk, normalise, 0)
-
-
-def project_kernel(masks, img, head, place_ref, gain_ref, x_ref, *refs):
-    blocks = refs[: len(masks)]
-    q_ref, kv_ref, w_ref, sems = refs[len(masks) :]
-    depth = blocks[0].shape[0]
+    for low in range(0, img + txt, chunk):
+        for start in range(0, width, chunk):
+            stop = min(start + chunk, width)
+            if low < img:
+                high = min(low + chunk, img)
+                values, group = img_ref[start:stop, low:high].T, 0
+            else:
+                high = min(low + chunk, img + txt)
+                values, group = txt_ref[low - img : high - img, start:stop], 3
+            normed = (values.astype(F32) - columns[low:high, 0:1]) * columns[low:high, 1:2]
+            stretch = 1.0 + mod_ref[group + 1 : group + 2, start:stop]
+            normed = (normed * stretch + mod_ref[group : group + 1, start:stop]).astype(BF16)
+            for n, out_ref in enumerate(out_refs):
+                top, bottom = max(low, n * split), min(high, (n + 1) * split)
+                if top < bottom:
+                    out_ref[top - n * split : bottom - n * split, start:stop] = normed[
+                        top - low : bottom - low
+                    ]
+
+
+def project_kernel(routes, masks, img, head, place_ref, gain_ref, *refs):
+    lines = []
+    for _ in range(2):
+        lines.append(refs[: len(routes)])
+        refs = refs[len(routes) :]
+    blocks, refs = refs[: len(masks)], refs[len(masks) :]
+    q_ref, kv_ref, x_ref, w_ref, img_ref, txt_ref, sems_x, sems_w = refs
+    split = lines[0][0].shape[0]
+    txt = 2 * split - img
+    count, width = x_ref.shape[0], x_ref.shape[2]
     half = q_ref.shape[1]
     place = place_ref[0]
-    copies = []
-    for n, (ref, mask) in enumerate(zip(blocks, masks)):
-        owner = 0 if mask is None else jnp.bitwise_xor(place, mask)
-        copies.append(
-            pltpu.make_async_copy(
-                ref, w_ref.at[pl.ds(pl.multiple_of(owner * depth, 16), depth)], sems.at[n]
-            )
-        )
-    for copy in copies:
-        copy.start()
-    for copy in copies:
-        copy.wait()
+    for n, line in enumerate(lines):
+        target = lambda owner, n=n: x_ref.at[owner, pl.ds(n * split, split)]
+        line_copies(line, routes, place_ref[1], target, sems_x.at[n], "start")
+    chips = {}
+    if masks == [None]:
+        chips[0] = [pltpu.make_async_copy(blocks[0], w_ref, sems_w.at[0])]
+    else:
+        depth = blocks[0].shape[0]
+        for n, (ref, mask) in enumerate(zip(blocks, masks)):
+            owner = jnp.bitwise_xor(place, mask)
+            here = pl.ds(pl.multiple_of(owner % 2 * depth, 16), depth)
+            copy = pltpu.make_async_copy(ref, w_ref.at[owner // 2, here], sems_w.at[n])
+            chips.setdefault(mask // 2, []).append(copy)
+    for copies in chips.values():
+        for copy in copies:
+            copy.start()
+    for n, line in enumerate(lines):
+        target = lambda owner, n=n: x_ref.at[owner, pl.ds(n * split, split)]
+        line_copies(line, routes, place_ref[1], target, sems_x.at[n], "wait")
+    for k in range(count):
+        for copy in chips.get(k, ()):
+            copy.wait()
+        chip = jnp.bitwise_xor(place // 2, k)
+        for ref, low, rows, first, parts in ((img_ref, 0, img, 0, 3), (txt_ref, img, txt, 3, 2)):
+            for part in range(parts):
+                term = jnp.dot(
+                    x_ref[chip, low : low + rows],
+                    w_ref[chip, :, (first + part) * half : (first + part + 1) * half],
+                    preferred_element_type=F32,
+                )
+                ref[part] = term if k == 0 else ref[part] + term
+
     row = lax.broadcasted_iota(jnp.int32, (half, half), 0) // head
     col = lax.broadcasted_iota(jnp.int32, (half, half), 1) // head
     mean_of = jnp.where(row == col, 1.0 / head, 0.0).astype(BF16)
-
-    def product(part, low, high):
-        return jnp.dot(
-            x_ref[low:high],
-            w_ref[:, part * half : (part + 1) * half],
-            preferred_element_type=F32,
-        )
 
     def head_norm(values, gain):
         square = values * values
@@ -194,14 +227,14 @@
             square = square - term.astype(F32)
         return (values * lax.rsqrt(mean_square + EPS_NORM) * gain).astype(BF16)
 
-    tokens = x_ref.shape[0]
     scaling = head ** (-0.5)
-    queries = head_norm(product(0, 0, img), gain_ref[0:1])
+    queries = head_norm(img_ref[0], gain_ref[0:1])
     q_ref[...] = (queries.astype(F32) * scaling).astype(BF16)
-    kv_ref[:img, :half] = head_norm(product(1, 0, img), gain_ref[1:2])
-    kv_ref[:img, half:] = product(2, 0, img).astype(BF16)
-    kv_ref[img:, :half] = head_norm(product(3, img, tokens), gain_ref[2:3])
-    kv_ref[img:, half:] = product(4, img, tokens).astype(BF16)
+    kv_ref[:img, :half] = head_norm(img_ref[1], gain_ref[1:2])
+    kv_ref[:img, half:] = img_ref[2].astype(BF16)
+    kv_ref[img : img + txt, :half] = head_norm(txt_ref[0], gain_ref[2:3])
+    kv_ref[img : img + txt, half:] = txt_ref[1].astype(BF16)
+    kv_ref[img + txt :] = jnp.zeros((kv_ref.shape[0] - img - txt, 2 * half), BF16)
 
 
 def attend_kernel(img, txt, head, place_ref, q_ref, own_ref, peer_ref, out_ref):
@@ -243,9 +276,9 @@
 
 
 def output_kernel(
-    offsets, count, masks, place_ref, gate_ref, out_mod_ref, x_ref, *refs
+    routes, count, masks, place_ref, gate_ref, out_mod_ref, x_ref, *refs
 ):
-    n_lines = len(offsets)
+    n_lines = len(routes)
     firsts, refs = refs[:n_lines], refs[n_lines:]
     seconds, refs = refs[:n_lines], refs[n_lines:]
     weights, refs = refs[: len(masks)], refs[len(masks) :]
@@ -266,7 +299,7 @@
             target = lambda owner, n=n: a_ref.at[
                 pl.ds(pl.multiple_of((2 * owner + n) * half, half), half)
             ]
-            line_copies(blocks, offsets, col, count, target, sems, act)
+            line_copies(blocks, routes, col, target, sems, act)
     for copy in copies:
         copy.wait()
     depth = w_ref.shape[2]
@@ -348,12 +381,32 @@
     length = lax.dynamic_index_in_dim(text_len, request, 0, keepdims=False)
     place = jnp.stack([row_pos, col_pos, length]).astype(jnp.int32)
 
+    wide = -(-width // 128) * 128
     room = -(-txt // 128) * 128
     tokens = img + room
-    x_own = jnp.concatenate(
-        [hidden_img.T, jnp.pad(hidden_txt.T, ((0, 0), (0, room - txt)))], axis=1
-    )
-    x_blocks = line_gather(x_own, "col")
+    mod_part = call(
+        mod_kernel,
+        jax.ShapeDtypeStruct((requests, 8, wide), F32),
+        [SMEM, VMEM, VMEM],
+        [],
+        cost(2 * requests * cond.shape[1] * 7 * width, mod_weight.size * 2),
+    )(place, cond, jnp.moveaxis(mod_weight, 1, 0))
+    mod_own = mod_part[0]
+    for k in range(1, requests):
+        mod_own = mod_own + swap(mod_part[k], "row", 2 * k)
+    mod_own = mod_own + swap(mod_own, "row", 1)
+    stats = call(
+        stats_kernel,
+        jax.ShapeDtypeStruct((8, tokens), F32),
+        [VMEM, VMEM],
+        [],
+        cost(4 * width * tokens, 2 * width * tokens),
+    )(hidden_img.T, hidden_txt)
+    mask = 1
+    while mask < col_count:
+        stats = stats + swap(stats, "col", mask)
+        mask *= 2
+
     chip_masks = [1 << bit for bit in range(1, row_count.bit_length() - 1)]
     packed = call(
         pack_kernel,
@@ -363,63 +416,48 @@
         cost(0, 20 * qkv_weight.shape[0] * half),
         (VMEM, VMEM),
     )(jnp.moveaxis(qkv_weight, 1, 0), kv_text_weight)
+    packed, mod_own = lax.optimization_barrier((packed, mod_own))
     gathered = []
     for n in range(2):
         order = chip_masks[::-1] if n == 0 else chip_masks
         gathered.append(doubling_gather(packed[n], "row", order + [1]))
 
-    wide = -(-width // 128) * 128
-    mod_part = call(
-        mod_kernel,
-        jax.ShapeDtypeStruct((requests, 8, wide), F32),
-        [SMEM, VMEM, VMEM],
+    split = (img + txt) // 2
+    ready = call(
+        functools.partial(norm_kernel, full_width),
+        (jax.ShapeDtypeStruct((split, width), BF16),) * 2,
+        [VMEM] * 4,
         [],
-        cost(2 * requests * cond.shape[1] * 7 * width, mod_weight.size * 2),
-    )(place, cond, jnp.moveaxis(mod_weight, 1, 0))
-    first = chip_masks[-1]
-    mod_part, gathered[0][first] = lax.optimization_barrier((mod_part, gathered[0][first]))
-    mod_own = mod_part[0]
-    for k in range(1, requests):
-        mod_own = mod_own + swap(mod_part[k], "row", 2 * k)
-    mod_own = mod_own + swap(mod_own, "row", 1)
-    norm_mod = lax.dynamic_update_slice_in_dim(
-        jnp.zeros((8, full_width), F32), mod_own[:, :width], col_pos * width, 1
-    )
-    mask = 1
-    while mask < col_count:
-        norm_mod = norm_mod + swap(norm_mod, "col", mask)
-        mask *= 2
-    mod_own = mod_own[:, :width]
-
-    x_blocks, offsets, count = in_line(x_blocks, "col")
-    ready = call(
-        functools.partial(norm_kernel, offsets, count, img),
-        jax.ShapeDtypeStruct((tokens, full_width), BF16),
-        [SMEM, VMEM] + [ANY] * len(offsets),
-        [
-            pltpu.VMEM((full_width, tokens), BF16),
-            pltpu.VMEM((tokens, 128), F32),
-            pltpu.VMEM((tokens, 128), F32),
-            pltpu.SemaphoreType.DMA((len(offsets),)),
-        ],
-        cost(12 * full_width * tokens, 4 * full_width * tokens),
-    )(place, norm_mod, *x_blocks)
+        cost(12 * width * tokens, 4 * width * tokens),
+        (VMEM, VMEM),
+    )(hidden_img.T, hidden_txt, stats, mod_own)
+    lines = [line_gather(part, "col") for part in ready]
+    routes = [entry[1:] for entry in lines[0]]
 
     gains = jnp.tile(jnp.concatenate([q_gain[None], k_gain], axis=0), (1, half // head))
     attended = []
     for n in range(2):
         blocks, masks = in_order(gathered[n], "row")
+        if masks == [None]:
+            blocks = [blocks[0].reshape(col_count, width, 5 * half)]
         queries, pair = call(
-            functools.partial(project_kernel, masks, img, head),
+            functools.partial(project_kernel, routes, masks, img, head),
             (
                 jax.ShapeDtypeStruct((img, half), BF16),
                 jax.ShapeDtypeStruct((tokens, 2 * half), BF16),
             ),
-            [SMEM, VMEM, VMEM] + [ANY] * len(masks),
-            [pltpu.VMEM((full_width, 5 * half), BF16), pltpu.SemaphoreType.DMA((len(masks),))],
+            [SMEM, VMEM] + [ANY] * (2 * len(routes) + len(masks)),
+            [
+                pltpu.VMEM((col_count, img + txt, width), BF16),
+                pltpu.VMEM((col_count, width, 5 * half), BF16),
+                pltpu.VMEM((3, img, half), F32),
+                pltpu.VMEM((2, txt, half), F32),
+                pltpu.SemaphoreType.DMA((2, len(routes))),
+                pltpu.SemaphoreType.DMA((len(masks),)),
+            ],
             cost(2 * full_width * half * (3 * img + 2 * txt), 10 * full_width * half),
             (VMEM, VMEM),
-        )(place, gains, ready, *blocks)
+        )(place, gains, *[entry[0] for line in lines for entry in line], *blocks)
         peer = swap(pair, "row", 1)
         attended.append(
             call(
@@ -439,28 +477,28 @@
     out_packed = jnp.concatenate([out_weight.T, tail], axis=0)
     out_blocks = doubling_gather(out_packed, "row", [1] + chip_masks)
     masks = sorted(out_blocks)
-    offsets = list(range(1 - col_count, col_count))
     lines = [line_gather(block, "col") for block in attended]
     per_col = row_count // col_count
-    out_mod = mod_own[5:7].reshape(2, per_col, width // per_col).swapaxes(0, 1)
+    out_mod = mod_own[5:7, :width].reshape(2, per_col, width // per_col).swapaxes(0, 1)
     partial_sum = call(
-        functools.partial(output_kernel, offsets, col_count, masks),
+        functools.partial(output_kernel, routes, col_count, masks),
         jax.ShapeDtypeStruct((patch + 8, img + 128), F32),
-        [SMEM, VMEM, VMEM, VMEM] + [ANY] * (2 * len(offsets) + len(masks)),
+        [SMEM, VMEM, VMEM, VMEM] + [ANY] * (2 * len(routes) + len(masks)),
         [
             pltpu.VMEM((part_cols * col_count, img), BF16),
             pltpu.VMEM((row_count,) + out_packed.shape, BF16),
-            pltpu.SemaphoreType.DMA((len(offsets),)),
-            pltpu.SemaphoreType.DMA((len(offsets),)),
+            pltpu.SemaphoreType.DMA((len(routes),)),
+            pltpu.SemaphoreType.DMA((len(routes),)),
             pltpu.SemaphoreType.DMA((len(masks),)),
         ],
         cost(2 * part_cols * col_count * width * img, 8 * part_cols * col_count * width),
+        vmem=48,
     )(
         place,
-        mod_own[2][:, None],
+        mod_own[2, :width][:, None],
         out_mod,
         hidden_img.T,
-        *[line[k] for line in lines for k in offsets],
+        *[entry[0] for line in lines for entry in line],
         *[out_blocks[k] for k in masks],
     )
     mask = 1

time: 229 us -> 224 us (0.978)
  starting transfers between devices: 86.1 us -> 43.8 us
  waiting for transfers between devices: 71 us -> 113 us
  Pallas kernels: 42.7 us -> 37.3 us
  local copies, waits for them, and re-layouts: 22.1 us -> 24.8 us
    ppermute x18 -> x16, waiting for transfers between devices: 15.3 us -> 60 us  [line_gather(): send = lambda held, route: lax.ppermute(held, axis, route)]
    ppermute x18 -> x16, starting transfers between devices: 57.7 us -> 18.5 us  [line_gather(): send = lambda held, route: lax.ppermute(held, axis, route)]
    pallas_call x4 -> x5, Pallas kernels: 28.6 us -> 23.9 us  [the longest x2 17.2 us: per_device(): call(functools.partial(project_kernel, routes, masks, img, head), (jax.Sh...]
    unnamed x59 -> x70, local copies, waits for them, and re-layouts: 18.9 us -> 22.4 us
    ppermute x31 -> x35, starting transfers between devices: 28.5 us -> 25.3 us  [swap(): return lax.ppermute(block, axis, [(i, i ^ mask) for i in range(count)])]
    ppermute x31 -> x35, waiting for transfers between devices: 55.7 us -> 52.9 us  [swap(): return lax.ppermute(block, axis, [(i, i ^ mask) for i in range(count)])]
  transfers between devices with their start and end apart: 49 -> 51, of which waited for: 14 -> 21; matrix products, arithmetic and copies ran while one was open for 3% -> 0% of each run, Pallas kernels for 15% -> 13%
where the time goes in v3:
time: 224 us; the launch traced here: 223 us
  waiting for transfers between devices  113 us (50%)
  starting transfers between devices  43.8 us (20%)
  Pallas kernels  37.3 us (17%)
  local copies, waits for them, and re-layouts  24.8 us (11%)
  between operations  2.56 us (1%)
    ppermute x16, waiting for transfers between devices, line_gather(): send = lambda held, route: lax.ppermute(held, axis, route)  60 us
    ppermute x35, waiting for transfers between devices, swap(): return lax.ppermute(block, axis, [(i, i ^ mask) for i in range(count)])  52.9 us
    ppermute x35, starting transfers between devices, swap(): return lax.ppermute(block, axis, [(i, i ^ mask) for i in range(count)])  25.3 us
    unnamed x70, local copies, waits for them, and re-layouts  22.4 us
    ppermute x16, starting transfers between devices, line_gather(): send = lambda held, route: lax.ppermute(held, axis, route)  18.5 us
    pallas_call x2, Pallas kernels, per_device(): call(functools.partial(project_kernel, routes, masks, img, head), (jax.Sh...  17.2 us
    pallas_call x2, Pallas kernels, per_device(): call(functools.partial(attend_kernel, img, txt, head), jax.ShapeDtypeStru...  10.8 us
    pallas_call x1, Pallas kernels, per_device(): call(functools.partial(output_kernel, routes, col_count, masks), jax.Shap...  5.74 us
  transfers between devices with their start and end apart: 51, of which 21 were waited for; matrix products, arithmetic and copies ran while one was open for 0% of the time, Pallas kernels for 13%

profile of v3, /device:TPU:0, one launch (start us, length us, event | category | flops | bytes accessed | tf_op | source)
XLA Modules:
  0.0 223.0 jit_solution(7845538466546824082)
XLA Ops:
  0.7 1.3 dynamic_slice.7
  2.7 1.8 copy-done.1
  5.2 1.0 shard_map.141
  6.2 3.0 %collective-permute-start = (f32[8,640]{1,0:T(8,128)S(1)}, f32[8,640]{1,0:T(8,128)S(1)}, u32[]{:S(2)}, u32[]{:S(2)}) collective-permute-start(f32[8,640]{1,0:T(8,128)S(1)} %get-tuple-element.30), channel_id=1, source_target_pairs={{0,8},{4,12},{8,0},{12,4},{16,24},{20,28},{24,16},{28,20},{1,9},{5... | collective-permute-start | bytes 61448 | tf_op jit(solution)/shard_map/ppermute | solution.py:21
  9.2 1.5 collective-permute-start.1
  11.0 2.1 collective-permute-start.4
  13.1 2.4 %collective-permute-done.2 = f32[8,640]{1,0:T(8,128)S(1)} collective-permute-done((f32[8,640]{1,0:T(8,128)S(1)}, f32[8,640]{1,0:T(8,128)S(1)}, u32[]{:S(2)}, u32[]{:S(2)}) %collective-permute-start.2) | collective-permute-done | bytes 20512 | tf_op jit(solution)/shard_map/ppermute | solution.py:21
  15.6 2.7 %collective-permute-start.5 = (f32[8,640]{1,0:T(8,128)S(1)}, f32[8,640]{1,0:T(8,128)S(1)}, u32[]{:S(2)}, u32[]{:S(2)}) collective-permute-start(f32[8,640]{1,0:T(8,128)S(1)} %add.66), channel_id=1, source_target_pairs={{0,2},{1,3},{2,0},{3,1},{4,6},{5,7},{6,4},{7,5},{8,10},{9,11},{10,... | collective-permute-start | bytes 61448 | tf_op jit(solution)/shard_map/ppermute | solution.py:21
  18.2 1.6 shard_map.140
  21.1 1.6 collective-permute-start.6
  24.5 8.5 %collective-permute-done.6.refs_1_ = bf16[304,608]{1,0:T(8,128)(2,1)S(1)} collective-permute-done((bf16[304,608]{1,0:T(8,128)(2,1)S(1)}, bf16[304,608]{1,0:T(8,128)(2,1)S(1)}, u32[]{:S(2)}, u32[]{:S(2)}) %collective-permute-start.6) | collective-permute-done | bytes 369696 | tf_op jit(solution)/shard_map/ppermute | solution.py:21
  33.7 6.4 %collective-permute-done.11.refs_7_ = bf16[304,608]{1,0:T(8,128)(2,1)S(1)} collective-permute-done((bf16[304,608]{1,0:T(8,128)(2,1)S(1)}, bf16[304,608]{1,0:T(8,128)(2,1)S(1)}, u32[]{:S(2)}, u32[]{:S(2)}) %collective-permute-start.11) | collective-permute-done | bytes 369696 | tf_op jit(solution)/shard_map/ppermute | solution.py:21
  40.8 1.3 collective-permute-start.13
  42.1 1.3 collective-permute-start.8
  44.5 11.5 %collective-permute-done.13.refs_9_ = bf16[304,608]{1,0:T(8,128)(2,1)S(1)} collective-permute-done((bf16[304,608]{1,0:T(8,128)(2,1)S(1)}, bf16[304,608]{1,0:T(8,128)(2,1)S(1)}, u32[]{:S(2)}, u32[]{:S(2)}) %collective-permute-start.13) | collective-permute-done | bytes 369696 | tf_op jit(solution)/shard_map/ppermute | solution.py:33
  57.3 4.5 %collective-permute-done.8.refs_3_ = bf16[304,608]{1,0:T(8,128)(2,1)S(1)} collective-permute-done((bf16[304,608]{1,0:T(8,128)(2,1)S(1)}, bf16[304,608]{1,0:T(8,128)(2,1)S(1)}, u32[]{:S(2)}, u32[]{:S(2)}) %collective-permute-start.8) | collective-permute-done | bytes 369696 | tf_op jit(solution)/shard_map/ppermute | solution.py:33
  62.5 1.9 collective-permute-done.32.refs_16_
  64.3 0.9 copy-done.13
  65.2 0.9 copy-done.17
  66.6 0.9 copy-done.15
  67.5 13.6 %collective-permute-done.19.refs_16_ = bf16[304,1280]{1,0:T(8,128)(2,1)} collective-permute-done((bf16[304,1280]{1,0:T(8,128)(2,1)}, bf16[304,1280]{1,0:T(8,128)(2,1)}, u32[]{:S(2)}, u32[]{:S(2)}) %collective-permute-start.19) | collective-permute-done | bytes 778272 | tf_op jit(solution)/shard_map/ppermute | solution.py:21
  81.1 1.5 collective-permute-start.21
  82.6 1.3 collective-permute-start.10
  83.9 19.3 %collective-permute-done.10.refs_5_ = bf16[304,608]{1,0:T(8,128)(2,1)S(1)} collective-permute-done((bf16[304,608]{1,0:T(8,128)(2,1)S(1)}, bf16[304,608]{1,0:T(8,128)(2,1)S(1)}, u32[]{:S(2)}, u32[]{:S(2)}) %collective-permute-start.10) | collective-permute-done | bytes 369696 | tf_op jit(solution)/shard_map/ppermute | solution.py:33
  104.0 1.3 collective-permute-start.15
  105.4 8.2 %collective-permute-done.15.refs_11_ = bf16[304,608]{1,0:T(8,128)(2,1)S(1)} collective-permute-done((bf16[304,608]{1,0:T(8,128)(2,1)S(1)}, bf16[304,608]{1,0:T(8,128)(2,1)S(1)}, u32[]{:S(2)}, u32[]{:S(2)}) %collective-permute-start.15) | collective-permute-done | bytes 369696 | tf_op jit(solution)/shard_map/ppermute | solution.py:33
  114.4 0.9 copy-done.19
  115.8 0.9 copy-done.21
  117.3 1.0 copy-done.3
  118.3 1.0 copy-done.5
  119.3 1.0 copy-done.7
  120.3 1.0 copy-done.9
  121.3 1.1 copy-done.12
  122.4 1.1 copy-done.14
  123.6 1.1 copy-done.16
  124.7 1.1 copy-done.18
  125.8 1.1 copy-done.20
  127.0 1.1 copy-done.22
  128.1 9.0 %shard_map.146 = (bf16[512,256]{1,0:T(8,128)(2,1)S(1)}, bf16[640,512]{1,0:T(8,128)(2,1)S(1)}) custom-call(s32[3]{0:T(128)S(1)} %pad_add_fusion.place_ref, f32[3,256]{1,0:T(4,128)S(1)} %tile.10.gain_ref, bf16[304,608]{1,0:T(8,128)(2,1)S(1)} %get-tuple-element.16.refs_0_, bf16[304,608]{1,0:T(8,128)(2,1)S(1)} %collective-permute-done.6.refs_1_, ...), custom_call_target="tpu_custom_call" | custom-call | flops 2151677952 | bytes 6225920 | tf_op jit(solution)/shard_map/pallas_call | solution.py:443
  137.3 8.2 %shard_map.144 = (bf16[512,256]{1,0:T(8,128)(2,1)S(1)}, bf16[640,512]{1,0:T(8,128)(2,1)S(1)}) custom-call(s32[3]{0:T(128)S(1)} %pad_add_fusion.place_ref, f32[3,256]{1,0:T(4,128)S(1)} %tile.10.gain_ref, bf16[304,608]{1,0:T(8,128)(2,1)S(1)} %get-tuple-element.16.refs_0_, bf16[304,608]{1,0:T(8,128)(2,1)S(1)} %collective-permute-done.6.refs_1_, ...), custom_call_target="tpu_custom_call" | custom-call | flops 2151677952 | bytes 6225920 | tf_op jit(solution)/shard_map/pallas_call | solution.py:443
  146.2 1.7 collective-permute-start.43
  148.3 1.7 collective-permute-start.44
  150.3 5.4 %shard_map.147.refs_6_ = bf16[256,512]{1,0:T(8,128)(2,1)S(1)} custom-call(s32[3]{0:T(128)S(1)} %pad_add_fusion.place_ref, bf16[512,256]{1,0:T(8,128)(2,1)S(1)} %get-tuple-element.22.q_ref, bf16[640,512]{1,0:T(8,128)(2,1)S(1)} %get-tuple-element.23.own_ref, bf16[640,512]{1,0:T(8,128)(2,1)S(1)} %collective-permute-done.36.peer_ref), custom_call_target="tpu_custom_call" | custom-call | flops 671088640 | bytes 1310720 | tf_op jit(solution)/shard_map/pallas_call | solution.py:463
  155.8 5.4 %shard_map.145.refs_0_ = bf16[256,512]{1,0:T(8,128)(2,1)S(1)} custom-call(s32[3]{0:T(128)S(1)} %pad_add_fusion.place_ref, bf16[512,256]{1,0:T(8,128)(2,1)S(1)} %get-tuple-element.19.q_ref, bf16[640,512]{1,0:T(8,128)(2,1)S(1)} %get-tuple-element.20.own_ref, bf16[640,512]{1,0:T(8,128)(2,1)S(1)} %collective-permute-done.23.peer_ref), custom_call_target="tpu_custom_call" | custom-call | flops 671088640 | bytes 1310720 | tf_op jit(solution)/shard_map/pallas_call | solution.py:463
  161.2 2.1 collective-permute-start.24
  163.3 1.7 collective-permute-start.47
  165.4 1.4 collective-permute-start.38
  167.6 1.4 collective-permute-start.25
  169.0 1.4 collective-permute-start.40
  170.4 1.4 collective-permute-start.27
  172.5 2.5 %collective-permute-done.47.refs_18_ = bf16[736,256]{1,0:T(8,128)(2,1)S(1)} collective-permute-done((bf16[736,256]{1,0:T(8,128)(2,1)S(1)}, bf16[736,256]{1,0:T(8,128)(2,1)S(1)}, u32[]{:S(2)}, u32[]{:S(2)}) %collective-permute-start.47) | collective-permute-done | bytes 376864 | tf_op jit(solution)/shard_map/ppermute | solution.py:21
  175.2 1.3 collective-permute-start.39
  176.5 1.3 collective-permute-start.26
  177.8 1.3 collective-permute-start.41
  179.2 1.3 collective-permute-start.28
  180.7 4.3 %collective-permute-done.48.refs_19_ = bf16[736,256]{1,0:T(8,128)(2,1)} collective-permute-done((bf16[736,256]{1,0:T(8,128)(2,1)S(1)}, bf16[736,256]{1,0:T(8,128)(2,1)}, u32[]{:S(2)}, u32[]{:S(2)}) %collective-permute-start.48) | collective-permute-done | bytes 376864 | tf_op jit(solution)/shard_map/ppermute | solution.py:21
  185.1 1.8 collective-permute-done.39.refs_9_
  186.9 5.6 %collective-permute-done.26.refs_3_ = bf16[256,512]{1,0:T(8,128)(2,1)} collective-permute-done((bf16[256,512]{1,0:T(8,128)(2,1)}, bf16[256,512]{1,0:T(8,128)(2,1)}, u32[]{:S(2)}, u32[]{:S(2)}) %collective-permute-start.26) | collective-permute-done | bytes 262176 | tf_op jit(solution)/shard_map/ppermute | solution.py:33
  192.5 5.6 %collective-permute-done.41.refs_11_ = bf16[256,512]{1,0:T(8,128)(2,1)} collective-permute-done((bf16[256,512]{1,0:T(8,128)(2,1)}, bf16[256,512]{1,0:T(8,128)(2,1)}, u32[]{:S(2)}, u32[]{:S(2)}) %collective-permute-start.41) | collective-permute-done | bytes 262176 | tf_op jit(solution)/shard_map/ppermute | solution.py:33
  198.1 3.5 %collective-permute-done.28.refs_5_ = bf16[256,512]{1,0:T(8,128)(2,1)} collective-permute-done((bf16[256,512]{1,0:T(8,128)(2,1)}, bf16[256,512]{1,0:T(8,128)(2,1)}, u32[]{:S(2)}, u32[]{:S(2)}) %collective-permute-start.28) | collective-permute-done | bytes 262176 | tf_op jit(solution)/shard_map/ppermute | solution.py:33
  201.6 0.9 copy-done.26
  202.5 5.7 %shard_map.148 = f32[72,640]{1,0:T(8,128)S(1)} custom-call(s32[3]{0:T(128)S(1)} %pad_add_fusion.place_ref, f32[608,1]{1,0:T(8,128)S(1)} %copy.18.gate_ref, f32[2,2,304]{2,1,0:T(2,128)S(1)} %bitcast.50, bf16[608,512]{1,0:T(8,128)(2,1)} %bitcast.45, bf16[256,512]{1,0:T(8,128)(2,1)S(1)} %shard_map.145.refs_0_, bf16[256,512]{1,0:T(8,128)(2,1)S(1)} %copy-done.26, ...), custom_call_target="tpu_custom_call" | custom-call | flops 1275068416 | bytes 9961472 | tf_op jit(solution)/shard_map/pallas_call | solution.py:483
  208.3 5.5 %collective-permute-done.49 = f32[72,640]{1,0:T(8,128)S(1)} collective-permute-done((f32[72,640]{1,0:T(8,128)S(1)}, f32[72,640]{1,0:T(8,128)S(1)}, u32[]{:S(2)}, u32[]{:S(2)}) %collective-permute-start.49) | collective-permute-done | bytes 184352 | tf_op jit(solution)/shard_map/ppermute | solution.py:21
  216.2 5.8 %collective-permute-done.50 = f32[72,640]{1,0:T(8,128)S(1)} collective-permute-done((f32[72,640]{1,0:T(8,128)S(1)}, f32[72,640]{1,0:T(8,128)S(1)}, u32[]{:S(2)}, u32[]{:S(2)}) %collective-permute-start.50) | collective-permute-done | bytes 184352 | tf_op jit(solution)/shard_map/ppermute | solution.py:21
  (141 shorter events, 18.6 us)
Async XLA Ops:
  0.6 10.2 %copy-start = (bf16[512,608]{0,1:T(8,128)(2,1)S(1)}, bf16[512,608]{0,1:T(8,128)(2,1)}, u32[]{:S(2)}) copy-start(bf16[512,608]{0,1:T(8,128)(2,1)} %param.13) | copy-start | bytes 1867780
  2.7 1.8 copy-start.1
  5.1 5.6 %copy-start.24 = (bf16[96,608]{1,0:T(8,128)(2,1)S(1)}, bf16[96,608]{1,0:T(8,128)(2,1)}, u32[]{:S(2)}) copy-start(bf16[96,608]{1,0:T(8,128)(2,1)} %txt_ref.3) | copy-start | bytes 350212
  5.1 13.1 %copy-start.10 = (bf16[304,3,512]{2,0,1:T(8,128)(2,1)S(1)}, bf16[304,3,512]{2,0,1:T(8,128)(2,1)}, u32[]{:S(2)}) copy-start(bf16[304,3,512]{2,0,1:T(8,128)(2,1)} %param.20) | copy-start | bytes 2801668
  5.1 13.1 %copy-start.23 = (bf16[304,2,512]{2,1,0:T(2,128)(2,1)S(1)}, bf16[304,2,512]{2,1,0:T(2,128)(2,1)}, u32[]{:S(2)}) copy-start(bf16[304,2,512]{2,1,0:T(2,128)(2,1)} %kv_ref.1) | copy-start | bytes 1867780
  5.2 112.1 %copy-start.32 = (f32[2,64]{1,0:T(2,128)S(1)}, f32[2,64]{1,0:T(2,128)}, u32[]{:S(2)}) copy-start(f32[2,64]{1,0:T(2,128)} %param.23) | copy-start | bytes 1540
  5.2 112.1 %copy-start.33 = (f32[64]{0:T(128)S(1)}, f32[64]{0:T(128)}, u32[]{:S(2)}) copy-start(f32[64]{0:T(128)} %param.22) | copy-start | bytes 772
  6.2 6.8 %collective-permute-start = (f32[8,640]{1,0:T(8,128)S(1)}, f32[8,640]{1,0:T(8,128)S(1)}, u32[]{:S(2)}, u32[]{:S(2)}) collective-permute-start(f32[8,640]{1,0:T(8,128)S(1)} %get-tuple-element.30), channel_id=1, source_target_pairs={{0,8},{4,12},{8,0},{12,4},{16,24},{20,28},{24,16},{28,20},{1,9},{5... | collective-permute-start | bytes 61448 | tf_op jit(solution)/shard_map/ppermute | solution.py:21
  9.2 3.8 %collective-permute-start.1 = (f32[8,640]{1,0:T(8,128)S(1)}, f32[8,640]{1,0:T(8,128)S(1)}, u32[]{:S(2)}, u32[]{:S(2)}) collective-permute-start(f32[8,640]{1,0:T(8,128)S(1)} %get-tuple-element.32), channel_id=1, source_target_pairs={{0,16},{4,20},{8,24},{12,28},{16,0},{20,4},{24,8},{28,12},{1,17},{... | collective-permute-start | bytes 61448 | tf_op jit(solution)/shard_map/ppermute | solution.py:21
  10.8 4.7 %collective-permute-start.2 = (f32[8,640]{1,0:T(8,128)S(1)}, f32[8,640]{1,0:T(8,128)S(1)}, u32[]{:S(2)}, u32[]{:S(2)}) collective-permute-start(f32[8,640]{1,0:T(8,128)S(1)} %get-tuple-element.31), channel_id=1, source_target_pairs={{0,24},{4,28},{8,16},{12,20},{16,8},{20,12},{24,0},{28,4},{1,25},{... | collective-permute-start | bytes 61448 | tf_op jit(solution)/shard_map/ppermute | solution.py:21
  11.0 4.6 %collective-permute-start.4 = (f32[8,640]{1,0:T(8,128)S(1)}, f32[8,640]{1,0:T(8,128)S(1)}, u32[]{:S(2)}, u32[]{:S(2)}) collective-permute-start(f32[8,640]{1,0:T(8,128)S(1)} %shard_map.142), channel_id=1, source_target_pairs={{0,1},{1,0},{2,3},{3,2},{4,5},{5,4},{6,7},{7,6},{8,9},{9,8},{10,11... | collective-permute-start | bytes 61448 | tf_op jit(solution)/shard_map/ppermute | solution.py:21
  15.5 4.4 %collective-permute-start.3 = (f32[8,640]{1,0:T(8,128)S(1)}, f32[8,640]{1,0:T(8,128)S(1)}, u32[]{:S(2)}, u32[]{:S(2)}) collective-permute-start(f32[8,640]{1,0:T(8,128)S(1)} %fusion.6), channel_id=1, source_target_pairs={{0,4},{4,0},{8,12},{12,8},{16,20},{20,16},{24,28},{28,24},{1,5},{5... | collective-permute-start | bytes 61448 | tf_op jit(solution)/shard_map/ppermute | solution.py:21
  15.6 4.7 %collective-permute-start.5 = (f32[8,640]{1,0:T(8,128)S(1)}, f32[8,640]{1,0:T(8,128)S(1)}, u32[]{:S(2)}, u32[]{:S(2)}) collective-permute-start(f32[8,640]{1,0:T(8,128)S(1)} %add.66), channel_id=1, source_target_pairs={{0,2},{1,3},{2,0},{3,1},{4,6},{5,7},{6,4},{7,5},{8,10},{9,11},{10,... | collective-permute-start | bytes 61448 | tf_op jit(solution)/shard_map/ppermute | solution.py:21
  19.8 93.8 %copy-start.11 = (bf16[304,1280]{1,0:T(8,128)(2,1)}, bf16[304,1280]{1,0:T(8,128)(2,1)S(1)}, u32[]{:S(2)}) copy-start(bf16[304,1280]{1,0:T(8,128)(2,1)S(1)} %get-tuple-element.21.refs_12_) | copy-start | bytes 2334724
  21.1 12.0 %collective-permute-start.6 = (bf16[304,608]{1,0:T(8,128)(2,1)S(1)}, bf16[304,608]{1,0:T(8,128)(2,1)S(1)}, u32[]{:S(2)}, u32[]{:S(2)}) collective-permute-start(bf16[304,608]{1,0:T(8,128)(2,1)S(1)} %get-tuple-element.16.refs_0_), channel_id=1, source_target_pairs={{0,1},{1,0},{2,3},{3,2},{4,5},{5,4},{6,7},{7,6},{8,9},{9,8},{10,11... | collective-permute-start | bytes 1109000 | tf_op jit(solution)/shard_map/ppermute | solution.py:21
  22.7 17.4 %collective-permute-start.11 = (bf16[304,608]{1,0:T(8,128)(2,1)S(1)}, bf16[304,608]{1,0:T(8,128)(2,1)S(1)}, u32[]{:S(2)}, u32[]{:S(2)}) collective-permute-start(bf16[304,608]{1,0:T(8,128)(2,1)S(1)} %get-tuple-element.17.refs_6_), channel_id=1, source_target_pairs={{0,1},{1,0},{2,3},{3,2},{4,5},{5,4},{6,7},{7,6},{8,9},{9,8},{10,11... | collective-permute-start | bytes 1109000 | tf_op jit(solution)/shard_map/ppermute | solution.py:21
  23.1 17.7 %collective-permute-start.12 = (bf16[304,608]{1,0:T(8,128)(2,1)S(1)}, bf16[304,608]{1,0:T(8,128)(2,1)S(1)}, u32[]{:S(2)}, u32[]{:S(2)}) collective-permute-start(bf16[304,608]{1,0:T(8,128)(2,1)S(1)} %get-tuple-element.17.refs_6_), channel_id=1, source_target_pairs={{1,2},{2,1},{5,6},{6,5},{9,10},{10,9},{13,14},{14,13},{17,18},{18,... | collective-permute-start | bytes 1109000 | tf_op jit(solution)/shard_map/ppermute | solution.py:33
  23.8 18.3 %collective-permute-start.7 = (bf16[304,608]{1,0:T(8,128)(2,1)S(1)}, bf16[304,608]{1,0:T(8,128)(2,1)S(1)}, u32[]{:S(2)}, u32[]{:S(2)}) collective-permute-start(bf16[304,608]{1,0:T(8,128)(2,1)S(1)} %get-tuple-element.16.refs_0_), channel_id=1, source_target_pairs={{1,2},{2,1},{5,6},{6,5},{9,10},{10,9},{13,14},{14,13},{17,18},{18,... | collective-permute-start | bytes 1109000 | tf_op jit(solution)/shard_map/ppermute | solution.py:33
  33.1 11.0 %collective-permute-start.9 = (bf16[304,608]{1,0:T(8,128)(2,1)S(1)}, bf16[304,608]{1,0:T(8,128)(2,1)S(1)}, u32[]{:S(2)}, u32[]{:S(2)}) collective-permute-start(bf16[304,608]{1,0:T(8,128)(2,1)S(1)} %collective-permute-done.6.refs_1_), channel_id=1, source_target_pairs={{1,2},{2,1},{5,6},{6,5},{9,10},{10,9},{13,14},{14,13},{17,18},{18,... | collective-permute-start | bytes 1109000 | tf_op jit(solution)/shard_map/ppermute | solution.py:33
  40.1 4.4 %collective-permute-start.14 = (bf16[304,608]{1,0:T(8,128)(2,1)S(1)}, bf16[304,608]{1,0:T(8,128)(2,1)S(1)}, u32[]{:S(2)}, u32[]{:S(2)}) collective-permute-start(bf16[304,608]{1,0:T(8,128)(2,1)S(1)} %collective-permute-done.11.refs_7_), channel_id=1, source_target_pairs={{1,2},{2,1},{5,6},{6,5},{9,10},{10,9},{13,14},{14,13},{17,18},{18,... | collective-permute-start | bytes 1109000 | tf_op jit(solution)/shard_map/ppermute | solution.py:33
  40.8 15.2 %collective-permute-start.13 = (bf16[304,608]{1,0:T(8,128)(2,1)S(1)}, bf16[304,608]{1,0:T(8,128)(2,1)S(1)}, u32[]{:S(2)}, u32[]{:S(2)}) collective-permute-start(bf16[304,608]{1,0:T(8,128)(2,1)S(1)} %collective-permute-done.12.refs_8_), channel_id=1, source_target_pairs={{1,0},{2,3},{5,4},{6,7},{9,8},{10,11},{13,12},{14,15},{17,16},{18,... | collective-permute-start | bytes 1109000 | tf_op jit(solution)/shard_map/ppermute | solution.py:33
  42.1 19.6 %collective-permute-start.8 = (bf16[304,608]{1,0:T(8,128)(2,1)S(1)}, bf16[304,608]{1,0:T(8,128)(2,1)S(1)}, u32[]{:S(2)}, u32[]{:S(2)}) collective-permute-start(bf16[304,608]{1,0:T(8,128)(2,1)S(1)} %collective-permute-done.7.refs_2_), channel_id=1, source_target_pairs={{1,0},{2,3},{5,4},{6,7},{9,8},{10,11},{13,12},{14,15},{17,16},{18,... | collective-permute-start | bytes 1109000 | tf_op jit(solution)/shard_map/ppermute | solution.py:33
  43.4 19.0 %collective-permute-start.30 = (bf16[304,1280]{1,0:T(8,128)(2,1)S(1)}, bf16[304,1280]{1,0:T(8,128)(2,1)S(1)}, u32[]{:S(2)}, u32[]{:S(2)}) collective-permute-start(bf16[304,1280]{1,0:T(8,128)(2,1)S(1)} %get-tuple-element.21.refs_12_), channel_id=1, source_target_pairs={{0,8},{4,12},{8,0},{12,4},{16,24},{20,28},{24,16},{28,20},{1,9},{5... | collective-permute-start | bytes 2334728 | tf_op jit(solution)/shard_map/ppermute | solution.py:21
  44.0 20.3 %collective-permute-start.32 = (bf16[304,1280]{1,0:T(8,128)(2,1)S(1)}, bf16[304,1280]{1,0:T(8,128)(2,1)S(1)}, u32[]{:S(2)}, u32[]{:S(2)}) collective-permute-start(bf16[304,1280]{1,0:T(8,128)(2,1)S(1)} %get-tuple-element.21.refs_12_), channel_id=1, source_target_pairs={{0,16},{4,20},{8,24},{12,28},{16,0},{20,4},{24,8},{28,12},{1,17},{... | collective-permute-start | bytes 2334728 | tf_op jit(solution)/shard_map/ppermute | solution.py:21
  44.5 20.7 %collective-permute-start.29 = (bf16[304,1280]{1,0:T(8,128)(2,1)S(1)}, bf16[304,1280]{1,0:T(8,128)(2,1)S(1)}, u32[]{:S(2)}, u32[]{:S(2)}) collective-permute-start(bf16[304,1280]{1,0:T(8,128)(2,1)S(1)} %get-tuple-element.21.refs_12_), channel_id=1, source_target_pairs={{0,4},{4,0},{8,12},{12,8},{16,20},{20,16},{24,28},{28,24},{1,5},{5... | collective-permute-start | bytes 2334728 | tf_op jit(solution)/shard_map/ppermute | solution.py:21
  56.8 24.4 %collective-permute-start.19 = (bf16[304,1280]{1,0:T(8,128)(2,1)}, bf16[304,1280]{1,0:T(8,128)(2,1)}, u32[]{:S(2)}, u32[]{:S(2)}) collective-permute-start(bf16[304,1280]{1,0:T(8,128)(2,1)} %get-tuple-element.18.refs_12_), channel_id=1, source_target_pairs={{0,16},{4,20},{8,24},{12,28},{16,0},{20,4},{24,8},{28,12},{1,17},{... | collective-permute-start | bytes 2334728 | tf_op jit(solution)/shard_map/ppermute | solution.py:21
  62.5 20.2 %collective-permute-start.17 = (bf16[304,1280]{1,0:T(8,128)(2,1)}, bf16[304,1280]{1,0:T(8,128)(2,1)}, u32[]{:S(2)}, u32[]{:S(2)}) collective-permute-start(bf16[304,1280]{1,0:T(8,128)(2,1)} %get-tuple-element.18.refs_12_), channel_id=1, source_target_pairs={{0,8},{4,12},{8,0},{12,4},{16,24},{20,28},{24,16},{28,20},{1,9},{5... | collective-permute-start | bytes 2334728 | tf_op jit(solution)/shard_map/ppermute | solution.py:21
  62.5 42.8 %collective-permute-start.34 = (bf16[304,1280]{1,0:T(8,128)(2,1)S(1)}, bf16[304,1280]{1,0:T(8,128)(2,1)}, u32[]{:S(2)}, u32[]{:S(2)}) collective-permute-start(bf16[304,1280]{1,0:T(8,128)(2,1)S(1)} %collective-permute-done.30.refs_14_), channel_id=1, source_target_pairs={{0,16},{4,20},{8,24},{12,28},{16,0},{20,4},{24,8},{28,12},{1,17},{... | collective-permute-start | bytes 2334728 | tf_op jit(solution)/shard_map/ppermute | solution.py:21
  64.3 50.1 %collective-permute-start.31 = (bf16[304,1280]{1,0:T(8,128)(2,1)S(1)}, bf16[304,1280]{1,0:T(8,128)(2,1)S(1)}, u32[]{:S(2)}, u32[]{:S(2)}) collective-permute-start(bf16[304,1280]{1,0:T(8,128)(2,1)S(1)} %collective-permute-done.30.refs_14_), channel_id=1, source_target_pairs={{0,4},{4,0},{8,12},{12,8},{16,20},{20,16},{24,28},{28,24},{1,5},{5... | collective-permute-start | bytes 2334728 | tf_op jit(solution)/shard_map/ppermute | solution.py:21
  66.1 49.7 %collective-permute-start.33 = (bf16[304,1280]{1,0:T(8,128)(2,1)S(1)}, bf16[304,1280]{1,0:T(8,128)(2,1)S(1)}, u32[]{:S(2)}, u32[]{:S(2)}) collective-permute-start(bf16[304,1280]{1,0:T(8,128)(2,1)S(1)} %collective-permute-done.32.refs_16_), channel_id=1, source_target_pairs={{0,4},{4,0},{8,12},{12,8},{16,20},{20,16},{24,28},{28,24},{1,5},{5... | collective-permute-start | bytes 2334728 | tf_op jit(solution)/shard_map/ppermute | solution.py:21
  81.1 35.6 %collective-permute-start.21 = (bf16[304,1280]{1,0:T(8,128)(2,1)}, bf16[304,1280]{1,0:T(8,128)(2,1)}, u32[]{:S(2)}, u32[]{:S(2)}) collective-permute-start(bf16[304,1280]{1,0:T(8,128)(2,1)} %collective-permute-done.19.refs_16_), channel_id=1, source_target_pairs={{0,8},{4,12},{8,0},{12,4},{16,24},{20,28},{24,16},{28,20},{1,9},{5... | collective-permute-start | bytes 2334728 | tf_op jit(solution)/shard_map/ppermute | solution.py:21
  82.6 20.6 %collective-permute-start.10 = (bf16[304,608]{1,0:T(8,128)(2,1)S(1)}, bf16[304,608]{1,0:T(8,128)(2,1)S(1)}, u32[]{:S(2)}, u32[]{:S(2)}) collective-permute-start(bf16[304,608]{1,0:T(8,128)(2,1)S(1)} %collective-permute-done.9.refs_4_), channel_id=1, source_target_pairs={{1,0},{2,3},{5,4},{6,7},{9,8},{10,11},{13,12},{14,15},{17,16},{18,... | collective-permute-start | bytes 1109000 | tf_op jit(solution)/shard_map/ppermute | solution.py:33
  104.0 9.6 %collective-permute-start.15 = (bf16[304,608]{1,0:T(8,128)(2,1)S(1)}, bf16[304,608]{1,0:T(8,128)(2,1)S(1)}, u32[]{:S(2)}, u32[]{:S(2)}) collective-permute-start(bf16[304,608]{1,0:T(8,128)(2,1)S(1)} %collective-permute-done.14.refs_10_), channel_id=1, source_target_pairs={{1,0},{2,3},{5,4},{6,7},{9,8},{10,11},{13,12},{14,15},{17,16},{18,... | collective-permute-start | bytes 1109000 | tf_op jit(solution)/shard_map/ppermute | solution.py:33
  105.3 12.0 %collective-permute-start.35 = (bf16[304,1280]{1,0:T(8,128)(2,1)}, bf16[304,1280]{1,0:T(8,128)(2,1)}, u32[]{:S(2)}, u32[]{:S(2)}) collective-permute-start(bf16[304,1280]{1,0:T(8,128)(2,1)} %collective-permute-done.34.refs_18_), channel_id=1, source_target_pairs={{0,4},{4,0},{8,12},{12,8},{16,20},{20,16},{24,28},{28,24},{1,5},{5... | collective-permute-start | bytes 2334728 | tf_op jit(solution)/shard_map/ppermute | solution.py:21
  114.4 22.9 %collective-permute-start.16 = (bf16[304,1280]{1,0:T(8,128)(2,1)}, bf16[304,1280]{1,0:T(8,128)(2,1)}, u32[]{:S(2)}, u32[]{:S(2)}) collective-permute-start(bf16[304,1280]{1,0:T(8,128)(2,1)} %get-tuple-element.18.refs_12_), channel_id=1, source_target_pairs={{0,4},{4,0},{8,12},{12,8},{16,20},{20,16},{24,28},{28,24},{1,5},{5... | collective-permute-start | bytes 2334728 | tf_op jit(solution)/shard_map/ppermute | solution.py:21
  115.3 22.0 %collective-permute-start.20 = (bf16[304,1280]{1,0:T(8,128)(2,1)}, bf16[304,1280]{1,0:T(8,128)(2,1)}, u32[]{:S(2)}, u32[]{:S(2)}) collective-permute-start(bf16[304,1280]{1,0:T(8,128)(2,1)} %collective-permute-done.19.refs_16_), channel_id=1, source_target_pairs={{0,4},{4,0},{8,12},{12,8},{16,20},{20,16},{24,28},{28,24},{1,5},{5... | collective-permute-start | bytes 2334728 | tf_op jit(solution)/shard_map/ppermute | solution.py:21
  116.7 20.5 %collective-permute-start.18 = (bf16[304,1280]{1,0:T(8,128)(2,1)}, bf16[304,1280]{1,0:T(8,128)(2,1)}, u32[]{:S(2)}, u32[]{:S(2)}) collective-permute-start(bf16[304,1280]{1,0:T(8,128)(2,1)} %collective-permute-done.17.refs_14_), channel_id=1, source_target_pairs={{0,4},{4,0},{8,12},{12,8},{16,20},{20,16},{24,28},{28,24},{1,5},{5... | collective-permute-start | bytes 2334728 | tf_op jit(solution)/shard_map/ppermute | solution.py:21
  116.7 20.6 %collective-permute-start.22 = (bf16[304,1280]{1,0:T(8,128)(2,1)}, bf16[304,1280]{1,0:T(8,128)(2,1)}, u32[]{:S(2)}, u32[]{:S(2)}) collective-permute-start(bf16[304,1280]{1,0:T(8,128)(2,1)} %collective-permute-done.21.refs_18_), channel_id=1, source_target_pairs={{0,4},{4,0},{8,12},{12,8},{16,20},{20,16},{24,28},{28,24},{1,5},{5... | collective-permute-start | bytes 2334728 | tf_op jit(solution)/shard_map/ppermute | solution.py:21
  137.1 8.9 %copy-start.31 = (bf16[304,64]{0,1:T(8,128)(2,1)S(1)}, bf16[304,64]{0,1:T(8,128)(2,1)}, u32[]{:S(2)}) copy-start(bf16[304,64]{0,1:T(8,128)(2,1)} %param.25) | copy-start | bytes 116740
  137.1 8.9 %copy-start.29 = (bf16[256,608]{0,1:T(8,128)(2,1)S(1)}, bf16[256,608]{0,1:T(8,128)(2,1)}, u32[]{:S(2)}) copy-start(bf16[256,608]{0,1:T(8,128)(2,1)} %param.24) | copy-start | bytes 933892
  137.2 12.9 %collective-permute-start.36 = (bf16[640,512]{1,0:T(8,128)(2,1)S(1)}, bf16[640,512]{1,0:T(8,128)(2,1)S(1)}, u32[]{:S(2)}, u32[]{:S(2)}) collective-permute-start(bf16[640,512]{1,0:T(8,128)(2,1)S(1)} %get-tuple-element.23.own_ref), channel_id=1, source_target_pairs={{0,4},{4,0},{8,12},{12,8},{16,20},{20,16},{24,28},{28,24},{1,5},{5... | collective-permute-start | bytes 1966088 | tf_op jit(solution)/shard_map/ppermute | solution.py:21
  145.5 10.2 %collective-permute-start.23 = (bf16[640,512]{1,0:T(8,128)(2,1)S(1)}, bf16[640,512]{1,0:T(8,128)(2,1)S(1)}, u32[]{:S(2)}, u32[]{:S(2)}) collective-permute-start(bf16[640,512]{1,0:T(8,128)(2,1)S(1)} %get-tuple-element.20.own_ref), channel_id=1, source_target_pairs={{0,4},{4,0},{8,12},{12,8},{16,20},{20,16},{24,28},{28,24},{1,5},{5... | collective-permute-start | bytes 1966088 | tf_op jit(solution)/shard_map/ppermute | solution.py:21
  146.1 2.2 collective-permute-start.42
  146.2 15.0 %collective-permute-start.43 = (bf16[736,256]{1,0:T(8,128)(2,1)S(1)}, bf16[736,256]{1,0:T(8,128)(2,1)S(1)}, u32[]{:S(2)}, u32[]{:S(2)}) collective-permute-start(bf16[736,256]{1,0:T(8,128)(2,1)S(1)} %pad_maximum_fusion.refs_12_), channel_id=1, source_target_pairs={{0,8},{4,12},{8,0},{12,4},{16,24},{20,28},{24,16},{28,20},{1,9},{5... | collective-permute-start | bytes 1130504 | tf_op jit(solution)/shard_map/ppermute | solution.py:21
  148.0 15.3 %collective-permute-start.45 = (bf16[736,256]{1,0:T(8,128)(2,1)S(1)}, bf16[736,256]{1,0:T(8,128)(2,1)S(1)}, u32[]{:S(2)}, u32[]{:S(2)}) collective-permute-start(bf16[736,256]{1,0:T(8,128)(2,1)S(1)} %pad_maximum_fusion.refs_12_), channel_id=1, source_target_pairs={{0,16},{4,20},{8,24},{12,28},{16,0},{20,4},{24,8},{28,12},{1,17},{... | collective-permute-start | bytes 1130504 | tf_op jit(solution)/shard_map/ppermute | solution.py:21
  148.3 17.1 %collective-permute-start.44 = (bf16[736,256]{1,0:T(8,128)(2,1)S(1)}, bf16[736,256]{1,0:T(8,128)(2,1)S(1)}, u32[]{:S(2)}, u32[]{:S(2)}) collective-permute-start(bf16[736,256]{1,0:T(8,128)(2,1)S(1)} %collective-permute-done.42.refs_13_), channel_id=1, source_target_pairs={{0,8},{4,12},{8,0},{12,4},{16,24},{20,28},{24,16},{28,20},{1,9},{5... | collective-permute-start | bytes 1130504 | tf_op jit(solution)/shard_map/ppermute | solution.py:21
  150.0 17.6 %collective-permute-start.46 = (bf16[736,256]{1,0:T(8,128)(2,1)S(1)}, bf16[736,256]{1,0:T(8,128)(2,1)S(1)}, u32[]{:S(2)}, u32[]{:S(2)}) collective-permute-start(bf16[736,256]{1,0:T(8,128)(2,1)S(1)} %collective-permute-done.42.refs_13_), channel_id=1, source_target_pairs={{0,16},{4,20},{8,24},{12,28},{16,0},{20,4},{24,8},{28,12},{1,17},{... | collective-permute-start | bytes 1130504 | tf_op jit(solution)/shard_map/ppermute | solution.py:21
  155.7 13.3 %collective-permute-start.37 = (bf16[256,512]{1,0:T(8,128)(2,1)S(1)}, bf16[256,512]{1,0:T(8,128)(2,1)S(1)}, u32[]{:S(2)}, u32[]{:S(2)}) collective-permute-start(bf16[256,512]{1,0:T(8,128)(2,1)S(1)} %shard_map.147.refs_6_), channel_id=1, source_target_pairs={{0,1},{1,0},{2,3},{3,2},{4,5},{5,4},{6,7},{7,6},{8,9},{9,8},{10,11... | collective-permute-start | bytes 786440 | tf_op jit(solution)/shard_map/ppermute | solution.py:21
  161.2 9.2 %collective-permute-start.24 = (bf16[256,512]{1,0:T(8,128)(2,1)S(1)}, bf16[256,512]{1,0:T(8,128)(2,1)S(1)}, u32[]{:S(2)}, u32[]{:S(2)}) collective-permute-start(bf16[256,512]{1,0:T(8,128)(2,1)S(1)} %shard_map.145.refs_0_), channel_id=1, source_target_pairs={{0,1},{1,0},{2,3},{3,2},{4,5},{5,4},{6,7},{7,6},{8,9},{9,8},{10,11... | collective-permute-start | bytes 786440 | tf_op jit(solution)/shard_map/ppermute | solution.py:21
  163.3 11.7 %collective-permute-start.47 = (bf16[736,256]{1,0:T(8,128)(2,1)S(1)}, bf16[736,256]{1,0:T(8,128)(2,1)S(1)}, u32[]{:S(2)}, u32[]{:S(2)}) collective-permute-start(bf16[736,256]{1,0:T(8,128)(2,1)S(1)} %collective-permute-done.43.refs_14_), channel_id=1, source_target_pairs={{0,16},{4,20},{8,24},{12,28},{16,0},{20,4},{24,8},{28,12},{1,17},{... | collective-permute-start | bytes 1130504 | tf_op jit(solution)/shard_map/ppermute | solution.py:21
  165.4 9.8 %collective-permute-start.38 = (bf16[256,512]{1,0:T(8,128)(2,1)S(1)}, bf16[256,512]{1,0:T(8,128)(2,1)}, u32[]{:S(2)}, u32[]{:S(2)}) collective-permute-start(bf16[256,512]{1,0:T(8,128)(2,1)S(1)} %shard_map.147.refs_6_), channel_id=1, source_target_pairs={{1,2},{2,1},{5,6},{6,5},{9,10},{10,9},{13,14},{14,13},{17,18},{18,... | collective-permute-start | bytes 786440 | tf_op jit(solution)/shard_map/ppermute | solution.py:33
  167.6 8.9 %collective-permute-start.25 = (bf16[256,512]{1,0:T(8,128)(2,1)S(1)}, bf16[256,512]{1,0:T(8,128)(2,1)}, u32[]{:S(2)}, u32[]{:S(2)}) collective-permute-start(bf16[256,512]{1,0:T(8,128)(2,1)S(1)} %shard_map.145.refs_0_), channel_id=1, source_target_pairs={{1,2},{2,1},{5,6},{6,5},{9,10},{10,9},{13,14},{14,13},{17,18},{18,... | collective-permute-start | bytes 786440 | tf_op jit(solution)/shard_map/ppermute | solution.py:33
  169.0 8.8 %collective-permute-start.40 = (bf16[256,512]{1,0:T(8,128)(2,1)S(1)}, bf16[256,512]{1,0:T(8,128)(2,1)}, u32[]{:S(2)}, u32[]{:S(2)}) collective-permute-start(bf16[256,512]{1,0:T(8,128)(2,1)S(1)} %collective-permute-done.37.refs_7_), channel_id=1, source_target_pairs={{1,2},{2,1},{5,6},{6,5},{9,10},{10,9},{13,14},{14,13},{17,18},{18,... | collective-permute-start | bytes 786440 | tf_op jit(solution)/shard_map/ppermute | solution.py:33
  170.4 8.8 %collective-permute-start.27 = (bf16[256,512]{1,0:T(8,128)(2,1)S(1)}, bf16[256,512]{1,0:T(8,128)(2,1)}, u32[]{:S(2)}, u32[]{:S(2)}) collective-permute-start(bf16[256,512]{1,0:T(8,128)(2,1)S(1)} %collective-permute-done.24.refs_1_), channel_id=1, source_target_pairs={{1,2},{2,1},{5,6},{6,5},{9,10},{10,9},{13,14},{14,13},{17,18},{18,... | collective-permute-start | bytes 786440 | tf_op jit(solution)/shard_map/ppermute | solution.py:33
  174.9 4.2 %copy-start.28 = (bf16[736,256]{1,0:T(8,128)(2,1)}, bf16[736,256]{1,0:T(8,128)(2,1)S(1)}, u32[]{:S(2)}) copy-start(bf16[736,256]{1,0:T(8,128)(2,1)S(1)} %collective-permute-done.47.refs_18_) | copy-start | bytes 1130500
  174.9 10.1 %collective-permute-start.48 = (bf16[736,256]{1,0:T(8,128)(2,1)S(1)}, bf16[736,256]{1,0:T(8,128)(2,1)}, u32[]{:S(2)}, u32[]{:S(2)}) collective-permute-start(bf16[736,256]{1,0:T(8,128)(2,1)S(1)} %collective-permute-done.44.refs_15_), channel_id=1, source_target_pairs={{0,16},{4,20},{8,24},{12,28},{16,0},{20,4},{24,8},{28,12},{1,17},{... | collective-permute-start | bytes 1130504 | tf_op jit(solution)/shard_map/ppermute | solution.py:21
  175.2 11.6 %collective-permute-start.39 = (bf16[256,512]{1,0:T(8,128)(2,1)}, bf16[256,512]{1,0:T(8,128)(2,1)}, u32[]{:S(2)}, u32[]{:S(2)}) collective-permute-start(bf16[256,512]{1,0:T(8,128)(2,1)} %collective-permute-done.38.refs_8_), channel_id=1, source_target_pairs={{1,0},{2,3},{5,4},{6,7},{9,8},{10,11},{13,12},{14,15},{17,16},{18,... | collective-permute-start | bytes 786440 | tf_op jit(solution)/shard_map/ppermute | solution.py:33
  176.5 16.0 %collective-permute-start.26 = (bf16[256,512]{1,0:T(8,128)(2,1)}, bf16[256,512]{1,0:T(8,128)(2,1)}, u32[]{:S(2)}, u32[]{:S(2)}) collective-permute-start(bf16[256,512]{1,0:T(8,128)(2,1)} %collective-permute-done.25.refs_2_), channel_id=1, source_target_pairs={{1,0},{2,3},{5,4},{6,7},{9,8},{10,11},{13,12},{14,15},{17,16},{18,... | collective-permute-start | bytes 786440 | tf_op jit(solution)/shard_map/ppermute | solution.py:33
  177.8 20.3 %collective-permute-start.41 = (bf16[256,512]{1,0:T(8,128)(2,1)}, bf16[256,512]{1,0:T(8,128)(2,1)}, u32[]{:S(2)}, u32[]{:S(2)}) collective-permute-start(bf16[256,512]{1,0:T(8,128)(2,1)} %collective-permute-done.40.refs_10_), channel_id=1, source_target_pairs={{1,0},{2,3},{5,4},{6,7},{9,8},{10,11},{13,12},{14,15},{17,16},{18,... | collective-permute-start | bytes 786440 | tf_op jit(solution)/shard_map/ppermute | solution.py:33
  179.2 22.4 %collective-permute-start.28 = (bf16[256,512]{1,0:T(8,128)(2,1)}, bf16[256,512]{1,0:T(8,128)(2,1)}, u32[]{:S(2)}, u32[]{:S(2)}) collective-permute-start(bf16[256,512]{1,0:T(8,128)(2,1)} %collective-permute-done.27.refs_4_), channel_id=1, source_target_pairs={{1,0},{2,3},{5,4},{6,7},{9,8},{10,11},{13,12},{14,15},{17,16},{18,... | collective-permute-start | bytes 786440 | tf_op jit(solution)/shard_map/ppermute | solution.py:33
  202.5 11.7 %copy-start.34 = (s32[4]{0:T(128)S(1)}, s32[4]{0:T(128)}, u32[]{:S(2)}) copy-start(s32[4]{0:T(128)} %param.16) | copy-start | bytes 52
  202.5 19.7 %copy-start.30 = (f32[512,64]{0,1:T(8,128)S(1)}, f32[512,64]{0,1:T(8,128)}, u32[]{:S(2)}) copy-start(f32[512,64]{0,1:T(8,128)} %param.17) | copy-start | bytes 393220
  208.3 5.6 %collective-permute-start.49 = (f32[72,640]{1,0:T(8,128)S(1)}, f32[72,640]{1,0:T(8,128)S(1)}, u32[]{:S(2)}, u32[]{:S(2)}) collective-permute-start(f32[72,640]{1,0:T(8,128)S(1)} %shard_map.148), channel_id=1, source_target_pairs={{0,1},{1,0},{2,3},{3,2},{4,5},{5,4},{6,7},{7,6},{8,9},{9,8},{10,11... | collective-permute-start | bytes 552968 | tf_op jit(solution)/shard_map/ppermute | solution.py:21
  213.9 8.1 %collective-permute-start.50 = (f32[72,640]{1,0:T(8,128)S(1)}, f32[72,640]{1,0:T(8,128)S(1)}, u32[]{:S(2)}, u32[]{:S(2)}) collective-permute-start(f32[72,640]{1,0:T(8,128)S(1)} %add.68), channel_id=1, source_target_pairs={{0,2},{1,3},{2,0},{3,1},{4,6},{5,7},{6,4},{7,5},{8,10},{9,11},{10,... | collective-permute-start | bytes 552968 | tf_op jit(solution)/shard_map/ppermute | solution.py:21
  (22 other events, 20.6 us)

commit v4 on v3

--- a/solution.py
+++ b/solution.py
@@ -11,7 +11,7 @@
 EPS_NORM = 1e-06
 F32 = jnp.float32
 BF16 = jnp.bfloat16
-ANY = pl.BlockSpec(memory_space=pl.ANY)
+HBM = pl.BlockSpec(memory_space=pltpu.HBM)
 VMEM = pl.BlockSpec(memory_space=pltpu.VMEM)
 SMEM = pl.BlockSpec(memory_space=pltpu.SMEM)
 
@@ -27,36 +27,78 @@
     return lax.ppermute(block, axis, route)
 
 
+def tie(*arrays):
+    return lax.optimization_barrier(arrays)
+
+
 def line_gather(block, axis):
-    count = lax.axis_size(axis)
+    held = {0: block}
+    for step in range(1, lax.axis_size(axis)):
+        held[-step] = shift(held[1 - step], axis, 1)
+        held[step] = shift(held[step - 1], axis, -1)
+    return [held[k] for k in sorted(held)]
+
+
+def line_routes(count):
     if count == 4:
-        send = lambda held, route: lax.ppermute(held, axis, route)
-        middle, outward = [(1, 2), (2, 1)], [(1, 0), (2, 3)]
-        pair = swap(block, axis, 1)
-        near = send(block, middle)
-        far = send(pair, middle)
+        near = lambda p: jnp.where(p < 2, 2, 1)
+        far = lambda p: jnp.where(p < 2, 3, 0)
         inner = lambda p: (p == 1) | (p == 2)
         outer = lambda p: (p == 0) | (p == 3)
-        other = lambda p: jnp.where(p < 2, 2, 1)
-        other_far = lambda p: jnp.where(p < 2, 3, 0)
         always = lambda p: p >= 0
         return [
-            (block, lambda p: p, always),
-            (pair, lambda p: jnp.bitwise_xor(p, 1), always),
-            (near, other, inner),
-            (send(near, outward), other, outer),
-            (far, other_far, inner),
-            (send(far, outward), other_far, outer),
+            (lambda p: p, always),
+            (lambda p: jnp.bitwise_xor(p, 1), always),
+            (near, inner),
+            (near, outer),
+            (far, inner),
+            (far, outer),
         ]
-    held = {0: block}
-    for step in range(1, count):
-        held[-step] = shift(held[1 - step], axis, 1)
-        held[step] = shift(held[step - 1], axis, -1)
     result = []
-    for offset in sorted(held):
+    for offset in range(1 - count, count):
         inside = lambda p, offset=offset: (p + offset >= 0) & (p + offset < count)
-        result.append((held[offset], lambda p, offset=offset: p + offset, inside))
+        result.append((lambda p, offset=offset: p + offset, inside))
     return result
+
+
+MIDDLE = [(1, 2), (2, 1)]
+OUTWARD = [(1, 0), (2, 3)]
+
+
+def line_four(block, axis):
+    pair = swap(block, axis, 1)
+    near = lax.ppermute(block, axis, MIDDLE)
+    far = lax.ppermute(pair, axis, MIDDLE)
+    near_end = lax.ppermute(near, axis, OUTWARD)
+    return [block, pair, near, near_end, far, lax.ppermute(far, axis, OUTWARD)]
+
+
+def gather_both(tokens, weights):
+    lines = [[block] for block in tokens]
+    out = lambda held: lax.ppermute(held, "col", OUTWARD)
+    for line in lines:
+        line += [swap(line[0], "col", 1), lax.ppermute(line[0], "col", MIDDLE)]
+    held = [{0: weights[0]}, {0: weights[1]}]
+    held[1][2] = swap(weights[1], "row", 2)
+    held[0][4] = swap(weights[0], "row", 4)
+    for n, line in enumerate(lines):
+        if n == 1:
+            line[1], line[2], held[1][2], held[0][4] = tie(
+                line[1], line[2], held[1][2], held[0][4]
+            )
+        line += [out(line[2]), lax.ppermute(line[1], "col", MIDDLE)]
+    held[0][2] = swap(weights[0], "row", 2)
+    held[1][4] = swap(weights[1], "row", 4)
+    held[0][6] = swap(held[0][4], "row", 2)
+    held[1][6] = swap(held[1][2], "row", 4)
+    for n, line in enumerate(lines):
+        if n == 1:
+            line[4], held[0][2], held[1][4] = tie(line[4], held[0][2], held[1][4])
+        line.append(out(line[4]))
+    for half in held:
+        for mask in list(half):
+            half[mask + 1] = swap(half[mask], "row", 1)
+    return lines, held
 
 
 def doubling_gather(block, axis, masks):
@@ -77,11 +119,11 @@
     return [joined[order].reshape((count * rows,) + joined.shape[2:])], [None]
 
 
-def cost(flops, touched, exps=0):
-    return pl.CostEstimate(flops=flops, bytes_accessed=touched, transcendentals=exps)
-
-
-def call(kernel, outs, in_specs, scratch, estimate, out_specs=None, vmem=24):
+def cost(us):
+    return pl.CostEstimate(flops=int(us * 1.15e9), bytes_accessed=0, transcendentals=0)
+
+
+def call(kernel, outs, in_specs, scratch, estimate, out_specs=None, vmem=16):
     if out_specs is None:
         out_specs = jax.tree.map(lambda _: VMEM, outs)
     return pl.pallas_call(
@@ -104,9 +146,9 @@
             getattr(copy, act)()
 
 
-def mod_kernel(place_ref, cond_ref, w_ref, out_ref):
+def mod_kernel(cond_ref, w_ref, out_ref):
     requests, groups, width = cond_ref.shape[0], w_ref.shape[0], w_ref.shape[2]
-    request = place_ref[0] // 2
+    request = lax.axis_index("row") // 2
     values = jnp.concatenate(
         [cond_ref[pl.ds(jnp.bitwise_xor(request, k), 1), :] for k in range(requests)], axis=0
     )
@@ -170,7 +212,7 @@
                     ]
 
 
-def project_kernel(routes, masks, img, head, place_ref, gain_ref, *refs):
+def project_kernel(routes, masks, img, head, gain_ref, *refs):
     lines = []
     for _ in range(2):
         lines.append(refs[: len(routes)])
@@ -181,10 +223,10 @@
     txt = 2 * split - img
     count, width = x_ref.shape[0], x_ref.shape[2]
     half = q_ref.shape[1]
-    place = place_ref[0]
+    place, col = lax.axis_index("row"), lax.axis_index("col")
     for n, line in enumerate(lines):
         target = lambda owner, n=n: x_ref.at[owner, pl.ds(n * split, split)]
-        line_copies(line, routes, place_ref[1], target, sems_x.at[n], "start")
+        line_copies(line, routes, col, target, sems_x.at[n], "start")
     chips = {}
     if masks == [None]:
         chips[0] = [pltpu.make_async_copy(blocks[0], w_ref, sems_w.at[0])]
@@ -200,7 +242,7 @@
             copy.start()
     for n, line in enumerate(lines):
         target = lambda owner, n=n: x_ref.at[owner, pl.ds(n * split, split)]
-        line_copies(line, routes, place_ref[1], target, sems_x.at[n], "wait")
+        line_copies(line, routes, col, target, sems_x.at[n], "wait")
     for k in range(count):
         for copy in chips.get(k, ()):
             copy.wait()
@@ -237,11 +279,12 @@
     kv_ref[img + txt :] = jnp.zeros((kv_ref.shape[0] - img - txt, 2 * half), BF16)
 
 
-def attend_kernel(img, txt, head, place_ref, q_ref, own_ref, peer_ref, out_ref):
+def attend_kernel(img, txt, head, length_ref, q_ref, own_ref, peer_ref, out_ref):
     queries, half = q_ref.shape
     room = own_ref.shape[0] - img
-    side = lax.rem(place_ref[0], 2)
-    length = place_ref[2]
+    place = lax.axis_index("row")
+    side = lax.rem(place, 2)
+    length = length_ref[place // 2]
     slot = lax.broadcasted_iota(jnp.int32, (room, 1), 0)
     parts = []
     for ref, owner in ((own_ref, side), (peer_ref, 1 - side)):
@@ -276,7 +319,7 @@
 
 
 def output_kernel(
-    routes, count, masks, place_ref, gate_ref, out_mod_ref, x_ref, *refs
+    routes, count, masks, gate_ref, out_mod_ref, x_ref, *refs
 ):
     n_lines = len(routes)
     firsts, refs = refs[:n_lines], refs[n_lines:]
@@ -285,8 +328,7 @@
     out_ref, a_ref, w_ref, sems_a, sems_b, sems_w = refs
     width, tokens = x_ref.shape
     half = firsts[0].shape[0]
-    place = place_ref[0]
-    col = place_ref[1]
+    place, col = lax.axis_index("row"), lax.axis_index("col")
     copies = []
     for n, (ref, mask) in enumerate(zip(weights, masks)):
         owner = jnp.bitwise_xor(place, mask)
@@ -369,8 +411,7 @@
     final_weight,
 ):
     row_count, col_count = lax.axis_size("row"), lax.axis_size("col")
-    row_pos, col_pos = lax.axis_index("row"), lax.axis_index("col")
-    request = row_pos // 2
+    request = lax.axis_index("row") // 2
     requests = cond.shape[0]
     img, width = hidden_img.shape
     txt = hidden_txt.shape[0]
@@ -378,8 +419,6 @@
     part_cols = qkv_weight.shape[2]
     half = part_cols // 2
     full_width = width * col_count
-    length = lax.dynamic_index_in_dim(text_len, request, 0, keepdims=False)
-    place = jnp.stack([row_pos, col_pos, length]).astype(jnp.int32)
 
     wide = -(-width // 128) * 128
     room = -(-txt // 128) * 128
@@ -387,10 +426,10 @@
     mod_part = call(
         mod_kernel,
         jax.ShapeDtypeStruct((requests, 8, wide), F32),
-        [SMEM, VMEM, VMEM],
+        [VMEM, VMEM],
         [],
-        cost(2 * requests * cond.shape[1] * 7 * width, mod_weight.size * 2),
-    )(place, cond, jnp.moveaxis(mod_weight, 1, 0))
+        cost(2),
+    )(cond, jnp.moveaxis(mod_weight, 1, 0))
     mod_own = mod_part[0]
     for k in range(1, requests):
         mod_own = mod_own + swap(mod_part[k], "row", 2 * k)
@@ -400,7 +439,7 @@
         jax.ShapeDtypeStruct((8, tokens), F32),
         [VMEM, VMEM],
         [],
-        cost(4 * width * tokens, 2 * width * tokens),
+        cost(1),
     )(hidden_img.T, hidden_txt)
     mask = 1
     while mask < col_count:
@@ -413,26 +452,26 @@
         (jax.ShapeDtypeStruct((qkv_weight.shape[0], 5 * half), BF16),) * 2,
         [VMEM, VMEM],
         [],
-        cost(0, 20 * qkv_weight.shape[0] * half),
+        cost(2),
         (VMEM, VMEM),
     )(jnp.moveaxis(qkv_weight, 1, 0), kv_text_weight)
     packed, mod_own = lax.optimization_barrier((packed, mod_own))
-    gathered = []
-    for n in range(2):
-        order = chip_masks[::-1] if n == 0 else chip_masks
-        gathered.append(doubling_gather(packed[n], "row", order + [1]))
-
     split = (img + txt) // 2
     ready = call(
         functools.partial(norm_kernel, full_width),
         (jax.ShapeDtypeStruct((split, width), BF16),) * 2,
         [VMEM] * 4,
         [],
-        cost(12 * width * tokens, 4 * width * tokens),
+        cost(1),
         (VMEM, VMEM),
     )(hidden_img.T, hidden_txt, stats, mod_own)
-    lines = [line_gather(part, "col") for part in ready]
-    routes = [entry[1:] for entry in lines[0]]
+    routes = line_routes(col_count)
+    small = col_count == 4 and row_count == 8
+    if small:
+        lines, gathered = gather_both(ready, packed)
+    else:
+        lines = [line_gather(part, "col") for part in ready]
+        gathered = [doubling_gather(part, "row", chip_masks + [1]) for part in packed]
 
     gains = jnp.tile(jnp.concatenate([q_gain[None], k_gain], axis=0), (1, half // head))
     attended = []
@@ -446,7 +485,7 @@
                 jax.ShapeDtypeStruct((img, half), BF16),
                 jax.ShapeDtypeStruct((tokens, 2 * half), BF16),
             ),
-            [SMEM, VMEM] + [ANY] * (2 * len(routes) + len(masks)),
+            [VMEM] + [HBM] * (2 * len(routes) + len(masks)),
             [
                 pltpu.VMEM((col_count, img + txt, width), BF16),
                 pltpu.VMEM((col_count, width, 5 * half), BF16),
@@ -455,9 +494,10 @@
                 pltpu.SemaphoreType.DMA((2, len(routes))),
                 pltpu.SemaphoreType.DMA((len(masks),)),
             ],
-            cost(2 * full_width * half * (3 * img + 2 * txt), 10 * full_width * half),
+            cost(8),
             (VMEM, VMEM),
-        )(place, gains, *[entry[0] for line in lines for entry in line], *blocks)
+            vmem=56,
+        )(gains, *[part for line in lines for part in line], *blocks)
         peer = swap(pair, "row", 1)
         attended.append(
             call(
@@ -465,8 +505,9 @@
                 jax.ShapeDtypeStruct((half, img), BF16),
                 [SMEM, VMEM, VMEM, VMEM],
                 [],
-                cost(8 * half * tokens * img, 8 * half * tokens, 2 * tokens * img * half // head),
-            )(place, queries, pair, peer)
+                cost(6),
+                vmem=24,
+            )(text_len, queries, pair, peer)
         )
 
     head_depth, patch = final_weight.shape
@@ -477,13 +518,13 @@
     out_packed = jnp.concatenate([out_weight.T, tail], axis=0)
     out_blocks = doubling_gather(out_packed, "row", [1] + chip_masks)
     masks = sorted(out_blocks)
-    lines = [line_gather(block, "col") for block in attended]
+    lines = [(line_four if small else line_gather)(block, "col") for block in attended]
     per_col = row_count // col_count
     out_mod = mod_own[5:7, :width].reshape(2, per_col, width // per_col).swapaxes(0, 1)
     partial_sum = call(
         functools.partial(output_kernel, routes, col_count, masks),
         jax.ShapeDtypeStruct((patch + 8, img + 128), F32),
-        [SMEM, VMEM, VMEM, VMEM] + [ANY] * (2 * len(routes) + len(masks)),
+        [VMEM, VMEM, VMEM] + [HBM] * (2 * len(routes) + len(masks)),
         [
             pltpu.VMEM((part_cols * col_count, img), BF16),
             pltpu.VMEM((row_count,) + out_packed.shape, BF16),
@@ -491,14 +532,13 @@
             pltpu.SemaphoreType.DMA((len(routes),)),
             pltpu.SemaphoreType.DMA((len(masks),)),
         ],
-        cost(2 * part_cols * col_count * width * img, 8 * part_cols * col_count * width),
-        vmem=48,
+        cost(5),
+        vmem=56,
     )(
-        place,
         mod_own[2, :width][:, None],
         out_mod,
         hidden_img.T,
-        *[entry[0] for line in lines for entry in line],
+        *[part for line in lines for part in line],
         *[out_blocks[k] for k in masks],
     )
     mask = 1

time: 224 us -> 198 us (0.88)
  local copies, waits for them, and re-layouts: 24.8 us -> 7.75 us
  waiting for transfers between devices: 113 us -> 101 us
    unnamed x70 -> x100, local copies, waits for them, and re-layouts: 22.4 us -> 4.69 us
    ppermute x16, waiting for transfers between devices: 60 us -> 48.4 us  [the longest x4 31.5 us: gather_both(): out = lambda held: lax.ppermute(held, 'col', OUTWARD)]
  transfers between devices with their start and end apart: 51 -> 51, of which waited for: 21 -> 25; matrix products, arithmetic and copies ran while one was open for 0% -> 1% of each run, Pallas kernels for 13% -> 16%
where the time goes in v4:
time: 198 us; the launch traced here: 197 us
  waiting for transfers between devices  101 us (51%)
  starting transfers between devices  45.5 us (23%)
  Pallas kernels  38.7 us (20%)
  local copies, waits for them, and re-layouts  7.75 us (4%)
  between operations  2.92 us (1%)
    ppermute x35, waiting for transfers between devices, swap(): return lax.ppermute(block, axis, [(i, i ^ mask) for i in range(count)])  52.4 us
    ppermute x4, waiting for transfers between devices, gather_both(): out = lambda held: lax.ppermute(held, 'col', OUTWARD)  31.5 us
    ppermute x35, starting transfers between devices, swap(): return lax.ppermute(block, axis, [(i, i ^ mask) for i in range(count)])  26.8 us
    pallas_call x2, Pallas kernels, per_device(): call(functools.partial(project_kernel, routes, masks, img, head), (jax.Sh...  18.4 us
    pallas_call x2, Pallas kernels, per_device(): call(functools.partial(attend_kernel, img, txt, head), jax.ShapeDtypeStru...  11 us
    ppermute x2, waiting for transfers between devices, line_four(): return [block, pair, near, near_end, far, lax.ppermute(far, axis, OUTWARD)]  9.11 us
    ppermute x2, waiting for transfers between devices, line_four(): near_end = lax.ppermute(near, axis, OUTWARD)  7.72 us
    pallas_call x1, Pallas kernels, per_device(): call(functools.partial(output_kernel, routes, col_count, masks), jax.Shap...  6.52 us
  transfers between devices with their start and end apart: 51, of which 25 were waited for; matrix products, arithmetic and copies ran while one was open for 1% of the time, Pallas kernels for 16%

profile of v4, /device:TPU:0, one launch (start us, length us, event | category | flops | bytes accessed | tf_op | source)
XLA Modules:
  0.0 197.5 jit_solution(17088777600864714156)
XLA Ops:
  0.6 1.8 copy-done
  2.4 0.7 copy-done.13
  3.6 3.0 %collective-permute-start = (f32[8,640]{1,0:T(8,128)S(1)}, f32[8,640]{1,0:T(8,128)S(1)}, u32[]{:S(2)}, u32[]{:S(2)}) collective-permute-start(f32[8,640]{1,0:T(8,128)S(1)} %get-tuple-element.44), channel_id=1, source_target_pairs={{0,8},{4,12},{8,0},{12,4},{16,24},{20,28},{24,16},{28,20},{1,9},{5... | collective-permute-start | bytes 61448 | tf_op jit(solution)/shard_map/ppermute | solution.py:21
  6.6 1.5 collective-permute-start.1
  8.4 2.0 %collective-permute-done.1 = f32[8,640]{1,0:T(8,128)S(1)} collective-permute-done((f32[8,640]{1,0:T(8,128)S(1)}, f32[8,640]{1,0:T(8,128)S(1)}, u32[]{:S(2)}, u32[]{:S(2)}) %collective-permute-start.1) | collective-permute-done | bytes 20512 | tf_op jit(solution)/shard_map/ppermute | solution.py:21
  10.4 2.4 %collective-permute-done.2 = f32[8,640]{1,0:T(8,128)S(1)} collective-permute-done((f32[8,640]{1,0:T(8,128)S(1)}, f32[8,640]{1,0:T(8,128)S(1)}, u32[]{:S(2)}, u32[]{:S(2)}) %collective-permute-start.2) | collective-permute-done | bytes 20512 | tf_op jit(solution)/shard_map/ppermute | solution.py:21
  13.0 1.3 shard_map.140
  15.2 1.6 collective-permute-start.4
  16.8 2.2 %collective-permute-done.4 = f32[8,640]{1,0:T(8,128)S(1)} collective-permute-done((f32[8,640]{1,0:T(8,128)S(1)}, f32[8,640]{1,0:T(8,128)S(1)}, u32[]{:S(2)}, u32[]{:S(2)}) %collective-permute-start.4) | collective-permute-done | bytes 20512 | tf_op jit(solution)/shard_map/ppermute | solution.py:21
  19.0 2.6 %collective-permute-start.5 = (f32[8,640]{1,0:T(8,128)S(1)}, f32[8,640]{1,0:T(8,128)S(1)}, u32[]{:S(2)}, u32[]{:S(2)}) collective-permute-start(f32[8,640]{1,0:T(8,128)S(1)} %add.64), channel_id=1, source_target_pairs={{0,2},{1,3},{2,0},{3,1},{4,6},{5,7},{6,4},{7,5},{8,10},{9,11},{10,... | collective-permute-start | bytes 61448 | tf_op jit(solution)/shard_map/ppermute | solution.py:21
  22.1 1.6 collective-permute-done.5
  23.7 0.7 shard_map.143
  24.5 1.6 collective-permute-start.11
  26.1 0.7 collective-permute-start.12
  26.8 1.6 collective-permute-start.17
  28.4 5.4 %collective-permute-done.11.refs_7_ = bf16[304,608]{1,0:T(8,128)(2,1)S(1)} collective-permute-done((bf16[304,608]{1,0:T(8,128)(2,1)S(1)}, bf16[304,608]{1,0:T(8,128)(2,1)S(1)}, u32[]{:S(2)}, u32[]{:S(2)}) %collective-permute-start.11) | collective-permute-done | bytes 369696 | tf_op jit(solution)/shard_map/ppermute | solution.py:21
  33.8 1.6 collective-permute-start.6
  35.3 0.7 collective-permute-start.7
  36.6 5.3 %collective-permute-done.14.refs_16_ = bf16[304,1280]{1,0:T(8,128)(2,1)S(1)} collective-permute-done((bf16[304,1280]{1,0:T(8,128)(2,1)S(1)}, bf16[304,1280]{1,0:T(8,128)(2,1)S(1)}, u32[]{:S(2)}, u32[]{:S(2)}) %collective-permute-start.14) | collective-permute-done | bytes 778272 | tf_op jit(solution)/shard_map/ppermute | solution.py:21
  42.0 0.7 collective-permute-start.34
  42.8 0.7 collective-permute-start.9
  43.5 1.4 collective-permute-start.16
  44.9 5.9 %collective-permute-done.17.refs_14_ = bf16[304,1280]{1,0:T(8,128)(2,1)S(1)} collective-permute-done((bf16[304,1280]{1,0:T(8,128)(2,1)S(1)}, bf16[304,1280]{1,0:T(8,128)(2,1)S(1)}, u32[]{:S(2)}, u32[]{:S(2)}) %collective-permute-start.17) | collective-permute-done | bytes 778272 | tf_op jit(solution)/shard_map/ppermute | solution.py:21
  50.8 1.3 collective-permute-start.8
  52.1 6.6 %collective-permute-done.18.refs_16_ = bf16[304,1280]{1,0:T(8,128)(2,1)} collective-permute-done((bf16[304,1280]{1,0:T(8,128)(2,1)S(1)}, bf16[304,1280]{1,0:T(8,128)(2,1)}, u32[]{:S(2)}, u32[]{:S(2)}) %collective-permute-start.18) | collective-permute-done | bytes 778272 | tf_op jit(solution)/shard_map/ppermute | solution.py:21
  58.7 1.3 collective-permute-start.10
  60.1 11.0 %collective-permute-done.8.refs_3_ = bf16[304,608]{1,0:T(8,128)(2,1)S(1)} collective-permute-done((bf16[304,608]{1,0:T(8,128)(2,1)S(1)}, bf16[304,608]{1,0:T(8,128)(2,1)S(1)}, u32[]{:S(2)}, u32[]{:S(2)}) %collective-permute-start.8) | collective-permute-done | bytes 369696 | tf_op jit(solution)/shard_map/ppermute | solution.py:78
  71.1 1.5 collective-permute-start.23
  72.6 0.8 collective-permute-done.34.refs_18_
  73.4 1.9 collective-permute-done.10.refs_5_
  75.3 1.3 collective-permute-start.15
  76.6 10.2 %collective-permute-done.15.refs_9_ = bf16[304,608]{1,0:T(8,128)(2,1)S(1)} collective-permute-done((bf16[304,608]{1,0:T(8,128)(2,1)S(1)}, bf16[304,608]{1,0:T(8,128)(2,1)S(1)}, u32[]{:S(2)}, u32[]{:S(2)}) %collective-permute-start.15) | collective-permute-done | bytes 369696 | tf_op jit(solution)/shard_map/ppermute | solution.py:78
  86.8 1.5 collective-permute-start.19
  88.4 0.7 tile.10.gain_ref
  89.1 8.5 %collective-permute-done.19.refs_11_ = bf16[304,608]{1,0:T(8,128)(2,1)} collective-permute-done((bf16[304,608]{1,0:T(8,128)(2,1)}, bf16[304,608]{1,0:T(8,128)(2,1)}, u32[]{:S(2)}, u32[]{:S(2)}) %collective-permute-start.19) | collective-permute-done | bytes 369696 | tf_op jit(solution)/shard_map/ppermute | solution.py:78
  98.7 9.2 %shard_map.146 = (bf16[512,256]{1,0:T(8,128)(2,1)}, bf16[640,512]{1,0:T(8,128)(2,1)}) custom-call(f32[3,256]{1,0:T(4,128)} %tile.10.gain_ref, bf16[304,608]{1,0:T(8,128)(2,1)} %copy-done.8, bf16[304,608]{1,0:T(8,128)(2,1)} %copy-done.33, bf16[304,608]{1,0:T(8,128)(2,1)} %copy-done.34, bf16[304,608]{1,0:T(8,128)(2,1)} %copy-done.36, ...), custom_call_target="tpu_custom_call" | custom-call | flops 9200000000 | tf_op jit(solution)/shard_map/pallas_call | solution.py:482
  109.7 0.9 copy-done.30
  110.6 9.2 %shard_map.144 = (bf16[512,256]{1,0:T(8,128)(2,1)}, bf16[640,512]{1,0:T(8,128)(2,1)}) custom-call(f32[3,256]{1,0:T(4,128)} %tile.10.gain_ref, bf16[304,608]{1,0:T(8,128)(2,1)} %copy-done.8, bf16[304,608]{1,0:T(8,128)(2,1)} %copy-done.33, bf16[304,608]{1,0:T(8,128)(2,1)} %copy-done.34, bf16[304,608]{1,0:T(8,128)(2,1)} %copy-done.36, ...), custom_call_target="tpu_custom_call" | custom-call | flops 9200000000 | tf_op jit(solution)/shard_map/pallas_call | solution.py:482
  120.0 1.5 collective-permute-start.43
  122.6 1.5 collective-permute-start.46
  124.1 5.4 %shard_map.147.refs_6_ = bf16[256,512]{1,0:T(8,128)(2,1)S(1)} custom-call(s32[4]{0:T(128)S(1)} %copy-done.14, bf16[512,256]{1,0:T(8,128)(2,1)S(1)} %copy-done.15, bf16[640,512]{1,0:T(8,128)(2,1)S(1)} %copy-done.4, bf16[640,512]{1,0:T(8,128)(2,1)S(1)} %collective-permute-done.36.peer_ref), custom_call_target="tpu_custom_call" | custom-call | flops 6899999744 | tf_op jit(solution)/shard_map/pallas_call | solution.py:503
  129.7 5.6 %shard_map.145.refs_0_ = bf16[256,512]{1,0:T(8,128)(2,1)S(1)} custom-call(s32[4]{0:T(128)S(1)} %copy-done.14, bf16[512,256]{1,0:T(8,128)(2,1)S(1)} %copy-done.16, bf16[640,512]{1,0:T(8,128)(2,1)S(1)} %copy-done.5, bf16[640,512]{1,0:T(8,128)(2,1)S(1)} %collective-permute-done.25.peer_ref), custom_call_target="tpu_custom_call" | custom-call | flops 6899999744 | tf_op jit(solution)/shard_map/pallas_call | solution.py:503
  135.3 2.1 %collective-permute-start.26 = (bf16[256,512]{1,0:T(8,128)(2,1)S(1)}, bf16[256,512]{1,0:T(8,128)(2,1)S(1)}, u32[]{:S(2)}, u32[]{:S(2)}) collective-permute-start(bf16[256,512]{1,0:T(8,128)(2,1)S(1)} %shard_map.145.refs_0_), channel_id=1, source_target_pairs={{0,1},{1,0},{2,3},{3,2},{4,5},{5,4},{6,7},{7,6},{8,9},{9,8},{10,11... | collective-permute-start | bytes 786440 | tf_op jit(solution)/shard_map/ppermute | solution.py:21
  137.9 1.2 collective-permute-done.44.refs_15_
  139.1 1.4 collective-permute-start.38
  140.5 0.8 collective-permute-done.46.refs_17_
  141.9 1.4 collective-permute-start.40
  143.3 1.4 collective-permute-start.29
  144.7 3.7 %collective-permute-done.47.refs_18_ = bf16[736,256]{1,0:T(8,128)(2,1)S(1)} collective-permute-done((bf16[736,256]{1,0:T(8,128)(2,1)S(1)}, bf16[736,256]{1,0:T(8,128)(2,1)S(1)}, u32[]{:S(2)}, u32[]{:S(2)}) %collective-permute-start.47) | collective-permute-done | bytes 376864 | tf_op jit(solution)/shard_map/ppermute | solution.py:21
  148.9 1.3 collective-permute-start.39
  150.2 1.3 collective-permute-start.28
  151.5 1.3 collective-permute-start.41
  152.8 1.3 collective-permute-start.30
  154.1 0.9 copy.18.gate_ref
  155.7 2.5 %collective-permute-done.48.refs_19_ = bf16[736,256]{1,0:T(8,128)(2,1)S(1)} collective-permute-done((bf16[736,256]{1,0:T(8,128)(2,1)S(1)}, bf16[736,256]{1,0:T(8,128)(2,1)S(1)}, u32[]{:S(2)}, u32[]{:S(2)}) %collective-permute-start.48) | collective-permute-done | bytes 376864 | tf_op jit(solution)/shard_map/ppermute | solution.py:21
  158.2 2.1 %collective-permute-done.39.refs_9_ = bf16[256,512]{1,0:T(8,128)(2,1)} collective-permute-done((bf16[256,512]{1,0:T(8,128)(2,1)}, bf16[256,512]{1,0:T(8,128)(2,1)}, u32[]{:S(2)}, u32[]{:S(2)}) %collective-permute-start.39) | collective-permute-done | bytes 262176 | tf_op jit(solution)/shard_map/ppermute | solution.py:72
  160.3 5.6 %collective-permute-done.28.refs_3_ = bf16[256,512]{1,0:T(8,128)(2,1)} collective-permute-done((bf16[256,512]{1,0:T(8,128)(2,1)S(1)}, bf16[256,512]{1,0:T(8,128)(2,1)}, u32[]{:S(2)}, u32[]{:S(2)}) %collective-permute-start.28) | collective-permute-done | bytes 262176 | tf_op jit(solution)/shard_map/ppermute | solution.py:72
  165.9 5.6 %collective-permute-done.41.refs_11_ = bf16[256,512]{1,0:T(8,128)(2,1)} collective-permute-done((bf16[256,512]{1,0:T(8,128)(2,1)}, bf16[256,512]{1,0:T(8,128)(2,1)}, u32[]{:S(2)}, u32[]{:S(2)}) %collective-permute-start.41) | collective-permute-done | bytes 262176 | tf_op jit(solution)/shard_map/ppermute | solution.py:73
  171.6 3.5 %collective-permute-done.30.refs_5_ = bf16[256,512]{1,0:T(8,128)(2,1)} collective-permute-done((bf16[256,512]{1,0:T(8,128)(2,1)}, bf16[256,512]{1,0:T(8,128)(2,1)}, u32[]{:S(2)}, u32[]{:S(2)}) %collective-permute-start.30) | collective-permute-done | bytes 262176 | tf_op jit(solution)/shard_map/ppermute | solution.py:73
  175.1 6.5 %shard_map.148 = f32[72,640]{1,0:T(8,128)} custom-call(f32[608,1]{1,0:T(8,128)} %copy.18.gate_ref, f32[2,2,304]{2,1,0:T(2,128)} %bitcast.54, bf16[608,512]{1,0:T(8,128)(2,1)} %bitcast.45, bf16[256,512]{1,0:T(8,128)(2,1)} %copy-done.11, bf16[256,512]{1,0:T(8,128)(2,1)} %copy-done.47, bf16[256,512]{1,0:T(8,128)(2,1)} %copy-done.48, ...), custom_call_target="tpu_custom_call" | custom-call | flops 5750000128 | tf_op jit(solution)/shard_map/pallas_call | solution.py:524
  181.7 5.7 %collective-permute-done.49 = f32[72,640]{1,0:T(8,128)S(1)} collective-permute-done((f32[72,640]{1,0:T(8,128)}, f32[72,640]{1,0:T(8,128)S(1)}, u32[]{:S(2)}, u32[]{:S(2)}) %collective-permute-start.49) | collective-permute-done | bytes 184352 | tf_op jit(solution)/shard_map/ppermute | solution.py:21
  187.5 1.0 add.66
  190.5 5.9 %collective-permute-done.50 = f32[72,640]{1,0:T(8,128)S(1)} collective-permute-done((f32[72,640]{1,0:T(8,128)S(1)}, f32[72,640]{1,0:T(8,128)S(1)}, u32[]{:S(2)}, u32[]{:S(2)}) %collective-permute-start.50) | collective-permute-done | bytes 184352 | tf_op jit(solution)/shard_map/ppermute | solution.py:21
  196.7 0.8 fusion.2
  (169 shorter events, 10.7 us)
Async XLA Ops:
  3.6 4.8 %collective-permute-start = (f32[8,640]{1,0:T(8,128)S(1)}, f32[8,640]{1,0:T(8,128)S(1)}, u32[]{:S(2)}, u32[]{:S(2)}) collective-permute-start(f32[8,640]{1,0:T(8,128)S(1)} %get-tuple-element.44), channel_id=1, source_target_pairs={{0,8},{4,12},{8,0},{12,4},{16,24},{20,28},{24,16},{28,20},{1,9},{5... | collective-permute-start | bytes 61448 | tf_op jit(solution)/shard_map/ppermute | solution.py:21
  6.6 3.8 %collective-permute-start.1 = (f32[8,640]{1,0:T(8,128)S(1)}, f32[8,640]{1,0:T(8,128)S(1)}, u32[]{:S(2)}, u32[]{:S(2)}) collective-permute-start(f32[8,640]{1,0:T(8,128)S(1)} %get-tuple-element.46), channel_id=1, source_target_pairs={{0,16},{4,20},{8,24},{12,28},{16,0},{20,4},{24,8},{28,12},{1,17},{... | collective-permute-start | bytes 61448 | tf_op jit(solution)/shard_map/ppermute | solution.py:21
  8.2 4.7 %collective-permute-start.2 = (f32[8,640]{1,0:T(8,128)S(1)}, f32[8,640]{1,0:T(8,128)S(1)}, u32[]{:S(2)}, u32[]{:S(2)}) collective-permute-start(f32[8,640]{1,0:T(8,128)S(1)} %get-tuple-element.45), channel_id=1, source_target_pairs={{0,24},{4,28},{8,16},{12,20},{16,8},{20,12},{24,0},{28,4},{1,25},{... | collective-permute-start | bytes 61448 | tf_op jit(solution)/shard_map/ppermute | solution.py:21
  12.8 1.5 collective-permute-start.3
  14.3 83.3 %copy-start.2 = (bf16[304,1280]{1,0:T(8,128)(2,1)}, bf16[304,1280]{1,0:T(8,128)(2,1)S(1)}, u32[]{:S(2)}) copy-start(bf16[304,1280]{1,0:T(8,128)(2,1)S(1)} %get-tuple-element.26.refs_12_) | copy-start | bytes 2334724
  14.3 21.7 %collective-permute-start.13 = (bf16[304,1280]{1,0:T(8,128)(2,1)S(1)}, bf16[304,1280]{1,0:T(8,128)(2,1)S(1)}, u32[]{:S(2)}, u32[]{:S(2)}) collective-permute-start(bf16[304,1280]{1,0:T(8,128)(2,1)S(1)} %get-tuple-element.25.refs_12_), channel_id=1, source_target_pairs={{0,8},{4,12},{8,0},{12,4},{16,24},{20,28},{24,16},{28,20},{1,9},{5... | collective-permute-start | bytes 2334728 | tf_op jit(solution)/shard_map/ppermute | solution.py:21
  15.1 73.2 %copy-start.21 = (f32[2,64]{1,0:T(2,128)S(1)}, f32[2,64]{1,0:T(2,128)}, u32[]{:S(2)}) copy-start(f32[2,64]{1,0:T(2,128)} %param.23) | copy-start | bytes 1540
  15.2 73.2 %copy-start.22 = (f32[64]{0:T(128)S(1)}, f32[64]{0:T(128)}, u32[]{:S(2)}) copy-start(f32[64]{0:T(128)} %param.22) | copy-start | bytes 772
  15.2 73.9 %copy-start.20 = (bf16[304,64]{0,1:T(8,128)(2,1)S(1)}, bf16[304,64]{0,1:T(8,128)(2,1)}, u32[]{:S(2)}) copy-start(bf16[304,64]{0,1:T(8,128)(2,1)} %param.25) | copy-start | bytes 116740
  15.2 73.9 %copy-start.18 = (bf16[256,608]{0,1:T(8,128)(2,1)S(1)}, bf16[256,608]{0,1:T(8,128)(2,1)}, u32[]{:S(2)}) copy-start(bf16[256,608]{0,1:T(8,128)(2,1)} %param.24) | copy-start | bytes 933892
  15.2 3.8 %collective-permute-start.4 = (f32[8,640]{1,0:T(8,128)S(1)}, f32[8,640]{1,0:T(8,128)S(1)}, u32[]{:S(2)}, u32[]{:S(2)}) collective-permute-start(f32[8,640]{1,0:T(8,128)S(1)} %shard_map.142), channel_id=1, source_target_pairs={{0,1},{1,0},{2,3},{3,2},{4,5},{5,4},{6,7},{7,6},{8,9},{9,8},{10,11... | collective-permute-start | bytes 61448 | tf_op jit(solution)/shard_map/ppermute | solution.py:21
  19.0 4.7 %collective-permute-start.5 = (f32[8,640]{1,0:T(8,128)S(1)}, f32[8,640]{1,0:T(8,128)S(1)}, u32[]{:S(2)}, u32[]{:S(2)}) collective-permute-start(f32[8,640]{1,0:T(8,128)S(1)} %add.64), channel_id=1, source_target_pairs={{0,2},{1,3},{2,0},{3,1},{4,6},{5,7},{6,4},{7,5},{8,10},{9,11},{10,... | collective-permute-start | bytes 61448 | tf_op jit(solution)/shard_map/ppermute | solution.py:21
  21.6 20.3 %collective-permute-start.14 = (bf16[304,1280]{1,0:T(8,128)(2,1)S(1)}, bf16[304,1280]{1,0:T(8,128)(2,1)S(1)}, u32[]{:S(2)}, u32[]{:S(2)}) collective-permute-start(bf16[304,1280]{1,0:T(8,128)(2,1)S(1)} %get-tuple-element.26.refs_12_), channel_id=1, source_target_pairs={{0,16},{4,20},{8,24},{12,28},{16,0},{20,4},{24,8},{28,12},{1,17},{... | collective-permute-start | bytes 2334728 | tf_op jit(solution)/shard_map/ppermute | solution.py:21
  24.5 74.3 %copy-start.8 = (bf16[304,608]{1,0:T(8,128)(2,1)}, bf16[304,608]{1,0:T(8,128)(2,1)S(1)}, u32[]{:S(2)}) copy-start(bf16[304,608]{1,0:T(8,128)(2,1)S(1)} %get-tuple-element.23.refs_0_) | copy-start | bytes 1108996
  24.5 74.2 %copy-start.9 = (bf16[304,608]{1,0:T(8,128)(2,1)}, bf16[304,608]{1,0:T(8,128)(2,1)S(1)}, u32[]{:S(2)}) copy-start(bf16[304,608]{1,0:T(8,128)(2,1)S(1)} %get-tuple-element.24.refs_6_) | copy-start | bytes 1108996
  24.5 9.3 %collective-permute-start.11 = (bf16[304,608]{1,0:T(8,128)(2,1)S(1)}, bf16[304,608]{1,0:T(8,128)(2,1)S(1)}, u32[]{:S(2)}, u32[]{:S(2)}) collective-permute-start(bf16[304,608]{1,0:T(8,128)(2,1)S(1)} %get-tuple-element.24.refs_6_), channel_id=1, source_target_pairs={{0,1},{1,0},{2,3},{3,2},{4,5},{5,4},{6,7},{7,6},{8,9},{9,8},{10,11... | collective-permute-start | bytes 1109000 | tf_op jit(solution)/shard_map/ppermute | solution.py:21
  26.1 9.2 %collective-permute-start.12 = (bf16[304,608]{1,0:T(8,128)(2,1)S(1)}, bf16[304,608]{1,0:T(8,128)(2,1)S(1)}, u32[]{:S(2)}, u32[]{:S(2)}) collective-permute-start(bf16[304,608]{1,0:T(8,128)(2,1)S(1)} %get-tuple-element.24.refs_6_), channel_id=1, source_target_pairs={{1,2},{2,1},{5,6},{6,5},{9,10},{10,9},{13,14},{14,13},{17,18},{18,... | collective-permute-start | bytes 1109000 | tf_op jit(solution)/shard_map/ppermute | solution.py:80
  26.8 24.0 %collective-permute-start.17 = (bf16[304,1280]{1,0:T(8,128)(2,1)S(1)}, bf16[304,1280]{1,0:T(8,128)(2,1)S(1)}, u32[]{:S(2)}, u32[]{:S(2)}) collective-permute-start(bf16[304,1280]{1,0:T(8,128)(2,1)S(1)} %get-tuple-element.26.refs_12_), channel_id=1, source_target_pairs={{0,8},{4,12},{8,0},{12,4},{16,24},{20,28},{24,16},{28,20},{1,9},{5... | collective-permute-start | bytes 2334728 | tf_op jit(solution)/shard_map/ppermute | solution.py:21
  33.7 54.5 %copy-start.31 = (bf16[304,608]{1,0:T(8,128)(2,1)}, bf16[304,608]{1,0:T(8,128)(2,1)S(1)}, u32[]{:S(2)}) copy-start(bf16[304,608]{1,0:T(8,128)(2,1)S(1)} %collective-permute-done.11.refs_7_) | copy-start | bytes 1108996
  33.8 8.3 %collective-permute-start.6 = (bf16[304,608]{1,0:T(8,128)(2,1)S(1)}, bf16[304,608]{1,0:T(8,128)(2,1)S(1)}, u32[]{:S(2)}, u32[]{:S(2)}) collective-permute-start(bf16[304,608]{1,0:T(8,128)(2,1)S(1)} %get-tuple-element.23.refs_0_), channel_id=1, source_target_pairs={{0,1},{1,0},{2,3},{3,2},{4,5},{5,4},{6,7},{7,6},{8,9},{9,8},{10,11... | collective-permute-start | bytes 1109000 | tf_op jit(solution)/shard_map/ppermute | solution.py:21
  35.3 52.9 %copy-start.32 = (bf16[304,608]{1,0:T(8,128)(2,1)}, bf16[304,608]{1,0:T(8,128)(2,1)S(1)}, u32[]{:S(2)}) copy-start(bf16[304,608]{1,0:T(8,128)(2,1)S(1)} %collective-permute-done.12.refs_8_) | copy-start | bytes 1108996
  35.3 7.4 %collective-permute-start.7 = (bf16[304,608]{1,0:T(8,128)(2,1)S(1)}, bf16[304,608]{1,0:T(8,128)(2,1)S(1)}, u32[]{:S(2)}, u32[]{:S(2)}) collective-permute-start(bf16[304,608]{1,0:T(8,128)(2,1)S(1)} %get-tuple-element.23.refs_0_), channel_id=1, source_target_pairs={{1,2},{2,1},{5,6},{6,5},{9,10},{10,9},{13,14},{14,13},{17,18},{18,... | collective-permute-start | bytes 1109000 | tf_op jit(solution)/shard_map/ppermute | solution.py:80
  36.0 62.7 %copy-start.24 = (bf16[304,1280]{1,0:T(8,128)(2,1)}, bf16[304,1280]{1,0:T(8,128)(2,1)S(1)}, u32[]{:S(2)}) copy-start(bf16[304,1280]{1,0:T(8,128)(2,1)S(1)} %collective-permute-done.13.refs_14_) | copy-start | bytes 2334724
  36.0 22.7 %collective-permute-start.18 = (bf16[304,1280]{1,0:T(8,128)(2,1)S(1)}, bf16[304,1280]{1,0:T(8,128)(2,1)}, u32[]{:S(2)}, u32[]{:S(2)}) collective-permute-start(bf16[304,1280]{1,0:T(8,128)(2,1)S(1)} %get-tuple-element.25.refs_12_), channel_id=1, source_target_pairs={{0,16},{4,20},{8,24},{12,28},{16,0},{20,4},{24,8},{28,12},{1,17},{... | collective-permute-start | bytes 2334728 | tf_op jit(solution)/shard_map/ppermute | solution.py:21
  41.9 66.0 %copy-start.23 = (bf16[304,1280]{1,0:T(8,128)(2,1)}, bf16[304,1280]{1,0:T(8,128)(2,1)S(1)}, u32[]{:S(2)}) copy-start(bf16[304,1280]{1,0:T(8,128)(2,1)S(1)} %collective-permute-done.14.refs_16_) | copy-start | bytes 2334724
  41.9 30.7 %collective-permute-start.31 = (bf16[304,1280]{1,0:T(8,128)(2,1)S(1)}, bf16[304,1280]{1,0:T(8,128)(2,1)S(1)}, u32[]{:S(2)}, u32[]{:S(2)}) collective-permute-start(bf16[304,1280]{1,0:T(8,128)(2,1)S(1)} %get-tuple-element.25.refs_12_), channel_id=1, source_target_pairs={{0,4},{4,0},{8,12},{12,8},{16,20},{20,16},{24,28},{28,24},{1,5},{5... | collective-permute-start | bytes 2334728 | tf_op jit(solution)/shard_map/ppermute | solution.py:21
  42.0 46.2 %copy-start.33 = (bf16[304,608]{1,0:T(8,128)(2,1)}, bf16[304,608]{1,0:T(8,128)(2,1)S(1)}, u32[]{:S(2)}) copy-start(bf16[304,608]{1,0:T(8,128)(2,1)S(1)} %collective-permute-done.6.refs_1_) | copy-start | bytes 1108996
  42.0 31.4 %collective-permute-start.34 = (bf16[304,1280]{1,0:T(8,128)(2,1)S(1)}, bf16[304,1280]{1,0:T(8,128)(2,1)}, u32[]{:S(2)}, u32[]{:S(2)}) collective-permute-start(bf16[304,1280]{1,0:T(8,128)(2,1)S(1)} %collective-permute-done.13.refs_14_), channel_id=1, source_target_pairs={{0,16},{4,20},{8,24},{12,28},{16,0},{20,4},{24,8},{28,12},{1,17},{... | collective-permute-start | bytes 2334728 | tf_op jit(solution)/shard_map/ppermute | solution.py:21
  42.8 45.5 %copy-start.34 = (bf16[304,608]{1,0:T(8,128)(2,1)}, bf16[304,608]{1,0:T(8,128)(2,1)S(1)}, u32[]{:S(2)}) copy-start(bf16[304,608]{1,0:T(8,128)(2,1)S(1)} %collective-permute-done.7.refs_2_) | copy-start | bytes 1108996
  42.8 0.7 collective-permute-start.9
  43.5 16.6 %collective-permute-start.16 = (bf16[304,608]{1,0:T(8,128)(2,1)S(1)}, bf16[304,608]{1,0:T(8,128)(2,1)}, u32[]{:S(2)}, u32[]{:S(2)}) collective-permute-start(bf16[304,608]{1,0:T(8,128)(2,1)S(1)} %collective-permute-done.11.refs_7_), channel_id=1, source_target_pairs={{1,2},{2,1},{5,6},{6,5},{9,10},{10,9},{13,14},{14,13},{17,18},{18,... | collective-permute-start | bytes 1109000 | tf_op jit(solution)/shard_map/ppermute | solution.py:89
  50.8 20.3 %collective-permute-start.8 = (bf16[304,608]{1,0:T(8,128)(2,1)S(1)}, bf16[304,608]{1,0:T(8,128)(2,1)S(1)}, u32[]{:S(2)}, u32[]{:S(2)}) collective-permute-start(bf16[304,608]{1,0:T(8,128)(2,1)S(1)} %collective-permute-done.7.refs_2_), channel_id=1, source_target_pairs={{1,0},{2,3},{5,4},{6,7},{9,8},{10,11},{13,12},{14,15},{17,16},{18,... | collective-permute-start | bytes 1109000 | tf_op jit(solution)/shard_map/ppermute | solution.py:78
  58.7 16.6 %collective-permute-start.10 = (bf16[304,608]{1,0:T(8,128)(2,1)S(1)}, bf16[304,608]{1,0:T(8,128)(2,1)S(1)}, u32[]{:S(2)}, u32[]{:S(2)}) collective-permute-start(bf16[304,608]{1,0:T(8,128)(2,1)S(1)} %collective-permute-done.9.refs_4_), channel_id=1, source_target_pairs={{1,0},{2,3},{5,4},{6,7},{9,8},{10,11},{13,12},{14,15},{17,16},{18,... | collective-permute-start | bytes 1109000 | tf_op jit(solution)/shard_map/ppermute | solution.py:78
  60.0 37.6 %collective-permute-start.32 = (bf16[304,1280]{1,0:T(8,128)(2,1)S(1)}, bf16[304,1280]{1,0:T(8,128)(2,1)}, u32[]{:S(2)}, u32[]{:S(2)}) collective-permute-start(bf16[304,1280]{1,0:T(8,128)(2,1)S(1)} %collective-permute-done.13.refs_14_), channel_id=1, source_target_pairs={{0,4},{4,0},{8,12},{12,8},{16,20},{20,16},{24,28},{28,24},{1,5},{5... | collective-permute-start | bytes 2334728 | tf_op jit(solution)/shard_map/ppermute | solution.py:21
  71.1 27.0 %collective-permute-start.23 = (bf16[304,1280]{1,0:T(8,128)(2,1)S(1)}, bf16[304,1280]{1,0:T(8,128)(2,1)}, u32[]{:S(2)}, u32[]{:S(2)}) collective-permute-start(bf16[304,1280]{1,0:T(8,128)(2,1)S(1)} %collective-permute-done.14.refs_16_), channel_id=1, source_target_pairs={{0,8},{4,12},{8,0},{12,4},{16,24},{20,28},{24,16},{28,20},{1,9},{5... | collective-permute-start | bytes 2334728 | tf_op jit(solution)/shard_map/ppermute | solution.py:21
  72.6 25.6 %collective-permute-start.33 = (bf16[304,1280]{1,0:T(8,128)(2,1)}, bf16[304,1280]{1,0:T(8,128)(2,1)}, u32[]{:S(2)}, u32[]{:S(2)}) collective-permute-start(bf16[304,1280]{1,0:T(8,128)(2,1)} %collective-permute-done.18.refs_16_), channel_id=1, source_target_pairs={{0,4},{4,0},{8,12},{12,8},{16,20},{20,16},{24,28},{28,24},{1,5},{5... | collective-permute-start | bytes 2334728 | tf_op jit(solution)/shard_map/ppermute | solution.py:21
  73.4 25.2 %collective-permute-start.35 = (bf16[304,1280]{1,0:T(8,128)(2,1)}, bf16[304,1280]{1,0:T(8,128)(2,1)}, u32[]{:S(2)}, u32[]{:S(2)}) collective-permute-start(bf16[304,1280]{1,0:T(8,128)(2,1)} %collective-permute-done.34.refs_18_), channel_id=1, source_target_pairs={{0,4},{4,0},{8,12},{12,8},{16,20},{20,16},{24,28},{28,24},{1,5},{5... | collective-permute-start | bytes 2334728 | tf_op jit(solution)/shard_map/ppermute | solution.py:21
  75.3 11.5 %collective-permute-start.15 = (bf16[304,608]{1,0:T(8,128)(2,1)S(1)}, bf16[304,608]{1,0:T(8,128)(2,1)S(1)}, u32[]{:S(2)}, u32[]{:S(2)}) collective-permute-start(bf16[304,608]{1,0:T(8,128)(2,1)S(1)} %collective-permute-done.12.refs_8_), channel_id=1, source_target_pairs={{1,0},{2,3},{5,4},{6,7},{9,8},{10,11},{13,12},{14,15},{17,16},{18,... | collective-permute-start | bytes 1109000 | tf_op jit(solution)/shard_map/ppermute | solution.py:78
  86.8 10.9 %collective-permute-start.19 = (bf16[304,608]{1,0:T(8,128)(2,1)}, bf16[304,608]{1,0:T(8,128)(2,1)}, u32[]{:S(2)}, u32[]{:S(2)}) collective-permute-start(bf16[304,608]{1,0:T(8,128)(2,1)} %collective-permute-done.16.refs_10_), channel_id=1, source_target_pairs={{1,0},{2,3},{5,4},{6,7},{9,8},{10,11},{13,12},{14,15},{17,16},{18,... | collective-permute-start | bytes 1109000 | tf_op jit(solution)/shard_map/ppermute | solution.py:78
  97.6 24.4 %collective-permute-start.42 = (bf16[736,256]{1,0:T(8,128)(2,1)S(1)}, bf16[736,256]{1,0:T(8,128)(2,1)S(1)}, u32[]{:S(2)}, u32[]{:S(2)}) collective-permute-start(bf16[736,256]{1,0:T(8,128)(2,1)S(1)} %pad_maximum_fusion.refs_12_), channel_id=1, source_target_pairs={{0,4},{4,0},{8,12},{12,8},{16,20},{20,16},{24,28},{28,24},{1,5},{5... | collective-permute-start | bytes 1130504 | tf_op jit(solution)/shard_map/ppermute | solution.py:21
  97.6 10.3 %collective-permute-start.20 = (bf16[304,1280]{1,0:T(8,128)(2,1)S(1)}, bf16[304,1280]{1,0:T(8,128)(2,1)S(1)}, u32[]{:S(2)}, u32[]{:S(2)}) collective-permute-start(bf16[304,1280]{1,0:T(8,128)(2,1)S(1)} %get-tuple-element.26.refs_12_), channel_id=1, source_target_pairs={{0,4},{4,0},{8,12},{12,8},{16,20},{20,16},{24,28},{28,24},{1,5},{5... | collective-permute-start | bytes 2334728 | tf_op jit(solution)/shard_map/ppermute | solution.py:21
  98.1 10.4 %collective-permute-start.22 = (bf16[304,1280]{1,0:T(8,128)(2,1)S(1)}, bf16[304,1280]{1,0:T(8,128)(2,1)S(1)}, u32[]{:S(2)}, u32[]{:S(2)}) collective-permute-start(bf16[304,1280]{1,0:T(8,128)(2,1)S(1)} %collective-permute-done.14.refs_16_), channel_id=1, source_target_pairs={{0,4},{4,0},{8,12},{12,8},{16,20},{20,16},{24,28},{28,24},{1,5},{5... | collective-permute-start | bytes 2334728 | tf_op jit(solution)/shard_map/ppermute | solution.py:21
  98.2 10.3 %collective-permute-start.21 = (bf16[304,1280]{1,0:T(8,128)(2,1)}, bf16[304,1280]{1,0:T(8,128)(2,1)S(1)}, u32[]{:S(2)}, u32[]{:S(2)}) collective-permute-start(bf16[304,1280]{1,0:T(8,128)(2,1)} %copy-done.25), channel_id=1, source_target_pairs={{0,4},{4,0},{8,12},{12,8},{16,20},{20,16},{24,28},{28,24},{1,5},{5... | collective-permute-start | bytes 2334728 | tf_op jit(solution)/shard_map/ppermute | solution.py:21
  98.6 9.9 %collective-permute-start.24 = (bf16[304,1280]{1,0:T(8,128)(2,1)}, bf16[304,1280]{1,0:T(8,128)(2,1)S(1)}, u32[]{:S(2)}, u32[]{:S(2)}) collective-permute-start(bf16[304,1280]{1,0:T(8,128)(2,1)} %collective-permute-done.23.refs_18_), channel_id=1, source_target_pairs={{0,4},{4,0},{8,12},{12,8},{16,20},{20,16},{24,28},{28,24},{1,5},{5... | collective-permute-start | bytes 2334728 | tf_op jit(solution)/shard_map/ppermute | solution.py:21
  108.0 14.6 %collective-permute-start.36 = (bf16[640,512]{1,0:T(8,128)(2,1)}, bf16[640,512]{1,0:T(8,128)(2,1)S(1)}, u32[]{:S(2)}, u32[]{:S(2)}) collective-permute-start(bf16[640,512]{1,0:T(8,128)(2,1)} %get-tuple-element.37.own_ref), channel_id=1, source_target_pairs={{0,4},{4,0},{8,12},{12,8},{16,20},{20,16},{24,28},{28,24},{1,5},{5... | collective-permute-start | bytes 1966088 | tf_op jit(solution)/shard_map/ppermute | solution.py:21
  119.8 9.8 %collective-permute-start.25 = (bf16[640,512]{1,0:T(8,128)(2,1)}, bf16[640,512]{1,0:T(8,128)(2,1)S(1)}, u32[]{:S(2)}, u32[]{:S(2)}) collective-permute-start(bf16[640,512]{1,0:T(8,128)(2,1)} %get-tuple-element.33.own_ref), channel_id=1, source_target_pairs={{0,4},{4,0},{8,12},{12,8},{16,20},{20,16},{24,28},{28,24},{1,5},{5... | collective-permute-start | bytes 1966088 | tf_op jit(solution)/shard_map/ppermute | solution.py:21
  120.0 15.3 %collective-permute-start.43 = (bf16[736,256]{1,0:T(8,128)(2,1)S(1)}, bf16[736,256]{1,0:T(8,128)(2,1)S(1)}, u32[]{:S(2)}, u32[]{:S(2)}) collective-permute-start(bf16[736,256]{1,0:T(8,128)(2,1)S(1)} %pad_maximum_fusion.refs_12_), channel_id=1, source_target_pairs={{0,8},{4,12},{8,0},{12,4},{16,24},{20,28},{24,16},{28,20},{1,9},{5... | collective-permute-start | bytes 1130504 | tf_op jit(solution)/shard_map/ppermute | solution.py:21
  121.5 15.9 %collective-permute-start.45 = (bf16[736,256]{1,0:T(8,128)(2,1)S(1)}, bf16[736,256]{1,0:T(8,128)(2,1)S(1)}, u32[]{:S(2)}, u32[]{:S(2)}) collective-permute-start(bf16[736,256]{1,0:T(8,128)(2,1)S(1)} %pad_maximum_fusion.refs_12_), channel_id=1, source_target_pairs={{0,16},{4,20},{8,24},{12,28},{16,0},{20,4},{24,8},{28,12},{1,17},{... | collective-permute-start | bytes 1130504 | tf_op jit(solution)/shard_map/ppermute | solution.py:21
  122.0 17.1 %collective-permute-start.44 = (bf16[736,256]{1,0:T(8,128)(2,1)S(1)}, bf16[736,256]{1,0:T(8,128)(2,1)S(1)}, u32[]{:S(2)}, u32[]{:S(2)}) collective-permute-start(bf16[736,256]{1,0:T(8,128)(2,1)S(1)} %collective-permute-done.42.refs_13_), channel_id=1, source_target_pairs={{0,8},{4,12},{8,0},{12,4},{16,24},{20,28},{24,16},{28,20},{1,9},{5... | collective-permute-start | bytes 1130504 | tf_op jit(solution)/shard_map/ppermute | solution.py:21
  122.6 18.6 %collective-permute-start.46 = (bf16[736,256]{1,0:T(8,128)(2,1)S(1)}, bf16[736,256]{1,0:T(8,128)(2,1)S(1)}, u32[]{:S(2)}, u32[]{:S(2)}) collective-permute-start(bf16[736,256]{1,0:T(8,128)(2,1)S(1)} %collective-permute-done.42.refs_13_), channel_id=1, source_target_pairs={{0,16},{4,20},{8,24},{12,28},{16,0},{20,4},{24,8},{28,12},{1,17},{... | collective-permute-start | bytes 1130504 | tf_op jit(solution)/shard_map/ppermute | solution.py:21
  129.6 12.3 %collective-permute-start.37 = (bf16[256,512]{1,0:T(8,128)(2,1)S(1)}, bf16[256,512]{1,0:T(8,128)(2,1)S(1)}, u32[]{:S(2)}, u32[]{:S(2)}) collective-permute-start(bf16[256,512]{1,0:T(8,128)(2,1)S(1)} %shard_map.147.refs_6_), channel_id=1, source_target_pairs={{0,1},{1,0},{2,3},{3,2},{4,5},{5,4},{6,7},{7,6},{8,9},{9,8},{10,11... | collective-permute-start | bytes 786440 | tf_op jit(solution)/shard_map/ppermute | solution.py:21
  135.3 7.9 %collective-permute-start.26 = (bf16[256,512]{1,0:T(8,128)(2,1)S(1)}, bf16[256,512]{1,0:T(8,128)(2,1)S(1)}, u32[]{:S(2)}, u32[]{:S(2)}) collective-permute-start(bf16[256,512]{1,0:T(8,128)(2,1)S(1)} %shard_map.145.refs_0_), channel_id=1, source_target_pairs={{0,1},{1,0},{2,3},{3,2},{4,5},{5,4},{6,7},{7,6},{8,9},{9,8},{10,11... | collective-permute-start | bytes 786440 | tf_op jit(solution)/shard_map/ppermute | solution.py:21
  137.4 11.0 %collective-permute-start.47 = (bf16[736,256]{1,0:T(8,128)(2,1)S(1)}, bf16[736,256]{1,0:T(8,128)(2,1)S(1)}, u32[]{:S(2)}, u32[]{:S(2)}) collective-permute-start(bf16[736,256]{1,0:T(8,128)(2,1)S(1)} %collective-permute-done.43.refs_14_), channel_id=1, source_target_pairs={{0,16},{4,20},{8,24},{12,28},{16,0},{20,4},{24,8},{28,12},{1,17},{... | collective-permute-start | bytes 1130504 | tf_op jit(solution)/shard_map/ppermute | solution.py:21
  139.1 9.8 %collective-permute-start.38 = (bf16[256,512]{1,0:T(8,128)(2,1)S(1)}, bf16[256,512]{1,0:T(8,128)(2,1)}, u32[]{:S(2)}, u32[]{:S(2)}) collective-permute-start(bf16[256,512]{1,0:T(8,128)(2,1)S(1)} %shard_map.147.refs_6_), channel_id=1, source_target_pairs={{1,2},{2,1},{5,6},{6,5},{9,10},{10,9},{13,14},{14,13},{17,18},{18,... | collective-permute-start | bytes 786440 | tf_op jit(solution)/shard_map/ppermute | solution.py:70
  141.2 8.9 %collective-permute-start.27 = (bf16[256,512]{1,0:T(8,128)(2,1)S(1)}, bf16[256,512]{1,0:T(8,128)(2,1)S(1)}, u32[]{:S(2)}, u32[]{:S(2)}) collective-permute-start(bf16[256,512]{1,0:T(8,128)(2,1)S(1)} %shard_map.145.refs_0_), channel_id=1, source_target_pairs={{1,2},{2,1},{5,6},{6,5},{9,10},{10,9},{13,14},{14,13},{17,18},{18,... | collective-permute-start | bytes 786440 | tf_op jit(solution)/shard_map/ppermute | solution.py:70
  141.9 9.6 %collective-permute-start.40 = (bf16[256,512]{1,0:T(8,128)(2,1)S(1)}, bf16[256,512]{1,0:T(8,128)(2,1)}, u32[]{:S(2)}, u32[]{:S(2)}) collective-permute-start(bf16[256,512]{1,0:T(8,128)(2,1)S(1)} %collective-permute-done.37.refs_7_), channel_id=1, source_target_pairs={{1,2},{2,1},{5,6},{6,5},{9,10},{10,9},{13,14},{14,13},{17,18},{18,... | collective-permute-start | bytes 786440 | tf_op jit(solution)/shard_map/ppermute | solution.py:71
  143.3 9.5 %collective-permute-start.29 = (bf16[256,512]{1,0:T(8,128)(2,1)S(1)}, bf16[256,512]{1,0:T(8,128)(2,1)}, u32[]{:S(2)}, u32[]{:S(2)}) collective-permute-start(bf16[256,512]{1,0:T(8,128)(2,1)S(1)} %collective-permute-done.26.refs_1_), channel_id=1, source_target_pairs={{1,2},{2,1},{5,6},{6,5},{9,10},{10,9},{13,14},{14,13},{17,18},{18,... | collective-permute-start | bytes 786440 | tf_op jit(solution)/shard_map/ppermute | solution.py:71
  148.4 9.8 %collective-permute-start.48 = (bf16[736,256]{1,0:T(8,128)(2,1)S(1)}, bf16[736,256]{1,0:T(8,128)(2,1)S(1)}, u32[]{:S(2)}, u32[]{:S(2)}) collective-permute-start(bf16[736,256]{1,0:T(8,128)(2,1)S(1)} %collective-permute-done.44.refs_15_), channel_id=1, source_target_pairs={{0,16},{4,20},{8,24},{12,28},{16,0},{20,4},{24,8},{28,12},{1,17},{... | collective-permute-start | bytes 1130504 | tf_op jit(solution)/shard_map/ppermute | solution.py:21
  148.9 11.4 %collective-permute-start.39 = (bf16[256,512]{1,0:T(8,128)(2,1)}, bf16[256,512]{1,0:T(8,128)(2,1)}, u32[]{:S(2)}, u32[]{:S(2)}) collective-permute-start(bf16[256,512]{1,0:T(8,128)(2,1)} %collective-permute-done.38.refs_8_), channel_id=1, source_target_pairs={{1,0},{2,3},{5,4},{6,7},{9,8},{10,11},{13,12},{14,15},{17,16},{18,... | collective-permute-start | bytes 786440 | tf_op jit(solution)/shard_map/ppermute | solution.py:72
  150.2 15.8 %collective-permute-start.28 = (bf16[256,512]{1,0:T(8,128)(2,1)S(1)}, bf16[256,512]{1,0:T(8,128)(2,1)}, u32[]{:S(2)}, u32[]{:S(2)}) collective-permute-start(bf16[256,512]{1,0:T(8,128)(2,1)S(1)} %collective-permute-done.27.refs_2_), channel_id=1, source_target_pairs={{1,0},{2,3},{5,4},{6,7},{9,8},{10,11},{13,12},{14,15},{17,16},{18,... | collective-permute-start | bytes 786440 | tf_op jit(solution)/shard_map/ppermute | solution.py:72
  151.5 20.1 %collective-permute-start.41 = (bf16[256,512]{1,0:T(8,128)(2,1)}, bf16[256,512]{1,0:T(8,128)(2,1)}, u32[]{:S(2)}, u32[]{:S(2)}) collective-permute-start(bf16[256,512]{1,0:T(8,128)(2,1)} %collective-permute-done.40.refs_10_), channel_id=1, source_target_pairs={{1,0},{2,3},{5,4},{6,7},{9,8},{10,11},{13,12},{14,15},{17,16},{18,... | collective-permute-start | bytes 786440 | tf_op jit(solution)/shard_map/ppermute | solution.py:73
  152.8 22.2 %collective-permute-start.30 = (bf16[256,512]{1,0:T(8,128)(2,1)}, bf16[256,512]{1,0:T(8,128)(2,1)}, u32[]{:S(2)}, u32[]{:S(2)}) collective-permute-start(bf16[256,512]{1,0:T(8,128)(2,1)} %collective-permute-done.29.refs_4_), channel_id=1, source_target_pairs={{1,0},{2,3},{5,4},{6,7},{9,8},{10,11},{13,12},{14,15},{17,16},{18,... | collective-permute-start | bytes 786440 | tf_op jit(solution)/shard_map/ppermute | solution.py:73
  181.7 5.8 %collective-permute-start.49 = (f32[72,640]{1,0:T(8,128)}, f32[72,640]{1,0:T(8,128)S(1)}, u32[]{:S(2)}, u32[]{:S(2)}) collective-permute-start(f32[72,640]{1,0:T(8,128)} %shard_map.148), channel_id=1, source_target_pairs={{0,1},{1,0},{2,3},{3,2},{4,5},{5,4},{6,7},{7,6},{8,9},{9,8},{10,11... | collective-permute-start | bytes 552968 | tf_op jit(solution)/shard_map/ppermute | solution.py:21
  188.4 8.0 %collective-permute-start.50 = (f32[72,640]{1,0:T(8,128)S(1)}, f32[72,640]{1,0:T(8,128)S(1)}, u32[]{:S(2)}, u32[]{:S(2)}) collective-permute-start(f32[72,640]{1,0:T(8,128)S(1)} %add.66), channel_id=1, source_target_pairs={{0,2},{1,3},{2,0},{3,1},{4,6},{5,7},{6,4},{7,5},{8,10},{9,11},{10,... | collective-permute-start | bytes 552968 | tf_op jit(solution)/shard_map/ppermute | solution.py:21
  (37 other events, 630.7 us)

commit v5 on v4

v5 whole, which is shorter than its diff:
```python
import functools

import jax
import jax.numpy as jnp
from jax import lax
from jax.experimental import pallas as pl
from jax.experimental.pallas import tpu as pltpu
from jax.sharding import PartitionSpec as P

STEPS = 28
EPS_NORM = 1e-06
ATTEND = 6
PROJECT = 20
AHEAD = 2
EARLY = 48
F32 = jnp.float32
BF16 = jnp.bfloat16
HBM = pl.BlockSpec(memory_space=pltpu.HBM)
VMEM = pl.BlockSpec(memory_space=pltpu.VMEM)
SMEM = pl.BlockSpec(memory_space=pltpu.SMEM)


def swap(block, axis, mask):
    count = lax.axis_size(axis)
    return lax.ppermute(block, axis, [(i, i ^ mask) for i in range(count)])


def shift(block, axis, step):
    count = lax.axis_size(axis)
    route = [(i, i + step) for i in range(count) if 0 <= i + step < count]
    return lax.ppermute(block, axis, route)


def tie(*arrays):
    return lax.optimization_barrier(arrays)


def line_gather(block, axis):
    held = {0: block}
    for step in range(1, lax.axis_size(axis)):
        held[-step] = shift(held[1 - step], axis, 1)
        held[step] = shift(held[step - 1], axis, -1)
    return [held[k] for k in sorted(held)]


def line_routes(count):
    if count == 4:
        near = lambda p: jnp.where(p < 2, 2, 1)
        far = lambda p: jnp.where(p < 2, 3, 0)
        inner = lambda p: (p == 1) | (p == 2)
        outer = lambda p: (p == 0) | (p == 3)
        always = lambda p: p >= 0
        return [
            (lambda p: p, always),
            (lambda p: jnp.bitwise_xor(p, 1), always),
            (near, inner),
            (near, outer),
            (far, inner),
            (far, outer),
        ]
    result = []
    for offset in range(1 - count, count):
        inside = lambda p, offset=offset: (p + offset >= 0) & (p + offset < count)
        result.append((lambda p, offset=offset: p + offset, inside))
    return result


def far_routes(count):
    routes = list(enumerate(line_routes(count)))
    if count == 4:
        return routes[:4], routes[4:], routes[4][1][0]
    far = lambda p: count - 1 - p
    early, late = [], []
    for n, (owner, held) in routes:
        is_far = lambda p, owner=owner: owner(p) == far(p)
        early.append((n, (owner, lambda p, held=held, is_far=is_far: held(p) & ~is_far(p))))
        late.append((n, (owner, lambda p, held=held, is_far=is_far: held(p) & is_far(p))))
    return early, late, far


MIDDLE = [(1, 2), (2, 1)]
OUTWARD = [(1, 0), (2, 3)]


def line_four(block, axis):
    pair = swap(block, axis, 1)
    near = lax.ppermute(block, axis, MIDDLE)
    far = lax.ppermute(pair, axis, MIDDLE)
    near_end = lax.ppermute(near, axis, OUTWARD)
    return [block, pair, near, near_end, far, lax.ppermute(far, axis, OUTWARD)]


def gather_both(tokens, weights):
    send = lambda held, route: lax.ppermute(held, "col", route)
    first, second = weights
    pair, near = swap(tokens, "col", 1), send(tokens, MIDDLE)
    first_y, second_x = swap(first, "row", 4), swap(second, "row", 2)
    pair, near, first_y, second_x, first, second = tie(
        pair, near, first_y, second_x, first, second
    )
    near_end, far = send(near, OUTWARD), send(pair, MIDDLE)
    first_x, second_y = swap(first, "row", 2), swap(second, "row", 4)
    near_end, far, first_x, second_y, first_y, second_x, tokens, pair, near = tie(
        near_end, far, first_x, second_y, first_y, second_x, tokens, pair, near
    )
    far_end = send(far, OUTWARD)
    other = lambda held: swap(held, "row", 1)
    peer = other(tokens)
    peer, pair, near, near_end, far = tie(peer, pair, near, near_end, far)
    peers = [peer, other(pair), other(near), other(near_end), other(far), other(far_end)]
    held = [
        {0: first, 4: first_y, 2: first_x, 6: swap(first_y, "row", 2)},
        {0: second, 2: second_x, 4: second_y, 6: swap(second_x, "row", 4)},
    ]
    return [tokens, pair, near, near_end, far, far_end], peers, held


def direct_gather(block, axis, masks):
    return {mask: swap(block, axis, mask) if mask else block for mask in masks}


def doubling_gather(block, axis, masks):
    held = {0: block}
    for mask in masks:
        for known in list(held):
            held[known | mask] = swap(held[known], axis, mask)
    return held


def in_order(pieces, axis):
    masks, place = sorted(pieces[0]), lax.axis_index(axis)
    core = place % 2
    joined = jnp.stack([jnp.stack([piece[k] for k in masks]) for piece in pieces], axis=1)
    joined = joined[jnp.bitwise_xor(jnp.arange(len(masks)), place // 2)]
    joined = jnp.where(core == 0, joined, joined[:, ::-1])
    return joined.reshape(joined.shape[0], -1, joined.shape[-1])


def cost(us):
    return pl.CostEstimate(flops=int(us * 1.15e9), bytes_accessed=0, transcendentals=0)


def call(kernel, outs, in_specs, scratch, estimate, out_specs=None, vmem=16):
    if out_specs is None:
        out_specs = jax.tree.map(lambda _: VMEM, outs)
    return pl.pallas_call(
        kernel,
        out_shape=outs,
        in_specs=in_specs,
        out_specs=out_specs,
        scratch_shapes=scratch,
        cost_estimate=estimate,
        compiler_params=pltpu.CompilerParams(vmem_limit_bytes=vmem * 1024 * 1024),
    )


def line_copies(refs, routes, place, target, sems, act):
    for n, (ref, (owner, held)) in enumerate(zip(refs, routes)):

        @pl.when(held(place))
        def _():
            copy = pltpu.make_async_copy(ref, target(owner(place)), sems.at[n])
            getattr(copy, act)()


def mod_kernel(cond_ref, w_ref, out_ref):
    requests, groups, width = cond_ref.shape[0], w_ref.shape[0], w_ref.shape[2]
    request = lax.axis_index("row") // 2
    values = jnp.concatenate(
        [cond_ref[pl.ds(jnp.bitwise_xor(request, k), 1), :] for k in range(requests)], axis=0
    )
    activated = (values * (1.0 / (1.0 + jnp.exp(-values)))).astype(BF16)
    out_ref[...] = jnp.zeros(out_ref.shape, F32)
    for group in range(groups):
        out_ref[:, group, :width] = jnp.dot(
            activated, w_ref[group], preferred_element_type=F32
        )


def pack_kernel(qkv_ref, kv_ref, keep_ref, give_ref):
    half = keep_ref.shape[1] // 5
    first = lax.axis_index("row") % 2 == 0
    for k in range(5):
        rows = qkv_ref[k] if k < 3 else kv_ref[:, k - 3]
        low, high = rows[:, :half], rows[:, half:]
        here = slice(k * half, (k + 1) * half)
        keep_ref[:, here] = jnp.where(first, low, high)
        give_ref[:, here] = jnp.where(first, high, low)


def stats_kernel(img_ref, txt_ref, out_ref):
    img = img_ref.shape[1]
    txt = txt_ref.shape[0]
    out_ref[...] = jnp.zeros(out_ref.shape, F32)
    for values, low, high in (
        (img_ref[...].astype(F32), 0, img),
        (txt_ref[...].astype(F32).T, img, img + txt),
    ):
        out_ref[0:1, low:high] = jnp.sum(values, axis=0, keepdims=True)
        out_ref[1:2, low:high] = jnp.sum(values * values, axis=0, keepdims=True)


def norm_kernel(total, img_ref, txt_ref, stats_ref, mod_ref, out_ref):
    width, img = img_ref.shape
    txt = txt_ref.shape[0]
    stats = stats_ref[...] / total
    row = lax.broadcasted_iota(jnp.int32, stats.shape, 0)
    average = stats[0:1]
    inverse = lax.rsqrt(stats[1:2] - average * average + EPS_NORM)
    columns = jnp.where(row == 0, average, inverse).T
    chunk = 128
    for low in range(0, img + txt, chunk):
        for start in range(0, width, chunk):
            stop = min(start + chunk, width)
            if low < img:
                high = min(low + chunk, img)
                values, group = img_ref[start:stop, low:high].T, 0
            else:
                high = min(low + chunk, img + txt)
                values, group = txt_ref[low - img : high - img, start:stop], 3
            normed = (values.astype(F32) - columns[low:high, 0:1]) * columns[low:high, 1:2]
            stretch = 1.0 + mod_ref[group + 1 : group + 2, start:stop]
            normed = normed * stretch + mod_ref[group : group + 1, start:stop]
            out_ref[low:high, start:stop] = normed.astype(BF16)


def attend(img, txt, head, length_ref, queries, keys, values, out_ref):
    width = queries.shape[1]
    place = lax.axis_index("row")
    side = lax.rem(place, 2)
    slot = lax.broadcasted_iota(jnp.int32, (2 * txt, 1), 0)
    other = (slot >= txt).astype(jnp.int32)
    owner = jnp.where(other == 1, 1 - side, side)
    allowed = owner * txt + slot - other * txt < length_ref[place // 2]
    turned = values.T
    ones = jnp.ones((16, keys.shape[0]), BF16)
    rows = [
        jnp.concatenate([turned[k * head : (k + 1) * head], ones], axis=0)
        for k in range(width // head)
    ]
    lane = lax.broadcasted_iota(jnp.int32, (1, width), 1) // head
    step = 256 if img % 256 == 0 else img

    def scores_of(k, low):
        query = jnp.where(lane == k, queries[low : low + step], 0.0).astype(BF16)
        score = lax.dot_general(
            keys, query, (((1,), (1,)), ((), ())), preferred_element_type=F32
        )
        tail = jnp.where(allowed, score[2 * img :], -1e30)
        return jnp.concatenate([score[: 2 * img], tail], axis=0)

    work = [(k, low) for k in range(width // head) for low in range(0, img, step)]
    ahead = scores_of(*work[0])
    for n, (k, low) in enumerate(work):
        scores = ahead
        if n + 1 < len(work):
            ahead = scores_of(*work[n + 1])
        weights = jnp.exp(scores - jnp.max(scores, axis=0, keepdims=True)).astype(BF16)
        mixed = jnp.dot(rows[k], weights, preferred_element_type=F32)
        out_ref[k * head : (k + 1) * head, low : low + step] = (
            mixed[:head] / mixed[head : head + 1]
        ).astype(BF16)


def attend_kernel(img, txt, head, length_ref, q_ref, k_ref, v_ref, out_ref, *scratch):
    parts, sems = scratch[:-1], scratch[-1]
    copies = [
        pltpu.make_async_copy(ref, part, sems.at[n])
        for n, (ref, part) in enumerate(zip((q_ref, k_ref, v_ref), parts))
    ]
    for copy in copies:
        copy.start()
    for copy in copies:
        copy.wait()
    attend(img, txt, head, length_ref, *[part[...] for part in parts], out_ref)


def project_kernel(routes, masks, img, head, length_ref, gain_ref, *refs):
    lines = refs[: len(routes)], refs[len(routes) : 2 * len(routes)]
    refs = refs[2 * len(routes) :]
    n_blocks = 2 * len(masks) if masks else 1
    blocks, refs = refs[:n_blocks], refs[n_blocks:]
    outs, (x_ref, w_ref, img_ref, txt_ref, sems_x, sems_w) = refs[:-6], refs[-6:]
    tokens = lines[0][0].shape[0]
    txt = tokens - img
    count, _, width = x_ref.shape
    half = img_ref.shape[1] // 3
    place, col = lax.axis_index("row"), lax.axis_index("col")
    chip, core = place // 2, lax.rem(place, 2)

    def copy_lines(act):
        for n, line in enumerate(lines):
            for k, (low, high, to) in enumerate(
                ((0, img, n * img), (img, tokens, 2 * img + n * txt))
            ):
                parts = [ref.at[pl.ds(low, high - low)] for ref in line]
                target = lambda owner: x_ref.at[owner, pl.ds(to, high - low)]
                line_copies(parts, routes, col, target, sems_x.at[n, k], act)

    copy_lines("start")
    stages = []
    for k in range(count):
        copies = []
        if not masks:
            if k == 0:
                copies.append(pltpu.make_async_copy(blocks[0], w_ref, sems_w.at[0, 0]))
        else:
            depth = blocks[0].shape[0]
            for piece in range(2):
                row = jnp.where(core == piece, 0, depth)
                target = w_ref.at[
                    jnp.bitwise_xor(chip, k), pl.ds(pl.multiple_of(row, 16), depth)
                ]
                ref = blocks[piece * len(masks) + k]
                copies.append(pltpu.make_async_copy(ref, target, sems_w.at[piece, k]))
        stages.append(copies)

    def start(n):
        for copy in stages[n] if n < count else ():
            copy.start()

    for n in range(AHEAD):
        start(n)
    row = lax.broadcasted_iota(jnp.int32, (half, half), 0) // head
    column = lax.broadcasted_iota(jnp.int32, (half, half), 1) // head
    mean_of = jnp.where(row == column, 1.0 / head, 0.0).astype(BF16)

    def head_norm(values, gain):
        square = values * values
        mean_square = jnp.zeros_like(square)
        for _ in range(3):
            term = square.astype(BF16)
            mean_square += jnp.dot(term, mean_of, preferred_element_type=F32)
            square = square - term.astype(F32)
        return (values * lax.rsqrt(mean_square + EPS_NORM) * gain).astype(BF16)

    copy_lines("wait")
    for k in range(count):
        for copy in stages[k]:
            copy.wait()
        start(k + AHEAD)
        here = jnp.bitwise_xor(chip, k)
        for ref, low, high, first, parts in (
            (img_ref, 0, 2 * img, 0, 3),
            (txt_ref, 2 * img, 2 * tokens, 3, 2),
        ):
            term = jnp.dot(
                x_ref[here, low:high],
                w_ref[here, :, first * half : (first + parts) * half],
                preferred_element_type=F32,
            )
            ref[...] = term if k == 0 else ref[...] + term
    scaling = head ** (-0.5)
    queries = head_norm(img_ref[:, :half], gain_ref[0:1])
    queries = (queries.astype(F32) * scaling).astype(BF16)
    keys = jnp.concatenate(
        [
            head_norm(img_ref[:, half : 2 * half], gain_ref[1:2]),
            head_norm(txt_ref[:, :half], gain_ref[2:3]),
        ],
        axis=0,
    )
    values = jnp.concatenate(
        [img_ref[:, 2 * half :].astype(BF16), txt_ref[:, half:].astype(BF16)], axis=0
    )
    for ref, part in zip(outs[1:], (queries[img:], keys, values)):
        ref[...] = part
    attend(img, txt, head, length_ref, queries[:img], keys, values, outs[0])


def place_heads(lines, routes, col, target, sems):
    core = lax.rem(lax.axis_index("row"), 2)
    size = lines[0][0].shape[0]
    for act in ("start", "wait"):
        for n, line in enumerate(lines):
            rows = pl.ds(pl.multiple_of(jnp.where(core == n, 0, size), 16), size)
            line_copies(line, routes, col, lambda owner: target(owner, rows), sems.at[n], act)


def early_kernel(routes, far, masks, mod_ref, *refs):
    n_lines = len(routes)
    lines = [refs[n * n_lines : (n + 1) * n_lines] for n in range(2)]
    refs = refs[2 * n_lines :]
    weights, refs = refs[:2], refs[2:]
    sum_ref, far_ref, gain_ref, const_ref, a_ref, w_ref, sems_a, sems_w = refs
    width = sum_ref.shape[0]
    count = a_ref.shape[0]
    depth = w_ref.shape[2]
    place, col = lax.axis_index("row"), lax.axis_index("col")
    copies = []
    for k, ref in enumerate(weights):
        for n, mask in enumerate(masks):
            target = w_ref.at[jnp.bitwise_xor(place, mask + k)]
            source = ref.at[pl.ds(n * w_ref.shape[1], w_ref.shape[1])]
            copies.append(pltpu.make_async_copy(source, target, sems_w.at[k, n]))
    for copy in copies:
        copy.start()
    place_heads(lines, routes, col, lambda owner, rows: a_ref.at[owner, rows], sems_a)
    for copy in copies:
        copy.wait()
    per_col = w_ref.shape[0] // count
    farthest = far(col)
    total = None
    for k in range(1, count):
        owner = lax.rem(farthest + k, count)
        for n in range(per_col):
            term = jnp.dot(
                w_ref[owner * per_col + n, :width],
                a_ref[owner, n * depth : (n + 1) * depth],
                preferred_element_type=F32,
            )
            total = term if total is None else total + term
    sum_ref[...] = total
    for n in range(per_col):
        far_ref[:, n * depth : (n + 1) * depth] = w_ref[farthest * per_col + n, :width]

    patch = gain_ref.shape[0] // 3
    slab = width // per_col
    gains = jnp.zeros((patch, 1), F32)
    shifts = jnp.zeros((patch, 1), F32)
    for n in range(per_col):
        for k in range((w_ref.shape[1] - width) // patch):
            low, high = k * depth, min((k + 1) * depth, slab)
            if low >= high:
                continue
            piece = w_ref[col * per_col + n, width + k * patch : width + (k + 1) * patch]
            here = slice(n * slab + low, n * slab + high)
            linear = piece[:, : high - low].astype(F32)
            gained = linear * (1.0 + mod_ref[6:7, here])
            shifts += jnp.sum(linear * mod_ref[5:6, here], axis=1, keepdims=True)
            gains += jnp.sum(gained, axis=1, keepdims=True)
            for t in range(3):
                term = gained.astype(BF16)
                gain_ref[t * patch : (t + 1) * patch, here] = term
                gained = gained - term.astype(F32)
    lane = lax.broadcasted_iota(jnp.int32, const_ref.shape, 1)
    const_ref[...] = jnp.where(lane == 0, gains, jnp.where(lane == 1, shifts, 0.0))


def late_kernel(routes, mod_ref, x_ref, sum_ref, far_ref, gain_ref, const_ref, *refs):
    n_lines = len(routes)
    lines = [refs[n * n_lines : (n + 1) * n_lines] for n in range(2)]
    out_ref, a_ref, sems_a = refs[2 * n_lines :]
    width, tokens = x_ref.shape
    col = lax.axis_index("col")
    place_heads(lines, routes, col, lambda owner, rows: a_ref.at[rows], sems_a)
    gate = mod_ref[...].T[:width, 2:3]
    projected = sum_ref[...] + jnp.dot(far_ref[...], a_ref[...], preferred_element_type=F32)
    updated = (x_ref[...].astype(F32) + gate * projected).astype(BF16)
    wide = updated.astype(F32)
    sums = jnp.sum(wide, axis=0, keepdims=True)
    squares = jnp.sum(wide * wide, axis=0, keepdims=True)
    patch = const_ref.shape[0]
    terms = jnp.dot(gain_ref[...], updated, preferred_element_type=F32)
    out_ref[:patch, :tokens] = terms[:patch] + terms[patch : 2 * patch] + terms[2 * patch :]
    row = lax.broadcasted_iota(jnp.int32, (8, tokens), 0)
    out_ref[patch:, :tokens] = jnp.where(row == 0, sums, jnp.where(row == 1, squares, 0.0))
    out_ref[:patch, tokens:] = const_ref[...]
    out_ref[patch:, tokens:] = jnp.zeros((8, 128), F32)


def sigma_of(step_now):
    remain = 1.0 - step_now.astype(F32) / STEPS
    return 3.0 * remain / (1.0 + 2.0 * remain)


def per_device(
    hidden_img,
    hidden_txt,
    text_len,
    step_index,
    latent,
    cond,
    mod_weight,
    qkv_weight,
    kv_text_weight,
    q_gain,
    k_gain,
    out_weight,
    final_weight,
):
    row_count, col_count = lax.axis_size("row"), lax.axis_size("col")
    request = lax.axis_index("row") // 2
    requests = cond.shape[0]
    img, width = hidden_img.shape
    txt = hidden_txt.shape[0]
    head = q_gain.shape[0]
    part_cols = qkv_weight.shape[2]
    half = part_cols // 2
    full_width = width * col_count

    wide = -(-width // 128) * 128
    room = -(-txt // 128) * 128
    tokens = img + room
    mod_part = call(
        mod_kernel,
        jax.ShapeDtypeStruct((requests, 8, wide), F32),
        [VMEM, VMEM],
        [],
        cost(2),
    )(cond, jnp.moveaxis(mod_weight, 1, 0))
    mod_own = mod_part[0]
    for k in range(1, requests):
        mod_own = mod_own + swap(mod_part[k], "row", 2 * k)
    stats = call(
        stats_kernel,
        jax.ShapeDtypeStruct((8, tokens), F32),
        [VMEM, VMEM],
        [],
        cost(1),
    )(hidden_img.T, hidden_txt)
    stats = sum((swap(stats, "col", mask) for mask in range(1, col_count)), stats)

    chip_masks = [1 << bit for bit in range(1, row_count.bit_length() - 1)]
    packed = call(
        pack_kernel,
        (jax.ShapeDtypeStruct((qkv_weight.shape[0], 5 * half), BF16),) * 2,
        [VMEM, VMEM],
        [],
        cost(2),
        (VMEM, VMEM),
    )(jnp.moveaxis(qkv_weight, 1, 0), kv_text_weight)
    packed = packed[0], swap(packed[1], "row", 1)
    *packed, mod_own = tie(*packed, mod_own)
    mod_own = mod_own + swap(mod_own, "row", 1)
    ready = call(
        functools.partial(norm_kernel, full_width),
        jax.ShapeDtypeStruct((img + txt, width), BF16),
        [VMEM] * 4,
        [],
        cost(1),
    )(hidden_img.T, hidden_txt, stats, mod_own)
    routes = line_routes(col_count)
    small = col_count == 4 and row_count == 8
    if small:
        ready, *packed = tie(ready, *packed)
        line, peer_line, gathered = gather_both(ready, packed)
    else:
        line = line_gather(ready, "col")
        peer_line = [swap(part, "row", 1) for part in line]
        gathered = [doubling_gather(part, "row", chip_masks) for part in packed]

    if gathered[0][0].shape[0] % 16 == 0:
        masks = sorted(gathered[0])
        blocks = [piece[k] for piece in gathered for k in masks]
    else:
        masks, blocks = [], [in_order(gathered, "row")]
    gains = jnp.tile(jnp.concatenate([q_gain[None], k_gain], axis=0), (1, half // head))
    heads_out = jax.ShapeDtypeStruct((half, img), BF16)
    rest = [jax.ShapeDtypeStruct((rows, half), BF16) for rows in (img, *[2 * (img + txt)] * 2)]
    projected = call(
        functools.partial(project_kernel, routes, masks, img, head),
        (heads_out, *rest),
        [SMEM, VMEM] + [HBM] * (2 * len(routes) + len(blocks)),
        [
            pltpu.VMEM((col_count, 2 * (img + txt), width), BF16),
            pltpu.VMEM((col_count, width, 5 * half), BF16),
            pltpu.VMEM((2 * img, 3 * half), F32),
            pltpu.VMEM((2 * txt, 2 * half), F32),
            pltpu.SemaphoreType.DMA((2, 2, len(routes))),
            pltpu.SemaphoreType.DMA((2, max(len(masks), 1))),
        ],
        cost(PROJECT),
        (VMEM,) * 4,
        vmem=56,
    )(text_len, gains, *line, *peer_line, *blocks)
    head_depth, patch = final_weight.shape
    depth = out_weight.shape[0]
    folds = -(-head_depth // depth)
    tail = jnp.pad(final_weight.T, ((0, 0), (0, folds * depth - head_depth)))
    tail = jnp.swapaxes(tail.reshape(patch, folds, depth), 0, 1).reshape(folds * patch, depth)
    out_packed = jnp.concatenate([out_weight.T, tail], axis=0)
    masks = list(range(0, row_count, 2))
    out_blocks = direct_gather(out_packed, "row", masks)

    own_heads, *rest = projected
    others = [out_blocks[k] for k in masks[1:]]
    *rest, = tie(*rest, *others)
    rest, others = rest[:3], rest[3:]
    give = call(
        functools.partial(attend_kernel, img, txt, head),
        heads_out,
        [SMEM, HBM, HBM, HBM],
        [pltpu.VMEM(part.shape, BF16) for part in rest] + [pltpu.SemaphoreType.DMA((3,))],
        cost(ATTEND),
        vmem=24,
    )(text_len, *rest)
    attended = [own_heads, swap(give, "row", 1)]
    lines = [(line_four if small else line_gather)(block, "col") for block in attended]
    own_rows = jnp.concatenate([out_packed, *others], axis=0)
    other_rows = swap(own_rows, "row", 1)
    early, late, far = far_routes(col_count)
    sems = pltpu.SemaphoreType.DMA((2, len(routes)))
    bundle = call(
        functools.partial(early_kernel, [route for _, route in early], far, masks),
        (
            jax.ShapeDtypeStruct((width, img), F32),
            jax.ShapeDtypeStruct((width, part_cols), BF16),
            jax.ShapeDtypeStruct((3 * patch, width), BF16),
            jax.ShapeDtypeStruct((patch, 128), F32),
        ),
        [VMEM] + [HBM] * (2 * len(early) + 2),
        [
            pltpu.VMEM((col_count, part_cols, img), BF16),
            pltpu.VMEM((row_count,) + out_packed.shape, BF16),
            sems,
            pltpu.SemaphoreType.DMA((2, len(masks))),
        ],
        cost(5),
        (VMEM,) * 4,
        vmem=EARLY,
    )(
        mod_own,
        *[line[k] for line in lines for k, _ in early],
        own_rows,
        other_rows,
    )
    partial_sum = call(
        functools.partial(late_kernel, [route for _, route in late]),
        jax.ShapeDtypeStruct((patch + 8, img + 128), F32),
        [VMEM] * 6 + [HBM] * (2 * len(late)),
        [pltpu.VMEM((part_cols, img), BF16), sems],
        cost(3),
        vmem=24,
    )(mod_own, hidden_img.T, *bundle, *[line[k] for line in lines for k, _ in late])
    mask = 1
    while mask < col_count:
        partial_sum = partial_sum + swap(partial_sum, "col", mask)
        mask *= 2
    average = partial_sum[patch : patch + 1, :img] / full_width
    mean_square = partial_sum[patch + 1 : patch + 2, :img] / full_width
    inverse = lax.rsqrt(mean_square - average * average + EPS_NORM)
    gains = partial_sum[:patch, img : img + 1]
    shifts = partial_sum[:patch, img + 1 : img + 2]
    velocity = inverse * (partial_sum[:patch, :img] - average * gains) + shifts
    step_now = lax.dynamic_index_in_dim(step_index, request, 0, keepdims=False)
    sigma_step = sigma_of(step_now + 1) - sigma_of(step_now)
    latent_next = latent.T + sigma_step * velocity
    return (velocity.T, latent_next.T)


def solution(mesh):
    in_specs = (
        P("row", "col"),
        P("row", "col"),
        P(),
        P(),
        P("row", None),
        P(None, "row"),
        P("row", None, "col"),
        P("row", None, "col"),
        P("row", None, "col"),
        P(),
        P(),
        P("row", "col"),
        P("row", None),
    )
    out_specs = (P("row", None), P("row", None))
    return jax.shard_map(
        per_device, mesh=mesh, in_specs=in_specs, out_specs=out_specs, check_vma=False
    )
```

time: 198 us -> 177 us (0.89)
  Pallas kernels: 38.7 us -> 30.2 us
  starting transfers between devices: 45.5 us -> 37.3 us
  waiting for transfers between devices: 101 us -> 99 us
    pallas_call x6 -> x5, Pallas kernels: 36.7 us -> 27.6 us  [the longest x1 17.3 us: per_device(): call(functools.partial(project_kernel, routes, masks, img, head), (heads_...]
    ppermute x35 -> x30, waiting for transfers between devices: 52.4 us -> 44.6 us  [swap(): return lax.ppermute(block, axis, [(i, i ^ mask) for i in range(count)])]
    ppermute x8 -> x4, waiting for transfers between devices: 31.5 us -> 36.9 us  [gather_both(): send = lambda held, route: lax.ppermute(held, 'col', route)]
    ppermute x2, waiting for transfers between devices: 7.72 us -> 11.8 us  [line_four(): near_end = lax.ppermute(near, axis, OUTWARD)]
    ppermute x2, waiting for transfers between devices: 9.11 us -> 5.58 us  [line_four(): return [block, pair, near, near_end, far, lax.ppermute(far, axis, OUTWARD)]]
    ppermute x35 -> x30, starting transfers between devices: 26.8 us -> 23.6 us  [swap(): return lax.ppermute(block, axis, [(i, i ^ mask) for i in range(count)])]
    ppermute x8 -> x4, starting transfers between devices: 8.74 us -> 5.84 us  [gather_both(): send = lambda held, route: lax.ppermute(held, 'col', route)]
    unnamed x100 -> x60, local copies, waits for them, and re-layouts: 4.69 us -> 5.45 us
  transfers between devices with their start and end apart: 51 -> 42, of which waited for: 25 -> 15; matrix products, arithmetic and copies ran while one was open for 1% -> 1% of each run, Pallas kernels for 16% -> 15%
where the time goes in v5:
time: 177 us
  waiting for transfers between devices  99 us (56%)
  starting transfers between devices  37.3 us (21%)
  Pallas kernels  30.2 us (17%)
  local copies, waits for them, and re-layouts  6.94 us (4%)
  between operations  2.63 us (1%)
    ppermute x30, waiting for transfers between devices, swap(): return lax.ppermute(block, axis, [(i, i ^ mask) for i in range(count)])  44.6 us
    ppermute x4, waiting for transfers between devices, gather_both(): send = lambda held, route: lax.ppermute(held, 'col', route)  36.9 us
    ppermute x30, starting transfers between devices, swap(): return lax.ppermute(block, axis, [(i, i ^ mask) for i in range(count)])  23.6 us
    pallas_call x1, Pallas kernels, per_device(): call(functools.partial(project_kernel, routes, masks, img, head), (heads_...  17.3 us
    ppermute x2, waiting for transfers between devices, line_four(): near_end = lax.ppermute(near, axis, OUTWARD)  11.8 us
    ppermute x4, starting transfers between devices, gather_both(): send = lambda held, route: lax.ppermute(held, 'col', route)  5.84 us
    ppermute x2, waiting for transfers between devices, line_four(): return [block, pair, near, near_end, far, lax.ppermute(far, axis, OUTWARD)]  5.58 us
    unnamed x60, local copies, waits for them, and re-layouts  5.45 us
  transfers between devices with their start and end apart: 42, of which 15 were waited for; matrix products, arithmetic and copies ran while one was open for 1% of the time, Pallas kernels for 15%

profile of v5, /device:TPU:0, one launch (start us, length us, event | category | flops | bytes accessed | tf_op | source)
XLA Modules:
  0.0 176.9 jit_solution(10712039140959617584)
XLA Ops:
  0.6 1.2 copy-done.1
  1.8 1.1 copy-done.4
  2.9 1.9 %shard_map.140 = (bf16[304,1280]{1,0:T(8,128)(2,1)S(1)}, bf16[304,1280]{1,0:T(8,128)(2,1)S(1)}) custom-call(bf16[3,304,512]{2,1,0:T(8,128)(2,1)S(1)} %bitcast.40, bf16[304,2,512]{2,1,0:T(2,128)(2,1)S(1)} %copy-done.4), custom_call_target="tpu_custom_call" | custom-call | flops 2300000000 | tf_op jit(solution)/shard_map/pallas_call | solution.py:515
  4.8 0.5 collective-permute-start
  5.3 0.5 shard_map.141
  5.8 2.6 %collective-permute-start.1 = (f32[8,640]{1,0:T(8,128)S(1)}, f32[8,640]{1,0:T(8,128)S(1)}, u32[]{:S(2)}, u32[]{:S(2)}) collective-permute-start(f32[8,640]{1,0:T(8,128)S(1)} %get-tuple-element.92), channel_id=1, source_target_pairs={{0,8},{4,12},{8,0},{12,4},{16,24},{20,28},{24,16},{28,20},{1,9},{5... | collective-permute-start | bytes 61448 | tf_op jit(solution)/shard_map/ppermute | solution.py:25
  8.4 1.5 collective-permute-start.2
  10.0 0.2 shard_map.142
  10.2 2.1 %collective-permute-start.5 = (f32[8,640]{1,0:T(8,128)S(1)}, f32[8,640]{1,0:T(8,128)S(1)}, u32[]{:S(2)}, u32[]{:S(2)}) collective-permute-start(f32[8,640]{1,0:T(8,128)S(1)} %shard_map.142), channel_id=1, source_target_pairs={{0,1},{1,0},{2,3},{3,2},{4,5},{5,4},{6,7},{7,6},{8,9},{9,8},{10,11... | collective-permute-start | bytes 61448 | tf_op jit(solution)/shard_map/ppermute | solution.py:25
  12.3 2.6 %collective-permute-start.6 = (f32[8,640]{1,0:T(8,128)S(1)}, f32[8,640]{1,0:T(8,128)S(1)}, u32[]{:S(2)}, u32[]{:S(2)}) collective-permute-start(f32[8,640]{1,0:T(8,128)S(1)} %shard_map.142), channel_id=1, source_target_pairs={{0,2},{1,3},{2,0},{3,1},{4,6},{5,7},{6,4},{7,5},{8,10},{9,11},{10,... | collective-permute-start | bytes 61448 | tf_op jit(solution)/shard_map/ppermute | solution.py:25
  14.9 1.0 collective-permute-start.7
  15.9 1.1 collective-permute-done.6
  17.1 3.4 %collective-permute-done.7 = f32[8,640]{1,0:T(8,128)S(1)} collective-permute-done((f32[8,640]{1,0:T(8,128)S(1)}, f32[8,640]{1,0:T(8,128)S(1)}, u32[]{:S(2)}, u32[]{:S(2)}) %collective-permute-start.7) | collective-permute-done | bytes 20512 | tf_op jit(solution)/shard_map/ppermute | solution.py:25
  20.5 0.7 shard_map.143.refs_0_
  21.3 1.6 collective-permute-start.10
  22.9 1.5 collective-permute-start.11
  24.4 1.5 collective-permute-start.9
  25.9 15.3 %collective-permute-done.8.refs_1_ = bf16[608,608]{1,0:T(8,128)(2,1)} collective-permute-done((bf16[608,608]{1,0:T(8,128)(2,1)S(1)}, bf16[608,608]{1,0:T(8,128)(2,1)}, u32[]{:S(2)}, u32[]{:S(2)}) %collective-permute-start.8) | collective-permute-done | bytes 739360 | tf_op jit(solution)/shard_map/ppermute | solution.py:25
  41.2 0.6 collective-permute-start.14
  41.8 0.5 collective-permute-start.15
  42.3 1.3 collective-permute-start.12
  43.6 1.6 collective-permute-start.13
  45.2 15.6 %collective-permute-done.12.refs_3_ = bf16[608,608]{1,0:T(8,128)(2,1)} collective-permute-done((bf16[608,608]{1,0:T(8,128)(2,1)}, bf16[608,608]{1,0:T(8,128)(2,1)}, u32[]{:S(2)}, u32[]{:S(2)}) %collective-permute-start.12) | collective-permute-done | bytes 739360 | tf_op jit(solution)/shard_map/ppermute | solution.py:94
  60.8 1.6 collective-permute-start.23
  62.4 1.5 collective-permute-start.24
  63.9 1.5 collective-permute-start.17
  65.4 0.8 collective-permute-done.16.refs_6_
  66.3 0.4 collective-permute-start.19
  66.7 21.4 %collective-permute-done.17.refs_5_ = bf16[608,608]{1,0:T(8,128)(2,1)} collective-permute-done((bf16[608,608]{1,0:T(8,128)(2,1)}, bf16[608,608]{1,0:T(8,128)(2,1)}, u32[]{:S(2)}, u32[]{:S(2)}) %collective-permute-start.17) | collective-permute-done | bytes 739360 | tf_op jit(solution)/shard_map/ppermute | solution.py:94
  88.0 0.5 collective-permute-start.21
  88.7 0.8 copy-done.25
  89.5 0.7 tile.10.gain_ref
  90.3 0.6 collective-permute-start.28
  90.9 0.5 collective-permute-start.29
  91.4 2.4 %collective-permute-start.30 = (bf16[736,256]{1,0:T(8,128)(2,1)S(1)}, bf16[736,256]{1,0:T(8,128)(2,1)S(1)}, u32[]{:S(2)}, u32[]{:S(2)}) collective-permute-start(bf16[736,256]{1,0:T(8,128)(2,1)S(1)} %pad_maximum_fusion), channel_id=1, source_target_pairs={{0,24},{4,28},{8,16},{12,20},{16,8},{20,12},{24,0},{28,4},{1,25},{... | collective-permute-start | bytes 1130504 | tf_op jit(solution)/shard_map/ppermute | solution.py:25
  93.8 17.3 %shard_map.144 = (bf16[256,512]{1,0:T(8,128)(2,1)}, bf16[512,256]{1,0:T(8,128)(2,1)}, bf16[1216,256]{1,0:T(8,128)(2,1)}, bf16[1216,256]{1,0:T(8,128)(2,1)}) custom-call(s32[4]{0:T(128)} %length_ref.3, f32[3,256]{1,0:T(4,128)} %tile.10.gain_ref, bf16[608,608]{1,0:T(8,128)(2,1)} %copy-done.3, bf16[608,608]{1,0:T(8,128)(2,1)} %collective-permute-done.8.refs_1_, ...), custom_call_target="tpu_custom_call" | custom-call | flops 23000000512 | tf_op jit(solution)/shard_map/pallas_call | solution.py:551
  111.4 0.4 copy-done.9
  111.8 0.4 copy-done.10
  112.3 0.2 copy-done.11
  112.5 5.1 %shard_map.145 = bf16[256,512]{1,0:T(8,128)(2,1)S(1)} custom-call(s32[4]{0:T(128)S(1)} %copy-done.9, bf16[512,256]{1,0:T(8,128)(2,1)S(1)} %copy-done.12, bf16[1216,256]{1,0:T(8,128)(2,1)S(1)} %copy-done.10, bf16[1216,256]{1,0:T(8,128)(2,1)S(1)} %copy-done.11), custom_call_target="tpu_custom_call" | custom-call | flops 6899999744 | tf_op jit(solution)/shard_map/pallas_call | solution.py:580
  117.8 1.4 collective-permute-done.31.refs_4_
  119.2 0.6 collective-permute-start.32
  119.8 0.7 collective-permute-start.26
  120.5 0.7 collective-permute-start.33
  121.2 5.7 %collective-permute-done.25.refs_1_ = bf16[256,512]{1,0:T(8,128)(2,1)S(1)} collective-permute-done((bf16[256,512]{1,0:T(8,128)(2,1)S(1)}, bf16[256,512]{1,0:T(8,128)(2,1)S(1)}, u32[]{:S(2)}, u32[]{:S(2)}) %collective-permute-start.25) | collective-permute-done | bytes 262176 | tf_op jit(solution)/shard_map/ppermute | solution.py:25
  126.9 0.7 collective-permute-start.36
  127.6 4.5 %collective-permute-done.32.refs_5_ = bf16[256,512]{1,0:T(8,128)(2,1)S(1)} collective-permute-done((bf16[256,512]{1,0:T(8,128)(2,1)S(1)}, bf16[256,512]{1,0:T(8,128)(2,1)S(1)}, u32[]{:S(2)}, u32[]{:S(2)}) %collective-permute-start.32) | collective-permute-done | bytes 262176 | tf_op jit(solution)/shard_map/ppermute | solution.py:25
  132.1 0.7 collective-permute-start.38
  132.7 1.3 collective-permute-start.27
  134.0 1.3 collective-permute-start.34
  135.4 1.3 collective-permute-start.37
  136.7 1.3 collective-permute-start.39
  138.0 6.2 %collective-permute-done.27.refs_3_ = bf16[256,512]{1,0:T(8,128)(2,1)S(1)} collective-permute-done((bf16[256,512]{1,0:T(8,128)(2,1)S(1)}, bf16[256,512]{1,0:T(8,128)(2,1)S(1)}, u32[]{:S(2)}, u32[]{:S(2)}) %collective-permute-start.27) | collective-permute-done | bytes 262176 | tf_op jit(solution)/shard_map/ppermute | solution.py:89
  144.1 5.6 %collective-permute-done.34.refs_7_ = bf16[256,512]{1,0:T(8,128)(2,1)S(1)} collective-permute-done((bf16[256,512]{1,0:T(8,128)(2,1)S(1)}, bf16[256,512]{1,0:T(8,128)(2,1)S(1)}, u32[]{:S(2)}, u32[]{:S(2)}) %collective-permute-start.34) | collective-permute-done | bytes 262176 | tf_op jit(solution)/shard_map/ppermute | solution.py:89
  149.7 1.2 copy-done.18
  150.9 3.3 %shard_map.146 = (f32[608,512]{1,0:T(8,128)S(1)}, bf16[608,512]{1,0:T(8,128)(2,1)S(1)}, bf16[192,608]{1,0:T(8,128)(2,1)S(1)}, f32[64,128]{1,0:T(8,128)S(1)}) custom-call(f32[8,640]{1,0:T(8,128)S(1)} %add.66.mod_ref, bf16[256,512]{1,0:T(8,128)(2,1)S(1)} %copy-done.6, bf16[256,512]{1,0:T(8,128)(2,1)S(1)} %collective-permute-done.25.refs_1_, ...), custom_call_target="tpu_custom_call" | custom-call | flops 5750000128 | tf_op jit(solution)/shard_map/pallas_call | solution.py:594
  154.3 1.1 collective-permute-done.37.refs_1_
  155.4 4.5 %collective-permute-done.39.refs_3_ = bf16[256,512]{1,0:T(8,128)(2,1)S(1)} collective-permute-done((bf16[256,512]{1,0:T(8,128)(2,1)S(1)}, bf16[256,512]{1,0:T(8,128)(2,1)S(1)}, u32[]{:S(2)}, u32[]{:S(2)}) %collective-permute-start.39) | collective-permute-done | bytes 262176 | tf_op jit(solution)/shard_map/ppermute | solution.py:90
  159.8 1.1 shard_map.147
  161.0 5.5 %collective-permute-done.40 = f32[72,640]{1,0:T(8,128)S(1)} collective-permute-done((f32[72,640]{1,0:T(8,128)S(1)}, f32[72,640]{1,0:T(8,128)S(1)}, u32[]{:S(2)}, u32[]{:S(2)}) %collective-permute-start.40) | collective-permute-done | bytes 184352 | tf_op jit(solution)/shard_map/ppermute | solution.py:25
  166.6 0.5 collective-permute-start.41
  167.1 0.6 dynamic_slice.4
  169.1 6.8 %collective-permute-done.41 = f32[72,640]{1,0:T(8,128)S(1)} collective-permute-done((f32[72,640]{1,0:T(8,128)S(1)}, f32[72,640]{1,0:T(8,128)S(1)}, u32[]{:S(2)}, u32[]{:S(2)}) %collective-permute-start.41) | collective-permute-done | bytes 184352 | tf_op jit(solution)/shard_map/ppermute | solution.py:25
  176.1 0.8 fusion.2
  (105 shorter events, 1.3 us)
Async XLA Ops:
  2.9 2.4 %copy-start = (bf16[304,7,608]{2,0,1:T(8,128)(2,1)S(1)}, bf16[304,7,608]{2,0,1:T(8,128)(2,1)}, u32[]{:S(2)}) copy-start(bf16[304,7,608]{2,0,1:T(8,128)(2,1)} %param.19) | copy-start | bytes 7762948
  2.9 2.4 %copy-start.8 = (f32[4,304]{1,0:T(4,128)S(1)}, f32[4,304]{1,0:T(4,128)}, u32[]{:S(2)}) copy-start(f32[4,304]{1,0:T(4,128)} %cond_ref.1) | copy-start | bytes 14596
  4.8 36.5 %copy-start.2 = (bf16[304,1280]{1,0:T(8,128)(2,1)}, bf16[304,1280]{1,0:T(8,128)(2,1)S(1)}, u32[]{:S(2)}) copy-start(bf16[304,1280]{1,0:T(8,128)(2,1)S(1)} %get-tuple-element.54.refs_12_) | copy-start | bytes 2334724
  4.8 11.1 %collective-permute-start = (bf16[304,1280]{1,0:T(8,128)(2,1)S(1)}, bf16[304,1280]{1,0:T(8,128)(2,1)S(1)}, u32[]{:S(2)}, u32[]{:S(2)}) collective-permute-start(bf16[304,1280]{1,0:T(8,128)(2,1)S(1)} %get-tuple-element.45), channel_id=1, source_target_pairs={{0,4},{4,0},{8,12},{12,8},{16,20},{20,16},{24,28},{28,24},{1,5},{5... | collective-permute-start | bytes 2334728 | tf_op jit(solution)/shard_map/ppermute | solution.py:25
  5.3 4.7 %copy-start.5 = (bf16[512,608]{0,1:T(8,128)(2,1)S(1)}, bf16[512,608]{0,1:T(8,128)(2,1)}, u32[]{:S(2)}) copy-start(bf16[512,608]{0,1:T(8,128)(2,1)} %param.13) | copy-start | bytes 1867780
  5.3 4.7 %copy-start.7 = (bf16[96,608]{1,0:T(8,128)(2,1)S(1)}, bf16[96,608]{1,0:T(8,128)(2,1)}, u32[]{:S(2)}) copy-start(bf16[96,608]{1,0:T(8,128)(2,1)} %txt_ref.3) | copy-start | bytes 350212
  5.8 6.4 %collective-permute-start.1 = (f32[8,640]{1,0:T(8,128)S(1)}, f32[8,640]{1,0:T(8,128)S(1)}, u32[]{:S(2)}, u32[]{:S(2)}) collective-permute-start(f32[8,640]{1,0:T(8,128)S(1)} %get-tuple-element.92), channel_id=1, source_target_pairs={{0,8},{4,12},{8,0},{12,4},{16,24},{20,28},{24,16},{28,20},{1,9},{5... | collective-permute-start | bytes 61448 | tf_op jit(solution)/shard_map/ppermute | solution.py:25
  8.4 6.4 %collective-permute-start.2 = (f32[8,640]{1,0:T(8,128)S(1)}, f32[8,640]{1,0:T(8,128)S(1)}, u32[]{:S(2)}, u32[]{:S(2)}) collective-permute-start(f32[8,640]{1,0:T(8,128)S(1)} %get-tuple-element.94), channel_id=1, source_target_pairs={{0,16},{4,20},{8,24},{12,28},{16,0},{20,4},{24,8},{28,12},{1,17},{... | collective-permute-start | bytes 61448 | tf_op jit(solution)/shard_map/ppermute | solution.py:25
  9.9 5.9 %collective-permute-start.3 = (f32[8,640]{1,0:T(8,128)S(1)}, f32[8,640]{1,0:T(8,128)S(1)}, u32[]{:S(2)}, u32[]{:S(2)}) collective-permute-start(f32[8,640]{1,0:T(8,128)S(1)} %get-tuple-element.93), channel_id=1, source_target_pairs={{0,24},{4,28},{8,16},{12,20},{16,8},{20,12},{24,0},{28,4},{1,25},{... | collective-permute-start | bytes 61448 | tf_op jit(solution)/shard_map/ppermute | solution.py:25
  10.2 5.8 %collective-permute-start.5 = (f32[8,640]{1,0:T(8,128)S(1)}, f32[8,640]{1,0:T(8,128)S(1)}, u32[]{:S(2)}, u32[]{:S(2)}) collective-permute-start(f32[8,640]{1,0:T(8,128)S(1)} %shard_map.142), channel_id=1, source_target_pairs={{0,1},{1,0},{2,3},{3,2},{4,5},{5,4},{6,7},{7,6},{8,9},{9,8},{10,11... | collective-permute-start | bytes 61448 | tf_op jit(solution)/shard_map/ppermute | solution.py:25
  12.3 4.8 %collective-permute-start.6 = (f32[8,640]{1,0:T(8,128)S(1)}, f32[8,640]{1,0:T(8,128)S(1)}, u32[]{:S(2)}, u32[]{:S(2)}) collective-permute-start(f32[8,640]{1,0:T(8,128)S(1)} %shard_map.142), channel_id=1, source_target_pairs={{0,2},{1,3},{2,0},{3,1},{4,6},{5,7},{6,4},{7,5},{8,10},{9,11},{10,... | collective-permute-start | bytes 61448 | tf_op jit(solution)/shard_map/ppermute | solution.py:25
  14.9 5.6 %collective-permute-start.7 = (f32[8,640]{1,0:T(8,128)S(1)}, f32[8,640]{1,0:T(8,128)S(1)}, u32[]{:S(2)}, u32[]{:S(2)}) collective-permute-start(f32[8,640]{1,0:T(8,128)S(1)} %shard_map.142), channel_id=1, source_target_pairs={{0,3},{1,2},{2,1},{3,0},{4,7},{5,6},{6,5},{7,4},{8,11},{9,10},{10,... | collective-permute-start | bytes 61448 | tf_op jit(solution)/shard_map/ppermute | solution.py:25
  15.8 26.0 %copy-start.19 = (bf16[304,1280]{1,0:T(8,128)(2,1)}, bf16[304,1280]{1,0:T(8,128)(2,1)S(1)}, u32[]{:S(2)}) copy-start(bf16[304,1280]{1,0:T(8,128)(2,1)S(1)} %collective-permute-done.refs_16_) | copy-start | bytes 2334724
  15.8 4.6 %collective-permute-start.4 = (f32[8,640]{1,0:T(8,128)S(1)}, f32[8,640]{1,0:T(8,128)S(1)}, u32[]{:S(2)}, u32[]{:S(2)}) collective-permute-start(f32[8,640]{1,0:T(8,128)S(1)} %fusion.6), channel_id=1, source_target_pairs={{0,4},{4,0},{8,12},{12,8},{16,20},{20,16},{24,28},{28,24},{1,5},{5... | collective-permute-start | bytes 61448 | tf_op jit(solution)/shard_map/ppermute | solution.py:25
  20.5 69.0 %copy-start.16 = (f32[2,64]{1,0:T(2,128)S(1)}, f32[2,64]{1,0:T(2,128)}, u32[]{:S(2)}) copy-start(f32[2,64]{1,0:T(2,128)} %param.23) | copy-start | bytes 1540
  20.5 69.0 %copy-start.17 = (f32[64]{0:T(128)S(1)}, f32[64]{0:T(128)}, u32[]{:S(2)}) copy-start(f32[64]{0:T(128)} %param.22) | copy-start | bytes 772
  20.5 69.6 %copy-start.15 = (bf16[304,64]{0,1:T(8,128)(2,1)S(1)}, bf16[304,64]{0,1:T(8,128)(2,1)}, u32[]{:S(2)}) copy-start(bf16[304,64]{0,1:T(8,128)(2,1)} %param.25) | copy-start | bytes 116740
  20.5 69.7 %copy-start.13 = (bf16[256,608]{0,1:T(8,128)(2,1)S(1)}, bf16[256,608]{0,1:T(8,128)(2,1)}, u32[]{:S(2)}) copy-start(bf16[256,608]{0,1:T(8,128)(2,1)} %param.24) | copy-start | bytes 933892
  21.3 72.6 %copy-start.3 = (bf16[608,608]{1,0:T(8,128)(2,1)}, bf16[608,608]{1,0:T(8,128)(2,1)S(1)}, u32[]{:S(2)}) copy-start(bf16[608,608]{1,0:T(8,128)(2,1)S(1)} %shard_map.143.refs_0_) | copy-start | bytes 2217988
  21.3 19.9 %collective-permute-start.10 = (bf16[304,1280]{1,0:T(8,128)(2,1)S(1)}, bf16[304,1280]{1,0:T(8,128)(2,1)S(1)}, u32[]{:S(2)}, u32[]{:S(2)}) collective-permute-start(bf16[304,1280]{1,0:T(8,128)(2,1)S(1)} %get-tuple-element.54.refs_12_), channel_id=1, source_target_pairs={{0,16},{4,20},{8,24},{12,28},{16,0},{20,4},{24,8},{28,12},{1,17},{... | collective-permute-start | bytes 2334728 | tf_op jit(solution)/shard_map/ppermute | solution.py:25
  22.9 18.3 %collective-permute-start.11 = (bf16[304,1280]{1,0:T(8,128)(2,1)S(1)}, bf16[304,1280]{1,0:T(8,128)(2,1)S(1)}, u32[]{:S(2)}, u32[]{:S(2)}) collective-permute-start(bf16[304,1280]{1,0:T(8,128)(2,1)S(1)} %collective-permute-done.refs_16_), channel_id=1, source_target_pairs={{0,8},{4,12},{8,0},{12,4},{16,24},{20,28},{24,16},{28,20},{1,9},{5... | collective-permute-start | bytes 2334728 | tf_op jit(solution)/shard_map/ppermute | solution.py:25
  24.4 16.8 %collective-permute-start.8 = (bf16[608,608]{1,0:T(8,128)(2,1)S(1)}, bf16[608,608]{1,0:T(8,128)(2,1)}, u32[]{:S(2)}, u32[]{:S(2)}) collective-permute-start(bf16[608,608]{1,0:T(8,128)(2,1)S(1)} %shard_map.143.refs_0_), channel_id=1, source_target_pairs={{0,1},{1,0},{2,3},{3,2},{4,5},{5,4},{6,7},{7,6},{8,9},{9,8},{10,11... | collective-permute-start | bytes 2217992 | tf_op jit(solution)/shard_map/ppermute | solution.py:25
  24.4 16.8 %collective-permute-start.9 = (bf16[608,608]{1,0:T(8,128)(2,1)S(1)}, bf16[608,608]{1,0:T(8,128)(2,1)}, u32[]{:S(2)}, u32[]{:S(2)}) collective-permute-start(bf16[608,608]{1,0:T(8,128)(2,1)S(1)} %shard_map.143.refs_0_), channel_id=1, source_target_pairs={{1,2},{2,1},{5,6},{6,5},{9,10},{10,9},{13,14},{14,13},{17,18},{18,... | collective-permute-start | bytes 2217992 | tf_op jit(solution)/shard_map/ppermute | solution.py:94
  41.2 47.4 %copy-start.20 = (bf16[304,1280]{1,0:T(8,128)(2,1)}, bf16[304,1280]{1,0:T(8,128)(2,1)S(1)}, u32[]{:S(2)}) copy-start(bf16[304,1280]{1,0:T(8,128)(2,1)S(1)} %collective-permute-done.10.refs_14_) | copy-start | bytes 2334724
  41.2 47.4 %copy-start.21 = (bf16[304,1280]{1,0:T(8,128)(2,1)}, bf16[304,1280]{1,0:T(8,128)(2,1)S(1)}, u32[]{:S(2)}) copy-start(bf16[304,1280]{1,0:T(8,128)(2,1)S(1)} %collective-permute-done.11.refs_17_) | copy-start | bytes 2334724
  41.2 19.5 %collective-permute-start.14 = (bf16[304,1280]{1,0:T(8,128)(2,1)S(1)}, bf16[304,1280]{1,0:T(8,128)(2,1)S(1)}, u32[]{:S(2)}, u32[]{:S(2)}) collective-permute-start(bf16[304,1280]{1,0:T(8,128)(2,1)S(1)} %get-tuple-element.54.refs_12_), channel_id=1, source_target_pairs={{0,8},{4,12},{8,0},{12,4},{16,24},{20,28},{24,16},{28,20},{1,9},{5... | collective-permute-start | bytes 2334728 | tf_op jit(solution)/shard_map/ppermute | solution.py:25
  41.8 18.9 %collective-permute-start.15 = (bf16[304,1280]{1,0:T(8,128)(2,1)S(1)}, bf16[304,1280]{1,0:T(8,128)(2,1)S(1)}, u32[]{:S(2)}, u32[]{:S(2)}) collective-permute-start(bf16[304,1280]{1,0:T(8,128)(2,1)S(1)} %collective-permute-done.refs_16_), channel_id=1, source_target_pairs={{0,16},{4,20},{8,24},{12,28},{16,0},{20,4},{24,8},{28,12},{1,17},{... | collective-permute-start | bytes 2334728 | tf_op jit(solution)/shard_map/ppermute | solution.py:25
  42.3 18.4 %collective-permute-start.12 = (bf16[608,608]{1,0:T(8,128)(2,1)}, bf16[608,608]{1,0:T(8,128)(2,1)}, u32[]{:S(2)}, u32[]{:S(2)}) collective-permute-start(bf16[608,608]{1,0:T(8,128)(2,1)} %collective-permute-done.9.refs_2_), channel_id=1, source_target_pairs={{1,0},{2,3},{5,4},{6,7},{9,8},{10,11},{13,12},{14,15},{17,16},{18,... | collective-permute-start | bytes 2217992 | tf_op jit(solution)/shard_map/ppermute | solution.py:94
  43.6 17.1 %collective-permute-start.13 = (bf16[608,608]{1,0:T(8,128)(2,1)}, bf16[608,608]{1,0:T(8,128)(2,1)}, u32[]{:S(2)}, u32[]{:S(2)}) collective-permute-start(bf16[608,608]{1,0:T(8,128)(2,1)} %collective-permute-done.8.refs_1_), channel_id=1, source_target_pairs={{1,2},{2,1},{5,6},{6,5},{9,10},{10,9},{13,14},{14,13},{17,18},{18,... | collective-permute-start | bytes 2217992 | tf_op jit(solution)/shard_map/ppermute | solution.py:94
  60.8 27.9 %copy-start.22 = (bf16[304,1280]{1,0:T(8,128)(2,1)}, bf16[304,1280]{1,0:T(8,128)(2,1)S(1)}, u32[]{:S(2)}) copy-start(bf16[304,1280]{1,0:T(8,128)(2,1)S(1)} %collective-permute-done.14.refs_13_) | copy-start | bytes 2334724
  60.8 27.8 %copy-start.23 = (bf16[304,1280]{1,0:T(8,128)(2,1)}, bf16[304,1280]{1,0:T(8,128)(2,1)S(1)}, u32[]{:S(2)}) copy-start(bf16[304,1280]{1,0:T(8,128)(2,1)S(1)} %collective-permute-done.15.refs_18_) | copy-start | bytes 2334724
  60.8 27.2 %collective-permute-start.23 = (bf16[304,1280]{1,0:T(8,128)(2,1)S(1)}, bf16[304,1280]{1,0:T(8,128)(2,1)S(1)}, u32[]{:S(2)}, u32[]{:S(2)}) collective-permute-start(bf16[304,1280]{1,0:T(8,128)(2,1)S(1)} %collective-permute-done.10.refs_14_), channel_id=1, source_target_pairs={{0,8},{4,12},{8,0},{12,4},{16,24},{20,28},{24,16},{28,20},{1,9},{5... | collective-permute-start | bytes 2334728 | tf_op jit(solution)/shard_map/ppermute | solution.py:25
  62.4 26.2 %collective-permute-start.24 = (bf16[304,1280]{1,0:T(8,128)(2,1)S(1)}, bf16[304,1280]{1,0:T(8,128)(2,1)S(1)}, u32[]{:S(2)}, u32[]{:S(2)}) collective-permute-start(bf16[304,1280]{1,0:T(8,128)(2,1)S(1)} %collective-permute-done.11.refs_17_), channel_id=1, source_target_pairs={{0,16},{4,20},{8,24},{12,28},{16,0},{20,4},{24,8},{28,12},{1,17},{... | collective-permute-start | bytes 2334728 | tf_op jit(solution)/shard_map/ppermute | solution.py:25
  63.9 2.3 %collective-permute-start.16 = (bf16[608,608]{1,0:T(8,128)(2,1)S(1)}, bf16[608,608]{1,0:T(8,128)(2,1)S(1)}, u32[]{:S(2)}, u32[]{:S(2)}) collective-permute-start(bf16[608,608]{1,0:T(8,128)(2,1)S(1)} %shard_map.143.refs_0_), channel_id=1, source_target_pairs={{0,4},{4,0},{8,12},{12,8},{16,20},{20,16},{24,28},{28,24},{1,5},{5... | collective-permute-start | bytes 2217992 | tf_op jit(solution)/shard_map/ppermute | solution.py:25
  63.9 24.1 %collective-permute-start.17 = (bf16[608,608]{1,0:T(8,128)(2,1)}, bf16[608,608]{1,0:T(8,128)(2,1)}, u32[]{:S(2)}, u32[]{:S(2)}) collective-permute-start(bf16[608,608]{1,0:T(8,128)(2,1)} %collective-permute-done.13.refs_4_), channel_id=1, source_target_pairs={{1,0},{2,3},{5,4},{6,7},{9,8},{10,11},{13,12},{14,15},{17,16},{18,... | collective-permute-start | bytes 2217992 | tf_op jit(solution)/shard_map/ppermute | solution.py:94
  66.2 22.5 %copy-start.26 = (bf16[608,608]{1,0:T(8,128)(2,1)}, bf16[608,608]{1,0:T(8,128)(2,1)S(1)}, u32[]{:S(2)}) copy-start(bf16[608,608]{1,0:T(8,128)(2,1)S(1)} %collective-permute-done.16.refs_6_) | copy-start | bytes 2217988
  66.2 24.1 %collective-permute-start.18 = (bf16[608,608]{1,0:T(8,128)(2,1)}, bf16[608,608]{1,0:T(8,128)(2,1)}, u32[]{:S(2)}, u32[]{:S(2)}) collective-permute-start(bf16[608,608]{1,0:T(8,128)(2,1)} %collective-permute-done.8.refs_1_), channel_id=1, source_target_pairs={{0,4},{4,0},{8,12},{12,8},{16,20},{20,16},{24,28},{28,24},{1,5},{5... | collective-permute-start | bytes 2217992 | tf_op jit(solution)/shard_map/ppermute | solution.py:25
  66.3 24.6 %collective-permute-start.19 = (bf16[608,608]{1,0:T(8,128)(2,1)}, bf16[608,608]{1,0:T(8,128)(2,1)}, u32[]{:S(2)}, u32[]{:S(2)}) collective-permute-start(bf16[608,608]{1,0:T(8,128)(2,1)} %collective-permute-done.9.refs_2_), channel_id=1, source_target_pairs={{0,4},{4,0},{8,12},{12,8},{16,20},{20,16},{24,28},{28,24},{1,5},{5... | collective-permute-start | bytes 2217992 | tf_op jit(solution)/shard_map/ppermute | solution.py:25
  88.0 3.4 %collective-permute-start.20 = (bf16[608,608]{1,0:T(8,128)(2,1)}, bf16[608,608]{1,0:T(8,128)(2,1)}, u32[]{:S(2)}, u32[]{:S(2)}) collective-permute-start(bf16[608,608]{1,0:T(8,128)(2,1)} %collective-permute-done.12.refs_3_), channel_id=1, source_target_pairs={{0,4},{4,0},{8,12},{12,8},{16,20},{20,16},{24,28},{28,24},{1,5},{5... | collective-permute-start | bytes 2217992 | tf_op jit(solution)/shard_map/ppermute | solution.py:25
  88.0 5.8 %copy-start.24 = (bf16[304,1280]{1,0:T(8,128)(2,1)}, bf16[304,1280]{1,0:T(8,128)(2,1)S(1)}, u32[]{:S(2)}) copy-start(bf16[304,1280]{1,0:T(8,128)(2,1)S(1)} %collective-permute-done.23.refs_15_) | copy-start | bytes 2334724
  88.0 5.8 %collective-permute-start.21 = (bf16[608,608]{1,0:T(8,128)(2,1)}, bf16[608,608]{1,0:T(8,128)(2,1)}, u32[]{:S(2)}, u32[]{:S(2)}) collective-permute-start(bf16[608,608]{1,0:T(8,128)(2,1)} %collective-permute-done.13.refs_4_), channel_id=1, source_target_pairs={{0,4},{4,0},{8,12},{12,8},{16,20},{20,16},{24,28},{28,24},{1,5},{5... | collective-permute-start | bytes 2217992 | tf_op jit(solution)/shard_map/ppermute | solution.py:25
  88.5 5.3 %collective-permute-start.22 = (bf16[608,608]{1,0:T(8,128)(2,1)}, bf16[608,608]{1,0:T(8,128)(2,1)}, u32[]{:S(2)}, u32[]{:S(2)}) collective-permute-start(bf16[608,608]{1,0:T(8,128)(2,1)} %collective-permute-done.17.refs_5_), channel_id=1, source_target_pairs={{0,4},{4,0},{8,12},{12,8},{16,20},{20,16},{24,28},{28,24},{1,5},{5... | collective-permute-start | bytes 2217992 | tf_op jit(solution)/shard_map/ppermute | solution.py:25
  90.3 20.9 %collective-permute-start.28 = (bf16[736,256]{1,0:T(8,128)(2,1)S(1)}, bf16[736,256]{1,0:T(8,128)(2,1)S(1)}, u32[]{:S(2)}, u32[]{:S(2)}) collective-permute-start(bf16[736,256]{1,0:T(8,128)(2,1)S(1)} %pad_maximum_fusion), channel_id=1, source_target_pairs={{0,8},{4,12},{8,0},{12,4},{16,24},{20,28},{24,16},{28,20},{1,9},{5... | collective-permute-start | bytes 1130504 | tf_op jit(solution)/shard_map/ppermute | solution.py:25
  90.9 20.3 %collective-permute-start.29 = (bf16[736,256]{1,0:T(8,128)(2,1)S(1)}, bf16[736,256]{1,0:T(8,128)(2,1)S(1)}, u32[]{:S(2)}, u32[]{:S(2)}) collective-permute-start(bf16[736,256]{1,0:T(8,128)(2,1)S(1)} %pad_maximum_fusion), channel_id=1, source_target_pairs={{0,16},{4,20},{8,24},{12,28},{16,0},{20,4},{24,8},{28,12},{1,17},{... | collective-permute-start | bytes 1130504 | tf_op jit(solution)/shard_map/ppermute | solution.py:25
  91.4 19.8 %collective-permute-start.30 = (bf16[736,256]{1,0:T(8,128)(2,1)S(1)}, bf16[736,256]{1,0:T(8,128)(2,1)S(1)}, u32[]{:S(2)}, u32[]{:S(2)}) collective-permute-start(bf16[736,256]{1,0:T(8,128)(2,1)S(1)} %pad_maximum_fusion), channel_id=1, source_target_pairs={{0,24},{4,28},{8,16},{12,20},{16,8},{20,12},{24,0},{28,4},{1,25},{... | collective-permute-start | bytes 1130504 | tf_op jit(solution)/shard_map/ppermute | solution.py:25
  111.2 1.3 copy-start.11
  111.2 1.3 copy-start.12
  111.3 6.4 %copy-start.6 = (bf16[256,512]{1,0:T(8,128)(2,1)S(1)}, bf16[256,512]{1,0:T(8,128)(2,1)}, u32[]{:S(2)}) copy-start(bf16[256,512]{1,0:T(8,128)(2,1)} %get-tuple-element.72.refs_0_) | copy-start | bytes 786436
  111.3 38.4 %collective-permute-start.35 = (bf16[2944,256]{1,0:T(8,128)(2,1)S(1)}, bf16[2944,256]{1,0:T(8,128)(2,1)S(1)}, u32[]{:S(2)}, u32[]{:S(2)}) collective-permute-start(bf16[2944,256]{1,0:T(8,128)(2,1)S(1)} %constant_dynamic-update-slice_fusion.refs_8_), channel_id=1, source_target_pairs={{0,4},{4,0},{8,12},{12,8},{16,20},{20,16},{24,28},{28,24},{1,5},{5... | collective-permute-start | bytes 4521992 | tf_op jit(solution)/shard_map/ppermute | solution.py:25
  117.6 1.6 collective-permute-start.31
  117.7 9.2 %collective-permute-start.25 = (bf16[256,512]{1,0:T(8,128)(2,1)S(1)}, bf16[256,512]{1,0:T(8,128)(2,1)S(1)}, u32[]{:S(2)}, u32[]{:S(2)}) collective-permute-start(bf16[256,512]{1,0:T(8,128)(2,1)S(1)} %copy-done.6), channel_id=1, source_target_pairs={{0,1},{1,0},{2,3},{3,2},{4,5},{5,4},{6,7},{7,6},{8,9},{9,8},{10,11... | collective-permute-start | bytes 786440 | tf_op jit(solution)/shard_map/ppermute | solution.py:25
  119.2 12.8 %collective-permute-start.32 = (bf16[256,512]{1,0:T(8,128)(2,1)S(1)}, bf16[256,512]{1,0:T(8,128)(2,1)S(1)}, u32[]{:S(2)}, u32[]{:S(2)}) collective-permute-start(bf16[256,512]{1,0:T(8,128)(2,1)S(1)} %collective-permute-done.31.refs_4_), channel_id=1, source_target_pairs={{0,1},{1,0},{2,3},{3,2},{4,5},{5,4},{6,7},{7,6},{8,9},{9,8},{10,11... | collective-permute-start | bytes 786440 | tf_op jit(solution)/shard_map/ppermute | solution.py:25
  119.8 12.9 %collective-permute-start.26 = (bf16[256,512]{1,0:T(8,128)(2,1)S(1)}, bf16[256,512]{1,0:T(8,128)(2,1)S(1)}, u32[]{:S(2)}, u32[]{:S(2)}) collective-permute-start(bf16[256,512]{1,0:T(8,128)(2,1)S(1)} %copy-done.6), channel_id=1, source_target_pairs={{1,2},{2,1},{5,6},{6,5},{9,10},{10,9},{13,14},{14,13},{17,18},{18,... | collective-permute-start | bytes 786440 | tf_op jit(solution)/shard_map/ppermute | solution.py:87
  120.5 13.6 %collective-permute-start.33 = (bf16[256,512]{1,0:T(8,128)(2,1)S(1)}, bf16[256,512]{1,0:T(8,128)(2,1)S(1)}, u32[]{:S(2)}, u32[]{:S(2)}) collective-permute-start(bf16[256,512]{1,0:T(8,128)(2,1)S(1)} %collective-permute-done.31.refs_4_), channel_id=1, source_target_pairs={{1,2},{2,1},{5,6},{6,5},{9,10},{10,9},{13,14},{14,13},{17,18},{18,... | collective-permute-start | bytes 786440 | tf_op jit(solution)/shard_map/ppermute | solution.py:87
  126.9 8.5 %collective-permute-start.36 = (bf16[256,512]{1,0:T(8,128)(2,1)S(1)}, bf16[256,512]{1,0:T(8,128)(2,1)S(1)}, u32[]{:S(2)}, u32[]{:S(2)}) collective-permute-start(bf16[256,512]{1,0:T(8,128)(2,1)S(1)} %collective-permute-done.25.refs_1_), channel_id=1, source_target_pairs={{1,2},{2,1},{5,6},{6,5},{9,10},{10,9},{13,14},{14,13},{17,18},{18,... | collective-permute-start | bytes 786440 | tf_op jit(solution)/shard_map/ppermute | solution.py:88
  132.1 4.6 %collective-permute-start.38 = (bf16[256,512]{1,0:T(8,128)(2,1)S(1)}, bf16[256,512]{1,0:T(8,128)(2,1)S(1)}, u32[]{:S(2)}, u32[]{:S(2)}) collective-permute-start(bf16[256,512]{1,0:T(8,128)(2,1)S(1)} %collective-permute-done.32.refs_5_), channel_id=1, source_target_pairs={{1,2},{2,1},{5,6},{6,5},{9,10},{10,9},{13,14},{14,13},{17,18},{18,... | collective-permute-start | bytes 786440 | tf_op jit(solution)/shard_map/ppermute | solution.py:88
  132.7 11.4 %collective-permute-start.27 = (bf16[256,512]{1,0:T(8,128)(2,1)S(1)}, bf16[256,512]{1,0:T(8,128)(2,1)S(1)}, u32[]{:S(2)}, u32[]{:S(2)}) collective-permute-start(bf16[256,512]{1,0:T(8,128)(2,1)S(1)} %collective-permute-done.26.refs_2_), channel_id=1, source_target_pairs={{1,0},{2,3},{5,4},{6,7},{9,8},{10,11},{13,12},{14,15},{17,16},{18,... | collective-permute-start | bytes 786440 | tf_op jit(solution)/shard_map/ppermute | solution.py:89
  134.0 15.7 %collective-permute-start.34 = (bf16[256,512]{1,0:T(8,128)(2,1)S(1)}, bf16[256,512]{1,0:T(8,128)(2,1)S(1)}, u32[]{:S(2)}, u32[]{:S(2)}) collective-permute-start(bf16[256,512]{1,0:T(8,128)(2,1)S(1)} %collective-permute-done.33.refs_6_), channel_id=1, source_target_pairs={{1,0},{2,3},{5,4},{6,7},{9,8},{10,11},{13,12},{14,15},{17,16},{18,... | collective-permute-start | bytes 786440 | tf_op jit(solution)/shard_map/ppermute | solution.py:89
  135.4 20.0 %collective-permute-start.37 = (bf16[256,512]{1,0:T(8,128)(2,1)S(1)}, bf16[256,512]{1,0:T(8,128)(2,1)S(1)}, u32[]{:S(2)}, u32[]{:S(2)}) collective-permute-start(bf16[256,512]{1,0:T(8,128)(2,1)S(1)} %collective-permute-done.36.refs_0_), channel_id=1, source_target_pairs={{1,0},{2,3},{5,4},{6,7},{9,8},{10,11},{13,12},{14,15},{17,16},{18,... | collective-permute-start | bytes 786440 | tf_op jit(solution)/shard_map/ppermute | solution.py:90
  136.7 23.2 %collective-permute-start.39 = (bf16[256,512]{1,0:T(8,128)(2,1)S(1)}, bf16[256,512]{1,0:T(8,128)(2,1)S(1)}, u32[]{:S(2)}, u32[]{:S(2)}) collective-permute-start(bf16[256,512]{1,0:T(8,128)(2,1)S(1)} %collective-permute-done.38.refs_2_), channel_id=1, source_target_pairs={{1,0},{2,3},{5,4},{6,7},{9,8},{10,11},{13,12},{14,15},{17,16},{18,... | collective-permute-start | bytes 786440 | tf_op jit(solution)/shard_map/ppermute | solution.py:90
  159.8 7.2 %copy-start.27 = (s32[4]{0:T(128)S(1)}, s32[4]{0:T(128)}, u32[]{:S(2)}) copy-start(s32[4]{0:T(128)} %param.16) | copy-start | bytes 52
  159.8 16.3 %copy-start.14 = (f32[512,64]{0,1:T(8,128)S(1)}, f32[512,64]{0,1:T(8,128)}, u32[]{:S(2)}) copy-start(f32[512,64]{0,1:T(8,128)} %param.17) | copy-start | bytes 393220
  161.0 5.6 %collective-permute-start.40 = (f32[72,640]{1,0:T(8,128)S(1)}, f32[72,640]{1,0:T(8,128)S(1)}, u32[]{:S(2)}, u32[]{:S(2)}) collective-permute-start(f32[72,640]{1,0:T(8,128)S(1)} %shard_map.147), channel_id=1, source_target_pairs={{0,1},{1,0},{2,3},{3,2},{4,5},{5,4},{6,7},{7,6},{8,9},{9,8},{10,11... | collective-permute-start | bytes 552968 | tf_op jit(solution)/shard_map/ppermute | solution.py:25
  166.6 9.3 %collective-permute-start.41 = (f32[72,640]{1,0:T(8,128)S(1)}, f32[72,640]{1,0:T(8,128)S(1)}, u32[]{:S(2)}, u32[]{:S(2)}) collective-permute-start(f32[72,640]{1,0:T(8,128)S(1)} %add.70), channel_id=1, source_target_pairs={{0,2},{1,3},{2,0},{3,1},{4,6},{5,7},{6,4},{7,5},{8,10},{9,11},{10,... | collective-permute-start | bytes 552968 | tf_op jit(solution)/shard_map/ppermute | solution.py:25
  (6 other events, 6.1 us)

commit v6 on v5

--- a/solution.py
+++ b/solution.py
@@ -10,8 +10,8 @@
 STEPS = 28
 EPS_NORM = 1e-06
 ATTEND = 6
+ATTEND_MIB = 56
 PROJECT = 20
-AHEAD = 2
 EARLY = 48
 F32 = jnp.float32
 BF16 = jnp.bfloat16
@@ -82,12 +82,20 @@
 OUTWARD = [(1, 0), (2, 3)]
 
 
-def line_four(block, axis):
-    pair = swap(block, axis, 1)
-    near = lax.ppermute(block, axis, MIDDLE)
-    far = lax.ppermute(pair, axis, MIDDLE)
-    near_end = lax.ppermute(near, axis, OUTWARD)
-    return [block, pair, near, near_end, far, lax.ppermute(far, axis, OUTWARD)]
+def gather_heads(keep, give, others):
+    send = lambda held, route: lax.ppermute(held, "col", route)
+    pair, near = swap(keep, "col", 1), send(keep, MIDDLE)
+    pair, near, give = tie(pair, near, give)
+    near_end, far = send(near, OUTWARD), send(pair, MIDDLE)
+    take = swap(give, "row", 1)
+    take_pair, take_near = swap(take, "col", 1), send(take, MIDDLE)
+    near_end, far, take_pair, take_near = tie(near_end, far, take_pair, take_near)
+    far_end = send(far, OUTWARD)
+    take_end, take_far = send(take_near, OUTWARD), send(take_pair, MIDDLE)
+    far_end, take_end, take_far, *others = tie(far_end, take_end, take_far, *others)
+    first = [keep, pair, near, near_end, far, far_end]
+    second = [take, take_pair, take_near, take_end, take_far, send(take_far, OUTWARD)]
+    return [first, second], others
 
 
 def gather_both(tokens, weights):
@@ -95,22 +103,23 @@
     first, second = weights
     pair, near = swap(tokens, "col", 1), send(tokens, MIDDLE)
     first_y, second_x = swap(first, "row", 4), swap(second, "row", 2)
+    other = lambda held: swap(held, "row", 1)
+    peer = other(tokens)
     pair, near, first_y, second_x, first, second = tie(
         pair, near, first_y, second_x, first, second
     )
     near_end, far = send(near, OUTWARD), send(pair, MIDDLE)
     first_x, second_y = swap(first, "row", 2), swap(second, "row", 4)
-    near_end, far, first_x, second_y, first_y, second_x, tokens, pair, near = tie(
-        near_end, far, first_x, second_y, first_y, second_x, tokens, pair, near
+    near_end, far, first_x, second_y, first_y, second_x, pair, near, peer = tie(
+        near_end, far, first_x, second_y, first_y, second_x, pair, near, peer
     )
     far_end = send(far, OUTWARD)
-    other = lambda held: swap(held, "row", 1)
-    peer = other(tokens)
-    peer, pair, near, near_end, far = tie(peer, pair, near, near_end, far)
+    first_d, second_d = swap(first_y, "row", 2), swap(second_x, "row", 4)
+    far_end, first_d, second_d = tie(far_end, first_d, second_d)
     peers = [peer, other(pair), other(near), other(near_end), other(far), other(far_end)]
     held = [
-        {0: first, 4: first_y, 2: first_x, 6: swap(first_y, "row", 2)},
-        {0: second, 2: second_x, 4: second_y, 6: swap(second_x, "row", 4)},
+        {0: first, 4: first_y, 2: first_x, 6: first_d},
+        {0: second, 2: second_x, 4: second_y, 6: second_d},
     ]
     return [tokens, pair, near, near_end, far, far_end], peers, held
 
@@ -209,6 +218,8 @@
     inverse = lax.rsqrt(stats[1:2] - average * average + EPS_NORM)
     columns = jnp.where(row == 0, average, inverse).T
     chunk = 128
+    if out_ref.shape[1] > width:
+        out_ref[:, width:] = jnp.zeros((img + txt, out_ref.shape[1] - width), BF16)
     for low in range(0, img + txt, chunk):
         for start in range(0, width, chunk):
             stop = min(start + chunk, width)
@@ -275,52 +286,52 @@
     attend(img, txt, head, length_ref, *[part[...] for part in parts], out_ref)
 
 
-def project_kernel(routes, masks, img, head, length_ref, gain_ref, *refs):
+def project_kernel(routes, masks, img, head, length_ref, q_gain_ref, k_gain_ref, *refs):
     lines = refs[: len(routes)], refs[len(routes) : 2 * len(routes)]
     refs = refs[2 * len(routes) :]
     n_blocks = 2 * len(masks) if masks else 1
     blocks, refs = refs[:n_blocks], refs[n_blocks:]
-    outs, (x_ref, w_ref, img_ref, txt_ref, sems_x, sems_w) = refs[:-6], refs[-6:]
-    tokens = lines[0][0].shape[0]
+    outs, refs = refs[:4], refs[4:]
+    x_ref, w_ref, img_ref, txt_ref, q_ref, k_ref, v_ref, sems_x, sems_w, sems_o = refs
+    tokens, wide = lines[0][0].shape
     txt = tokens - img
-    count, _, width = x_ref.shape
+    count = x_ref.shape[1] // wide
     half = img_ref.shape[1] // 3
     place, col = lax.axis_index("row"), lax.axis_index("col")
     chip, core = place // 2, lax.rem(place, 2)
 
-    def copy_lines(act):
-        for n, line in enumerate(lines):
-            for k, (low, high, to) in enumerate(
-                ((0, img, n * img), (img, tokens, 2 * img + n * txt))
-            ):
-                parts = [ref.at[pl.ds(low, high - low)] for ref in line]
-                target = lambda owner: x_ref.at[owner, pl.ds(to, high - low)]
-                line_copies(parts, routes, col, target, sems_x.at[n, k], act)
-
-    copy_lines("start")
-    stages = []
+    def copy_line(n, act):
+        for k, (low, high, to) in enumerate(
+            ((0, img, n * img), (img, tokens, 2 * img + n * txt))
+        ):
+            parts = [ref.at[pl.ds(low, high - low)] for ref in lines[n]]
+            target = lambda owner: x_ref.at[
+                pl.ds(to, high - low), pl.ds(pl.multiple_of(owner * wide, 128), wide)
+            ]
+            line_copies(parts, routes, col, target, sems_x.at[n, k], act)
+
+    copy_line(0, "start")
+    stages = [[], []]
+    if not masks:
+        width = blocks[0].shape[1]
+        for k in range(count):
+            target = w_ref.at[pl.ds(k * wide, width)]
+            stages[0].append(pltpu.make_async_copy(blocks[0].at[k], target, sems_w.at[0, k]))
+    else:
+        depth = blocks[0].shape[0]
+        width = 2 * depth
+        for k in range(count):
+            for piece in range(2):
+                row = jnp.bitwise_xor(chip, k) * wide + jnp.where(core == piece, 0, depth)
+                target = w_ref.at[pl.ds(pl.multiple_of(row, 16), depth)]
+                ref = blocks[piece * len(masks) + k]
+                copy = pltpu.make_async_copy(ref, target, sems_w.at[piece, k])
+                stages[2 * k // count].append(copy)
+    for copy in stages[0]:
+        copy.start()
     for k in range(count):
-        copies = []
-        if not masks:
-            if k == 0:
-                copies.append(pltpu.make_async_copy(blocks[0], w_ref, sems_w.at[0, 0]))
-        else:
-            depth = blocks[0].shape[0]
-            for piece in range(2):
-                row = jnp.where(core == piece, 0, depth)
-                target = w_ref.at[
-                    jnp.bitwise_xor(chip, k), pl.ds(pl.multiple_of(row, 16), depth)
-                ]
-                ref = blocks[piece * len(masks) + k]
-                copies.append(pltpu.make_async_copy(ref, target, sems_w.at[piece, k]))
-        stages.append(copies)
-
-    def start(n):
-        for copy in stages[n] if n < count else ():
-            copy.start()
-
-    for n in range(AHEAD):
-        start(n)
+        if wide > width:
+            w_ref[k * wide + width : (k + 1) * wide] = jnp.zeros((wide - width, 5 * half), BF16)
     row = lax.broadcasted_iota(jnp.int32, (half, half), 0) // head
     column = lax.broadcasted_iota(jnp.int32, (half, half), 1) // head
     mean_of = jnp.where(row == column, 1.0 / head, 0.0).astype(BF16)
@@ -328,44 +339,50 @@
     def head_norm(values, gain):
         square = values * values
         mean_square = jnp.zeros_like(square)
-        for _ in range(3):
+        for _ in range(2):
             term = square.astype(BF16)
             mean_square += jnp.dot(term, mean_of, preferred_element_type=F32)
             square = square - term.astype(F32)
         return (values * lax.rsqrt(mean_square + EPS_NORM) * gain).astype(BF16)
 
-    copy_lines("wait")
-    for k in range(count):
+    copy_line(0, "wait")
+    depth = count // 2 * wide
+    for k in range(2):
         for copy in stages[k]:
             copy.wait()
-        start(k + AHEAD)
-        here = jnp.bitwise_xor(chip, k)
-        for ref, low, high, first, parts in (
-            (img_ref, 0, 2 * img, 0, 3),
-            (txt_ref, 2 * img, 2 * tokens, 3, 2),
-        ):
-            term = jnp.dot(
-                x_ref[here, low:high],
-                w_ref[here, :, first * half : (first + parts) * half],
-                preferred_element_type=F32,
-            )
-            ref[...] = term if k == 0 else ref[...] + term
+        if k == 0:
+            for copy in stages[1]:
+                copy.start()
+        else:
+            copy_line(1, "start")
+        if not masks:
+            here = pl.ds(k * depth, depth)
+        else:
+            here = pl.ds(pl.multiple_of(jnp.bitwise_xor(2 * chip // count, k) * depth, 128), depth)
+        term = jnp.dot(x_ref[:img, here], w_ref[here, : 3 * half], preferred_element_type=F32)
+        img_ref[:img] = term if k == 0 else img_ref[:img] + term
+    copy_line(1, "wait")
+    img_ref[img:] = jnp.dot(
+        x_ref[img : 2 * img], w_ref[:, : 3 * half], preferred_element_type=F32
+    )
+    txt_ref[...] = jnp.dot(x_ref[2 * img :], w_ref[:, 3 * half :], preferred_element_type=F32)
     scaling = head ** (-0.5)
-    queries = head_norm(img_ref[:, :half], gain_ref[0:1])
-    queries = (queries.astype(F32) * scaling).astype(BF16)
-    keys = jnp.concatenate(
-        [
-            head_norm(img_ref[:, half : 2 * half], gain_ref[1:2]),
-            head_norm(txt_ref[:, :half], gain_ref[2:3]),
-        ],
-        axis=0,
-    )
-    values = jnp.concatenate(
-        [img_ref[:, 2 * half :].astype(BF16), txt_ref[:, half:].astype(BF16)], axis=0
-    )
-    for ref, part in zip(outs[1:], (queries[img:], keys, values)):
-        ref[...] = part
-    attend(img, txt, head, length_ref, queries[:img], keys, values, outs[0])
+    wide_gain = lambda gain: jnp.concatenate([gain] * (half // head), axis=1)
+    queries = head_norm(img_ref[:, :half], wide_gain(q_gain_ref[...]))
+    q_ref[...] = (queries.astype(F32) * scaling).astype(BF16)
+    k_ref[: 2 * img] = head_norm(img_ref[:, half : 2 * half], wide_gain(k_gain_ref[0:1]))
+    k_ref[2 * img :] = head_norm(txt_ref[:, :half], wide_gain(k_gain_ref[1:2]))
+    v_ref[: 2 * img] = img_ref[:, 2 * half :].astype(BF16)
+    v_ref[2 * img :] = txt_ref[:, half:].astype(BF16)
+    copies = [
+        pltpu.make_async_copy(part, ref, sems_o.at[n])
+        for n, (part, ref) in enumerate(zip((q_ref.at[pl.ds(img, img)], k_ref, v_ref), outs[1:]))
+    ]
+    for copy in copies:
+        copy.start()
+    attend(img, txt, head, length_ref, q_ref[:img], k_ref[...], v_ref[...], outs[0])
+    for copy in copies:
+        copy.wait()
 
 
 def place_heads(lines, routes, col, target, sems):
@@ -416,8 +433,8 @@
 
     patch = gain_ref.shape[0] // 3
     slab = width // per_col
-    gains = jnp.zeros((patch, 1), F32)
-    shifts = jnp.zeros((patch, 1), F32)
+    consts = jnp.zeros((8, patch), F32)
+    row = lax.broadcasted_iota(jnp.int32, (8, patch), 0)
     for n in range(per_col):
         for k in range((w_ref.shape[1] - width) // patch):
             low, high = k * depth, min((k + 1) * depth, slab)
@@ -427,14 +444,20 @@
             here = slice(n * slab + low, n * slab + high)
             linear = piece[:, : high - low].astype(F32)
             gained = linear * (1.0 + mod_ref[6:7, here])
-            shifts += jnp.sum(linear * mod_ref[5:6, here], axis=1, keepdims=True)
-            gains += jnp.sum(gained, axis=1, keepdims=True)
+            both = (jnp.sum(gained, axis=1, keepdims=True), linear * mod_ref[5:6, here])
+            both = jnp.concatenate(
+                [jnp.broadcast_to(both[0], (patch, 128)), jnp.broadcast_to(
+                    jnp.sum(both[1], axis=1, keepdims=True), (patch, 128))], axis=0
+            ).T
+            consts += jnp.where(
+                row == 2, both[:8, :patch], jnp.where(row == 3, both[:8, patch:], 0.0)
+            )
             for t in range(3):
                 term = gained.astype(BF16)
                 gain_ref[t * patch : (t + 1) * patch, here] = term
                 gained = gained - term.astype(F32)
-    lane = lax.broadcasted_iota(jnp.int32, const_ref.shape, 1)
-    const_ref[...] = jnp.where(lane == 0, gains, jnp.where(lane == 1, shifts, 0.0))
+    const_ref[...] = jnp.zeros(const_ref.shape, F32)
+    const_ref[:, :patch] = consts
 
 
 def late_kernel(routes, mod_ref, x_ref, sum_ref, far_ref, gain_ref, const_ref, *refs):
@@ -450,13 +473,11 @@
     wide = updated.astype(F32)
     sums = jnp.sum(wide, axis=0, keepdims=True)
     squares = jnp.sum(wide * wide, axis=0, keepdims=True)
-    patch = const_ref.shape[0]
+    patch = gain_ref.shape[0] // 3
     terms = jnp.dot(gain_ref[...], updated, preferred_element_type=F32)
-    out_ref[:patch, :tokens] = terms[:patch] + terms[patch : 2 * patch] + terms[2 * patch :]
+    out_ref[:patch] = terms[:patch] + terms[patch : 2 * patch] + terms[2 * patch :]
     row = lax.broadcasted_iota(jnp.int32, (8, tokens), 0)
-    out_ref[patch:, :tokens] = jnp.where(row == 0, sums, jnp.where(row == 1, squares, 0.0))
-    out_ref[:patch, tokens:] = const_ref[...]
-    out_ref[patch:, tokens:] = jnp.zeros((8, 128), F32)
+    out_ref[patch:] = jnp.where(row == 0, sums, jnp.where(row == 1, squares, const_ref[...]))
 
 
 def sigma_of(step_now):
@@ -525,7 +546,7 @@
     mod_own = mod_own + swap(mod_own, "row", 1)
     ready = call(
         functools.partial(norm_kernel, full_width),
-        jax.ShapeDtypeStruct((img + txt, width), BF16),
+        jax.ShapeDtypeStruct((img + txt, wide), BF16),
         [VMEM] * 4,
         [],
         cost(1),
@@ -545,25 +566,28 @@
         blocks = [piece[k] for piece in gathered for k in masks]
     else:
         masks, blocks = [], [in_order(gathered, "row")]
-    gains = jnp.tile(jnp.concatenate([q_gain[None], k_gain], axis=0), (1, half // head))
     heads_out = jax.ShapeDtypeStruct((half, img), BF16)
+    full_wide = col_count * wide
     rest = [jax.ShapeDtypeStruct((rows, half), BF16) for rows in (img, *[2 * (img + txt)] * 2)]
     projected = call(
         functools.partial(project_kernel, routes, masks, img, head),
         (heads_out, *rest),
-        [SMEM, VMEM] + [HBM] * (2 * len(routes) + len(blocks)),
+        [SMEM, VMEM, VMEM] + [HBM] * (2 * len(routes) + len(blocks)),
         [
-            pltpu.VMEM((col_count, 2 * (img + txt), width), BF16),
-            pltpu.VMEM((col_count, width, 5 * half), BF16),
+            pltpu.VMEM((2 * (img + txt), full_wide), BF16),
+            pltpu.VMEM((full_wide, 5 * half), BF16),
             pltpu.VMEM((2 * img, 3 * half), F32),
             pltpu.VMEM((2 * txt, 2 * half), F32),
+            pltpu.VMEM((2 * img, half), BF16),
+            *[pltpu.VMEM((2 * (img + txt), half), BF16)] * 2,
             pltpu.SemaphoreType.DMA((2, 2, len(routes))),
-            pltpu.SemaphoreType.DMA((2, max(len(masks), 1))),
+            pltpu.SemaphoreType.DMA((2, col_count)),
+            pltpu.SemaphoreType.DMA((3,)),
         ],
         cost(PROJECT),
-        (VMEM,) * 4,
+        (VMEM, HBM, HBM, HBM),
         vmem=56,
-    )(text_len, gains, *line, *peer_line, *blocks)
+    )(text_len, q_gain[None], k_gain, *line, *peer_line, *blocks)
     head_depth, patch = final_weight.shape
     depth = out_weight.shape[0]
     folds = -(-head_depth // depth)
@@ -574,19 +598,19 @@
     out_blocks = direct_gather(out_packed, "row", masks)
 
     own_heads, *rest = projected
-    others = [out_blocks[k] for k in masks[1:]]
-    *rest, = tie(*rest, *others)
-    rest, others = rest[:3], rest[3:]
     give = call(
         functools.partial(attend_kernel, img, txt, head),
         heads_out,
         [SMEM, HBM, HBM, HBM],
         [pltpu.VMEM(part.shape, BF16) for part in rest] + [pltpu.SemaphoreType.DMA((3,))],
         cost(ATTEND),
-        vmem=24,
+        vmem=ATTEND_MIB,
     )(text_len, *rest)
-    attended = [own_heads, swap(give, "row", 1)]
-    lines = [(line_four if small else line_gather)(block, "col") for block in attended]
+    others = [out_blocks[k] for k in masks[1:]]
+    if small:
+        lines, others = gather_heads(own_heads, give, others)
+    else:
+        lines = [line_gather(block, "col") for block in (own_heads, swap(give, "row", 1))]
     own_rows = jnp.concatenate([out_packed, *others], axis=0)
     other_rows = swap(own_rows, "row", 1)
     early, late, far = far_routes(col_count)
@@ -597,7 +621,7 @@
             jax.ShapeDtypeStruct((width, img), F32),
             jax.ShapeDtypeStruct((width, part_cols), BF16),
             jax.ShapeDtypeStruct((3 * patch, width), BF16),
-            jax.ShapeDtypeStruct((patch, 128), F32),
+            jax.ShapeDtypeStruct((8, img), F32),
         ),
         [VMEM] + [HBM] * (2 * len(early) + 2),
         [
@@ -617,7 +641,7 @@
     )
     partial_sum = call(
         functools.partial(late_kernel, [route for _, route in late]),
-        jax.ShapeDtypeStruct((patch + 8, img + 128), F32),
+        jax.ShapeDtypeStruct((patch + 8, img), F32),
         [VMEM] * 6 + [HBM] * (2 * len(late)),
         [pltpu.VMEM((part_cols, img), BF16), sems],
         cost(3),
@@ -627,12 +651,12 @@
     while mask < col_count:
         partial_sum = partial_sum + swap(partial_sum, "col", mask)
         mask *= 2
-    average = partial_sum[patch : patch + 1, :img] / full_width
-    mean_square = partial_sum[patch + 1 : patch + 2, :img] / full_width
+    average = partial_sum[patch : patch + 1] / full_width
+    mean_square = partial_sum[patch + 1 : patch + 2] / full_width
     inverse = lax.rsqrt(mean_square - average * average + EPS_NORM)
-    gains = partial_sum[:patch, img : img + 1]
-    shifts = partial_sum[:patch, img + 1 : img + 2]
-    velocity = inverse * (partial_sum[:patch, :img] - average * gains) + shifts
+    gains = partial_sum[patch + 2, :patch][:, None]
+    shifts = partial_sum[patch + 3, :patch][:, None]
+    velocity = inverse * (partial_sum[:patch] - average * gains) + shifts
     step_now = lax.dynamic_index_in_dim(step_index, request, 0, keepdims=False)
     sigma_step = sigma_of(step_now + 1) - sigma_of(step_now)
     latent_next = latent.T + sigma_step * velocity

time: 177 us -> 172 us (0.972)
  waiting for transfers between devices: 99 us -> 89 us
  starting transfers between devices: 37.3 us -> 43.1 us
  local copies, waits for them, and re-layouts: 6.94 us -> 5.09 us
    ppermute x8, waiting for transfers between devices: 17.4 us -> 9.77 us  [gather_heads(): send = lambda held, route: lax.ppermute(held, 'col', route)]
    ppermute x30, starting transfers between devices: 23.6 us -> 30.9 us  [swap(): return lax.ppermute(block, axis, [(i, i ^ mask) for i in range(count)])]
    ppermute x4, waiting for transfers between devices: 36.9 us -> 29.9 us  [gather_both(): send = lambda held, route: lax.ppermute(held, 'col', route)]
    ppermute x30, waiting for transfers between devices: 44.6 us -> 49.3 us  [swap(): return lax.ppermute(block, axis, [(i, i ^ mask) for i in range(count)])]
    unnamed x60 -> x68, local copies, waits for them, and re-layouts: 5.45 us -> 4.44 us
  transfers between devices with their start and end apart: 42 -> 42, of which waited for: 15 -> 19; matrix products, arithmetic and copies ran while one was open for 1% -> 0% of each run, Pallas kernels for 15% -> 6%
where the time goes in v6:
time: 172 us; the launch traced here: 171 us
  waiting for transfers between devices  89 us (52%)
  starting transfers between devices  43.1 us (25%)
  Pallas kernels  30.7 us (18%)
  local copies, waits for them, and re-layouts  5.09 us (3%)
  between operations  2.62 us (2%)
    ppermute x30, waiting for transfers between devices, swap(): return lax.ppermute(block, axis, [(i, i ^ mask) for i in range(count)])  49.3 us
    ppermute x30, starting transfers between devices, swap(): return lax.ppermute(block, axis, [(i, i ^ mask) for i in range(count)])  30.9 us
    ppermute x4, waiting for transfers between devices, gather_both(): send = lambda held, route: lax.ppermute(held, 'col', route)  29.9 us
    pallas_call x1, Pallas kernels, per_device(): call(functools.partial(project_kernel, routes, masks, img, head), (heads_...  16.1 us
    ppermute x8, waiting for transfers between devices, gather_heads(): send = lambda held, route: lax.ppermute(held, 'col', route)  9.77 us
    ppermute x8, starting transfers between devices, gather_heads(): send = lambda held, route: lax.ppermute(held, 'col', route)  8.05 us
    pallas_call x1, Pallas kernels, per_device(): call(functools.partial(attend_kernel, img, txt, head), heads_out, [SMEM,...  6.89 us
    unnamed x68, local copies, waits for them, and re-layouts  4.44 us
  transfers between devices with their start and end apart: 42, of which 19 were waited for; matrix products, arithmetic and copies ran while one was open for 0% of the time, Pallas kernels for 6%

profile of v6, /device:TPU:0, one launch (start us, length us, event | category | flops | bytes accessed | tf_op | source)
XLA Modules:
  0.0 171.4 jit_solution(7418603630278146994)
XLA Ops:
  0.6 1.2 copy-done.1
  1.8 1.1 copy-done.4
  2.9 1.9 %shard_map.140 = (bf16[304,1280]{1,0:T(8,128)(2,1)S(1)}, bf16[304,1280]{1,0:T(8,128)(2,1)S(1)}) custom-call(bf16[3,304,512]{2,1,0:T(8,128)(2,1)S(1)} %bitcast.44, bf16[304,2,512]{2,1,0:T(2,128)(2,1)S(1)} %copy-done.4), custom_call_target="tpu_custom_call" | custom-call | flops 2300000000 | tf_op jit(solution)/shard_map/pallas_call | solution.py:536
  4.8 0.5 collective-permute-start
  5.3 0.5 shard_map.141
  5.8 2.6 %collective-permute-start.1 = (f32[8,640]{1,0:T(8,128)S(1)}, f32[8,640]{1,0:T(8,128)S(1)}, u32[]{:S(2)}, u32[]{:S(2)}) collective-permute-start(f32[8,640]{1,0:T(8,128)S(1)} %get-tuple-element.102), channel_id=1, source_target_pairs={{0,8},{4,12},{8,0},{12,4},{16,24},{20,28},{24,16},{28,20},{1,9},{5... | collective-permute-start | bytes 61448 | tf_op jit(solution)/shard_map/ppermute | solution.py:25
  8.4 1.5 collective-permute-start.2
  10.2 2.1 %collective-permute-start.5 = (f32[8,640]{1,0:T(8,128)S(1)}, f32[8,640]{1,0:T(8,128)S(1)}, u32[]{:S(2)}, u32[]{:S(2)}) collective-permute-start(f32[8,640]{1,0:T(8,128)S(1)} %shard_map.142), channel_id=1, source_target_pairs={{0,1},{1,0},{2,3},{3,2},{4,5},{5,4},{6,7},{7,6},{8,9},{9,8},{10,11... | collective-permute-start | bytes 61448 | tf_op jit(solution)/shard_map/ppermute | solution.py:25
  12.3 2.6 %collective-permute-start.6 = (f32[8,640]{1,0:T(8,128)S(1)}, f32[8,640]{1,0:T(8,128)S(1)}, u32[]{:S(2)}, u32[]{:S(2)}) collective-permute-start(f32[8,640]{1,0:T(8,128)S(1)} %shard_map.142), channel_id=1, source_target_pairs={{0,2},{1,3},{2,0},{3,1},{4,6},{5,7},{6,4},{7,5},{8,10},{9,11},{10,... | collective-permute-start | bytes 61448 | tf_op jit(solution)/shard_map/ppermute | solution.py:25
  14.9 1.0 collective-permute-start.7
  15.9 1.1 collective-permute-done.6
  17.1 3.4 %collective-permute-done.7 = f32[8,640]{1,0:T(8,128)S(1)} collective-permute-done((f32[8,640]{1,0:T(8,128)S(1)}, f32[8,640]{1,0:T(8,128)S(1)}, u32[]{:S(2)}, u32[]{:S(2)}) %collective-permute-start.7) | collective-permute-done | bytes 20512 | tf_op jit(solution)/shard_map/ppermute | solution.py:25
  20.5 0.7 shard_map.143.refs_0_
  21.3 0.7 collective-permute-start.9
  22.0 1.6 collective-permute-start.10
  23.6 1.5 collective-permute-start.11
  25.1 13.5 %collective-permute-done.8.refs_1_ = bf16[608,640]{1,0:T(8,128)(2,1)S(1)} collective-permute-done((bf16[608,640]{1,0:T(8,128)(2,1)S(1)}, bf16[608,640]{1,0:T(8,128)(2,1)S(1)}, u32[]{:S(2)}, u32[]{:S(2)}) %collective-permute-start.8) | collective-permute-done | bytes 778272 | tf_op jit(solution)/shard_map/ppermute | solution.py:25
  38.6 0.8 collective-permute-done.10.refs_14_
  39.4 1.2 collective-permute-done.11.refs_17_
  40.6 1.3 collective-permute-start.12
  41.9 0.7 collective-permute-start.13
  42.6 1.6 collective-permute-start.14
  44.2 0.5 collective-permute-start.15
  44.7 15.0 %collective-permute-done.12.refs_3_ = bf16[608,640]{1,0:T(8,128)(2,1)S(1)} collective-permute-done((bf16[608,640]{1,0:T(8,128)(2,1)S(1)}, bf16[608,640]{1,0:T(8,128)(2,1)S(1)}, u32[]{:S(2)}, u32[]{:S(2)}) %collective-permute-start.12) | collective-permute-done | bytes 778272 | tf_op jit(solution)/shard_map/ppermute | solution.py:102
  59.8 0.2 collective-permute-done.15.refs_18_
  60.0 1.5 collective-permute-start.17
  61.5 1.4 collective-permute-start.18
  62.9 0.6 collective-permute-start.19
  63.5 0.5 collective-permute-start.20
  64.0 14.9 %collective-permute-done.17.refs_5_ = bf16[608,640]{1,0:T(8,128)(2,1)S(1)} collective-permute-done((bf16[608,640]{1,0:T(8,128)(2,1)S(1)}, bf16[608,640]{1,0:T(8,128)(2,1)S(1)}, u32[]{:S(2)}, u32[]{:S(2)}) %collective-permute-start.17) | collective-permute-done | bytes 778272 | tf_op jit(solution)/shard_map/ppermute | solution.py:102
  78.9 0.5 collective-permute-start.22
  79.5 1.7 collective-permute-done.21.refs_8_
  81.1 1.1 collective-permute-done.22.refs_9_
  82.3 1.1 collective-permute-done.24.refs_11_
  83.4 0.9 copy-done.30
  84.4 16.1 %shard_map.144 = (bf16[256,512]{1,0:T(8,128)(2,1)}, bf16[512,256]{1,0:T(8,128)(2,1)}, bf16[1216,256]{1,0:T(8,128)(2,1)}, bf16[1216,256]{1,0:T(8,128)(2,1)}) custom-call(s32[4]{0:T(128)} %length_ref.3, f32[1,64]{1,0:T(1,128)} %bitcast.55, f32[2,64]{1,0:T(2,128)} %k_gain_ref.1, bf16[608,640]{1,0:T(8,128)(2,1)} %copy-done.3, bf16[608,640]{1,0:T(8,128)(2,1)} %copy-done.14, ...), custom_call_target="tpu_custom_call" | custom-call | flops 23000000512 | tf_op jit(solution)/shard_map/pallas_call | solution.py:572
  100.5 1.0 collective-permute-start.25
  101.5 0.9 collective-permute-start.26
  102.4 6.9 %shard_map.145 = bf16[256,512]{1,0:T(8,128)(2,1)} custom-call(s32[4]{0:T(128)} %length_ref.3, bf16[512,256]{1,0:T(8,128)(2,1)} %get-tuple-element.76.q_ref, bf16[1216,256]{1,0:T(8,128)(2,1)} %get-tuple-element.77.k_ref, bf16[1216,256]{1,0:T(8,128)(2,1)} %get-tuple-element.78.v_ref), custom_call_target="tpu_custom_call" | custom-call | flops 6899999744 | tf_op jit(solution)/shard_map/pallas_call | solution.py:601
  109.5 1.3 collective-permute-start.35
  110.8 1.3 collective-permute-start.27
  112.1 0.7 collective-permute-start.28
  112.8 6.0 %collective-permute-start.30 = (bf16[256,512]{1,0:T(8,128)(2,1)S(1)}, bf16[256,512]{1,0:T(8,128)(2,1)S(1)}, u32[]{:S(2)}, u32[]{:S(2)}) collective-permute-start(bf16[256,512]{1,0:T(8,128)(2,1)S(1)} %collective-permute-done.29.refs_4_), channel_id=1, source_target_pairs={{0,1},{1,0},{2,3},{3,2},{4,5},{5,4},{6,7},{7,6},{8,9},{9,8},{10,11... | collective-permute-start | bytes 786440 | tf_op jit(solution)/shard_map/ppermute | solution.py:25
  118.7 0.7 collective-permute-start.31
  119.4 3.4 %collective-permute-done.27.refs_3_ = bf16[256,512]{1,0:T(8,128)(2,1)S(1)} collective-permute-done((bf16[256,512]{1,0:T(8,128)(2,1)S(1)}, bf16[256,512]{1,0:T(8,128)(2,1)S(1)}, u32[]{:S(2)}, u32[]{:S(2)}) %collective-permute-start.27) | collective-permute-done | bytes 262176 | tf_op jit(solution)/shard_map/ppermute | solution.py:86
  122.8 0.6 collective-permute-start.36
  123.4 2.3 %collective-permute-start.37 = (bf16[736,256]{1,0:T(8,128)(2,1)S(1)}, bf16[736,256]{1,0:T(8,128)(2,1)S(1)}, u32[]{:S(2)}, u32[]{:S(2)}) collective-permute-start(bf16[736,256]{1,0:T(8,128)(2,1)S(1)} %pad_maximum_fusion), channel_id=1, source_target_pairs={{0,24},{4,28},{8,16},{12,20},{16,8},{20,12},{24,0},{28,4},{1,25},{... | collective-permute-start | bytes 1130504 | tf_op jit(solution)/shard_map/ppermute | solution.py:25
  125.7 2.3 %collective-permute-done.30.refs_5_ = bf16[256,512]{1,0:T(8,128)(2,1)S(1)} collective-permute-done((bf16[256,512]{1,0:T(8,128)(2,1)S(1)}, bf16[256,512]{1,0:T(8,128)(2,1)S(1)}, u32[]{:S(2)}, u32[]{:S(2)}) %collective-permute-start.30) | collective-permute-done | bytes 262176 | tf_op jit(solution)/shard_map/ppermute | solution.py:25
  128.0 1.3 collective-permute-start.32
  129.3 1.3 collective-permute-start.33
  130.6 0.7 collective-permute-start.34
  131.3 9.5 %collective-permute-done.36 = bf16[736,256]{1,0:T(8,128)(2,1)S(1)} collective-permute-done((bf16[736,256]{1,0:T(8,128)(2,1)S(1)}, bf16[736,256]{1,0:T(8,128)(2,1)S(1)}, u32[]{:S(2)}, u32[]{:S(2)}) %collective-permute-start.36) | collective-permute-done | bytes 376864 | tf_op jit(solution)/shard_map/ppermute | solution.py:25
  140.8 3.6 %collective-permute-done.33.refs_7_ = bf16[256,512]{1,0:T(8,128)(2,1)S(1)} collective-permute-done((bf16[256,512]{1,0:T(8,128)(2,1)S(1)}, bf16[256,512]{1,0:T(8,128)(2,1)S(1)}, u32[]{:S(2)}, u32[]{:S(2)}) %collective-permute-start.33) | collective-permute-done | bytes 262176 | tf_op jit(solution)/shard_map/ppermute | solution.py:86
  144.6 1.3 collective-permute-start.39
  145.9 2.0 %collective-permute-done.38.refs_9_ = bf16[2944,256]{1,0:T(8,128)(2,1)S(1)} collective-permute-done((bf16[2944,256]{1,0:T(8,128)(2,1)S(1)}, bf16[2944,256]{1,0:T(8,128)(2,1)S(1)}, u32[]{:S(2)}, u32[]{:S(2)}) %collective-permute-start.38) | collective-permute-done | bytes 1507360 | tf_op jit(solution)/shard_map/ppermute | solution.py:25
  147.9 1.1 copy-done.12
  149.0 3.3 %shard_map.146 = (f32[608,512]{1,0:T(8,128)S(1)}, bf16[608,512]{1,0:T(8,128)(2,1)S(1)}, bf16[192,608]{1,0:T(8,128)(2,1)S(1)}, f32[8,512]{1,0:T(8,128)S(1)}) custom-call(f32[8,640]{1,0:T(8,128)S(1)} %add.66.mod_ref, bf16[256,512]{1,0:T(8,128)(2,1)S(1)} %copy-done.6, bf16[256,512]{1,0:T(8,128)(2,1)S(1)} %collective-permute-done.25.refs_1_, ...), custom_call_target="tpu_custom_call" | custom-call | flops 5750000128 | tf_op jit(solution)/shard_map/pallas_call | solution.py:618
  152.4 2.8 %collective-permute-done.39.refs_3_ = bf16[256,512]{1,0:T(8,128)(2,1)S(1)} collective-permute-done((bf16[256,512]{1,0:T(8,128)(2,1)S(1)}, bf16[256,512]{1,0:T(8,128)(2,1)S(1)}, u32[]{:S(2)}, u32[]{:S(2)}) %collective-permute-start.39) | collective-permute-done | bytes 262176 | tf_op jit(solution)/shard_map/ppermute | solution.py:86
  155.2 1.1 shard_map.147
  156.4 5.4 %collective-permute-done.40 = f32[72,512]{1,0:T(8,128)S(1)} collective-permute-done((f32[72,512]{1,0:T(8,128)S(1)}, f32[72,512]{1,0:T(8,128)S(1)}, u32[]{:S(2)}, u32[]{:S(2)}) %collective-permute-start.40) | collective-permute-done | bytes 147488 | tf_op jit(solution)/shard_map/ppermute | solution.py:25
  161.9 0.8 collective-permute-start.41
  162.7 0.6 dynamic_slice.4
  164.7 5.9 %collective-permute-done.41 = f32[72,512]{1,0:T(8,128)S(1)} collective-permute-done((f32[72,512]{1,0:T(8,128)S(1)}, f32[72,512]{1,0:T(8,128)S(1)}, u32[]{:S(2)}, u32[]{:S(2)}) %collective-permute-start.41) | collective-permute-done | bytes 147488 | tf_op jit(solution)/shard_map/ppermute | solution.py:25
  170.6 0.8 fusion.2
  (110 shorter events, 1.1 us)
Async XLA Ops:
  4.8 37.9 %copy-start.2 = (bf16[304,1280]{1,0:T(8,128)(2,1)}, bf16[304,1280]{1,0:T(8,128)(2,1)S(1)}, u32[]{:S(2)}) copy-start(bf16[304,1280]{1,0:T(8,128)(2,1)S(1)} %get-tuple-element.59.refs_12_) | copy-start | bytes 2334724
  4.8 11.1 %collective-permute-start = (bf16[304,1280]{1,0:T(8,128)(2,1)S(1)}, bf16[304,1280]{1,0:T(8,128)(2,1)S(1)}, u32[]{:S(2)}, u32[]{:S(2)}) collective-permute-start(bf16[304,1280]{1,0:T(8,128)(2,1)S(1)} %get-tuple-element.50), channel_id=1, source_target_pairs={{0,4},{4,0},{8,12},{12,8},{16,20},{20,16},{24,28},{28,24},{1,5},{5... | collective-permute-start | bytes 2334728 | tf_op jit(solution)/shard_map/ppermute | solution.py:25
  5.3 4.7 %copy-start.5 = (bf16[512,608]{0,1:T(8,128)(2,1)S(1)}, bf16[512,608]{0,1:T(8,128)(2,1)}, u32[]{:S(2)}) copy-start(bf16[512,608]{0,1:T(8,128)(2,1)} %param.13) | copy-start | bytes 1867780
  5.3 4.7 %copy-start.7 = (bf16[96,608]{1,0:T(8,128)(2,1)S(1)}, bf16[96,608]{1,0:T(8,128)(2,1)}, u32[]{:S(2)}) copy-start(bf16[96,608]{1,0:T(8,128)(2,1)} %txt_ref.3) | copy-start | bytes 350212
  5.8 6.4 %collective-permute-start.1 = (f32[8,640]{1,0:T(8,128)S(1)}, f32[8,640]{1,0:T(8,128)S(1)}, u32[]{:S(2)}, u32[]{:S(2)}) collective-permute-start(f32[8,640]{1,0:T(8,128)S(1)} %get-tuple-element.102), channel_id=1, source_target_pairs={{0,8},{4,12},{8,0},{12,4},{16,24},{20,28},{24,16},{28,20},{1,9},{5... | collective-permute-start | bytes 61448 | tf_op jit(solution)/shard_map/ppermute | solution.py:25
  8.4 6.4 %collective-permute-start.2 = (f32[8,640]{1,0:T(8,128)S(1)}, f32[8,640]{1,0:T(8,128)S(1)}, u32[]{:S(2)}, u32[]{:S(2)}) collective-permute-start(f32[8,640]{1,0:T(8,128)S(1)} %get-tuple-element.104), channel_id=1, source_target_pairs={{0,16},{4,20},{8,24},{12,28},{16,0},{20,4},{24,8},{28,12},{1,17},{... | collective-permute-start | bytes 61448 | tf_op jit(solution)/shard_map/ppermute | solution.py:25
  9.9 5.9 %collective-permute-start.3 = (f32[8,640]{1,0:T(8,128)S(1)}, f32[8,640]{1,0:T(8,128)S(1)}, u32[]{:S(2)}, u32[]{:S(2)}) collective-permute-start(f32[8,640]{1,0:T(8,128)S(1)} %get-tuple-element.103), channel_id=1, source_target_pairs={{0,24},{4,28},{8,16},{12,20},{16,8},{20,12},{24,0},{28,4},{1,25},{... | collective-permute-start | bytes 61448 | tf_op jit(solution)/shard_map/ppermute | solution.py:25
  10.2 5.8 %collective-permute-start.5 = (f32[8,640]{1,0:T(8,128)S(1)}, f32[8,640]{1,0:T(8,128)S(1)}, u32[]{:S(2)}, u32[]{:S(2)}) collective-permute-start(f32[8,640]{1,0:T(8,128)S(1)} %shard_map.142), channel_id=1, source_target_pairs={{0,1},{1,0},{2,3},{3,2},{4,5},{5,4},{6,7},{7,6},{8,9},{9,8},{10,11... | collective-permute-start | bytes 61448 | tf_op jit(solution)/shard_map/ppermute | solution.py:25
  12.3 4.8 %collective-permute-start.6 = (f32[8,640]{1,0:T(8,128)S(1)}, f32[8,640]{1,0:T(8,128)S(1)}, u32[]{:S(2)}, u32[]{:S(2)}) collective-permute-start(f32[8,640]{1,0:T(8,128)S(1)} %shard_map.142), channel_id=1, source_target_pairs={{0,2},{1,3},{2,0},{3,1},{4,6},{5,7},{6,4},{7,5},{8,10},{9,11},{10,... | collective-permute-start | bytes 61448 | tf_op jit(solution)/shard_map/ppermute | solution.py:25
  14.9 5.6 %collective-permute-start.7 = (f32[8,640]{1,0:T(8,128)S(1)}, f32[8,640]{1,0:T(8,128)S(1)}, u32[]{:S(2)}, u32[]{:S(2)}) collective-permute-start(f32[8,640]{1,0:T(8,128)S(1)} %shard_map.142), channel_id=1, source_target_pairs={{0,3},{1,2},{2,1},{3,0},{4,7},{5,6},{6,5},{7,4},{8,11},{9,10},{10,... | collective-permute-start | bytes 61448 | tf_op jit(solution)/shard_map/ppermute | solution.py:25
  15.8 28.4 %copy-start.13 = (bf16[304,1280]{1,0:T(8,128)(2,1)}, bf16[304,1280]{1,0:T(8,128)(2,1)S(1)}, u32[]{:S(2)}) copy-start(bf16[304,1280]{1,0:T(8,128)(2,1)S(1)} %collective-permute-done.refs_16_) | copy-start | bytes 2334724
  15.8 4.6 %collective-permute-start.4 = (f32[8,640]{1,0:T(8,128)S(1)}, f32[8,640]{1,0:T(8,128)S(1)}, u32[]{:S(2)}, u32[]{:S(2)}) collective-permute-start(f32[8,640]{1,0:T(8,128)S(1)} %fusion.6), channel_id=1, source_target_pairs={{0,4},{4,0},{8,12},{12,8},{16,20},{20,16},{24,28},{28,24},{1,5},{5... | collective-permute-start | bytes 61448 | tf_op jit(solution)/shard_map/ppermute | solution.py:25
  21.2 63.1 %copy-start.3 = (bf16[608,640]{1,0:T(8,128)(2,1)}, bf16[608,640]{1,0:T(8,128)(2,1)S(1)}, u32[]{:S(2)}) copy-start(bf16[608,640]{1,0:T(8,128)(2,1)S(1)} %shard_map.143.refs_0_) | copy-start | bytes 2334724
  21.2 17.4 %collective-permute-start.8 = (bf16[608,640]{1,0:T(8,128)(2,1)S(1)}, bf16[608,640]{1,0:T(8,128)(2,1)S(1)}, u32[]{:S(2)}, u32[]{:S(2)}) collective-permute-start(bf16[608,640]{1,0:T(8,128)(2,1)S(1)} %shard_map.143.refs_0_), channel_id=1, source_target_pairs={{0,1},{1,0},{2,3},{3,2},{4,5},{5,4},{6,7},{7,6},{8,9},{9,8},{10,11... | collective-permute-start | bytes 2334728 | tf_op jit(solution)/shard_map/ppermute | solution.py:25
  21.3 17.3 %collective-permute-start.9 = (bf16[608,640]{1,0:T(8,128)(2,1)S(1)}, bf16[608,640]{1,0:T(8,128)(2,1)S(1)}, u32[]{:S(2)}, u32[]{:S(2)}) collective-permute-start(bf16[608,640]{1,0:T(8,128)(2,1)S(1)} %shard_map.143.refs_0_), channel_id=1, source_target_pairs={{1,2},{2,1},{5,6},{6,5},{9,10},{10,9},{13,14},{14,13},{17,18},{18,... | collective-permute-start | bytes 2334728 | tf_op jit(solution)/shard_map/ppermute | solution.py:102
  22.0 17.4 %collective-permute-start.10 = (bf16[304,1280]{1,0:T(8,128)(2,1)S(1)}, bf16[304,1280]{1,0:T(8,128)(2,1)S(1)}, u32[]{:S(2)}, u32[]{:S(2)}) collective-permute-start(bf16[304,1280]{1,0:T(8,128)(2,1)S(1)} %get-tuple-element.59.refs_12_), channel_id=1, source_target_pairs={{0,16},{4,20},{8,24},{12,28},{16,0},{20,4},{24,8},{28,12},{1,17},{... | collective-permute-start | bytes 2334728 | tf_op jit(solution)/shard_map/ppermute | solution.py:25
  23.6 17.0 %collective-permute-start.11 = (bf16[304,1280]{1,0:T(8,128)(2,1)S(1)}, bf16[304,1280]{1,0:T(8,128)(2,1)S(1)}, u32[]{:S(2)}, u32[]{:S(2)}) collective-permute-start(bf16[304,1280]{1,0:T(8,128)(2,1)S(1)} %collective-permute-done.refs_16_), channel_id=1, source_target_pairs={{0,8},{4,12},{8,0},{12,4},{16,24},{20,28},{24,16},{28,20},{1,9},{5... | collective-permute-start | bytes 2334728 | tf_op jit(solution)/shard_map/ppermute | solution.py:25
  25.1 19.6 %collective-permute-start.16 = (bf16[608,640]{1,0:T(8,128)(2,1)S(1)}, bf16[608,640]{1,0:T(8,128)(2,1)S(1)}, u32[]{:S(2)}, u32[]{:S(2)}) collective-permute-start(bf16[608,640]{1,0:T(8,128)(2,1)S(1)} %shard_map.143.refs_0_), channel_id=1, source_target_pairs={{0,4},{4,0},{8,12},{12,8},{16,20},{20,16},{24,28},{28,24},{1,5},{5... | collective-permute-start | bytes 2334728 | tf_op jit(solution)/shard_map/ppermute | solution.py:25
  38.6 45.7 %copy-start.14 = (bf16[608,640]{1,0:T(8,128)(2,1)}, bf16[608,640]{1,0:T(8,128)(2,1)S(1)}, u32[]{:S(2)}) copy-start(bf16[608,640]{1,0:T(8,128)(2,1)S(1)} %collective-permute-done.8.refs_1_) | copy-start | bytes 2334724
  38.6 45.7 %copy-start.15 = (bf16[608,640]{1,0:T(8,128)(2,1)}, bf16[608,640]{1,0:T(8,128)(2,1)S(1)}, u32[]{:S(2)}) copy-start(bf16[608,640]{1,0:T(8,128)(2,1)S(1)} %collective-permute-done.9.refs_2_) | copy-start | bytes 2334724
  39.4 44.9 %copy-start.16 = (bf16[304,1280]{1,0:T(8,128)(2,1)}, bf16[304,1280]{1,0:T(8,128)(2,1)S(1)}, u32[]{:S(2)}) copy-start(bf16[304,1280]{1,0:T(8,128)(2,1)S(1)} %collective-permute-done.10.refs_14_) | copy-start | bytes 2334724
  40.6 43.7 %copy-start.17 = (bf16[304,1280]{1,0:T(8,128)(2,1)}, bf16[304,1280]{1,0:T(8,128)(2,1)S(1)}, u32[]{:S(2)}) copy-start(bf16[304,1280]{1,0:T(8,128)(2,1)S(1)} %collective-permute-done.11.refs_17_) | copy-start | bytes 2334724
  40.6 19.1 %collective-permute-start.12 = (bf16[608,640]{1,0:T(8,128)(2,1)S(1)}, bf16[608,640]{1,0:T(8,128)(2,1)S(1)}, u32[]{:S(2)}, u32[]{:S(2)}) collective-permute-start(bf16[608,640]{1,0:T(8,128)(2,1)S(1)} %collective-permute-done.9.refs_2_), channel_id=1, source_target_pairs={{1,0},{2,3},{5,4},{6,7},{9,8},{10,11},{13,12},{14,15},{17,16},{18,... | collective-permute-start | bytes 2334728 | tf_op jit(solution)/shard_map/ppermute | solution.py:102
  41.9 17.8 %collective-permute-start.13 = (bf16[608,640]{1,0:T(8,128)(2,1)S(1)}, bf16[608,640]{1,0:T(8,128)(2,1)S(1)}, u32[]{:S(2)}, u32[]{:S(2)}) collective-permute-start(bf16[608,640]{1,0:T(8,128)(2,1)S(1)} %collective-permute-done.8.refs_1_), channel_id=1, source_target_pairs={{1,2},{2,1},{5,6},{6,5},{9,10},{10,9},{13,14},{14,13},{17,18},{18,... | collective-permute-start | bytes 2334728 | tf_op jit(solution)/shard_map/ppermute | solution.py:102
  42.6 17.1 %collective-permute-start.14 = (bf16[304,1280]{1,0:T(8,128)(2,1)S(1)}, bf16[304,1280]{1,0:T(8,128)(2,1)S(1)}, u32[]{:S(2)}, u32[]{:S(2)}) collective-permute-start(bf16[304,1280]{1,0:T(8,128)(2,1)S(1)} %get-tuple-element.59.refs_12_), channel_id=1, source_target_pairs={{0,8},{4,12},{8,0},{12,4},{16,24},{20,28},{24,16},{28,20},{1,9},{5... | collective-permute-start | bytes 2334728 | tf_op jit(solution)/shard_map/ppermute | solution.py:25
  44.2 15.8 %collective-permute-start.15 = (bf16[304,1280]{1,0:T(8,128)(2,1)S(1)}, bf16[304,1280]{1,0:T(8,128)(2,1)S(1)}, u32[]{:S(2)}, u32[]{:S(2)}) collective-permute-start(bf16[304,1280]{1,0:T(8,128)(2,1)S(1)} %collective-permute-done.refs_16_), channel_id=1, source_target_pairs={{0,16},{4,20},{8,24},{12,28},{16,0},{20,4},{24,8},{28,12},{1,17},{... | collective-permute-start | bytes 2334728 | tf_op jit(solution)/shard_map/ppermute | solution.py:25
  44.7 39.6 %copy-start.18 = (bf16[608,640]{1,0:T(8,128)(2,1)}, bf16[608,640]{1,0:T(8,128)(2,1)S(1)}, u32[]{:S(2)}) copy-start(bf16[608,640]{1,0:T(8,128)(2,1)S(1)} %collective-permute-done.16.refs_6_) | copy-start | bytes 2334724
  59.8 24.6 %copy-start.19 = (bf16[608,640]{1,0:T(8,128)(2,1)}, bf16[608,640]{1,0:T(8,128)(2,1)S(1)}, u32[]{:S(2)}) copy-start(bf16[608,640]{1,0:T(8,128)(2,1)S(1)} %collective-permute-done.12.refs_3_) | copy-start | bytes 2334724
  59.8 22.5 %copy-start.20 = (bf16[608,640]{1,0:T(8,128)(2,1)}, bf16[608,640]{1,0:T(8,128)(2,1)S(1)}, u32[]{:S(2)}) copy-start(bf16[608,640]{1,0:T(8,128)(2,1)S(1)} %collective-permute-done.13.refs_4_) | copy-start | bytes 2334724
  59.8 22.5 %copy-start.21 = (bf16[304,1280]{1,0:T(8,128)(2,1)}, bf16[304,1280]{1,0:T(8,128)(2,1)S(1)}, u32[]{:S(2)}) copy-start(bf16[304,1280]{1,0:T(8,128)(2,1)S(1)} %collective-permute-done.14.refs_13_) | copy-start | bytes 2334724
  60.0 23.4 %copy-start.22 = (bf16[304,1280]{1,0:T(8,128)(2,1)}, bf16[304,1280]{1,0:T(8,128)(2,1)S(1)}, u32[]{:S(2)}) copy-start(bf16[304,1280]{1,0:T(8,128)(2,1)S(1)} %collective-permute-done.15.refs_18_) | copy-start | bytes 2334724
  60.0 18.9 %collective-permute-start.17 = (bf16[608,640]{1,0:T(8,128)(2,1)S(1)}, bf16[608,640]{1,0:T(8,128)(2,1)S(1)}, u32[]{:S(2)}, u32[]{:S(2)}) collective-permute-start(bf16[608,640]{1,0:T(8,128)(2,1)S(1)} %collective-permute-done.13.refs_4_), channel_id=1, source_target_pairs={{1,0},{2,3},{5,4},{6,7},{9,8},{10,11},{13,12},{14,15},{17,16},{18,... | collective-permute-start | bytes 2334728 | tf_op jit(solution)/shard_map/ppermute | solution.py:102
  61.5 17.4 %collective-permute-start.18 = (bf16[304,1280]{1,0:T(8,128)(2,1)S(1)}, bf16[304,1280]{1,0:T(8,128)(2,1)S(1)}, u32[]{:S(2)}, u32[]{:S(2)}) collective-permute-start(bf16[304,1280]{1,0:T(8,128)(2,1)S(1)} %collective-permute-done.10.refs_14_), channel_id=1, source_target_pairs={{0,8},{4,12},{8,0},{12,4},{16,24},{20,28},{24,16},{28,20},{1,9},{5... | collective-permute-start | bytes 2334728 | tf_op jit(solution)/shard_map/ppermute | solution.py:25
  62.9 16.5 %collective-permute-start.19 = (bf16[304,1280]{1,0:T(8,128)(2,1)S(1)}, bf16[304,1280]{1,0:T(8,128)(2,1)S(1)}, u32[]{:S(2)}, u32[]{:S(2)}) collective-permute-start(bf16[304,1280]{1,0:T(8,128)(2,1)S(1)} %collective-permute-done.11.refs_17_), channel_id=1, source_target_pairs={{0,16},{4,20},{8,24},{12,28},{16,0},{20,4},{24,8},{28,12},{1,17},{... | collective-permute-start | bytes 2334728 | tf_op jit(solution)/shard_map/ppermute | solution.py:25
  63.5 18.8 %collective-permute-start.23 = (bf16[608,640]{1,0:T(8,128)(2,1)S(1)}, bf16[608,640]{1,0:T(8,128)(2,1)S(1)}, u32[]{:S(2)}, u32[]{:S(2)}) collective-permute-start(bf16[608,640]{1,0:T(8,128)(2,1)S(1)} %collective-permute-done.13.refs_4_), channel_id=1, source_target_pairs={{0,4},{4,0},{8,12},{12,8},{16,20},{20,16},{24,28},{28,24},{1,5},{5... | collective-permute-start | bytes 2334728 | tf_op jit(solution)/shard_map/ppermute | solution.py:25
  63.5 16.0 %collective-permute-start.20 = (bf16[608,640]{1,0:T(8,128)(2,1)S(1)}, bf16[608,640]{1,0:T(8,128)(2,1)S(1)}, u32[]{:S(2)}, u32[]{:S(2)}) collective-permute-start(bf16[608,640]{1,0:T(8,128)(2,1)S(1)} %collective-permute-done.8.refs_1_), channel_id=1, source_target_pairs={{0,4},{4,0},{8,12},{12,8},{16,20},{20,16},{24,28},{28,24},{1,5},{5... | collective-permute-start | bytes 2334728 | tf_op jit(solution)/shard_map/ppermute | solution.py:25
  78.9 5.5 %copy-start.23 = (bf16[608,640]{1,0:T(8,128)(2,1)}, bf16[608,640]{1,0:T(8,128)(2,1)S(1)}, u32[]{:S(2)}) copy-start(bf16[608,640]{1,0:T(8,128)(2,1)S(1)} %collective-permute-done.17.refs_5_) | copy-start | bytes 2334724
  78.9 2.3 %collective-permute-start.21 = (bf16[608,640]{1,0:T(8,128)(2,1)S(1)}, bf16[608,640]{1,0:T(8,128)(2,1)S(1)}, u32[]{:S(2)}, u32[]{:S(2)}) collective-permute-start(bf16[608,640]{1,0:T(8,128)(2,1)S(1)} %collective-permute-done.9.refs_2_), channel_id=1, source_target_pairs={{0,4},{4,0},{8,12},{12,8},{16,20},{20,16},{24,28},{28,24},{1,5},{5... | collective-permute-start | bytes 2334728 | tf_op jit(solution)/shard_map/ppermute | solution.py:25
  78.9 5.5 %copy-start.24 = (bf16[304,1280]{1,0:T(8,128)(2,1)}, bf16[304,1280]{1,0:T(8,128)(2,1)S(1)}, u32[]{:S(2)}) copy-start(bf16[304,1280]{1,0:T(8,128)(2,1)S(1)} %collective-permute-done.18.refs_15_) | copy-start | bytes 2334724
  78.9 3.4 %collective-permute-start.22 = (bf16[608,640]{1,0:T(8,128)(2,1)S(1)}, bf16[608,640]{1,0:T(8,128)(2,1)S(1)}, u32[]{:S(2)}, u32[]{:S(2)}) collective-permute-start(bf16[608,640]{1,0:T(8,128)(2,1)S(1)} %collective-permute-done.12.refs_3_), channel_id=1, source_target_pairs={{0,4},{4,0},{8,12},{12,8},{16,20},{20,16},{24,28},{28,24},{1,5},{5... | collective-permute-start | bytes 2334728 | tf_op jit(solution)/shard_map/ppermute | solution.py:25
  79.4 4.0 %copy-start.25 = (bf16[304,1280]{1,0:T(8,128)(2,1)}, bf16[304,1280]{1,0:T(8,128)(2,1)S(1)}, u32[]{:S(2)}) copy-start(bf16[304,1280]{1,0:T(8,128)(2,1)S(1)} %collective-permute-done.19.refs_19_) | copy-start | bytes 2334724
  79.4 4.0 %collective-permute-start.24 = (bf16[608,640]{1,0:T(8,128)(2,1)S(1)}, bf16[608,640]{1,0:T(8,128)(2,1)S(1)}, u32[]{:S(2)}, u32[]{:S(2)}) collective-permute-start(bf16[608,640]{1,0:T(8,128)(2,1)S(1)} %collective-permute-done.17.refs_5_), channel_id=1, source_target_pairs={{0,4},{4,0},{8,12},{12,8},{16,20},{20,16},{24,28},{28,24},{1,5},{5... | collective-permute-start | bytes 2334728 | tf_op jit(solution)/shard_map/ppermute | solution.py:25
  100.5 8.8 %collective-permute-start.25 = (bf16[256,512]{1,0:T(8,128)(2,1)}, bf16[256,512]{1,0:T(8,128)(2,1)S(1)}, u32[]{:S(2)}, u32[]{:S(2)}) collective-permute-start(bf16[256,512]{1,0:T(8,128)(2,1)} %get-tuple-element.75.refs_0_), channel_id=1, source_target_pairs={{0,1},{1,0},{2,3},{3,2},{4,5},{5,4},{6,7},{7,6},{8,9},{9,8},{10,11... | collective-permute-start | bytes 786440 | tf_op jit(solution)/shard_map/ppermute | solution.py:25
  101.5 7.8 %collective-permute-start.26 = (bf16[256,512]{1,0:T(8,128)(2,1)}, bf16[256,512]{1,0:T(8,128)(2,1)S(1)}, u32[]{:S(2)}, u32[]{:S(2)}) collective-permute-start(bf16[256,512]{1,0:T(8,128)(2,1)} %get-tuple-element.75.refs_0_), channel_id=1, source_target_pairs={{1,2},{2,1},{5,6},{6,5},{9,10},{10,9},{13,14},{14,13},{17,18},{18,... | collective-permute-start | bytes 786440 | tf_op jit(solution)/shard_map/ppermute | solution.py:86
  102.4 7.0 %copy-start.11 = (bf16[304,64]{0,1:T(8,128)(2,1)S(1)}, bf16[304,64]{0,1:T(8,128)(2,1)}, u32[]{:S(2)}) copy-start(bf16[304,64]{0,1:T(8,128)(2,1)} %param.25) | copy-start | bytes 116740
  102.4 7.1 %copy-start.9 = (bf16[256,608]{0,1:T(8,128)(2,1)S(1)}, bf16[256,608]{0,1:T(8,128)(2,1)}, u32[]{:S(2)}) copy-start(bf16[256,608]{0,1:T(8,128)(2,1)} %param.24) | copy-start | bytes 933892
  109.3 3.4 %collective-permute-start.29 = (bf16[256,512]{1,0:T(8,128)(2,1)}, bf16[256,512]{1,0:T(8,128)(2,1)S(1)}, u32[]{:S(2)}, u32[]{:S(2)}) collective-permute-start(bf16[256,512]{1,0:T(8,128)(2,1)} %shard_map.145), channel_id=1, source_target_pairs={{0,4},{4,0},{8,12},{12,8},{16,20},{20,16},{24,28},{28,24},{1,5},{5... | collective-permute-start | bytes 786440 | tf_op jit(solution)/shard_map/ppermute | solution.py:25
  109.5 39.5 %copy-start.6 = (bf16[256,512]{1,0:T(8,128)(2,1)S(1)}, bf16[256,512]{1,0:T(8,128)(2,1)}, u32[]{:S(2)}) copy-start(bf16[256,512]{1,0:T(8,128)(2,1)} %get-tuple-element.75.refs_0_) | copy-start | bytes 786436
  109.5 21.1 %collective-permute-start.35 = (bf16[736,256]{1,0:T(8,128)(2,1)S(1)}, bf16[736,256]{1,0:T(8,128)(2,1)S(1)}, u32[]{:S(2)}, u32[]{:S(2)}) collective-permute-start(bf16[736,256]{1,0:T(8,128)(2,1)S(1)} %pad_maximum_fusion), channel_id=1, source_target_pairs={{0,8},{4,12},{8,0},{12,4},{16,24},{20,28},{24,16},{28,20},{1,9},{5... | collective-permute-start | bytes 1130504 | tf_op jit(solution)/shard_map/ppermute | solution.py:25
  110.8 12.0 %collective-permute-start.27 = (bf16[256,512]{1,0:T(8,128)(2,1)S(1)}, bf16[256,512]{1,0:T(8,128)(2,1)S(1)}, u32[]{:S(2)}, u32[]{:S(2)}) collective-permute-start(bf16[256,512]{1,0:T(8,128)(2,1)S(1)} %collective-permute-done.26.refs_2_), channel_id=1, source_target_pairs={{1,0},{2,3},{5,4},{6,7},{9,8},{10,11},{13,12},{14,15},{17,16},{18,... | collective-permute-start | bytes 786440 | tf_op jit(solution)/shard_map/ppermute | solution.py:86
  112.1 11.4 %collective-permute-start.28 = (bf16[256,512]{1,0:T(8,128)(2,1)S(1)}, bf16[256,512]{1,0:T(8,128)(2,1)S(1)}, u32[]{:S(2)}, u32[]{:S(2)}) collective-permute-start(bf16[256,512]{1,0:T(8,128)(2,1)S(1)} %collective-permute-done.25.refs_1_), channel_id=1, source_target_pairs={{1,2},{2,1},{5,6},{6,5},{9,10},{10,9},{13,14},{14,13},{17,18},{18,... | collective-permute-start | bytes 786440 | tf_op jit(solution)/shard_map/ppermute | solution.py:86
  112.8 15.2 %collective-permute-start.30 = (bf16[256,512]{1,0:T(8,128)(2,1)S(1)}, bf16[256,512]{1,0:T(8,128)(2,1)S(1)}, u32[]{:S(2)}, u32[]{:S(2)}) collective-permute-start(bf16[256,512]{1,0:T(8,128)(2,1)S(1)} %collective-permute-done.29.refs_4_), channel_id=1, source_target_pairs={{0,1},{1,0},{2,3},{3,2},{4,5},{5,4},{6,7},{7,6},{8,9},{9,8},{10,11... | collective-permute-start | bytes 786440 | tf_op jit(solution)/shard_map/ppermute | solution.py:25
  118.7 9.3 %collective-permute-start.31 = (bf16[256,512]{1,0:T(8,128)(2,1)S(1)}, bf16[256,512]{1,0:T(8,128)(2,1)S(1)}, u32[]{:S(2)}, u32[]{:S(2)}) collective-permute-start(bf16[256,512]{1,0:T(8,128)(2,1)S(1)} %collective-permute-done.29.refs_4_), channel_id=1, source_target_pairs={{1,2},{2,1},{5,6},{6,5},{9,10},{10,9},{13,14},{14,13},{17,18},{18,... | collective-permute-start | bytes 786440 | tf_op jit(solution)/shard_map/ppermute | solution.py:86
  122.8 18.0 %collective-permute-start.36 = (bf16[736,256]{1,0:T(8,128)(2,1)S(1)}, bf16[736,256]{1,0:T(8,128)(2,1)S(1)}, u32[]{:S(2)}, u32[]{:S(2)}) collective-permute-start(bf16[736,256]{1,0:T(8,128)(2,1)S(1)} %pad_maximum_fusion), channel_id=1, source_target_pairs={{0,16},{4,20},{8,24},{12,28},{16,0},{20,4},{24,8},{28,12},{1,17},{... | collective-permute-start | bytes 1130504 | tf_op jit(solution)/shard_map/ppermute | solution.py:25
  123.4 17.4 %collective-permute-start.37 = (bf16[736,256]{1,0:T(8,128)(2,1)S(1)}, bf16[736,256]{1,0:T(8,128)(2,1)S(1)}, u32[]{:S(2)}, u32[]{:S(2)}) collective-permute-start(bf16[736,256]{1,0:T(8,128)(2,1)S(1)} %pad_maximum_fusion), channel_id=1, source_target_pairs={{0,24},{4,28},{8,16},{12,20},{16,8},{20,12},{24,0},{28,4},{1,25},{... | collective-permute-start | bytes 1130504 | tf_op jit(solution)/shard_map/ppermute | solution.py:25
  128.0 12.8 %collective-permute-start.32 = (bf16[256,512]{1,0:T(8,128)(2,1)S(1)}, bf16[256,512]{1,0:T(8,128)(2,1)S(1)}, u32[]{:S(2)}, u32[]{:S(2)}) collective-permute-start(bf16[256,512]{1,0:T(8,128)(2,1)S(1)} %collective-permute-done.28.refs_0_), channel_id=1, source_target_pairs={{1,0},{2,3},{5,4},{6,7},{9,8},{10,11},{13,12},{14,15},{17,16},{18,... | collective-permute-start | bytes 786440 | tf_op jit(solution)/shard_map/ppermute | solution.py:86
  129.3 15.1 %collective-permute-start.33 = (bf16[256,512]{1,0:T(8,128)(2,1)S(1)}, bf16[256,512]{1,0:T(8,128)(2,1)S(1)}, u32[]{:S(2)}, u32[]{:S(2)}) collective-permute-start(bf16[256,512]{1,0:T(8,128)(2,1)S(1)} %collective-permute-done.31.refs_6_), channel_id=1, source_target_pairs={{1,0},{2,3},{5,4},{6,7},{9,8},{10,11},{13,12},{14,15},{17,16},{18,... | collective-permute-start | bytes 786440 | tf_op jit(solution)/shard_map/ppermute | solution.py:86
  130.6 13.8 %collective-permute-start.34 = (bf16[256,512]{1,0:T(8,128)(2,1)S(1)}, bf16[256,512]{1,0:T(8,128)(2,1)S(1)}, u32[]{:S(2)}, u32[]{:S(2)}) collective-permute-start(bf16[256,512]{1,0:T(8,128)(2,1)S(1)} %collective-permute-done.30.refs_5_), channel_id=1, source_target_pairs={{1,2},{2,1},{5,6},{6,5},{9,10},{10,9},{13,14},{14,13},{17,18},{18,... | collective-permute-start | bytes 786440 | tf_op jit(solution)/shard_map/ppermute | solution.py:86
  144.5 3.4 %collective-permute-start.38 = (bf16[2944,256]{1,0:T(8,128)(2,1)S(1)}, bf16[2944,256]{1,0:T(8,128)(2,1)S(1)}, u32[]{:S(2)}, u32[]{:S(2)}) collective-permute-start(bf16[2944,256]{1,0:T(8,128)(2,1)S(1)} %constant_dynamic-update-slice_fusion.refs_8_), channel_id=1, source_target_pairs={{0,4},{4,0},{8,12},{12,8},{16,20},{20,16},{24,28},{28,24},{1,5},{5... | collective-permute-start | bytes 4521992 | tf_op jit(solution)/shard_map/ppermute | solution.py:25
  144.6 10.6 %collective-permute-start.39 = (bf16[256,512]{1,0:T(8,128)(2,1)S(1)}, bf16[256,512]{1,0:T(8,128)(2,1)S(1)}, u32[]{:S(2)}, u32[]{:S(2)}) collective-permute-start(bf16[256,512]{1,0:T(8,128)(2,1)S(1)} %collective-permute-done.34.refs_2_), channel_id=1, source_target_pairs={{1,0},{2,3},{5,4},{6,7},{9,8},{10,11},{13,12},{14,15},{17,16},{18,... | collective-permute-start | bytes 786440 | tf_op jit(solution)/shard_map/ppermute | solution.py:86
  155.2 7.5 %copy-start.31 = (s32[4]{0:T(128)S(1)}, s32[4]{0:T(128)}, u32[]{:S(2)}) copy-start(s32[4]{0:T(128)} %param.16) | copy-start | bytes 52
  155.2 15.4 %copy-start.10 = (f32[512,64]{0,1:T(8,128)S(1)}, f32[512,64]{0,1:T(8,128)}, u32[]{:S(2)}) copy-start(f32[512,64]{0,1:T(8,128)} %param.17) | copy-start | bytes 393220
  156.3 5.5 %collective-permute-start.40 = (f32[72,512]{1,0:T(8,128)S(1)}, f32[72,512]{1,0:T(8,128)S(1)}, u32[]{:S(2)}, u32[]{:S(2)}) collective-permute-start(f32[72,512]{1,0:T(8,128)S(1)} %shard_map.147), channel_id=1, source_target_pairs={{0,1},{1,0},{2,3},{3,2},{4,5},{5,4},{6,7},{7,6},{8,9},{9,8},{10,11... | collective-permute-start | bytes 442376 | tf_op jit(solution)/shard_map/ppermute | solution.py:25
  161.9 8.7 %collective-permute-start.41 = (f32[72,512]{1,0:T(8,128)S(1)}, f32[72,512]{1,0:T(8,128)S(1)}, u32[]{:S(2)}, u32[]{:S(2)}) collective-permute-start(f32[72,512]{1,0:T(8,128)S(1)} %add.70), channel_id=1, source_target_pairs={{0,2},{1,3},{2,0},{3,1},{4,6},{5,7},{6,4},{7,5},{8,10},{9,11},{10,... | collective-permute-start | bytes 442376 | tf_op jit(solution)/shard_map/ppermute | solution.py:25
  (10 other events, 17.4 us)

commit v7 on v6

--- a/solution.py
+++ b/solution.py
@@ -9,8 +9,7 @@
 
 STEPS = 28
 EPS_NORM = 1e-06
-ATTEND = 6
-ATTEND_MIB = 56
+PROJECT_MIB = 44
 PROJECT = 20
 EARLY = 48
 F32 = jnp.float32
@@ -82,20 +81,18 @@
 OUTWARD = [(1, 0), (2, 3)]
 
 
-def gather_heads(keep, give, others):
+def gather_heads(keep, take, others):
     send = lambda held, route: lax.ppermute(held, "col", route)
-    pair, near = swap(keep, "col", 1), send(keep, MIDDLE)
-    pair, near, give = tie(pair, near, give)
+    join = lambda *held: jnp.concatenate(held, axis=0)
+    keep_pair, keep_near = swap(keep, "col", 1), send(keep, MIDDLE)
+    take_pair, take_near = swap(take, "col", 1), send(take, MIDDLE)
+    keep_pair, keep_near, take_pair, take_near, others = tie(
+        keep_pair, keep_near, take_pair, take_near, others
+    )
+    pair, near = join(keep_pair, take_pair), join(keep_near, take_near)
     near_end, far = send(near, OUTWARD), send(pair, MIDDLE)
-    take = swap(give, "row", 1)
-    take_pair, take_near = swap(take, "col", 1), send(take, MIDDLE)
-    near_end, far, take_pair, take_near = tie(near_end, far, take_pair, take_near)
-    far_end = send(far, OUTWARD)
-    take_end, take_far = send(take_near, OUTWARD), send(take_pair, MIDDLE)
-    far_end, take_end, take_far, *others = tie(far_end, take_end, take_far, *others)
-    first = [keep, pair, near, near_end, far, far_end]
-    second = [take, take_pair, take_near, take_end, take_far, send(take_far, OUTWARD)]
-    return [first, second], others
+    near_end, far = tie(near_end, far)
+    return [join(keep, take), pair, near, near_end, far, send(far, OUTWARD)], others
 
 
 def gather_both(tokens, weights):
@@ -235,7 +232,7 @@
             out_ref[low:high, start:stop] = normed.astype(BF16)
 
 
-def attend(img, txt, head, length_ref, queries, keys, values, out_ref):
+def attend(img, txt, head, length_ref, queries, keys, values, out_refs):
     width = queries.shape[1]
     place = lax.axis_index("row")
     side = lax.rem(place, 2)
@@ -260,7 +257,7 @@
         tail = jnp.where(allowed, score[2 * img :], -1e30)
         return jnp.concatenate([score[: 2 * img], tail], axis=0)
 
-    work = [(k, low) for k in range(width // head) for low in range(0, img, step)]
+    work = [(k, low) for low in range(0, 2 * img, step) for k in range(width // head)]
     ahead = scores_of(*work[0])
     for n, (k, low) in enumerate(work):
         scores = ahead
@@ -268,22 +265,10 @@
             ahead = scores_of(*work[n + 1])
         weights = jnp.exp(scores - jnp.max(scores, axis=0, keepdims=True)).astype(BF16)
         mixed = jnp.dot(rows[k], weights, preferred_element_type=F32)
-        out_ref[k * head : (k + 1) * head, low : low + step] = (
+        out_ref, at = out_refs[low // img], low % img
+        out_ref[k * head : (k + 1) * head, at : at + step] = (
             mixed[:head] / mixed[head : head + 1]
         ).astype(BF16)
-
-
-def attend_kernel(img, txt, head, length_ref, q_ref, k_ref, v_ref, out_ref, *scratch):
-    parts, sems = scratch[:-1], scratch[-1]
-    copies = [
-        pltpu.make_async_copy(ref, part, sems.at[n])
-        for n, (ref, part) in enumerate(zip((q_ref, k_ref, v_ref), parts))
-    ]
-    for copy in copies:
-        copy.start()
-    for copy in copies:
-        copy.wait()
-    attend(img, txt, head, length_ref, *[part[...] for part in parts], out_ref)
 
 
 def project_kernel(routes, masks, img, head, length_ref, q_gain_ref, k_gain_ref, *refs):
@@ -291,8 +276,8 @@
     refs = refs[2 * len(routes) :]
     n_blocks = 2 * len(masks) if masks else 1
     blocks, refs = refs[:n_blocks], refs[n_blocks:]
-    outs, refs = refs[:4], refs[4:]
-    x_ref, w_ref, img_ref, txt_ref, q_ref, k_ref, v_ref, sems_x, sems_w, sems_o = refs
+    outs, refs = refs[:2], refs[2:]
+    x_ref, w_ref, img_ref, txt_ref, q_ref, k_ref, v_ref, sems_x, sems_w = refs
     tokens, wide = lines[0][0].shape
     txt = tokens - img
     count = x_ref.shape[1] // wide
@@ -374,30 +359,22 @@
     k_ref[2 * img :] = head_norm(txt_ref[:, :half], wide_gain(k_gain_ref[1:2]))
     v_ref[: 2 * img] = img_ref[:, 2 * half :].astype(BF16)
     v_ref[2 * img :] = txt_ref[:, half:].astype(BF16)
-    copies = [
-        pltpu.make_async_copy(part, ref, sems_o.at[n])
-        for n, (part, ref) in enumerate(zip((q_ref.at[pl.ds(img, img)], k_ref, v_ref), outs[1:]))
-    ]
-    for copy in copies:
-        copy.start()
-    attend(img, txt, head, length_ref, q_ref[:img], k_ref[...], v_ref[...], outs[0])
-    for copy in copies:
-        copy.wait()
-
-
-def place_heads(lines, routes, col, target, sems):
+    attend(img, txt, head, length_ref, q_ref[...], k_ref[...], v_ref[...], outs)
+
+
+def place_heads(line, routes, col, target, sems):
     core = lax.rem(lax.axis_index("row"), 2)
-    size = lines[0][0].shape[0]
+    size = line[0].shape[0] // 2
     for act in ("start", "wait"):
-        for n, line in enumerate(lines):
+        for n in range(2):
             rows = pl.ds(pl.multiple_of(jnp.where(core == n, 0, size), 16), size)
-            line_copies(line, routes, col, lambda owner: target(owner, rows), sems.at[n], act)
+            parts = [ref.at[pl.ds(n * size, size)] for ref in line]
+            line_copies(parts, routes, col, lambda owner: target(owner, rows), sems.at[n], act)
 
 
 def early_kernel(routes, far, masks, mod_ref, *refs):
     n_lines = len(routes)
-    lines = [refs[n * n_lines : (n + 1) * n_lines] for n in range(2)]
-    refs = refs[2 * n_lines :]
+    line, refs = refs[:n_lines], refs[n_lines:]
     weights, refs = refs[:2], refs[2:]
     sum_ref, far_ref, gain_ref, const_ref, a_ref, w_ref, sems_a, sems_w = refs
     width = sum_ref.shape[0]
@@ -412,7 +389,7 @@
             copies.append(pltpu.make_async_copy(source, target, sems_w.at[k, n]))
     for copy in copies:
         copy.start()
-    place_heads(lines, routes, col, lambda owner, rows: a_ref.at[owner, rows], sems_a)
+    place_heads(line, routes, col, lambda owner, rows: a_ref.at[owner, rows], sems_a)
     for copy in copies:
         copy.wait()
     per_col = w_ref.shape[0] // count
@@ -462,11 +439,10 @@
 
 def late_kernel(routes, mod_ref, x_ref, sum_ref, far_ref, gain_ref, const_ref, *refs):
     n_lines = len(routes)
-    lines = [refs[n * n_lines : (n + 1) * n_lines] for n in range(2)]
-    out_ref, a_ref, sems_a = refs[2 * n_lines :]
+    line, (out_ref, a_ref, sems_a) = refs[:n_lines], refs[n_lines:]
     width, tokens = x_ref.shape
     col = lax.axis_index("col")
-    place_heads(lines, routes, col, lambda owner, rows: a_ref.at[rows], sems_a)
+    place_heads(line, routes, col, lambda owner, rows: a_ref.at[rows], sems_a)
     gate = mod_ref[...].T[:width, 2:3]
     projected = sum_ref[...] + jnp.dot(far_ref[...], a_ref[...], preferred_element_type=F32)
     updated = (x_ref[...].astype(F32) + gate * projected).astype(BF16)
@@ -568,10 +544,9 @@
         masks, blocks = [], [in_order(gathered, "row")]
     heads_out = jax.ShapeDtypeStruct((half, img), BF16)
     full_wide = col_count * wide
-    rest = [jax.ShapeDtypeStruct((rows, half), BF16) for rows in (img, *[2 * (img + txt)] * 2)]
     projected = call(
         functools.partial(project_kernel, routes, masks, img, head),
-        (heads_out, *rest),
+        (heads_out, heads_out),
         [SMEM, VMEM, VMEM] + [HBM] * (2 * len(routes) + len(blocks)),
         [
             pltpu.VMEM((2 * (img + txt), full_wide), BF16),
@@ -582,11 +557,10 @@
             *[pltpu.VMEM((2 * (img + txt), half), BF16)] * 2,
             pltpu.SemaphoreType.DMA((2, 2, len(routes))),
             pltpu.SemaphoreType.DMA((2, col_count)),
-            pltpu.SemaphoreType.DMA((3,)),
         ],
         cost(PROJECT),
-        (VMEM, HBM, HBM, HBM),
-        vmem=56,
+        (VMEM, VMEM),
+        vmem=PROJECT_MIB,
     )(text_len, q_gain[None], k_gain, *line, *peer_line, *blocks)
     head_depth, patch = final_weight.shape
     depth = out_weight.shape[0]
@@ -597,22 +571,14 @@
     masks = list(range(0, row_count, 2))
     out_blocks = direct_gather(out_packed, "row", masks)
 
-    own_heads, *rest = projected
-    give = call(
-        functools.partial(attend_kernel, img, txt, head),
-        heads_out,
-        [SMEM, HBM, HBM, HBM],
-        [pltpu.VMEM(part.shape, BF16) for part in rest] + [pltpu.SemaphoreType.DMA((3,))],
-        cost(ATTEND),
-        vmem=ATTEND_MIB,
-    )(text_len, *rest)
-    others = [out_blocks[k] for k in masks[1:]]
-    if small:
-        lines, others = gather_heads(own_heads, give, others)
-    else:
-        lines = [line_gather(block, "col") for block in (own_heads, swap(give, "row", 1))]
+    keep, give, *others = tie(*projected, *[out_blocks[k] for k in masks[1:]])
     own_rows = jnp.concatenate([out_packed, *others], axis=0)
     other_rows = swap(own_rows, "row", 1)
+    take = swap(give, "row", 1)
+    if small:
+        line, other_rows = gather_heads(keep, take, other_rows)
+    else:
+        line = line_gather(jnp.concatenate([keep, take], axis=0), "col")
     early, late, far = far_routes(col_count)
     sems = pltpu.SemaphoreType.DMA((2, len(routes)))
     bundle = call(
@@ -623,7 +589,7 @@
             jax.ShapeDtypeStruct((3 * patch, width), BF16),
             jax.ShapeDtypeStruct((8, img), F32),
         ),
-        [VMEM] + [HBM] * (2 * len(early) + 2),
+        [VMEM] + [HBM] * (len(early) + 2),
         [
             pltpu.VMEM((col_count, part_cols, img), BF16),
             pltpu.VMEM((row_count,) + out_packed.shape, BF16),
@@ -635,18 +601,18 @@
         vmem=EARLY,
     )(
         mod_own,
-        *[line[k] for line in lines for k, _ in early],
+        *[line[k] for k, _ in early],
         own_rows,
         other_rows,
     )
     partial_sum = call(
         functools.partial(late_kernel, [route for _, route in late]),
         jax.ShapeDtypeStruct((patch + 8, img), F32),
-        [VMEM] * 6 + [HBM] * (2 * len(late)),
+        [VMEM] * 6 + [HBM] * len(late),
         [pltpu.VMEM((part_cols, img), BF16), sems],
         cost(3),
         vmem=24,
-    )(mod_own, hidden_img.T, *bundle, *[line[k] for line in lines for k, _ in late])
+    )(mod_own, hidden_img.T, *bundle, *[line[k] for k, _ in late])
     mask = 1
     while mask < col_count:
         partial_sum = partial_sum + swap(partial_sum, "col", mask)

time: 172 us -> 164 us (0.953)
  starting transfers between devices: 43.1 us -> 36.7 us
  waiting for transfers between devices: 89 us -> 93.7 us
  Pallas kernels: 30.7 us -> 26.5 us
  local copies, waits for them, and re-layouts: 5.09 us -> 3.15 us
    ppermute x8 -> x5, waiting for transfers between devices: 9.77 us -> 24.7 us  [gather_heads(): send = lambda held, route: lax.ppermute(held, 'col', route)]
    ppermute x30, waiting for transfers between devices: 49.3 us -> 38.8 us  [swap(): return lax.ppermute(block, axis, [(i, i ^ mask) for i in range(count)])]
    pallas_call x1 -> x0, Pallas kernels: 6.89 us -> none  [per_device(): call(functools.partial(attend_kernel, img, txt, head), heads_out, [SMEM,...]
    ppermute x8 -> x5, starting transfers between devices: 8.05 us -> 4.82 us  [gather_heads(): send = lambda held, route: lax.ppermute(held, 'col', route)]
    ppermute x30, starting transfers between devices: 30.9 us -> 27.9 us  [swap(): return lax.ppermute(block, axis, [(i, i ^ mask) for i in range(count)])]
    pallas_call x1, Pallas kernels: 16.1 us -> 18.7 us  [per_device(): call(functools.partial(project_kernel, routes, masks, img, head), (heads_...]
    unnamed x68 -> x50, local copies, waits for them, and re-layouts: 4.44 us -> 2.46 us
  transfers between devices with their start and end apart: 42 -> 39, of which waited for: 19 -> 17; matrix products, arithmetic and copies ran while one was open for 0% -> 0% of each run, Pallas kernels for 6% -> 14%
where the time goes in v7:
time: 164 us; the launch traced here: 163 us
  waiting for transfers between devices  93.7 us (57%)
  starting transfers between devices  36.7 us (22%)
  Pallas kernels  26.5 us (16%)
  local copies, waits for them, and re-layouts  3.15 us (2%)
  between operations  2.58 us (2%)
    ppermute x30, waiting for transfers between devices, swap(): return lax.ppermute(block, axis, [(i, i ^ mask) for i in range(count)])  38.8 us
    ppermute x4, waiting for transfers between devices, gather_both(): send = lambda held, route: lax.ppermute(held, 'col', route)  30.1 us
    ppermute x30, starting transfers between devices, swap(): return lax.ppermute(block, axis, [(i, i ^ mask) for i in range(count)])  27.9 us
    ppermute x5, waiting for transfers between devices, gather_heads(): send = lambda held, route: lax.ppermute(held, 'col', route)  24.7 us
    pallas_call x1, Pallas kernels, per_device(): call(functools.partial(project_kernel, routes, masks, img, head), (heads_...  18.7 us
    ppermute x5, starting transfers between devices, gather_heads(): send = lambda held, route: lax.ppermute(held, 'col', route)  4.82 us
    ppermute x4, starting transfers between devices, gather_both(): send = lambda held, route: lax.ppermute(held, 'col', route)  3.98 us
    pallas_call x1, Pallas kernels, per_device(): call(functools.partial(early_kernel, [route for _, route in early], far,...  3.37 us
  transfers between devices with their start and end apart: 39, of which 17 were waited for; matrix products, arithmetic and copies ran while one was open for 0% of the time, Pallas kernels for 14%

profile of v7, /device:TPU:0, one launch (start us, length us, event | category | flops | bytes accessed | tf_op | source)
XLA Modules:
  0.0 163.5 jit_solution(3273839963881288130)
XLA Ops:
  0.6 1.2 copy-done.1
  1.8 1.1 copy-done.3
  2.9 1.9 %shard_map.140 = (bf16[304,1280]{1,0:T(8,128)(2,1)S(1)}, bf16[304,1280]{1,0:T(8,128)(2,1)S(1)}) custom-call(bf16[3,304,512]{2,1,0:T(8,128)(2,1)S(1)} %bitcast.44, bf16[304,2,512]{2,1,0:T(2,128)(2,1)S(1)} %copy-done.3), custom_call_target="tpu_custom_call" | custom-call | flops 2300000000 | tf_op jit(solution)/shard_map/pallas_call | solution.py:512
  4.8 0.5 collective-permute-start
  5.3 0.5 shard_map.141
  5.8 2.6 %collective-permute-start.1 = (f32[8,640]{1,0:T(8,128)S(1)}, f32[8,640]{1,0:T(8,128)S(1)}, u32[]{:S(2)}, u32[]{:S(2)}) collective-permute-start(f32[8,640]{1,0:T(8,128)S(1)} %get-tuple-element.96), channel_id=1, source_target_pairs={{0,8},{4,12},{8,0},{12,4},{16,24},{20,28},{24,16},{28,20},{1,9},{5... | collective-permute-start | bytes 61448 | tf_op jit(solution)/shard_map/ppermute | solution.py:24
  8.4 1.5 collective-permute-start.2
  9.9 0.0 collective-permute-start.3
  10.0 0.2 shard_map.142
  10.2 2.1 %collective-permute-start.5 = (f32[8,640]{1,0:T(8,128)S(1)}, f32[8,640]{1,0:T(8,128)S(1)}, u32[]{:S(2)}, u32[]{:S(2)}) collective-permute-start(f32[8,640]{1,0:T(8,128)S(1)} %shard_map.142), channel_id=1, source_target_pairs={{0,1},{1,0},{2,3},{3,2},{4,5},{5,4},{6,7},{7,6},{8,9},{9,8},{10,11... | collective-permute-start | bytes 61448 | tf_op jit(solution)/shard_map/ppermute | solution.py:24
  12.3 2.6 %collective-permute-start.6 = (f32[8,640]{1,0:T(8,128)S(1)}, f32[8,640]{1,0:T(8,128)S(1)}, u32[]{:S(2)}, u32[]{:S(2)}) collective-permute-start(f32[8,640]{1,0:T(8,128)S(1)} %shard_map.142), channel_id=1, source_target_pairs={{0,2},{1,3},{2,0},{3,1},{4,6},{5,7},{6,4},{7,5},{8,10},{9,11},{10,... | collective-permute-start | bytes 61448 | tf_op jit(solution)/shard_map/ppermute | solution.py:24
  14.9 1.0 collective-permute-start.7
  15.8 0.1 collective-permute-start.4
  15.9 1.1 collective-permute-done.6
  17.1 3.4 %collective-permute-done.7 = f32[8,640]{1,0:T(8,128)S(1)} collective-permute-done((f32[8,640]{1,0:T(8,128)S(1)}, f32[8,640]{1,0:T(8,128)S(1)}, u32[]{:S(2)}, u32[]{:S(2)}) %collective-permute-start.7) | collective-permute-done | bytes 20512 | tf_op jit(solution)/shard_map/ppermute | solution.py:24
  20.5 0.7 shard_map.143.refs_0_
  21.3 0.1 collective-permute-start.8
  21.4 0.7 collective-permute-start.9
  22.1 1.6 collective-permute-start.10
  23.7 1.5 collective-permute-start.11
  25.2 13.5 %collective-permute-done.8.refs_1_ = bf16[608,640]{1,0:T(8,128)(2,1)S(1)} collective-permute-done((bf16[608,640]{1,0:T(8,128)(2,1)S(1)}, bf16[608,640]{1,0:T(8,128)(2,1)S(1)}, u32[]{:S(2)}, u32[]{:S(2)}) %collective-permute-start.8) | collective-permute-done | bytes 778272 | tf_op jit(solution)/shard_map/ppermute | solution.py:24
  38.6 0.8 collective-permute-done.10.refs_14_
  39.4 1.2 collective-permute-done.11.refs_17_
  40.7 1.3 collective-permute-start.12
  42.0 0.7 collective-permute-start.13
  42.7 1.6 collective-permute-start.14
  44.3 0.5 collective-permute-start.15
  44.8 15.0 %collective-permute-done.12.refs_3_ = bf16[608,640]{1,0:T(8,128)(2,1)S(1)} collective-permute-done((bf16[608,640]{1,0:T(8,128)(2,1)S(1)}, bf16[608,640]{1,0:T(8,128)(2,1)S(1)}, u32[]{:S(2)}, u32[]{:S(2)}) %collective-permute-start.12) | collective-permute-done | bytes 778272 | tf_op jit(solution)/shard_map/ppermute | solution.py:99
  59.8 0.3 collective-permute-done.15.refs_18_
  60.1 1.3 collective-permute-start.17
  61.4 1.4 collective-permute-start.18
  62.7 0.6 collective-permute-start.19
  63.3 0.5 collective-permute-start.20
  63.8 15.1 %collective-permute-done.17.refs_5_ = bf16[608,640]{1,0:T(8,128)(2,1)S(1)} collective-permute-done((bf16[608,640]{1,0:T(8,128)(2,1)S(1)}, bf16[608,640]{1,0:T(8,128)(2,1)S(1)}, u32[]{:S(2)}, u32[]{:S(2)}) %collective-permute-start.17) | collective-permute-done | bytes 778272 | tf_op jit(solution)/shard_map/ppermute | solution.py:99
  78.9 0.5 collective-permute-start.22
  79.4 0.1 collective-permute-start.24
  79.6 1.1 collective-permute-start.25
  80.7 0.4 collective-permute-done.21.refs_8_
  81.1 0.6 collective-permute-start.26
  81.8 0.5 collective-permute-done.22.refs_9_
  82.2 1.4 collective-permute-start.27
  83.7 18.7 %shard_map.144 = (bf16[256,512]{1,0:T(8,128)(2,1)S(1)}, bf16[256,512]{1,0:T(8,128)(2,1)S(1)}) custom-call(s32[4]{0:T(128)S(1)} %copy-done.8, f32[1,64]{1,0:T(1,128)S(1)} %bitcast.48, f32[2,64]{1,0:T(2,128)S(1)} %copy-done.7, bf16[608,640]{1,0:T(8,128)(2,1)S(1)} %shard_map.143.refs_0_, bf16[608,640]{1,0:T(8,128)(2,1)S(1)} %collective-permute-done.8.refs_1_, ...), custom_call_target="tpu_custom_call" | custom-call | flops 23000000512 | tf_op jit(solution)/shard_map/pallas_call | solution.py:547
  102.6 0.1 collective-permute-start.33
  102.7 0.5 collective-permute-start.28
  103.1 2.0 %collective-permute-start.29 = (bf16[256,512]{1,0:T(8,128)(2,1)S(1)}, bf16[256,512]{1,0:T(8,128)(2,1)S(1)}, u32[]{:S(2)}, u32[]{:S(2)}) collective-permute-start(bf16[256,512]{1,0:T(8,128)(2,1)S(1)} %get-tuple-element.74), channel_id=1, source_target_pairs={{0,1},{1,0},{2,3},{3,2},{4,5},{5,4},{6,7},{7,6},{8,9},{9,8},{10,11... | collective-permute-start | bytes 786440 | tf_op jit(solution)/shard_map/ppermute | solution.py:24
  105.1 0.7 collective-permute-start.30
  105.8 0.5 collective-permute-done.28
  106.3 2.5 %collective-permute-start.31 = (bf16[256,512]{1,0:T(8,128)(2,1)S(1)}, bf16[256,512]{1,0:T(8,128)(2,1)S(1)}, u32[]{:S(2)}, u32[]{:S(2)}) collective-permute-start(bf16[256,512]{1,0:T(8,128)(2,1)S(1)} %collective-permute-done.28), channel_id=1, source_target_pairs={{0,1},{1,0},{2,3},{3,2},{4,5},{5,4},{6,7},{7,6},{8,9},{9,8},{10,11... | collective-permute-start | bytes 786440 | tf_op jit(solution)/shard_map/ppermute | solution.py:24
  108.9 0.7 collective-permute-start.32
  109.5 2.7 %collective-permute-done.29 = bf16[256,512]{1,0:T(8,128)(2,1)S(1)} collective-permute-done((bf16[256,512]{1,0:T(8,128)(2,1)S(1)}, bf16[256,512]{1,0:T(8,128)(2,1)S(1)}, u32[]{:S(2)}, u32[]{:S(2)}) %collective-permute-start.29) | collective-permute-done | bytes 262176 | tf_op jit(solution)/shard_map/ppermute | solution.py:24
  112.3 5.0 %collective-permute-done.31 = bf16[256,512]{1,0:T(8,128)(2,1)S(1)} collective-permute-done((bf16[256,512]{1,0:T(8,128)(2,1)S(1)}, bf16[256,512]{1,0:T(8,128)(2,1)S(1)}, u32[]{:S(2)}, u32[]{:S(2)}) %collective-permute-start.31) | collective-permute-done | bytes 262176 | tf_op jit(solution)/shard_map/ppermute | solution.py:24
  117.3 1.3 collective-permute-start.34
  118.7 0.7 collective-permute-start.35
  119.5 14.0 %collective-permute-done.34.refs_3_ = bf16[512,512]{1,0:T(8,128)(2,1)S(1)} collective-permute-done((bf16[512,512]{1,0:T(8,128)(2,1)S(1)}, bf16[512,512]{1,0:T(8,128)(2,1)S(1)}, u32[]{:S(2)}, u32[]{:S(2)}) %collective-permute-start.34) | collective-permute-done | bytes 524320 | tf_op jit(solution)/shard_map/ppermute | solution.py:85
  133.5 1.5 collective-permute-start.36
  135.0 3.4 %shard_map.145 = (f32[608,512]{1,0:T(8,128)S(1)}, bf16[608,512]{1,0:T(8,128)(2,1)S(1)}, bf16[192,608]{1,0:T(8,128)(2,1)S(1)}, f32[8,512]{1,0:T(8,128)S(1)}) custom-call(f32[8,640]{1,0:T(8,128)S(1)} %add.66.mod_ref, bf16[512,512]{1,0:T(8,128)(2,1)S(1)} %pad_maximum_fusion.refs_0_, bf16[512,512]{1,0:T(8,128)(2,1)S(1)} %constant_dynamic-update-slice_fusion.5.refs_1_, ...), custom_call_target="tpu_custom_call" | custom-call | flops 5750000128 | tf_op jit(solution)/shard_map/pallas_call | solution.py:584
  138.4 10.7 %collective-permute-done.36.refs_1_ = bf16[512,512]{1,0:T(8,128)(2,1)S(1)} collective-permute-done((bf16[512,512]{1,0:T(8,128)(2,1)S(1)}, bf16[512,512]{1,0:T(8,128)(2,1)S(1)}, u32[]{:S(2)}, u32[]{:S(2)}) %collective-permute-start.36) | collective-permute-done | bytes 524320 | tf_op jit(solution)/shard_map/ppermute | solution.py:85
  149.1 1.1 shard_map.146
  150.2 0.1 collective-permute-start.37
  150.3 5.1 %collective-permute-done.37 = f32[72,512]{1,0:T(8,128)S(1)} collective-permute-done((f32[72,512]{1,0:T(8,128)S(1)}, f32[72,512]{1,0:T(8,128)S(1)}, u32[]{:S(2)}, u32[]{:S(2)}) %collective-permute-start.37) | collective-permute-done | bytes 147488 | tf_op jit(solution)/shard_map/ppermute | solution.py:24
  155.4 1.0 collective-permute-start.38
  156.4 0.6 dynamic_slice.4
  158.4 4.2 %collective-permute-done.38 = f32[72,512]{1,0:T(8,128)S(1)} collective-permute-done((f32[72,512]{1,0:T(8,128)S(1)}, f32[72,512]{1,0:T(8,128)S(1)}, u32[]{:S(2)}, u32[]{:S(2)}) %collective-permute-start.38) | collective-permute-done | bytes 147488 | tf_op jit(solution)/shard_map/ppermute | solution.py:24
  162.7 0.8 fusion.2
  (88 shorter events, 0.5 us)
Async XLA Ops:
  0.6 1.2 copy-start.1
  1.8 1.1 copy-start.3
  2.9 2.4 %copy-start = (bf16[304,7,608]{2,0,1:T(8,128)(2,1)S(1)}, bf16[304,7,608]{2,0,1:T(8,128)(2,1)}, u32[]{:S(2)}) copy-start(bf16[304,7,608]{2,0,1:T(8,128)(2,1)} %param.19) | copy-start | bytes 7762948
  2.9 2.4 %copy-start.6 = (f32[4,304]{1,0:T(4,128)S(1)}, f32[4,304]{1,0:T(4,128)}, u32[]{:S(2)}) copy-start(f32[4,304]{1,0:T(4,128)} %cond_ref.1) | copy-start | bytes 14596
  4.8 37.9 %copy-start.2 = (bf16[304,1280]{1,0:T(8,128)(2,1)}, bf16[304,1280]{1,0:T(8,128)(2,1)S(1)}, u32[]{:S(2)}) copy-start(bf16[304,1280]{1,0:T(8,128)(2,1)S(1)} %get-tuple-element.56.refs_12_) | copy-start | bytes 2334724
  4.8 11.1 %collective-permute-start = (bf16[304,1280]{1,0:T(8,128)(2,1)S(1)}, bf16[304,1280]{1,0:T(8,128)(2,1)S(1)}, u32[]{:S(2)}, u32[]{:S(2)}) collective-permute-start(bf16[304,1280]{1,0:T(8,128)(2,1)S(1)} %get-tuple-element.47), channel_id=1, source_target_pairs={{0,4},{4,0},{8,12},{12,8},{16,20},{20,16},{24,28},{28,24},{1,5},{5... | collective-permute-start | bytes 2334728 | tf_op jit(solution)/shard_map/ppermute | solution.py:24
  5.3 4.7 %copy-start.4 = (bf16[512,608]{0,1:T(8,128)(2,1)S(1)}, bf16[512,608]{0,1:T(8,128)(2,1)}, u32[]{:S(2)}) copy-start(bf16[512,608]{0,1:T(8,128)(2,1)} %param.13) | copy-start | bytes 1867780
  5.3 4.7 %copy-start.5 = (bf16[96,608]{1,0:T(8,128)(2,1)S(1)}, bf16[96,608]{1,0:T(8,128)(2,1)}, u32[]{:S(2)}) copy-start(bf16[96,608]{1,0:T(8,128)(2,1)} %txt_ref.3) | copy-start | bytes 350212
  5.8 6.4 %collective-permute-start.1 = (f32[8,640]{1,0:T(8,128)S(1)}, f32[8,640]{1,0:T(8,128)S(1)}, u32[]{:S(2)}, u32[]{:S(2)}) collective-permute-start(f32[8,640]{1,0:T(8,128)S(1)} %get-tuple-element.96), channel_id=1, source_target_pairs={{0,8},{4,12},{8,0},{12,4},{16,24},{20,28},{24,16},{28,20},{1,9},{5... | collective-permute-start | bytes 61448 | tf_op jit(solution)/shard_map/ppermute | solution.py:24
  8.4 6.4 %collective-permute-start.2 = (f32[8,640]{1,0:T(8,128)S(1)}, f32[8,640]{1,0:T(8,128)S(1)}, u32[]{:S(2)}, u32[]{:S(2)}) collective-permute-start(f32[8,640]{1,0:T(8,128)S(1)} %get-tuple-element.98), channel_id=1, source_target_pairs={{0,16},{4,20},{8,24},{12,28},{16,0},{20,4},{24,8},{28,12},{1,17},{... | collective-permute-start | bytes 61448 | tf_op jit(solution)/shard_map/ppermute | solution.py:24
  9.9 5.9 %collective-permute-start.3 = (f32[8,640]{1,0:T(8,128)S(1)}, f32[8,640]{1,0:T(8,128)S(1)}, u32[]{:S(2)}, u32[]{:S(2)}) collective-permute-start(f32[8,640]{1,0:T(8,128)S(1)} %get-tuple-element.97), channel_id=1, source_target_pairs={{0,24},{4,28},{8,16},{12,20},{16,8},{20,12},{24,0},{28,4},{1,25},{... | collective-permute-start | bytes 61448 | tf_op jit(solution)/shard_map/ppermute | solution.py:24
  10.2 5.8 %collective-permute-start.5 = (f32[8,640]{1,0:T(8,128)S(1)}, f32[8,640]{1,0:T(8,128)S(1)}, u32[]{:S(2)}, u32[]{:S(2)}) collective-permute-start(f32[8,640]{1,0:T(8,128)S(1)} %shard_map.142), channel_id=1, source_target_pairs={{0,1},{1,0},{2,3},{3,2},{4,5},{5,4},{6,7},{7,6},{8,9},{9,8},{10,11... | collective-permute-start | bytes 61448 | tf_op jit(solution)/shard_map/ppermute | solution.py:24
  12.3 4.8 %collective-permute-start.6 = (f32[8,640]{1,0:T(8,128)S(1)}, f32[8,640]{1,0:T(8,128)S(1)}, u32[]{:S(2)}, u32[]{:S(2)}) collective-permute-start(f32[8,640]{1,0:T(8,128)S(1)} %shard_map.142), channel_id=1, source_target_pairs={{0,2},{1,3},{2,0},{3,1},{4,6},{5,7},{6,4},{7,5},{8,10},{9,11},{10,... | collective-permute-start | bytes 61448 | tf_op jit(solution)/shard_map/ppermute | solution.py:24
  14.9 5.6 %collective-permute-start.7 = (f32[8,640]{1,0:T(8,128)S(1)}, f32[8,640]{1,0:T(8,128)S(1)}, u32[]{:S(2)}, u32[]{:S(2)}) collective-permute-start(f32[8,640]{1,0:T(8,128)S(1)} %shard_map.142), channel_id=1, source_target_pairs={{0,3},{1,2},{2,1},{3,0},{4,7},{5,6},{6,5},{7,4},{8,11},{9,10},{10,... | collective-permute-start | bytes 61448 | tf_op jit(solution)/shard_map/ppermute | solution.py:24
  15.8 28.4 %copy-start.14 = (bf16[304,1280]{1,0:T(8,128)(2,1)}, bf16[304,1280]{1,0:T(8,128)(2,1)S(1)}, u32[]{:S(2)}) copy-start(bf16[304,1280]{1,0:T(8,128)(2,1)S(1)} %collective-permute-done.refs_16_) | copy-start | bytes 2334724
  15.8 4.6 %collective-permute-start.4 = (f32[8,640]{1,0:T(8,128)S(1)}, f32[8,640]{1,0:T(8,128)S(1)}, u32[]{:S(2)}, u32[]{:S(2)}) collective-permute-start(f32[8,640]{1,0:T(8,128)S(1)} %fusion.6), channel_id=1, source_target_pairs={{0,4},{4,0},{8,12},{12,8},{16,20},{20,16},{24,28},{28,24},{1,5},{5... | collective-permute-start | bytes 61448 | tf_op jit(solution)/shard_map/ppermute | solution.py:24
  20.5 59.0 %copy-start.12 = (bf16[304,64]{0,1:T(8,128)(2,1)S(1)}, bf16[304,64]{0,1:T(8,128)(2,1)}, u32[]{:S(2)}) copy-start(bf16[304,64]{0,1:T(8,128)(2,1)} %param.25) | copy-start | bytes 116740
  20.5 59.0 %copy-start.10 = (bf16[256,608]{0,1:T(8,128)(2,1)S(1)}, bf16[256,608]{0,1:T(8,128)(2,1)}, u32[]{:S(2)}) copy-start(bf16[256,608]{0,1:T(8,128)(2,1)} %param.24) | copy-start | bytes 933892
  21.2 62.5 %copy-start.7 = (f32[2,64]{1,0:T(2,128)S(1)}, f32[2,64]{1,0:T(2,128)}, u32[]{:S(2)}) copy-start(f32[2,64]{1,0:T(2,128)} %k_gain_ref.1) | copy-start | bytes 1540
  21.3 62.5 %copy-start.8 = (s32[4]{0:T(128)S(1)}, s32[4]{0:T(128)}, u32[]{:S(2)}) copy-start(s32[4]{0:T(128)} %length_ref.1) | copy-start | bytes 52
  21.3 62.5 %copy-start.9 = (f32[64]{0:T(128)S(1)}, f32[64]{0:T(128)}, u32[]{:S(2)}) copy-start(f32[64]{0:T(128)} %param.22) | copy-start | bytes 772
  21.3 17.4 %collective-permute-start.8 = (bf16[608,640]{1,0:T(8,128)(2,1)S(1)}, bf16[608,640]{1,0:T(8,128)(2,1)S(1)}, u32[]{:S(2)}, u32[]{:S(2)}) collective-permute-start(bf16[608,640]{1,0:T(8,128)(2,1)S(1)} %shard_map.143.refs_0_), channel_id=1, source_target_pairs={{0,1},{1,0},{2,3},{3,2},{4,5},{5,4},{6,7},{7,6},{8,9},{9,8},{10,11... | collective-permute-start | bytes 2334728 | tf_op jit(solution)/shard_map/ppermute | solution.py:24
  21.4 17.3 %collective-permute-start.9 = (bf16[608,640]{1,0:T(8,128)(2,1)S(1)}, bf16[608,640]{1,0:T(8,128)(2,1)S(1)}, u32[]{:S(2)}, u32[]{:S(2)}) collective-permute-start(bf16[608,640]{1,0:T(8,128)(2,1)S(1)} %shard_map.143.refs_0_), channel_id=1, source_target_pairs={{1,2},{2,1},{5,6},{6,5},{9,10},{10,9},{13,14},{14,13},{17,18},{18,... | collective-permute-start | bytes 2334728 | tf_op jit(solution)/shard_map/ppermute | solution.py:99
  22.1 17.4 %collective-permute-start.10 = (bf16[304,1280]{1,0:T(8,128)(2,1)S(1)}, bf16[304,1280]{1,0:T(8,128)(2,1)S(1)}, u32[]{:S(2)}, u32[]{:S(2)}) collective-permute-start(bf16[304,1280]{1,0:T(8,128)(2,1)S(1)} %get-tuple-element.56.refs_12_), channel_id=1, source_target_pairs={{0,16},{4,20},{8,24},{12,28},{16,0},{20,4},{24,8},{28,12},{1,17},{... | collective-permute-start | bytes 2334728 | tf_op jit(solution)/shard_map/ppermute | solution.py:24
  23.7 17.0 %collective-permute-start.11 = (bf16[304,1280]{1,0:T(8,128)(2,1)S(1)}, bf16[304,1280]{1,0:T(8,128)(2,1)S(1)}, u32[]{:S(2)}, u32[]{:S(2)}) collective-permute-start(bf16[304,1280]{1,0:T(8,128)(2,1)S(1)} %collective-permute-done.refs_16_), channel_id=1, source_target_pairs={{0,8},{4,12},{8,0},{12,4},{16,24},{20,28},{24,16},{28,20},{1,9},{5... | collective-permute-start | bytes 2334728 | tf_op jit(solution)/shard_map/ppermute | solution.py:24
  25.2 19.6 %collective-permute-start.16 = (bf16[608,640]{1,0:T(8,128)(2,1)S(1)}, bf16[608,640]{1,0:T(8,128)(2,1)S(1)}, u32[]{:S(2)}, u32[]{:S(2)}) collective-permute-start(bf16[608,640]{1,0:T(8,128)(2,1)S(1)} %shard_map.143.refs_0_), channel_id=1, source_target_pairs={{0,4},{4,0},{8,12},{12,8},{16,20},{20,16},{24,28},{28,24},{1,5},{5... | collective-permute-start | bytes 2334728 | tf_op jit(solution)/shard_map/ppermute | solution.py:24
  39.4 44.2 %copy-start.15 = (bf16[304,1280]{1,0:T(8,128)(2,1)}, bf16[304,1280]{1,0:T(8,128)(2,1)S(1)}, u32[]{:S(2)}) copy-start(bf16[304,1280]{1,0:T(8,128)(2,1)S(1)} %collective-permute-done.10.refs_14_) | copy-start | bytes 2334724
  40.7 43.0 %copy-start.16 = (bf16[304,1280]{1,0:T(8,128)(2,1)}, bf16[304,1280]{1,0:T(8,128)(2,1)S(1)}, u32[]{:S(2)}) copy-start(bf16[304,1280]{1,0:T(8,128)(2,1)S(1)} %collective-permute-done.11.refs_17_) | copy-start | bytes 2334724
  40.7 19.1 %collective-permute-start.12 = (bf16[608,640]{1,0:T(8,128)(2,1)S(1)}, bf16[608,640]{1,0:T(8,128)(2,1)S(1)}, u32[]{:S(2)}, u32[]{:S(2)}) collective-permute-start(bf16[608,640]{1,0:T(8,128)(2,1)S(1)} %collective-permute-done.9.refs_2_), channel_id=1, source_target_pairs={{1,0},{2,3},{5,4},{6,7},{9,8},{10,11},{13,12},{14,15},{17,16},{18,... | collective-permute-start | bytes 2334728 | tf_op jit(solution)/shard_map/ppermute | solution.py:99
  42.0 17.8 %collective-permute-start.13 = (bf16[608,640]{1,0:T(8,128)(2,1)S(1)}, bf16[608,640]{1,0:T(8,128)(2,1)S(1)}, u32[]{:S(2)}, u32[]{:S(2)}) collective-permute-start(bf16[608,640]{1,0:T(8,128)(2,1)S(1)} %collective-permute-done.8.refs_1_), channel_id=1, source_target_pairs={{1,2},{2,1},{5,6},{6,5},{9,10},{10,9},{13,14},{14,13},{17,18},{18,... | collective-permute-start | bytes 2334728 | tf_op jit(solution)/shard_map/ppermute | solution.py:99
  42.7 17.1 %collective-permute-start.14 = (bf16[304,1280]{1,0:T(8,128)(2,1)S(1)}, bf16[304,1280]{1,0:T(8,128)(2,1)S(1)}, u32[]{:S(2)}, u32[]{:S(2)}) collective-permute-start(bf16[304,1280]{1,0:T(8,128)(2,1)S(1)} %get-tuple-element.56.refs_12_), channel_id=1, source_target_pairs={{0,8},{4,12},{8,0},{12,4},{16,24},{20,28},{24,16},{28,20},{1,9},{5... | collective-permute-start | bytes 2334728 | tf_op jit(solution)/shard_map/ppermute | solution.py:24
  44.3 15.8 %collective-permute-start.15 = (bf16[304,1280]{1,0:T(8,128)(2,1)S(1)}, bf16[304,1280]{1,0:T(8,128)(2,1)S(1)}, u32[]{:S(2)}, u32[]{:S(2)}) collective-permute-start(bf16[304,1280]{1,0:T(8,128)(2,1)S(1)} %collective-permute-done.refs_16_), channel_id=1, source_target_pairs={{0,16},{4,20},{8,24},{12,28},{16,0},{20,4},{24,8},{28,12},{1,17},{... | collective-permute-start | bytes 2334728 | tf_op jit(solution)/shard_map/ppermute | solution.py:24
  59.8 23.9 %copy-start.17 = (bf16[304,1280]{1,0:T(8,128)(2,1)}, bf16[304,1280]{1,0:T(8,128)(2,1)S(1)}, u32[]{:S(2)}) copy-start(bf16[304,1280]{1,0:T(8,128)(2,1)S(1)} %collective-permute-done.14.refs_13_) | copy-start | bytes 2334724
  60.1 23.6 %copy-start.18 = (bf16[304,1280]{1,0:T(8,128)(2,1)}, bf16[304,1280]{1,0:T(8,128)(2,1)S(1)}, u32[]{:S(2)}) copy-start(bf16[304,1280]{1,0:T(8,128)(2,1)S(1)} %collective-permute-done.15.refs_18_) | copy-start | bytes 2334724
  60.1 18.8 %collective-permute-start.17 = (bf16[608,640]{1,0:T(8,128)(2,1)S(1)}, bf16[608,640]{1,0:T(8,128)(2,1)S(1)}, u32[]{:S(2)}, u32[]{:S(2)}) collective-permute-start(bf16[608,640]{1,0:T(8,128)(2,1)S(1)} %collective-permute-done.13.refs_4_), channel_id=1, source_target_pairs={{1,0},{2,3},{5,4},{6,7},{9,8},{10,11},{13,12},{14,15},{17,16},{18,... | collective-permute-start | bytes 2334728 | tf_op jit(solution)/shard_map/ppermute | solution.py:99
  61.4 17.5 %collective-permute-start.18 = (bf16[304,1280]{1,0:T(8,128)(2,1)S(1)}, bf16[304,1280]{1,0:T(8,128)(2,1)S(1)}, u32[]{:S(2)}, u32[]{:S(2)}) collective-permute-start(bf16[304,1280]{1,0:T(8,128)(2,1)S(1)} %collective-permute-done.10.refs_14_), channel_id=1, source_target_pairs={{0,8},{4,12},{8,0},{12,4},{16,24},{20,28},{24,16},{28,20},{1,9},{5... | collective-permute-start | bytes 2334728 | tf_op jit(solution)/shard_map/ppermute | solution.py:24
  62.7 16.7 %collective-permute-start.19 = (bf16[304,1280]{1,0:T(8,128)(2,1)S(1)}, bf16[304,1280]{1,0:T(8,128)(2,1)S(1)}, u32[]{:S(2)}, u32[]{:S(2)}) collective-permute-start(bf16[304,1280]{1,0:T(8,128)(2,1)S(1)} %collective-permute-done.11.refs_17_), channel_id=1, source_target_pairs={{0,16},{4,20},{8,24},{12,28},{16,0},{20,4},{24,8},{28,12},{1,17},{... | collective-permute-start | bytes 2334728 | tf_op jit(solution)/shard_map/ppermute | solution.py:24
  63.3 20.4 %collective-permute-start.23 = (bf16[608,640]{1,0:T(8,128)(2,1)S(1)}, bf16[608,640]{1,0:T(8,128)(2,1)S(1)}, u32[]{:S(2)}, u32[]{:S(2)}) collective-permute-start(bf16[608,640]{1,0:T(8,128)(2,1)S(1)} %collective-permute-done.13.refs_4_), channel_id=1, source_target_pairs={{0,4},{4,0},{8,12},{12,8},{16,20},{20,16},{24,28},{28,24},{1,5},{5... | collective-permute-start | bytes 2334728 | tf_op jit(solution)/shard_map/ppermute | solution.py:24
  63.3 16.3 %collective-permute-start.20 = (bf16[608,640]{1,0:T(8,128)(2,1)S(1)}, bf16[608,640]{1,0:T(8,128)(2,1)S(1)}, u32[]{:S(2)}, u32[]{:S(2)}) collective-permute-start(bf16[608,640]{1,0:T(8,128)(2,1)S(1)} %collective-permute-done.8.refs_1_), channel_id=1, source_target_pairs={{0,4},{4,0},{8,12},{12,8},{16,20},{20,16},{24,28},{28,24},{1,5},{5... | collective-permute-start | bytes 2334728 | tf_op jit(solution)/shard_map/ppermute | solution.py:24
  78.9 2.3 %collective-permute-start.21 = (bf16[608,640]{1,0:T(8,128)(2,1)S(1)}, bf16[608,640]{1,0:T(8,128)(2,1)S(1)}, u32[]{:S(2)}, u32[]{:S(2)}) collective-permute-start(bf16[608,640]{1,0:T(8,128)(2,1)S(1)} %collective-permute-done.9.refs_2_), channel_id=1, source_target_pairs={{0,4},{4,0},{8,12},{12,8},{16,20},{20,16},{24,28},{28,24},{1,5},{5... | collective-permute-start | bytes 2334728 | tf_op jit(solution)/shard_map/ppermute | solution.py:24
  78.9 4.8 %copy-start.19 = (bf16[304,1280]{1,0:T(8,128)(2,1)}, bf16[304,1280]{1,0:T(8,128)(2,1)S(1)}, u32[]{:S(2)}) copy-start(bf16[304,1280]{1,0:T(8,128)(2,1)S(1)} %collective-permute-done.18.refs_15_) | copy-start | bytes 2334724
  78.9 3.4 %collective-permute-start.22 = (bf16[608,640]{1,0:T(8,128)(2,1)S(1)}, bf16[608,640]{1,0:T(8,128)(2,1)S(1)}, u32[]{:S(2)}, u32[]{:S(2)}) collective-permute-start(bf16[608,640]{1,0:T(8,128)(2,1)S(1)} %collective-permute-done.12.refs_3_), channel_id=1, source_target_pairs={{0,4},{4,0},{8,12},{12,8},{16,20},{20,16},{24,28},{28,24},{1,5},{5... | collective-permute-start | bytes 2334728 | tf_op jit(solution)/shard_map/ppermute | solution.py:24
  79.4 4.3 %copy-start.20 = (bf16[304,1280]{1,0:T(8,128)(2,1)}, bf16[304,1280]{1,0:T(8,128)(2,1)S(1)}, u32[]{:S(2)}) copy-start(bf16[304,1280]{1,0:T(8,128)(2,1)S(1)} %collective-permute-done.19.refs_19_) | copy-start | bytes 2334724
  79.4 4.3 %collective-permute-start.24 = (bf16[608,640]{1,0:T(8,128)(2,1)S(1)}, bf16[608,640]{1,0:T(8,128)(2,1)S(1)}, u32[]{:S(2)}, u32[]{:S(2)}) collective-permute-start(bf16[608,640]{1,0:T(8,128)(2,1)S(1)} %collective-permute-done.17.refs_5_), channel_id=1, source_target_pairs={{0,4},{4,0},{8,12},{12,8},{16,20},{20,16},{24,28},{28,24},{1,5},{5... | collective-permute-start | bytes 2334728 | tf_op jit(solution)/shard_map/ppermute | solution.py:24
  79.6 22.8 %collective-permute-start.25 = (bf16[736,256]{1,0:T(8,128)(2,1)S(1)}, bf16[736,256]{1,0:T(8,128)(2,1)S(1)}, u32[]{:S(2)}, u32[]{:S(2)}) collective-permute-start(bf16[736,256]{1,0:T(8,128)(2,1)S(1)} %pad_maximum_fusion.1), channel_id=1, source_target_pairs={{0,8},{4,12},{8,0},{12,4},{16,24},{20,28},{24,16},{28,20},{1,9},{5... | collective-permute-start | bytes 1130504 | tf_op jit(solution)/shard_map/ppermute | solution.py:24
  81.1 21.3 %collective-permute-start.26 = (bf16[736,256]{1,0:T(8,128)(2,1)S(1)}, bf16[736,256]{1,0:T(8,128)(2,1)S(1)}, u32[]{:S(2)}, u32[]{:S(2)}) collective-permute-start(bf16[736,256]{1,0:T(8,128)(2,1)S(1)} %pad_maximum_fusion.1), channel_id=1, source_target_pairs={{0,16},{4,20},{8,24},{12,28},{16,0},{20,4},{24,8},{28,12},{1,17},{... | collective-permute-start | bytes 1130504 | tf_op jit(solution)/shard_map/ppermute | solution.py:24
  82.2 20.2 %collective-permute-start.27 = (bf16[736,256]{1,0:T(8,128)(2,1)S(1)}, bf16[736,256]{1,0:T(8,128)(2,1)S(1)}, u32[]{:S(2)}, u32[]{:S(2)}) collective-permute-start(bf16[736,256]{1,0:T(8,128)(2,1)S(1)} %pad_maximum_fusion.1), channel_id=1, source_target_pairs={{0,24},{4,28},{8,16},{12,20},{16,8},{20,12},{24,0},{28,4},{1,25},{... | collective-permute-start | bytes 1130504 | tf_op jit(solution)/shard_map/ppermute | solution.py:24
  102.6 14.7 %collective-permute-start.33 = (bf16[2944,256]{1,0:T(8,128)(2,1)S(1)}, bf16[2944,256]{1,0:T(8,128)(2,1)S(1)}, u32[]{:S(2)}, u32[]{:S(2)}) collective-permute-start(bf16[2944,256]{1,0:T(8,128)(2,1)S(1)} %constant_dynamic-update-slice_fusion.refs_4_), channel_id=1, source_target_pairs={{0,4},{4,0},{8,12},{12,8},{16,20},{20,16},{24,28},{28,24},{1,5},{5... | collective-permute-start | bytes 4521992 | tf_op jit(solution)/shard_map/ppermute | solution.py:24
  102.7 3.7 %collective-permute-start.28 = (bf16[256,512]{1,0:T(8,128)(2,1)S(1)}, bf16[256,512]{1,0:T(8,128)(2,1)S(1)}, u32[]{:S(2)}, u32[]{:S(2)}) collective-permute-start(bf16[256,512]{1,0:T(8,128)(2,1)S(1)} %get-tuple-element.75), channel_id=1, source_target_pairs={{0,4},{4,0},{8,12},{12,8},{16,20},{20,16},{24,28},{28,24},{1,5},{5... | collective-permute-start | bytes 786440 | tf_op jit(solution)/shard_map/ppermute | solution.py:24
  103.1 9.1 %collective-permute-start.29 = (bf16[256,512]{1,0:T(8,128)(2,1)S(1)}, bf16[256,512]{1,0:T(8,128)(2,1)S(1)}, u32[]{:S(2)}, u32[]{:S(2)}) collective-permute-start(bf16[256,512]{1,0:T(8,128)(2,1)S(1)} %get-tuple-element.74), channel_id=1, source_target_pairs={{0,1},{1,0},{2,3},{3,2},{4,5},{5,4},{6,7},{7,6},{8,9},{9,8},{10,11... | collective-permute-start | bytes 786440 | tf_op jit(solution)/shard_map/ppermute | solution.py:24
  105.1 7.2 %collective-permute-start.30 = (bf16[256,512]{1,0:T(8,128)(2,1)S(1)}, bf16[256,512]{1,0:T(8,128)(2,1)S(1)}, u32[]{:S(2)}, u32[]{:S(2)}) collective-permute-start(bf16[256,512]{1,0:T(8,128)(2,1)S(1)} %get-tuple-element.74), channel_id=1, source_target_pairs={{1,2},{2,1},{5,6},{6,5},{9,10},{10,9},{13,14},{14,13},{17,18},{18,... | collective-permute-start | bytes 786440 | tf_op jit(solution)/shard_map/ppermute | solution.py:85
  106.3 10.9 %collective-permute-start.31 = (bf16[256,512]{1,0:T(8,128)(2,1)S(1)}, bf16[256,512]{1,0:T(8,128)(2,1)S(1)}, u32[]{:S(2)}, u32[]{:S(2)}) collective-permute-start(bf16[256,512]{1,0:T(8,128)(2,1)S(1)} %collective-permute-done.28), channel_id=1, source_target_pairs={{0,1},{1,0},{2,3},{3,2},{4,5},{5,4},{6,7},{7,6},{8,9},{9,8},{10,11... | collective-permute-start | bytes 786440 | tf_op jit(solution)/shard_map/ppermute | solution.py:24
  108.9 8.4 %collective-permute-start.32 = (bf16[256,512]{1,0:T(8,128)(2,1)S(1)}, bf16[256,512]{1,0:T(8,128)(2,1)S(1)}, u32[]{:S(2)}, u32[]{:S(2)}) collective-permute-start(bf16[256,512]{1,0:T(8,128)(2,1)S(1)} %collective-permute-done.28), channel_id=1, source_target_pairs={{1,2},{2,1},{5,6},{6,5},{9,10},{10,9},{13,14},{14,13},{17,18},{18,... | collective-permute-start | bytes 786440 | tf_op jit(solution)/shard_map/ppermute | solution.py:85
  117.3 2.2 %copy-start.13 = (bf16[2944,256]{1,0:T(8,128)(2,1)}, bf16[2944,256]{1,0:T(8,128)(2,1)S(1)}, u32[]{:S(2)}) copy-start(bf16[2944,256]{1,0:T(8,128)(2,1)S(1)} %collective-permute-done.33.refs_5_) | copy-start | bytes 4521988
  117.3 16.2 %collective-permute-start.34 = (bf16[512,512]{1,0:T(8,128)(2,1)S(1)}, bf16[512,512]{1,0:T(8,128)(2,1)S(1)}, u32[]{:S(2)}, u32[]{:S(2)}) collective-permute-start(bf16[512,512]{1,0:T(8,128)(2,1)S(1)} %constant_dynamic-update-slice_fusion.7.refs_2_), channel_id=1, source_target_pairs={{1,0},{2,3},{5,4},{6,7},{9,8},{10,11},{13,12},{14,15},{17,16},{18,... | collective-permute-start | bytes 1572872 | tf_op jit(solution)/shard_map/ppermute | solution.py:85
  118.7 14.8 %collective-permute-start.35 = (bf16[512,512]{1,0:T(8,128)(2,1)S(1)}, bf16[512,512]{1,0:T(8,128)(2,1)S(1)}, u32[]{:S(2)}, u32[]{:S(2)}) collective-permute-start(bf16[512,512]{1,0:T(8,128)(2,1)S(1)} %constant_dynamic-update-slice_fusion.5.refs_1_), channel_id=1, source_target_pairs={{1,2},{2,1},{5,6},{6,5},{9,10},{10,9},{13,14},{14,13},{17,18},{18,... | collective-permute-start | bytes 1572872 | tf_op jit(solution)/shard_map/ppermute | solution.py:85
  133.5 15.6 %collective-permute-start.36 = (bf16[512,512]{1,0:T(8,128)(2,1)S(1)}, bf16[512,512]{1,0:T(8,128)(2,1)S(1)}, u32[]{:S(2)}, u32[]{:S(2)}) collective-permute-start(bf16[512,512]{1,0:T(8,128)(2,1)S(1)} %collective-permute-done.35.refs_0_), channel_id=1, source_target_pairs={{1,0},{2,3},{5,4},{6,7},{9,8},{10,11},{13,12},{14,15},{17,16},{18,... | collective-permute-start | bytes 1572872 | tf_op jit(solution)/shard_map/ppermute | solution.py:85
  149.1 7.4 %copy-start.21 = (s32[4]{0:T(128)S(1)}, s32[4]{0:T(128)}, u32[]{:S(2)}) copy-start(s32[4]{0:T(128)} %param.16) | copy-start | bytes 52
  149.1 13.6 %copy-start.11 = (f32[512,64]{0,1:T(8,128)S(1)}, f32[512,64]{0,1:T(8,128)}, u32[]{:S(2)}) copy-start(f32[512,64]{0,1:T(8,128)} %param.17) | copy-start | bytes 393220
  150.2 5.2 %collective-permute-start.37 = (f32[72,512]{1,0:T(8,128)S(1)}, f32[72,512]{1,0:T(8,128)S(1)}, u32[]{:S(2)}, u32[]{:S(2)}) collective-permute-start(f32[72,512]{1,0:T(8,128)S(1)} %shard_map.146), channel_id=1, source_target_pairs={{0,1},{1,0},{2,3},{3,2},{4,5},{5,4},{6,7},{7,6},{8,9},{9,8},{10,11... | collective-permute-start | bytes 442376 | tf_op jit(solution)/shard_map/ppermute | solution.py:24
  155.4 7.2 %collective-permute-start.38 = (f32[72,512]{1,0:T(8,128)S(1)}, f32[72,512]{1,0:T(8,128)S(1)}, u32[]{:S(2)}, u32[]{:S(2)}) collective-permute-start(f32[72,512]{1,0:T(8,128)S(1)} %add.70), channel_id=1, source_target_pairs={{0,2},{1,3},{2,0},{3,1},{4,6},{5,7},{6,4},{7,5},{8,10},{9,11},{10,... | collective-permute-start | bytes 442376 | tf_op jit(solution)/shard_map/ppermute | solution.py:24

commit v8 on v7

--- a/solution.py
+++ b/solution.py
@@ -11,7 +11,7 @@
 EPS_NORM = 1e-06
 PROJECT_MIB = 44
 PROJECT = 20
-EARLY = 48
+EARLY = 32
 F32 = jnp.float32
 BF16 = jnp.bfloat16
 HBM = pl.BlockSpec(memory_space=pltpu.HBM)
@@ -312,8 +312,9 @@
                 ref = blocks[piece * len(masks) + k]
                 copy = pltpu.make_async_copy(ref, target, sems_w.at[piece, k])
                 stages[2 * k // count].append(copy)
-    for copy in stages[0]:
+    for copy in stages[0] + stages[1]:
         copy.start()
+    copy_line(1, "start")
     for k in range(count):
         if wide > width:
             w_ref[k * wide + width : (k + 1) * wide] = jnp.zeros((wide - width, 5 * half), BF16)
@@ -335,11 +336,6 @@
     for k in range(2):
         for copy in stages[k]:
             copy.wait()
-        if k == 0:
-            for copy in stages[1]:
-                copy.start()
-        else:
-            copy_line(1, "start")
         if not masks:
             here = pl.ds(k * depth, depth)
         else:

time: 164 us -> 163 us (level)
  transfers between devices with their start and end apart: 39 -> 39, of which waited for: 17 -> 17; matrix products, arithmetic and copies ran while one was open for 0% -> 0% of each run, Pallas kernels for 14% -> 13%
where the time goes in v8:
time: 163 us; the launch traced here: 162 us
  waiting for transfers between devices  94.4 us (58%)
  starting transfers between devices  36.3 us (22%)
  Pallas kernels  25 us (15%)
  local copies, waits for them, and re-layouts  3.15 us (2%)
  between operations  2.56 us (2%)
    ppermute x30, waiting for transfers between devices, swap(): return lax.ppermute(block, axis, [(i, i ^ mask) for i in range(count)])  39.1 us
    ppermute x4, waiting for transfers between devices, gather_both(): send = lambda held, route: lax.ppermute(held, 'col', route)  30.1 us
    ppermute x30, starting transfers between devices, swap(): return lax.ppermute(block, axis, [(i, i ^ mask) for i in range(count)])  27.7 us
    ppermute x5, waiting for transfers between devices, gather_heads(): send = lambda held, route: lax.ppermute(held, 'col', route)  25.2 us
    pallas_call x1, Pallas kernels, per_device(): call(functools.partial(project_kernel, routes, masks, img, head), (heads_...  17.7 us
    ppermute x5, starting transfers between devices, gather_heads(): send = lambda held, route: lax.ppermute(held, 'col', route)  4.6 us
    ppermute x4, starting transfers between devices, gather_both(): send = lambda held, route: lax.ppermute(held, 'col', route)  3.98 us
  transfers between devices with their start and end apart: 39, of which 17 were waited for; matrix products, arithmetic and copies ran while one was open for 0% of the time, Pallas kernels for 13%

profile of v8, /device:TPU:0, one launch (start us, length us, event | category | flops | bytes accessed | tf_op | source)
XLA Modules:
  0.0 162.3 jit_solution(3981502081948709255)
XLA Ops:
  0.6 1.2 copy-done.1
  1.8 1.1 copy-done.3
  2.9 1.9 %shard_map.140 = (bf16[304,1280]{1,0:T(8,128)(2,1)S(1)}, bf16[304,1280]{1,0:T(8,128)(2,1)S(1)}) custom-call(bf16[3,304,512]{2,1,0:T(8,128)(2,1)S(1)} %bitcast.44, bf16[304,2,512]{2,1,0:T(2,128)(2,1)S(1)} %copy-done.3), custom_call_target="tpu_custom_call" | custom-call | flops 2300000000 | tf_op jit(solution)/shard_map/pallas_call | solution.py:508
  4.8 0.5 collective-permute-start
  5.3 0.5 shard_map.141
  5.8 2.6 %collective-permute-start.1 = (f32[8,640]{1,0:T(8,128)S(1)}, f32[8,640]{1,0:T(8,128)S(1)}, u32[]{:S(2)}, u32[]{:S(2)}) collective-permute-start(f32[8,640]{1,0:T(8,128)S(1)} %get-tuple-element.96), channel_id=1, source_target_pairs={{0,8},{4,12},{8,0},{12,4},{16,24},{20,28},{24,16},{28,20},{1,9},{5... | collective-permute-start | bytes 61448 | tf_op jit(solution)/shard_map/ppermute | solution.py:24
  8.4 1.5 collective-permute-start.2
  9.9 0.0 collective-permute-start.3
  10.0 0.2 shard_map.142
  10.2 2.1 %collective-permute-start.5 = (f32[8,640]{1,0:T(8,128)S(1)}, f32[8,640]{1,0:T(8,128)S(1)}, u32[]{:S(2)}, u32[]{:S(2)}) collective-permute-start(f32[8,640]{1,0:T(8,128)S(1)} %shard_map.142), channel_id=1, source_target_pairs={{0,1},{1,0},{2,3},{3,2},{4,5},{5,4},{6,7},{7,6},{8,9},{9,8},{10,11... | collective-permute-start | bytes 61448 | tf_op jit(solution)/shard_map/ppermute | solution.py:24
  12.3 2.6 %collective-permute-start.6 = (f32[8,640]{1,0:T(8,128)S(1)}, f32[8,640]{1,0:T(8,128)S(1)}, u32[]{:S(2)}, u32[]{:S(2)}) collective-permute-start(f32[8,640]{1,0:T(8,128)S(1)} %shard_map.142), channel_id=1, source_target_pairs={{0,2},{1,3},{2,0},{3,1},{4,6},{5,7},{6,4},{7,5},{8,10},{9,11},{10,... | collective-permute-start | bytes 61448 | tf_op jit(solution)/shard_map/ppermute | solution.py:24
  14.9 1.0 collective-permute-start.7
  15.8 0.1 collective-permute-start.4
  15.9 1.1 collective-permute-done.6
  17.1 3.4 %collective-permute-done.7 = f32[8,640]{1,0:T(8,128)S(1)} collective-permute-done((f32[8,640]{1,0:T(8,128)S(1)}, f32[8,640]{1,0:T(8,128)S(1)}, u32[]{:S(2)}, u32[]{:S(2)}) %collective-permute-start.7) | collective-permute-done | bytes 20512 | tf_op jit(solution)/shard_map/ppermute | solution.py:24
  20.5 0.7 shard_map.143.refs_0_
  21.3 0.1 collective-permute-start.8
  21.4 0.7 collective-permute-start.9
  22.1 1.6 collective-permute-start.10
  23.7 1.5 collective-permute-start.11
  25.2 13.5 %collective-permute-done.8.refs_1_ = bf16[608,640]{1,0:T(8,128)(2,1)S(1)} collective-permute-done((bf16[608,640]{1,0:T(8,128)(2,1)S(1)}, bf16[608,640]{1,0:T(8,128)(2,1)S(1)}, u32[]{:S(2)}, u32[]{:S(2)}) %collective-permute-start.8) | collective-permute-done | bytes 778272 | tf_op jit(solution)/shard_map/ppermute | solution.py:24
  38.6 0.8 collective-permute-done.10.refs_14_
  39.4 1.2 collective-permute-done.11.refs_17_
  40.7 1.3 collective-permute-start.12
  42.0 0.7 collective-permute-start.13
  42.7 1.6 collective-permute-start.14
  44.3 0.5 collective-permute-start.15
  44.8 15.0 %collective-permute-done.12.refs_3_ = bf16[608,640]{1,0:T(8,128)(2,1)S(1)} collective-permute-done((bf16[608,640]{1,0:T(8,128)(2,1)S(1)}, bf16[608,640]{1,0:T(8,128)(2,1)S(1)}, u32[]{:S(2)}, u32[]{:S(2)}) %collective-permute-start.12) | collective-permute-done | bytes 778272 | tf_op jit(solution)/shard_map/ppermute | solution.py:99
  59.8 0.3 collective-permute-done.15.refs_18_
  60.1 1.3 collective-permute-start.17
  61.4 1.4 collective-permute-start.18
  62.7 0.6 collective-permute-start.19
  63.3 0.5 collective-permute-start.20
  63.8 15.1 %collective-permute-done.17.refs_5_ = bf16[608,640]{1,0:T(8,128)(2,1)S(1)} collective-permute-done((bf16[608,640]{1,0:T(8,128)(2,1)S(1)}, bf16[608,640]{1,0:T(8,128)(2,1)S(1)}, u32[]{:S(2)}, u32[]{:S(2)}) %collective-permute-start.17) | collective-permute-done | bytes 778272 | tf_op jit(solution)/shard_map/ppermute | solution.py:99
  78.9 0.5 collective-permute-start.22
  79.4 0.1 collective-permute-start.24
  79.6 1.1 collective-permute-start.25
  80.7 0.4 collective-permute-done.21.refs_8_
  81.1 0.6 collective-permute-start.26
  81.8 0.5 collective-permute-done.22.refs_9_
  82.2 1.4 collective-permute-start.27
  83.7 17.7 %shard_map.144 = (bf16[256,512]{1,0:T(8,128)(2,1)S(1)}, bf16[256,512]{1,0:T(8,128)(2,1)S(1)}) custom-call(s32[4]{0:T(128)S(1)} %copy-done.8, f32[1,64]{1,0:T(1,128)S(1)} %bitcast.48, f32[2,64]{1,0:T(2,128)S(1)} %copy-done.7, bf16[608,640]{1,0:T(8,128)(2,1)S(1)} %shard_map.143.refs_0_, bf16[608,640]{1,0:T(8,128)(2,1)S(1)} %collective-permute-done.8.refs_1_, ...), custom_call_target="tpu_custom_call" | custom-call | flops 23000000512 | tf_op jit(solution)/shard_map/pallas_call | solution.py:543
  101.6 0.1 collective-permute-start.33
  101.7 0.5 collective-permute-start.28
  102.2 2.0 %collective-permute-start.29 = (bf16[256,512]{1,0:T(8,128)(2,1)S(1)}, bf16[256,512]{1,0:T(8,128)(2,1)S(1)}, u32[]{:S(2)}, u32[]{:S(2)}) collective-permute-start(bf16[256,512]{1,0:T(8,128)(2,1)S(1)} %get-tuple-element.74), channel_id=1, source_target_pairs={{0,1},{1,0},{2,3},{3,2},{4,5},{5,4},{6,7},{7,6},{8,9},{9,8},{10,11... | collective-permute-start | bytes 786440 | tf_op jit(solution)/shard_map/ppermute | solution.py:24
  104.1 0.7 collective-permute-start.30
  104.8 0.6 collective-permute-done.28
  105.3 2.5 %collective-permute-start.31 = (bf16[256,512]{1,0:T(8,128)(2,1)S(1)}, bf16[256,512]{1,0:T(8,128)(2,1)S(1)}, u32[]{:S(2)}, u32[]{:S(2)}) collective-permute-start(bf16[256,512]{1,0:T(8,128)(2,1)S(1)} %collective-permute-done.28), channel_id=1, source_target_pairs={{0,1},{1,0},{2,3},{3,2},{4,5},{5,4},{6,7},{7,6},{8,9},{9,8},{10,11... | collective-permute-start | bytes 786440 | tf_op jit(solution)/shard_map/ppermute | solution.py:24
  107.9 0.7 collective-permute-start.32
  108.6 2.7 %collective-permute-done.29 = bf16[256,512]{1,0:T(8,128)(2,1)S(1)} collective-permute-done((bf16[256,512]{1,0:T(8,128)(2,1)S(1)}, bf16[256,512]{1,0:T(8,128)(2,1)S(1)}, u32[]{:S(2)}, u32[]{:S(2)}) %collective-permute-start.29) | collective-permute-done | bytes 262176 | tf_op jit(solution)/shard_map/ppermute | solution.py:24
  111.3 5.0 %collective-permute-done.31 = bf16[256,512]{1,0:T(8,128)(2,1)S(1)} collective-permute-done((bf16[256,512]{1,0:T(8,128)(2,1)S(1)}, bf16[256,512]{1,0:T(8,128)(2,1)S(1)}, u32[]{:S(2)}, u32[]{:S(2)}) %collective-permute-start.31) | collective-permute-done | bytes 262176 | tf_op jit(solution)/shard_map/ppermute | solution.py:24
  116.3 1.3 collective-permute-start.34
  117.7 0.7 collective-permute-start.35
  118.4 14.0 %collective-permute-done.34.refs_3_ = bf16[512,512]{1,0:T(8,128)(2,1)S(1)} collective-permute-done((bf16[512,512]{1,0:T(8,128)(2,1)S(1)}, bf16[512,512]{1,0:T(8,128)(2,1)S(1)}, u32[]{:S(2)}, u32[]{:S(2)}) %collective-permute-start.34) | collective-permute-done | bytes 524320 | tf_op jit(solution)/shard_map/ppermute | solution.py:85
  132.5 1.3 collective-permute-start.36
  133.8 2.9 %shard_map.145 = (f32[608,512]{1,0:T(8,128)S(1)}, bf16[608,512]{1,0:T(8,128)(2,1)S(1)}, bf16[192,608]{1,0:T(8,128)(2,1)S(1)}, f32[8,512]{1,0:T(8,128)S(1)}) custom-call(f32[8,640]{1,0:T(8,128)S(1)} %add.66.mod_ref, bf16[512,512]{1,0:T(8,128)(2,1)S(1)} %pad_maximum_fusion.refs_0_, bf16[512,512]{1,0:T(8,128)(2,1)S(1)} %constant_dynamic-update-slice_fusion.5.refs_1_, ...), custom_call_target="tpu_custom_call" | custom-call | flops 5750000128 | tf_op jit(solution)/shard_map/pallas_call | solution.py:580
  136.7 11.2 %collective-permute-done.36.refs_1_ = bf16[512,512]{1,0:T(8,128)(2,1)S(1)} collective-permute-done((bf16[512,512]{1,0:T(8,128)(2,1)S(1)}, bf16[512,512]{1,0:T(8,128)(2,1)S(1)}, u32[]{:S(2)}, u32[]{:S(2)}) %collective-permute-start.36) | collective-permute-done | bytes 524320 | tf_op jit(solution)/shard_map/ppermute | solution.py:85
  147.8 1.1 shard_map.146
  148.9 0.1 collective-permute-start.37
  149.0 5.1 %collective-permute-done.37 = f32[72,512]{1,0:T(8,128)S(1)} collective-permute-done((f32[72,512]{1,0:T(8,128)S(1)}, f32[72,512]{1,0:T(8,128)S(1)}, u32[]{:S(2)}, u32[]{:S(2)}) %collective-permute-start.37) | collective-permute-done | bytes 147488 | tf_op jit(solution)/shard_map/ppermute | solution.py:24
  154.2 0.9 collective-permute-start.38
  155.0 0.6 dynamic_slice.4
  157.0 4.4 %collective-permute-done.38 = f32[72,512]{1,0:T(8,128)S(1)} collective-permute-done((f32[72,512]{1,0:T(8,128)S(1)}, f32[72,512]{1,0:T(8,128)S(1)}, u32[]{:S(2)}, u32[]{:S(2)}) %collective-permute-start.38) | collective-permute-done | bytes 147488 | tf_op jit(solution)/shard_map/ppermute | solution.py:24
  161.5 0.8 fusion.2
  (86 shorter events, 0.5 us)
Async XLA Ops:
  0.6 1.2 copy-start.1
  1.8 1.1 copy-start.3
  2.9 2.4 %copy-start = (bf16[304,7,608]{2,0,1:T(8,128)(2,1)S(1)}, bf16[304,7,608]{2,0,1:T(8,128)(2,1)}, u32[]{:S(2)}) copy-start(bf16[304,7,608]{2,0,1:T(8,128)(2,1)} %param.19) | copy-start | bytes 7762948
  2.9 2.4 %copy-start.6 = (f32[4,304]{1,0:T(4,128)S(1)}, f32[4,304]{1,0:T(4,128)}, u32[]{:S(2)}) copy-start(f32[4,304]{1,0:T(4,128)} %cond_ref.1) | copy-start | bytes 14596
  4.8 37.9 %copy-start.2 = (bf16[304,1280]{1,0:T(8,128)(2,1)}, bf16[304,1280]{1,0:T(8,128)(2,1)S(1)}, u32[]{:S(2)}) copy-start(bf16[304,1280]{1,0:T(8,128)(2,1)S(1)} %get-tuple-element.56.refs_12_) | copy-start | bytes 2334724
  4.8 11.1 %collective-permute-start = (bf16[304,1280]{1,0:T(8,128)(2,1)S(1)}, bf16[304,1280]{1,0:T(8,128)(2,1)S(1)}, u32[]{:S(2)}, u32[]{:S(2)}) collective-permute-start(bf16[304,1280]{1,0:T(8,128)(2,1)S(1)} %get-tuple-element.47), channel_id=1, source_target_pairs={{0,4},{4,0},{8,12},{12,8},{16,20},{20,16},{24,28},{28,24},{1,5},{5... | collective-permute-start | bytes 2334728 | tf_op jit(solution)/shard_map/ppermute | solution.py:24
  5.3 4.7 %copy-start.4 = (bf16[512,608]{0,1:T(8,128)(2,1)S(1)}, bf16[512,608]{0,1:T(8,128)(2,1)}, u32[]{:S(2)}) copy-start(bf16[512,608]{0,1:T(8,128)(2,1)} %param.13) | copy-start | bytes 1867780
  5.3 4.7 %copy-start.5 = (bf16[96,608]{1,0:T(8,128)(2,1)S(1)}, bf16[96,608]{1,0:T(8,128)(2,1)}, u32[]{:S(2)}) copy-start(bf16[96,608]{1,0:T(8,128)(2,1)} %txt_ref.3) | copy-start | bytes 350212
  5.8 6.4 %collective-permute-start.1 = (f32[8,640]{1,0:T(8,128)S(1)}, f32[8,640]{1,0:T(8,128)S(1)}, u32[]{:S(2)}, u32[]{:S(2)}) collective-permute-start(f32[8,640]{1,0:T(8,128)S(1)} %get-tuple-element.96), channel_id=1, source_target_pairs={{0,8},{4,12},{8,0},{12,4},{16,24},{20,28},{24,16},{28,20},{1,9},{5... | collective-permute-start | bytes 61448 | tf_op jit(solution)/shard_map/ppermute | solution.py:24
  8.4 6.4 %collective-permute-start.2 = (f32[8,640]{1,0:T(8,128)S(1)}, f32[8,640]{1,0:T(8,128)S(1)}, u32[]{:S(2)}, u32[]{:S(2)}) collective-permute-start(f32[8,640]{1,0:T(8,128)S(1)} %get-tuple-element.98), channel_id=1, source_target_pairs={{0,16},{4,20},{8,24},{12,28},{16,0},{20,4},{24,8},{28,12},{1,17},{... | collective-permute-start | bytes 61448 | tf_op jit(solution)/shard_map/ppermute | solution.py:24
  9.9 5.9 %collective-permute-start.3 = (f32[8,640]{1,0:T(8,128)S(1)}, f32[8,640]{1,0:T(8,128)S(1)}, u32[]{:S(2)}, u32[]{:S(2)}) collective-permute-start(f32[8,640]{1,0:T(8,128)S(1)} %get-tuple-element.97), channel_id=1, source_target_pairs={{0,24},{4,28},{8,16},{12,20},{16,8},{20,12},{24,0},{28,4},{1,25},{... | collective-permute-start | bytes 61448 | tf_op jit(solution)/shard_map/ppermute | solution.py:24
  10.2 5.8 %collective-permute-start.5 = (f32[8,640]{1,0:T(8,128)S(1)}, f32[8,640]{1,0:T(8,128)S(1)}, u32[]{:S(2)}, u32[]{:S(2)}) collective-permute-start(f32[8,640]{1,0:T(8,128)S(1)} %shard_map.142), channel_id=1, source_target_pairs={{0,1},{1,0},{2,3},{3,2},{4,5},{5,4},{6,7},{7,6},{8,9},{9,8},{10,11... | collective-permute-start | bytes 61448 | tf_op jit(solution)/shard_map/ppermute | solution.py:24
  12.3 4.8 %collective-permute-start.6 = (f32[8,640]{1,0:T(8,128)S(1)}, f32[8,640]{1,0:T(8,128)S(1)}, u32[]{:S(2)}, u32[]{:S(2)}) collective-permute-start(f32[8,640]{1,0:T(8,128)S(1)} %shard_map.142), channel_id=1, source_target_pairs={{0,2},{1,3},{2,0},{3,1},{4,6},{5,7},{6,4},{7,5},{8,10},{9,11},{10,... | collective-permute-start | bytes 61448 | tf_op jit(solution)/shard_map/ppermute | solution.py:24
  14.9 5.6 %collective-permute-start.7 = (f32[8,640]{1,0:T(8,128)S(1)}, f32[8,640]{1,0:T(8,128)S(1)}, u32[]{:S(2)}, u32[]{:S(2)}) collective-permute-start(f32[8,640]{1,0:T(8,128)S(1)} %shard_map.142), channel_id=1, source_target_pairs={{0,3},{1,2},{2,1},{3,0},{4,7},{5,6},{6,5},{7,4},{8,11},{9,10},{10,... | collective-permute-start | bytes 61448 | tf_op jit(solution)/shard_map/ppermute | solution.py:24
  15.8 28.4 %copy-start.13 = (bf16[304,1280]{1,0:T(8,128)(2,1)}, bf16[304,1280]{1,0:T(8,128)(2,1)S(1)}, u32[]{:S(2)}) copy-start(bf16[304,1280]{1,0:T(8,128)(2,1)S(1)} %collective-permute-done.refs_16_) | copy-start | bytes 2334724
  15.8 4.6 %collective-permute-start.4 = (f32[8,640]{1,0:T(8,128)S(1)}, f32[8,640]{1,0:T(8,128)S(1)}, u32[]{:S(2)}, u32[]{:S(2)}) collective-permute-start(f32[8,640]{1,0:T(8,128)S(1)} %fusion.6), channel_id=1, source_target_pairs={{0,4},{4,0},{8,12},{12,8},{16,20},{20,16},{24,28},{28,24},{1,5},{5... | collective-permute-start | bytes 61448 | tf_op jit(solution)/shard_map/ppermute | solution.py:24
  20.5 59.0 %copy-start.12 = (bf16[304,64]{0,1:T(8,128)(2,1)S(1)}, bf16[304,64]{0,1:T(8,128)(2,1)}, u32[]{:S(2)}) copy-start(bf16[304,64]{0,1:T(8,128)(2,1)} %param.25) | copy-start | bytes 116740
  20.5 59.0 %copy-start.10 = (bf16[256,608]{0,1:T(8,128)(2,1)S(1)}, bf16[256,608]{0,1:T(8,128)(2,1)}, u32[]{:S(2)}) copy-start(bf16[256,608]{0,1:T(8,128)(2,1)} %param.24) | copy-start | bytes 933892
  21.2 62.5 %copy-start.7 = (f32[2,64]{1,0:T(2,128)S(1)}, f32[2,64]{1,0:T(2,128)}, u32[]{:S(2)}) copy-start(f32[2,64]{1,0:T(2,128)} %k_gain_ref.1) | copy-start | bytes 1540
  21.3 62.5 %copy-start.8 = (s32[4]{0:T(128)S(1)}, s32[4]{0:T(128)}, u32[]{:S(2)}) copy-start(s32[4]{0:T(128)} %length_ref.1) | copy-start | bytes 52
  21.3 62.5 %copy-start.9 = (f32[64]{0:T(128)S(1)}, f32[64]{0:T(128)}, u32[]{:S(2)}) copy-start(f32[64]{0:T(128)} %param.22) | copy-start | bytes 772
  21.3 17.4 %collective-permute-start.8 = (bf16[608,640]{1,0:T(8,128)(2,1)S(1)}, bf16[608,640]{1,0:T(8,128)(2,1)S(1)}, u32[]{:S(2)}, u32[]{:S(2)}) collective-permute-start(bf16[608,640]{1,0:T(8,128)(2,1)S(1)} %shard_map.143.refs_0_), channel_id=1, source_target_pairs={{0,1},{1,0},{2,3},{3,2},{4,5},{5,4},{6,7},{7,6},{8,9},{9,8},{10,11... | collective-permute-start | bytes 2334728 | tf_op jit(solution)/shard_map/ppermute | solution.py:24
  21.4 17.3 %collective-permute-start.9 = (bf16[608,640]{1,0:T(8,128)(2,1)S(1)}, bf16[608,640]{1,0:T(8,128)(2,1)S(1)}, u32[]{:S(2)}, u32[]{:S(2)}) collective-permute-start(bf16[608,640]{1,0:T(8,128)(2,1)S(1)} %shard_map.143.refs_0_), channel_id=1, source_target_pairs={{1,2},{2,1},{5,6},{6,5},{9,10},{10,9},{13,14},{14,13},{17,18},{18,... | collective-permute-start | bytes 2334728 | tf_op jit(solution)/shard_map/ppermute | solution.py:99
  22.1 17.4 %collective-permute-start.10 = (bf16[304,1280]{1,0:T(8,128)(2,1)S(1)}, bf16[304,1280]{1,0:T(8,128)(2,1)S(1)}, u32[]{:S(2)}, u32[]{:S(2)}) collective-permute-start(bf16[304,1280]{1,0:T(8,128)(2,1)S(1)} %get-tuple-element.56.refs_12_), channel_id=1, source_target_pairs={{0,16},{4,20},{8,24},{12,28},{16,0},{20,4},{24,8},{28,12},{1,17},{... | collective-permute-start | bytes 2334728 | tf_op jit(solution)/shard_map/ppermute | solution.py:24
  23.7 17.0 %collective-permute-start.11 = (bf16[304,1280]{1,0:T(8,128)(2,1)S(1)}, bf16[304,1280]{1,0:T(8,128)(2,1)S(1)}, u32[]{:S(2)}, u32[]{:S(2)}) collective-permute-start(bf16[304,1280]{1,0:T(8,128)(2,1)S(1)} %collective-permute-done.refs_16_), channel_id=1, source_target_pairs={{0,8},{4,12},{8,0},{12,4},{16,24},{20,28},{24,16},{28,20},{1,9},{5... | collective-permute-start | bytes 2334728 | tf_op jit(solution)/shard_map/ppermute | solution.py:24
  25.2 19.6 %collective-permute-start.16 = (bf16[608,640]{1,0:T(8,128)(2,1)S(1)}, bf16[608,640]{1,0:T(8,128)(2,1)S(1)}, u32[]{:S(2)}, u32[]{:S(2)}) collective-permute-start(bf16[608,640]{1,0:T(8,128)(2,1)S(1)} %shard_map.143.refs_0_), channel_id=1, source_target_pairs={{0,4},{4,0},{8,12},{12,8},{16,20},{20,16},{24,28},{28,24},{1,5},{5... | collective-permute-start | bytes 2334728 | tf_op jit(solution)/shard_map/ppermute | solution.py:24
  39.4 44.2 %copy-start.14 = (bf16[304,1280]{1,0:T(8,128)(2,1)}, bf16[304,1280]{1,0:T(8,128)(2,1)S(1)}, u32[]{:S(2)}) copy-start(bf16[304,1280]{1,0:T(8,128)(2,1)S(1)} %collective-permute-done.10.refs_14_) | copy-start | bytes 2334724
  40.7 43.0 %copy-start.15 = (bf16[304,1280]{1,0:T(8,128)(2,1)}, bf16[304,1280]{1,0:T(8,128)(2,1)S(1)}, u32[]{:S(2)}) copy-start(bf16[304,1280]{1,0:T(8,128)(2,1)S(1)} %collective-permute-done.11.refs_17_) | copy-start | bytes 2334724
  40.7 19.1 %collective-permute-start.12 = (bf16[608,640]{1,0:T(8,128)(2,1)S(1)}, bf16[608,640]{1,0:T(8,128)(2,1)S(1)}, u32[]{:S(2)}, u32[]{:S(2)}) collective-permute-start(bf16[608,640]{1,0:T(8,128)(2,1)S(1)} %collective-permute-done.9.refs_2_), channel_id=1, source_target_pairs={{1,0},{2,3},{5,4},{6,7},{9,8},{10,11},{13,12},{14,15},{17,16},{18,... | collective-permute-start | bytes 2334728 | tf_op jit(solution)/shard_map/ppermute | solution.py:99
  42.0 17.8 %collective-permute-start.13 = (bf16[608,640]{1,0:T(8,128)(2,1)S(1)}, bf16[608,640]{1,0:T(8,128)(2,1)S(1)}, u32[]{:S(2)}, u32[]{:S(2)}) collective-permute-start(bf16[608,640]{1,0:T(8,128)(2,1)S(1)} %collective-permute-done.8.refs_1_), channel_id=1, source_target_pairs={{1,2},{2,1},{5,6},{6,5},{9,10},{10,9},{13,14},{14,13},{17,18},{18,... | collective-permute-start | bytes 2334728 | tf_op jit(solution)/shard_map/ppermute | solution.py:99
  42.7 17.1 %collective-permute-start.14 = (bf16[304,1280]{1,0:T(8,128)(2,1)S(1)}, bf16[304,1280]{1,0:T(8,128)(2,1)S(1)}, u32[]{:S(2)}, u32[]{:S(2)}) collective-permute-start(bf16[304,1280]{1,0:T(8,128)(2,1)S(1)} %get-tuple-element.56.refs_12_), channel_id=1, source_target_pairs={{0,8},{4,12},{8,0},{12,4},{16,24},{20,28},{24,16},{28,20},{1,9},{5... | collective-permute-start | bytes 2334728 | tf_op jit(solution)/shard_map/ppermute | solution.py:24
  44.3 15.8 %collective-permute-start.15 = (bf16[304,1280]{1,0:T(8,128)(2,1)S(1)}, bf16[304,1280]{1,0:T(8,128)(2,1)S(1)}, u32[]{:S(2)}, u32[]{:S(2)}) collective-permute-start(bf16[304,1280]{1,0:T(8,128)(2,1)S(1)} %collective-permute-done.refs_16_), channel_id=1, source_target_pairs={{0,16},{4,20},{8,24},{12,28},{16,0},{20,4},{24,8},{28,12},{1,17},{... | collective-permute-start | bytes 2334728 | tf_op jit(solution)/shard_map/ppermute | solution.py:24
  59.8 23.9 %copy-start.16 = (bf16[304,1280]{1,0:T(8,128)(2,1)}, bf16[304,1280]{1,0:T(8,128)(2,1)S(1)}, u32[]{:S(2)}) copy-start(bf16[304,1280]{1,0:T(8,128)(2,1)S(1)} %collective-permute-done.14.refs_13_) | copy-start | bytes 2334724
  60.1 23.6 %copy-start.17 = (bf16[304,1280]{1,0:T(8,128)(2,1)}, bf16[304,1280]{1,0:T(8,128)(2,1)S(1)}, u32[]{:S(2)}) copy-start(bf16[304,1280]{1,0:T(8,128)(2,1)S(1)} %collective-permute-done.15.refs_18_) | copy-start | bytes 2334724
  60.1 18.8 %collective-permute-start.17 = (bf16[608,640]{1,0:T(8,128)(2,1)S(1)}, bf16[608,640]{1,0:T(8,128)(2,1)S(1)}, u32[]{:S(2)}, u32[]{:S(2)}) collective-permute-start(bf16[608,640]{1,0:T(8,128)(2,1)S(1)} %collective-permute-done.13.refs_4_), channel_id=1, source_target_pairs={{1,0},{2,3},{5,4},{6,7},{9,8},{10,11},{13,12},{14,15},{17,16},{18,... | collective-permute-start | bytes 2334728 | tf_op jit(solution)/shard_map/ppermute | solution.py:99
  61.4 17.5 %collective-permute-start.18 = (bf16[304,1280]{1,0:T(8,128)(2,1)S(1)}, bf16[304,1280]{1,0:T(8,128)(2,1)S(1)}, u32[]{:S(2)}, u32[]{:S(2)}) collective-permute-start(bf16[304,1280]{1,0:T(8,128)(2,1)S(1)} %collective-permute-done.10.refs_14_), channel_id=1, source_target_pairs={{0,8},{4,12},{8,0},{12,4},{16,24},{20,28},{24,16},{28,20},{1,9},{5... | collective-permute-start | bytes 2334728 | tf_op jit(solution)/shard_map/ppermute | solution.py:24
  62.7 16.7 %collective-permute-start.19 = (bf16[304,1280]{1,0:T(8,128)(2,1)S(1)}, bf16[304,1280]{1,0:T(8,128)(2,1)S(1)}, u32[]{:S(2)}, u32[]{:S(2)}) collective-permute-start(bf16[304,1280]{1,0:T(8,128)(2,1)S(1)} %collective-permute-done.11.refs_17_), channel_id=1, source_target_pairs={{0,16},{4,20},{8,24},{12,28},{16,0},{20,4},{24,8},{28,12},{1,17},{... | collective-permute-start | bytes 2334728 | tf_op jit(solution)/shard_map/ppermute | solution.py:24
  63.3 20.4 %collective-permute-start.23 = (bf16[608,640]{1,0:T(8,128)(2,1)S(1)}, bf16[608,640]{1,0:T(8,128)(2,1)S(1)}, u32[]{:S(2)}, u32[]{:S(2)}) collective-permute-start(bf16[608,640]{1,0:T(8,128)(2,1)S(1)} %collective-permute-done.13.refs_4_), channel_id=1, source_target_pairs={{0,4},{4,0},{8,12},{12,8},{16,20},{20,16},{24,28},{28,24},{1,5},{5... | collective-permute-start | bytes 2334728 | tf_op jit(solution)/shard_map/ppermute | solution.py:24
  63.3 16.3 %collective-permute-start.20 = (bf16[608,640]{1,0:T(8,128)(2,1)S(1)}, bf16[608,640]{1,0:T(8,128)(2,1)S(1)}, u32[]{:S(2)}, u32[]{:S(2)}) collective-permute-start(bf16[608,640]{1,0:T(8,128)(2,1)S(1)} %collective-permute-done.8.refs_1_), channel_id=1, source_target_pairs={{0,4},{4,0},{8,12},{12,8},{16,20},{20,16},{24,28},{28,24},{1,5},{5... | collective-permute-start | bytes 2334728 | tf_op jit(solution)/shard_map/ppermute | solution.py:24
  78.9 2.3 %collective-permute-start.21 = (bf16[608,640]{1,0:T(8,128)(2,1)S(1)}, bf16[608,640]{1,0:T(8,128)(2,1)S(1)}, u32[]{:S(2)}, u32[]{:S(2)}) collective-permute-start(bf16[608,640]{1,0:T(8,128)(2,1)S(1)} %collective-permute-done.9.refs_2_), channel_id=1, source_target_pairs={{0,4},{4,0},{8,12},{12,8},{16,20},{20,16},{24,28},{28,24},{1,5},{5... | collective-permute-start | bytes 2334728 | tf_op jit(solution)/shard_map/ppermute | solution.py:24
  78.9 4.8 %copy-start.18 = (bf16[304,1280]{1,0:T(8,128)(2,1)}, bf16[304,1280]{1,0:T(8,128)(2,1)S(1)}, u32[]{:S(2)}) copy-start(bf16[304,1280]{1,0:T(8,128)(2,1)S(1)} %collective-permute-done.18.refs_15_) | copy-start | bytes 2334724
  78.9 3.4 %collective-permute-start.22 = (bf16[608,640]{1,0:T(8,128)(2,1)S(1)}, bf16[608,640]{1,0:T(8,128)(2,1)S(1)}, u32[]{:S(2)}, u32[]{:S(2)}) collective-permute-start(bf16[608,640]{1,0:T(8,128)(2,1)S(1)} %collective-permute-done.12.refs_3_), channel_id=1, source_target_pairs={{0,4},{4,0},{8,12},{12,8},{16,20},{20,16},{24,28},{28,24},{1,5},{5... | collective-permute-start | bytes 2334728 | tf_op jit(solution)/shard_map/ppermute | solution.py:24
  79.4 4.3 %copy-start.19 = (bf16[304,1280]{1,0:T(8,128)(2,1)}, bf16[304,1280]{1,0:T(8,128)(2,1)S(1)}, u32[]{:S(2)}) copy-start(bf16[304,1280]{1,0:T(8,128)(2,1)S(1)} %collective-permute-done.19.refs_19_) | copy-start | bytes 2334724
  79.4 4.3 %collective-permute-start.24 = (bf16[608,640]{1,0:T(8,128)(2,1)S(1)}, bf16[608,640]{1,0:T(8,128)(2,1)S(1)}, u32[]{:S(2)}, u32[]{:S(2)}) collective-permute-start(bf16[608,640]{1,0:T(8,128)(2,1)S(1)} %collective-permute-done.17.refs_5_), channel_id=1, source_target_pairs={{0,4},{4,0},{8,12},{12,8},{16,20},{20,16},{24,28},{28,24},{1,5},{5... | collective-permute-start | bytes 2334728 | tf_op jit(solution)/shard_map/ppermute | solution.py:24
  79.6 21.9 %collective-permute-start.25 = (bf16[736,256]{1,0:T(8,128)(2,1)S(1)}, bf16[736,256]{1,0:T(8,128)(2,1)S(1)}, u32[]{:S(2)}, u32[]{:S(2)}) collective-permute-start(bf16[736,256]{1,0:T(8,128)(2,1)S(1)} %pad_maximum_fusion.1), channel_id=1, source_target_pairs={{0,8},{4,12},{8,0},{12,4},{16,24},{20,28},{24,16},{28,20},{1,9},{5... | collective-permute-start | bytes 1130504 | tf_op jit(solution)/shard_map/ppermute | solution.py:24
  81.1 20.3 %collective-permute-start.26 = (bf16[736,256]{1,0:T(8,128)(2,1)S(1)}, bf16[736,256]{1,0:T(8,128)(2,1)S(1)}, u32[]{:S(2)}, u32[]{:S(2)}) collective-permute-start(bf16[736,256]{1,0:T(8,128)(2,1)S(1)} %pad_maximum_fusion.1), channel_id=1, source_target_pairs={{0,16},{4,20},{8,24},{12,28},{16,0},{20,4},{24,8},{28,12},{1,17},{... | collective-permute-start | bytes 1130504 | tf_op jit(solution)/shard_map/ppermute | solution.py:24
  82.2 19.2 %collective-permute-start.27 = (bf16[736,256]{1,0:T(8,128)(2,1)S(1)}, bf16[736,256]{1,0:T(8,128)(2,1)S(1)}, u32[]{:S(2)}, u32[]{:S(2)}) collective-permute-start(bf16[736,256]{1,0:T(8,128)(2,1)S(1)} %pad_maximum_fusion.1), channel_id=1, source_target_pairs={{0,24},{4,28},{8,16},{12,20},{16,8},{20,12},{24,0},{28,4},{1,25},{... | collective-permute-start | bytes 1130504 | tf_op jit(solution)/shard_map/ppermute | solution.py:24
  101.6 14.7 %collective-permute-start.33 = (bf16[2944,256]{1,0:T(8,128)(2,1)S(1)}, bf16[2944,256]{1,0:T(8,128)(2,1)S(1)}, u32[]{:S(2)}, u32[]{:S(2)}) collective-permute-start(bf16[2944,256]{1,0:T(8,128)(2,1)S(1)} %constant_dynamic-update-slice_fusion.refs_4_), channel_id=1, source_target_pairs={{0,4},{4,0},{8,12},{12,8},{16,20},{20,16},{24,28},{28,24},{1,5},{5... | collective-permute-start | bytes 4521992 | tf_op jit(solution)/shard_map/ppermute | solution.py:24
  101.7 3.7 %collective-permute-start.28 = (bf16[256,512]{1,0:T(8,128)(2,1)S(1)}, bf16[256,512]{1,0:T(8,128)(2,1)S(1)}, u32[]{:S(2)}, u32[]{:S(2)}) collective-permute-start(bf16[256,512]{1,0:T(8,128)(2,1)S(1)} %get-tuple-element.75), channel_id=1, source_target_pairs={{0,4},{4,0},{8,12},{12,8},{16,20},{20,16},{24,28},{28,24},{1,5},{5... | collective-permute-start | bytes 786440 | tf_op jit(solution)/shard_map/ppermute | solution.py:24
  102.2 9.1 %collective-permute-start.29 = (bf16[256,512]{1,0:T(8,128)(2,1)S(1)}, bf16[256,512]{1,0:T(8,128)(2,1)S(1)}, u32[]{:S(2)}, u32[]{:S(2)}) collective-permute-start(bf16[256,512]{1,0:T(8,128)(2,1)S(1)} %get-tuple-element.74), channel_id=1, source_target_pairs={{0,1},{1,0},{2,3},{3,2},{4,5},{5,4},{6,7},{7,6},{8,9},{9,8},{10,11... | collective-permute-start | bytes 786440 | tf_op jit(solution)/shard_map/ppermute | solution.py:24
  104.1 7.2 %collective-permute-start.30 = (bf16[256,512]{1,0:T(8,128)(2,1)S(1)}, bf16[256,512]{1,0:T(8,128)(2,1)S(1)}, u32[]{:S(2)}, u32[]{:S(2)}) collective-permute-start(bf16[256,512]{1,0:T(8,128)(2,1)S(1)} %get-tuple-element.74), channel_id=1, source_target_pairs={{1,2},{2,1},{5,6},{6,5},{9,10},{10,9},{13,14},{14,13},{17,18},{18,... | collective-permute-start | bytes 786440 | tf_op jit(solution)/shard_map/ppermute | solution.py:85
  105.3 10.9 %collective-permute-start.31 = (bf16[256,512]{1,0:T(8,128)(2,1)S(1)}, bf16[256,512]{1,0:T(8,128)(2,1)S(1)}, u32[]{:S(2)}, u32[]{:S(2)}) collective-permute-start(bf16[256,512]{1,0:T(8,128)(2,1)S(1)} %collective-permute-done.28), channel_id=1, source_target_pairs={{0,1},{1,0},{2,3},{3,2},{4,5},{5,4},{6,7},{7,6},{8,9},{9,8},{10,11... | collective-permute-start | bytes 786440 | tf_op jit(solution)/shard_map/ppermute | solution.py:24
  107.9 8.4 %collective-permute-start.32 = (bf16[256,512]{1,0:T(8,128)(2,1)S(1)}, bf16[256,512]{1,0:T(8,128)(2,1)S(1)}, u32[]{:S(2)}, u32[]{:S(2)}) collective-permute-start(bf16[256,512]{1,0:T(8,128)(2,1)S(1)} %collective-permute-done.28), channel_id=1, source_target_pairs={{1,2},{2,1},{5,6},{6,5},{9,10},{10,9},{13,14},{14,13},{17,18},{18,... | collective-permute-start | bytes 786440 | tf_op jit(solution)/shard_map/ppermute | solution.py:85
  116.3 16.1 %collective-permute-start.34 = (bf16[512,512]{1,0:T(8,128)(2,1)S(1)}, bf16[512,512]{1,0:T(8,128)(2,1)S(1)}, u32[]{:S(2)}, u32[]{:S(2)}) collective-permute-start(bf16[512,512]{1,0:T(8,128)(2,1)S(1)} %constant_dynamic-update-slice_fusion.7.refs_2_), channel_id=1, source_target_pairs={{1,0},{2,3},{5,4},{6,7},{9,8},{10,11},{13,12},{14,15},{17,16},{18,... | collective-permute-start | bytes 1572872 | tf_op jit(solution)/shard_map/ppermute | solution.py:85
  117.7 14.8 %collective-permute-start.35 = (bf16[512,512]{1,0:T(8,128)(2,1)S(1)}, bf16[512,512]{1,0:T(8,128)(2,1)S(1)}, u32[]{:S(2)}, u32[]{:S(2)}) collective-permute-start(bf16[512,512]{1,0:T(8,128)(2,1)S(1)} %constant_dynamic-update-slice_fusion.5.refs_1_), channel_id=1, source_target_pairs={{1,2},{2,1},{5,6},{6,5},{9,10},{10,9},{13,14},{14,13},{17,18},{18,... | collective-permute-start | bytes 1572872 | tf_op jit(solution)/shard_map/ppermute | solution.py:85
  132.5 15.3 %collective-permute-start.36 = (bf16[512,512]{1,0:T(8,128)(2,1)S(1)}, bf16[512,512]{1,0:T(8,128)(2,1)S(1)}, u32[]{:S(2)}, u32[]{:S(2)}) collective-permute-start(bf16[512,512]{1,0:T(8,128)(2,1)S(1)} %collective-permute-done.35.refs_0_), channel_id=1, source_target_pairs={{1,0},{2,3},{5,4},{6,7},{9,8},{10,11},{13,12},{14,15},{17,16},{18,... | collective-permute-start | bytes 1572872 | tf_op jit(solution)/shard_map/ppermute | solution.py:85
  147.8 7.2 %copy-start.20 = (s32[4]{0:T(128)S(1)}, s32[4]{0:T(128)}, u32[]{:S(2)}) copy-start(s32[4]{0:T(128)} %param.16) | copy-start | bytes 52
  147.8 13.7 %copy-start.11 = (f32[512,64]{0,1:T(8,128)S(1)}, f32[512,64]{0,1:T(8,128)}, u32[]{:S(2)}) copy-start(f32[512,64]{0,1:T(8,128)} %param.17) | copy-start | bytes 393220
  148.9 5.2 %collective-permute-start.37 = (f32[72,512]{1,0:T(8,128)S(1)}, f32[72,512]{1,0:T(8,128)S(1)}, u32[]{:S(2)}, u32[]{:S(2)}) collective-permute-start(f32[72,512]{1,0:T(8,128)S(1)} %shard_map.146), channel_id=1, source_target_pairs={{0,1},{1,0},{2,3},{3,2},{4,5},{5,4},{6,7},{7,6},{8,9},{9,8},{10,11... | collective-permute-start | bytes 442376 | tf_op jit(solution)/shard_map/ppermute | solution.py:24
  154.2 7.3 %collective-permute-start.38 = (f32[72,512]{1,0:T(8,128)S(1)}, f32[72,512]{1,0:T(8,128)S(1)}, u32[]{:S(2)}, u32[]{:S(2)}) collective-permute-start(f32[72,512]{1,0:T(8,128)S(1)} %add.70), channel_id=1, source_target_pairs={{0,2},{1,3},{2,0},{3,1},{4,6},{5,7},{6,4},{7,5},{8,10},{9,11},{10,... | collective-permute-start | bytes 442376 | tf_op jit(solution)/shard_map/ppermute | solution.py:24

commit v9 on v8

--- a/solution.py
+++ b/solution.py
@@ -526,7 +526,6 @@
     routes = line_routes(col_count)
     small = col_count == 4 and row_count == 8
     if small:
-        ready, *packed = tie(ready, *packed)
         line, peer_line, gathered = gather_both(ready, packed)
     else:
         line = line_gather(ready, "col")

time: 163 us -> 161 us (0.988)
  transfers between devices with their start and end apart: 39 -> 39, of which waited for: 17 -> 15; matrix products, arithmetic and copies ran while one was open for 0% -> 0% of each run, Pallas kernels for 13% -> 14%
where the time goes in v9:
time: 161 us
  waiting for transfers between devices  94 us (58%)
  starting transfers between devices  35.4 us (22%)
  Pallas kernels  25 us (16%)
  local copies, waits for them, and re-layouts  3.14 us (2%)
  between operations  2.57 us (2%)
    ppermute x30, waiting for transfers between devices, swap(): return lax.ppermute(block, axis, [(i, i ^ mask) for i in range(count)])  38.8 us
    ppermute x4, waiting for transfers between devices, gather_both(): send = lambda held, route: lax.ppermute(held, 'col', route)  30.5 us
    ppermute x30, starting transfers between devices, swap(): return lax.ppermute(block, axis, [(i, i ^ mask) for i in range(count)])  26.8 us
    ppermute x5, waiting for transfers between devices, gather_heads(): send = lambda held, route: lax.ppermute(held, 'col', route)  24.7 us
    pallas_call x1, Pallas kernels, per_device(): call(functools.partial(project_kernel, routes, masks, img, head), (heads_...  17.7 us
    ppermute x5, starting transfers between devices, gather_heads(): send = lambda held, route: lax.ppermute(held, 'col', route)  4.6 us
    ppermute x4, starting transfers between devices, gather_both(): send = lambda held, route: lax.ppermute(held, 'col', route)  3.99 us
  transfers between devices with their start and end apart: 39, of which 15 were waited for; matrix products, arithmetic and copies ran while one was open for 0% of the time, Pallas kernels for 14%

profile of v9, /device:TPU:0, one launch (start us, length us, event | category | flops | bytes accessed | tf_op | source)
XLA Modules:
  0.0 161.1 jit_solution(15353474490436022398)
XLA Ops:
  0.6 1.2 copy-done.1
  1.8 1.1 copy-done.3
  2.9 1.9 %shard_map.140 = (bf16[304,1280]{1,0:T(8,128)(2,1)S(1)}, bf16[304,1280]{1,0:T(8,128)(2,1)S(1)}) custom-call(bf16[3,304,512]{2,1,0:T(8,128)(2,1)S(1)} %bitcast.44, bf16[304,2,512]{2,1,0:T(2,128)(2,1)S(1)} %copy-done.3), custom_call_target="tpu_custom_call" | custom-call | flops 2300000000 | tf_op jit(solution)/shard_map/pallas_call | solution.py:508
  4.8 0.5 collective-permute-start
  5.3 0.5 shard_map.141
  5.8 2.6 %collective-permute-start.1 = (f32[8,640]{1,0:T(8,128)S(1)}, f32[8,640]{1,0:T(8,128)S(1)}, u32[]{:S(2)}, u32[]{:S(2)}) collective-permute-start(f32[8,640]{1,0:T(8,128)S(1)} %get-tuple-element.90), channel_id=1, source_target_pairs={{0,8},{4,12},{8,0},{12,4},{16,24},{20,28},{24,16},{28,20},{1,9},{5... | collective-permute-start | bytes 61448 | tf_op jit(solution)/shard_map/ppermute | solution.py:24
  8.4 1.5 collective-permute-start.2
  9.9 0.0 collective-permute-start.3
  10.0 0.2 shard_map.142
  10.2 2.1 %collective-permute-start.5 = (f32[8,640]{1,0:T(8,128)S(1)}, f32[8,640]{1,0:T(8,128)S(1)}, u32[]{:S(2)}, u32[]{:S(2)}) collective-permute-start(f32[8,640]{1,0:T(8,128)S(1)} %shard_map.142), channel_id=1, source_target_pairs={{0,1},{1,0},{2,3},{3,2},{4,5},{5,4},{6,7},{7,6},{8,9},{9,8},{10,11... | collective-permute-start | bytes 61448 | tf_op jit(solution)/shard_map/ppermute | solution.py:24
  12.3 2.6 %collective-permute-start.6 = (f32[8,640]{1,0:T(8,128)S(1)}, f32[8,640]{1,0:T(8,128)S(1)}, u32[]{:S(2)}, u32[]{:S(2)}) collective-permute-start(f32[8,640]{1,0:T(8,128)S(1)} %shard_map.142), channel_id=1, source_target_pairs={{0,2},{1,3},{2,0},{3,1},{4,6},{5,7},{6,4},{7,5},{8,10},{9,11},{10,... | collective-permute-start | bytes 61448 | tf_op jit(solution)/shard_map/ppermute | solution.py:24
  14.9 1.0 collective-permute-start.7
  15.8 0.1 collective-permute-start.4
  15.9 1.1 collective-permute-done.6
  17.1 3.4 %collective-permute-done.7 = f32[8,640]{1,0:T(8,128)S(1)} collective-permute-done((f32[8,640]{1,0:T(8,128)S(1)}, f32[8,640]{1,0:T(8,128)S(1)}, u32[]{:S(2)}, u32[]{:S(2)}) %collective-permute-start.7) | collective-permute-done | bytes 20512 | tf_op jit(solution)/shard_map/ppermute | solution.py:24
  20.4 1.6 collective-permute-start.10
  22.0 1.5 collective-permute-start.11
  23.6 0.7 shard_map.143.refs_0_
  24.3 0.1 collective-permute-start.8
  24.4 0.7 collective-permute-start.9
  25.1 0.1 collective-permute-start.16
  25.2 12.6 %collective-permute-done.10.refs_14_ = bf16[304,1280]{1,0:T(8,128)(2,1)S(1)} collective-permute-done((bf16[304,1280]{1,0:T(8,128)(2,1)S(1)}, bf16[304,1280]{1,0:T(8,128)(2,1)S(1)}, u32[]{:S(2)}, u32[]{:S(2)}) %collective-permute-start.10) | collective-permute-done | bytes 778272 | tf_op jit(solution)/shard_map/ppermute | solution.py:24
  37.8 1.2 collective-permute-done.11.refs_17_
  39.1 2.1 %collective-permute-done.8.refs_1_ = bf16[608,640]{1,0:T(8,128)(2,1)S(1)} collective-permute-done((bf16[608,640]{1,0:T(8,128)(2,1)S(1)}, bf16[608,640]{1,0:T(8,128)(2,1)S(1)}, u32[]{:S(2)}, u32[]{:S(2)}) %collective-permute-start.8) | collective-permute-done | bytes 778272 | tf_op jit(solution)/shard_map/ppermute | solution.py:24
  41.1 1.3 collective-permute-start.12
  42.4 0.7 collective-permute-start.13
  43.2 0.6 collective-permute-start.14
  43.8 0.5 collective-permute-start.15
  44.3 15.5 %collective-permute-done.12.refs_3_ = bf16[608,640]{1,0:T(8,128)(2,1)S(1)} collective-permute-done((bf16[608,640]{1,0:T(8,128)(2,1)S(1)}, bf16[608,640]{1,0:T(8,128)(2,1)S(1)}, u32[]{:S(2)}, u32[]{:S(2)}) %collective-permute-start.12) | collective-permute-done | bytes 778272 | tf_op jit(solution)/shard_map/ppermute | solution.py:99
  59.8 1.3 collective-permute-start.17
  61.1 1.0 collective-permute-start.18
  62.1 0.5 collective-permute-start.19
  62.6 0.5 collective-permute-start.20
  63.2 14.9 %collective-permute-done.17.refs_5_ = bf16[608,640]{1,0:T(8,128)(2,1)S(1)} collective-permute-done((bf16[608,640]{1,0:T(8,128)(2,1)S(1)}, bf16[608,640]{1,0:T(8,128)(2,1)S(1)}, u32[]{:S(2)}, u32[]{:S(2)}) %collective-permute-start.17) | collective-permute-done | bytes 778272 | tf_op jit(solution)/shard_map/ppermute | solution.py:99
  78.1 0.5 collective-permute-start.22
  78.6 0.1 collective-permute-start.24
  78.8 1.5 collective-permute-start.25
  80.3 0.0 collective-permute-done.21.refs_8_
  80.3 0.5 collective-permute-start.26
  80.8 0.6 collective-permute-done.22.refs_9_
  81.4 1.8 %collective-permute-start.27 = (bf16[736,256]{1,0:T(8,128)(2,1)S(1)}, bf16[736,256]{1,0:T(8,128)(2,1)S(1)}, u32[]{:S(2)}, u32[]{:S(2)}) collective-permute-start(bf16[736,256]{1,0:T(8,128)(2,1)S(1)} %pad_maximum_fusion.1), channel_id=1, source_target_pairs={{0,24},{4,28},{8,16},{12,20},{16,8},{20,12},{24,0},{28,4},{1,25},{... | collective-permute-start | bytes 1130504 | tf_op jit(solution)/shard_map/ppermute | solution.py:24
  83.3 17.7 %shard_map.144 = (bf16[256,512]{1,0:T(8,128)(2,1)S(1)}, bf16[256,512]{1,0:T(8,128)(2,1)S(1)}) custom-call(s32[4]{0:T(128)S(1)} %copy-done.8, f32[1,64]{1,0:T(1,128)S(1)} %bitcast.48, f32[2,64]{1,0:T(2,128)S(1)} %copy-done.7, bf16[608,640]{1,0:T(8,128)(2,1)S(1)} %shard_map.143.refs_0_, bf16[608,640]{1,0:T(8,128)(2,1)S(1)} %collective-permute-done.8.refs_1_, ...), custom_call_target="tpu_custom_call" | custom-call | flops 23000000512 | tf_op jit(solution)/shard_map/pallas_call | solution.py:542
  101.2 0.1 collective-permute-start.33
  101.3 0.5 collective-permute-start.28
  101.8 1.6 collective-permute-start.29
  103.3 0.7 collective-permute-start.30
  104.0 0.9 collective-permute-done.28
  104.9 2.0 %collective-permute-start.31 = (bf16[256,512]{1,0:T(8,128)(2,1)S(1)}, bf16[256,512]{1,0:T(8,128)(2,1)S(1)}, u32[]{:S(2)}, u32[]{:S(2)}) collective-permute-start(bf16[256,512]{1,0:T(8,128)(2,1)S(1)} %collective-permute-done.28), channel_id=1, source_target_pairs={{0,1},{1,0},{2,3},{3,2},{4,5},{5,4},{6,7},{7,6},{8,9},{9,8},{10,11... | collective-permute-start | bytes 786440 | tf_op jit(solution)/shard_map/ppermute | solution.py:24
  106.9 0.7 collective-permute-start.32
  107.6 3.3 %collective-permute-done.29 = bf16[256,512]{1,0:T(8,128)(2,1)S(1)} collective-permute-done((bf16[256,512]{1,0:T(8,128)(2,1)S(1)}, bf16[256,512]{1,0:T(8,128)(2,1)S(1)}, u32[]{:S(2)}, u32[]{:S(2)}) %collective-permute-start.29) | collective-permute-done | bytes 262176 | tf_op jit(solution)/shard_map/ppermute | solution.py:24
  110.9 4.7 %collective-permute-done.31 = bf16[256,512]{1,0:T(8,128)(2,1)S(1)} collective-permute-done((bf16[256,512]{1,0:T(8,128)(2,1)S(1)}, bf16[256,512]{1,0:T(8,128)(2,1)S(1)}, u32[]{:S(2)}, u32[]{:S(2)}) %collective-permute-start.31) | collective-permute-done | bytes 262176 | tf_op jit(solution)/shard_map/ppermute | solution.py:24
  115.7 1.3 collective-permute-start.34
  117.1 0.7 collective-permute-start.35
  117.8 13.8 %collective-permute-done.34.refs_3_ = bf16[512,512]{1,0:T(8,128)(2,1)S(1)} collective-permute-done((bf16[512,512]{1,0:T(8,128)(2,1)S(1)}, bf16[512,512]{1,0:T(8,128)(2,1)S(1)}, u32[]{:S(2)}, u32[]{:S(2)}) %collective-permute-start.34) | collective-permute-done | bytes 524320 | tf_op jit(solution)/shard_map/ppermute | solution.py:85
  131.6 1.3 collective-permute-start.36
  132.9 2.9 %shard_map.145 = (f32[608,512]{1,0:T(8,128)S(1)}, bf16[608,512]{1,0:T(8,128)(2,1)S(1)}, bf16[192,608]{1,0:T(8,128)(2,1)S(1)}, f32[8,512]{1,0:T(8,128)S(1)}) custom-call(f32[8,640]{1,0:T(8,128)S(1)} %add.66.mod_ref, bf16[512,512]{1,0:T(8,128)(2,1)S(1)} %pad_maximum_fusion.refs_0_, bf16[512,512]{1,0:T(8,128)(2,1)S(1)} %constant_dynamic-update-slice_fusion.5.refs_1_, ...), custom_call_target="tpu_custom_call" | custom-call | flops 5750000128 | tf_op jit(solution)/shard_map/pallas_call | solution.py:579
  135.8 10.9 %collective-permute-done.36.refs_1_ = bf16[512,512]{1,0:T(8,128)(2,1)S(1)} collective-permute-done((bf16[512,512]{1,0:T(8,128)(2,1)S(1)}, bf16[512,512]{1,0:T(8,128)(2,1)S(1)}, u32[]{:S(2)}, u32[]{:S(2)}) %collective-permute-start.36) | collective-permute-done | bytes 524320 | tf_op jit(solution)/shard_map/ppermute | solution.py:85
  146.7 1.1 shard_map.146
  147.8 0.1 collective-permute-start.37
  147.9 5.3 %collective-permute-done.37 = f32[72,512]{1,0:T(8,128)S(1)} collective-permute-done((f32[72,512]{1,0:T(8,128)S(1)}, f32[72,512]{1,0:T(8,128)S(1)}, u32[]{:S(2)}, u32[]{:S(2)}) %collective-permute-start.37) | collective-permute-done | bytes 147488 | tf_op jit(solution)/shard_map/ppermute | solution.py:24
  153.3 1.5 collective-permute-start.38
  154.8 0.6 dynamic_slice.4
  156.8 3.4 %collective-permute-done.38 = f32[72,512]{1,0:T(8,128)S(1)} collective-permute-done((f32[72,512]{1,0:T(8,128)S(1)}, f32[72,512]{1,0:T(8,128)S(1)}, u32[]{:S(2)}, u32[]{:S(2)}) %collective-permute-start.38) | collective-permute-done | bytes 147488 | tf_op jit(solution)/shard_map/ppermute | solution.py:24
  160.3 0.8 fusion.2
  (86 shorter events, 0.5 us)
Async XLA Ops:
  0.6 1.2 copy-start.1
  1.8 1.1 copy-start.3
  2.9 2.4 %copy-start = (bf16[304,7,608]{2,0,1:T(8,128)(2,1)S(1)}, bf16[304,7,608]{2,0,1:T(8,128)(2,1)}, u32[]{:S(2)}) copy-start(bf16[304,7,608]{2,0,1:T(8,128)(2,1)} %param.19) | copy-start | bytes 7762948
  2.9 2.4 %copy-start.6 = (f32[4,304]{1,0:T(4,128)S(1)}, f32[4,304]{1,0:T(4,128)}, u32[]{:S(2)}) copy-start(f32[4,304]{1,0:T(4,128)} %cond_ref.1) | copy-start | bytes 14596
  4.8 38.4 %copy-start.2 = (bf16[304,1280]{1,0:T(8,128)(2,1)}, bf16[304,1280]{1,0:T(8,128)(2,1)S(1)}, u32[]{:S(2)}) copy-start(bf16[304,1280]{1,0:T(8,128)(2,1)S(1)} %get-tuple-element.50.refs_12_) | copy-start | bytes 2334724
  4.8 11.1 %collective-permute-start = (bf16[304,1280]{1,0:T(8,128)(2,1)S(1)}, bf16[304,1280]{1,0:T(8,128)(2,1)S(1)}, u32[]{:S(2)}, u32[]{:S(2)}) collective-permute-start(bf16[304,1280]{1,0:T(8,128)(2,1)S(1)} %get-tuple-element.44), channel_id=1, source_target_pairs={{0,4},{4,0},{8,12},{12,8},{16,20},{20,16},{24,28},{28,24},{1,5},{5... | collective-permute-start | bytes 2334728 | tf_op jit(solution)/shard_map/ppermute | solution.py:24
  5.3 4.7 %copy-start.4 = (bf16[512,608]{0,1:T(8,128)(2,1)S(1)}, bf16[512,608]{0,1:T(8,128)(2,1)}, u32[]{:S(2)}) copy-start(bf16[512,608]{0,1:T(8,128)(2,1)} %param.13) | copy-start | bytes 1867780
  5.3 4.7 %copy-start.5 = (bf16[96,608]{1,0:T(8,128)(2,1)S(1)}, bf16[96,608]{1,0:T(8,128)(2,1)}, u32[]{:S(2)}) copy-start(bf16[96,608]{1,0:T(8,128)(2,1)} %txt_ref.3) | copy-start | bytes 350212
  5.8 6.4 %collective-permute-start.1 = (f32[8,640]{1,0:T(8,128)S(1)}, f32[8,640]{1,0:T(8,128)S(1)}, u32[]{:S(2)}, u32[]{:S(2)}) collective-permute-start(f32[8,640]{1,0:T(8,128)S(1)} %get-tuple-element.90), channel_id=1, source_target_pairs={{0,8},{4,12},{8,0},{12,4},{16,24},{20,28},{24,16},{28,20},{1,9},{5... | collective-permute-start | bytes 61448 | tf_op jit(solution)/shard_map/ppermute | solution.py:24
  8.4 6.4 %collective-permute-start.2 = (f32[8,640]{1,0:T(8,128)S(1)}, f32[8,640]{1,0:T(8,128)S(1)}, u32[]{:S(2)}, u32[]{:S(2)}) collective-permute-start(f32[8,640]{1,0:T(8,128)S(1)} %get-tuple-element.92), channel_id=1, source_target_pairs={{0,16},{4,20},{8,24},{12,28},{16,0},{20,4},{24,8},{28,12},{1,17},{... | collective-permute-start | bytes 61448 | tf_op jit(solution)/shard_map/ppermute | solution.py:24
  9.9 5.9 %collective-permute-start.3 = (f32[8,640]{1,0:T(8,128)S(1)}, f32[8,640]{1,0:T(8,128)S(1)}, u32[]{:S(2)}, u32[]{:S(2)}) collective-permute-start(f32[8,640]{1,0:T(8,128)S(1)} %get-tuple-element.91), channel_id=1, source_target_pairs={{0,24},{4,28},{8,16},{12,20},{16,8},{20,12},{24,0},{28,4},{1,25},{... | collective-permute-start | bytes 61448 | tf_op jit(solution)/shard_map/ppermute | solution.py:24
  10.2 5.8 %collective-permute-start.5 = (f32[8,640]{1,0:T(8,128)S(1)}, f32[8,640]{1,0:T(8,128)S(1)}, u32[]{:S(2)}, u32[]{:S(2)}) collective-permute-start(f32[8,640]{1,0:T(8,128)S(1)} %shard_map.142), channel_id=1, source_target_pairs={{0,1},{1,0},{2,3},{3,2},{4,5},{5,4},{6,7},{7,6},{8,9},{9,8},{10,11... | collective-permute-start | bytes 61448 | tf_op jit(solution)/shard_map/ppermute | solution.py:24
  12.3 4.8 %collective-permute-start.6 = (f32[8,640]{1,0:T(8,128)S(1)}, f32[8,640]{1,0:T(8,128)S(1)}, u32[]{:S(2)}, u32[]{:S(2)}) collective-permute-start(f32[8,640]{1,0:T(8,128)S(1)} %shard_map.142), channel_id=1, source_target_pairs={{0,2},{1,3},{2,0},{3,1},{4,6},{5,7},{6,4},{7,5},{8,10},{9,11},{10,... | collective-permute-start | bytes 61448 | tf_op jit(solution)/shard_map/ppermute | solution.py:24
  14.9 5.6 %collective-permute-start.7 = (f32[8,640]{1,0:T(8,128)S(1)}, f32[8,640]{1,0:T(8,128)S(1)}, u32[]{:S(2)}, u32[]{:S(2)}) collective-permute-start(f32[8,640]{1,0:T(8,128)S(1)} %shard_map.142), channel_id=1, source_target_pairs={{0,3},{1,2},{2,1},{3,0},{4,7},{5,6},{6,5},{7,4},{8,11},{9,10},{10,... | collective-permute-start | bytes 61448 | tf_op jit(solution)/shard_map/ppermute | solution.py:24
  15.8 27.9 %copy-start.13 = (bf16[304,1280]{1,0:T(8,128)(2,1)}, bf16[304,1280]{1,0:T(8,128)(2,1)S(1)}, u32[]{:S(2)}) copy-start(bf16[304,1280]{1,0:T(8,128)(2,1)S(1)} %collective-permute-done.refs_16_) | copy-start | bytes 2334724
  15.8 7.7 %collective-permute-start.4 = (f32[8,640]{1,0:T(8,128)S(1)}, f32[8,640]{1,0:T(8,128)S(1)}, u32[]{:S(2)}, u32[]{:S(2)}) collective-permute-start(f32[8,640]{1,0:T(8,128)S(1)} %fusion.6), channel_id=1, source_target_pairs={{0,4},{4,0},{8,12},{12,8},{16,20},{20,16},{24,28},{28,24},{1,5},{5... | collective-permute-start | bytes 61448 | tf_op jit(solution)/shard_map/ppermute | solution.py:24
  20.4 17.4 %collective-permute-start.10 = (bf16[304,1280]{1,0:T(8,128)(2,1)S(1)}, bf16[304,1280]{1,0:T(8,128)(2,1)S(1)}, u32[]{:S(2)}, u32[]{:S(2)}) collective-permute-start(bf16[304,1280]{1,0:T(8,128)(2,1)S(1)} %get-tuple-element.50.refs_12_), channel_id=1, source_target_pairs={{0,16},{4,20},{8,24},{12,28},{16,0},{20,4},{24,8},{28,12},{1,17},{... | collective-permute-start | bytes 2334728 | tf_op jit(solution)/shard_map/ppermute | solution.py:24
  22.0 17.0 %collective-permute-start.11 = (bf16[304,1280]{1,0:T(8,128)(2,1)S(1)}, bf16[304,1280]{1,0:T(8,128)(2,1)S(1)}, u32[]{:S(2)}, u32[]{:S(2)}) collective-permute-start(bf16[304,1280]{1,0:T(8,128)(2,1)S(1)} %collective-permute-done.refs_16_), channel_id=1, source_target_pairs={{0,8},{4,12},{8,0},{12,4},{16,24},{20,28},{24,16},{28,20},{1,9},{5... | collective-permute-start | bytes 2334728 | tf_op jit(solution)/shard_map/ppermute | solution.py:24
  23.5 55.1 %copy-start.12 = (bf16[304,64]{0,1:T(8,128)(2,1)S(1)}, bf16[304,64]{0,1:T(8,128)(2,1)}, u32[]{:S(2)}) copy-start(bf16[304,64]{0,1:T(8,128)(2,1)} %param.25) | copy-start | bytes 116740
  23.5 55.2 %copy-start.10 = (bf16[256,608]{0,1:T(8,128)(2,1)S(1)}, bf16[256,608]{0,1:T(8,128)(2,1)}, u32[]{:S(2)}) copy-start(bf16[256,608]{0,1:T(8,128)(2,1)} %param.24) | copy-start | bytes 933892
  24.3 59.0 %copy-start.7 = (f32[2,64]{1,0:T(2,128)S(1)}, f32[2,64]{1,0:T(2,128)}, u32[]{:S(2)}) copy-start(f32[2,64]{1,0:T(2,128)} %k_gain_ref.1) | copy-start | bytes 1540
  24.3 59.0 %copy-start.8 = (s32[4]{0:T(128)S(1)}, s32[4]{0:T(128)}, u32[]{:S(2)}) copy-start(s32[4]{0:T(128)} %length_ref.1) | copy-start | bytes 52
  24.3 59.0 %copy-start.9 = (f32[64]{0:T(128)S(1)}, f32[64]{0:T(128)}, u32[]{:S(2)}) copy-start(f32[64]{0:T(128)} %param.22) | copy-start | bytes 772
  24.3 16.8 %collective-permute-start.8 = (bf16[608,640]{1,0:T(8,128)(2,1)S(1)}, bf16[608,640]{1,0:T(8,128)(2,1)S(1)}, u32[]{:S(2)}, u32[]{:S(2)}) collective-permute-start(bf16[608,640]{1,0:T(8,128)(2,1)S(1)} %shard_map.143.refs_0_), channel_id=1, source_target_pairs={{0,1},{1,0},{2,3},{3,2},{4,5},{5,4},{6,7},{7,6},{8,9},{9,8},{10,11... | collective-permute-start | bytes 2334728 | tf_op jit(solution)/shard_map/ppermute | solution.py:24
  24.4 16.7 %collective-permute-start.9 = (bf16[608,640]{1,0:T(8,128)(2,1)S(1)}, bf16[608,640]{1,0:T(8,128)(2,1)S(1)}, u32[]{:S(2)}, u32[]{:S(2)}) collective-permute-start(bf16[608,640]{1,0:T(8,128)(2,1)S(1)} %shard_map.143.refs_0_), channel_id=1, source_target_pairs={{1,2},{2,1},{5,6},{6,5},{9,10},{10,9},{13,14},{14,13},{17,18},{18,... | collective-permute-start | bytes 2334728 | tf_op jit(solution)/shard_map/ppermute | solution.py:99
  25.1 19.1 %collective-permute-start.16 = (bf16[608,640]{1,0:T(8,128)(2,1)S(1)}, bf16[608,640]{1,0:T(8,128)(2,1)S(1)}, u32[]{:S(2)}, u32[]{:S(2)}) collective-permute-start(bf16[608,640]{1,0:T(8,128)(2,1)S(1)} %shard_map.143.refs_0_), channel_id=1, source_target_pairs={{0,4},{4,0},{8,12},{12,8},{16,20},{20,16},{24,28},{28,24},{1,5},{5... | collective-permute-start | bytes 2334728 | tf_op jit(solution)/shard_map/ppermute | solution.py:24
  37.8 45.5 %copy-start.14 = (bf16[304,1280]{1,0:T(8,128)(2,1)}, bf16[304,1280]{1,0:T(8,128)(2,1)S(1)}, u32[]{:S(2)}) copy-start(bf16[304,1280]{1,0:T(8,128)(2,1)S(1)} %collective-permute-done.10.refs_14_) | copy-start | bytes 2334724
  39.0 44.2 %copy-start.15 = (bf16[304,1280]{1,0:T(8,128)(2,1)}, bf16[304,1280]{1,0:T(8,128)(2,1)S(1)}, u32[]{:S(2)}) copy-start(bf16[304,1280]{1,0:T(8,128)(2,1)S(1)} %collective-permute-done.11.refs_17_) | copy-start | bytes 2334724
  41.1 18.7 %collective-permute-start.12 = (bf16[608,640]{1,0:T(8,128)(2,1)S(1)}, bf16[608,640]{1,0:T(8,128)(2,1)S(1)}, u32[]{:S(2)}, u32[]{:S(2)}) collective-permute-start(bf16[608,640]{1,0:T(8,128)(2,1)S(1)} %collective-permute-done.9.refs_2_), channel_id=1, source_target_pairs={{1,0},{2,3},{5,4},{6,7},{9,8},{10,11},{13,12},{14,15},{17,16},{18,... | collective-permute-start | bytes 2334728 | tf_op jit(solution)/shard_map/ppermute | solution.py:99
  42.4 17.4 %collective-permute-start.13 = (bf16[608,640]{1,0:T(8,128)(2,1)S(1)}, bf16[608,640]{1,0:T(8,128)(2,1)S(1)}, u32[]{:S(2)}, u32[]{:S(2)}) collective-permute-start(bf16[608,640]{1,0:T(8,128)(2,1)S(1)} %collective-permute-done.8.refs_1_), channel_id=1, source_target_pairs={{1,2},{2,1},{5,6},{6,5},{9,10},{10,9},{13,14},{14,13},{17,18},{18,... | collective-permute-start | bytes 2334728 | tf_op jit(solution)/shard_map/ppermute | solution.py:99
  43.2 16.7 %collective-permute-start.14 = (bf16[304,1280]{1,0:T(8,128)(2,1)S(1)}, bf16[304,1280]{1,0:T(8,128)(2,1)S(1)}, u32[]{:S(2)}, u32[]{:S(2)}) collective-permute-start(bf16[304,1280]{1,0:T(8,128)(2,1)S(1)} %get-tuple-element.50.refs_12_), channel_id=1, source_target_pairs={{0,8},{4,12},{8,0},{12,4},{16,24},{20,28},{24,16},{28,20},{1,9},{5... | collective-permute-start | bytes 2334728 | tf_op jit(solution)/shard_map/ppermute | solution.py:24
  43.8 16.1 %collective-permute-start.15 = (bf16[304,1280]{1,0:T(8,128)(2,1)S(1)}, bf16[304,1280]{1,0:T(8,128)(2,1)S(1)}, u32[]{:S(2)}, u32[]{:S(2)}) collective-permute-start(bf16[304,1280]{1,0:T(8,128)(2,1)S(1)} %collective-permute-done.refs_16_), channel_id=1, source_target_pairs={{0,16},{4,20},{8,24},{12,28},{16,0},{20,4},{24,8},{28,12},{1,17},{... | collective-permute-start | bytes 2334728 | tf_op jit(solution)/shard_map/ppermute | solution.py:24
  59.8 23.5 %copy-start.16 = (bf16[304,1280]{1,0:T(8,128)(2,1)}, bf16[304,1280]{1,0:T(8,128)(2,1)S(1)}, u32[]{:S(2)}) copy-start(bf16[304,1280]{1,0:T(8,128)(2,1)S(1)} %collective-permute-done.14.refs_13_) | copy-start | bytes 2334724
  59.8 23.5 %copy-start.17 = (bf16[304,1280]{1,0:T(8,128)(2,1)}, bf16[304,1280]{1,0:T(8,128)(2,1)S(1)}, u32[]{:S(2)}) copy-start(bf16[304,1280]{1,0:T(8,128)(2,1)S(1)} %collective-permute-done.15.refs_18_) | copy-start | bytes 2334724
  59.8 18.2 %collective-permute-start.17 = (bf16[608,640]{1,0:T(8,128)(2,1)S(1)}, bf16[608,640]{1,0:T(8,128)(2,1)S(1)}, u32[]{:S(2)}, u32[]{:S(2)}) collective-permute-start(bf16[608,640]{1,0:T(8,128)(2,1)S(1)} %collective-permute-done.13.refs_4_), channel_id=1, source_target_pairs={{1,0},{2,3},{5,4},{6,7},{9,8},{10,11},{13,12},{14,15},{17,16},{18,... | collective-permute-start | bytes 2334728 | tf_op jit(solution)/shard_map/ppermute | solution.py:99
  61.1 16.9 %collective-permute-start.18 = (bf16[304,1280]{1,0:T(8,128)(2,1)S(1)}, bf16[304,1280]{1,0:T(8,128)(2,1)S(1)}, u32[]{:S(2)}, u32[]{:S(2)}) collective-permute-start(bf16[304,1280]{1,0:T(8,128)(2,1)S(1)} %collective-permute-done.10.refs_14_), channel_id=1, source_target_pairs={{0,8},{4,12},{8,0},{12,4},{16,24},{20,28},{24,16},{28,20},{1,9},{5... | collective-permute-start | bytes 2334728 | tf_op jit(solution)/shard_map/ppermute | solution.py:24
  62.1 16.4 %collective-permute-start.19 = (bf16[304,1280]{1,0:T(8,128)(2,1)S(1)}, bf16[304,1280]{1,0:T(8,128)(2,1)S(1)}, u32[]{:S(2)}, u32[]{:S(2)}) collective-permute-start(bf16[304,1280]{1,0:T(8,128)(2,1)S(1)} %collective-permute-done.11.refs_17_), channel_id=1, source_target_pairs={{0,16},{4,20},{8,24},{12,28},{16,0},{20,4},{24,8},{28,12},{1,17},{... | collective-permute-start | bytes 2334728 | tf_op jit(solution)/shard_map/ppermute | solution.py:24
  62.6 20.6 %collective-permute-start.23 = (bf16[608,640]{1,0:T(8,128)(2,1)S(1)}, bf16[608,640]{1,0:T(8,128)(2,1)S(1)}, u32[]{:S(2)}, u32[]{:S(2)}) collective-permute-start(bf16[608,640]{1,0:T(8,128)(2,1)S(1)} %collective-permute-done.13.refs_4_), channel_id=1, source_target_pairs={{0,4},{4,0},{8,12},{12,8},{16,20},{20,16},{24,28},{28,24},{1,5},{5... | collective-permute-start | bytes 2334728 | tf_op jit(solution)/shard_map/ppermute | solution.py:24
  62.6 16.1 %collective-permute-start.20 = (bf16[608,640]{1,0:T(8,128)(2,1)S(1)}, bf16[608,640]{1,0:T(8,128)(2,1)S(1)}, u32[]{:S(2)}, u32[]{:S(2)}) collective-permute-start(bf16[608,640]{1,0:T(8,128)(2,1)S(1)} %collective-permute-done.8.refs_1_), channel_id=1, source_target_pairs={{0,4},{4,0},{8,12},{12,8},{16,20},{20,16},{24,28},{28,24},{1,5},{5... | collective-permute-start | bytes 2334728 | tf_op jit(solution)/shard_map/ppermute | solution.py:24
  78.1 2.3 %collective-permute-start.21 = (bf16[608,640]{1,0:T(8,128)(2,1)S(1)}, bf16[608,640]{1,0:T(8,128)(2,1)S(1)}, u32[]{:S(2)}, u32[]{:S(2)}) collective-permute-start(bf16[608,640]{1,0:T(8,128)(2,1)S(1)} %collective-permute-done.9.refs_2_), channel_id=1, source_target_pairs={{0,4},{4,0},{8,12},{12,8},{16,20},{20,16},{24,28},{28,24},{1,5},{5... | collective-permute-start | bytes 2334728 | tf_op jit(solution)/shard_map/ppermute | solution.py:24
  78.1 5.2 %copy-start.18 = (bf16[304,1280]{1,0:T(8,128)(2,1)}, bf16[304,1280]{1,0:T(8,128)(2,1)S(1)}, u32[]{:S(2)}) copy-start(bf16[304,1280]{1,0:T(8,128)(2,1)S(1)} %collective-permute-done.18.refs_15_) | copy-start | bytes 2334724
  78.1 3.4 %collective-permute-start.22 = (bf16[608,640]{1,0:T(8,128)(2,1)S(1)}, bf16[608,640]{1,0:T(8,128)(2,1)S(1)}, u32[]{:S(2)}, u32[]{:S(2)}) collective-permute-start(bf16[608,640]{1,0:T(8,128)(2,1)S(1)} %collective-permute-done.12.refs_3_), channel_id=1, source_target_pairs={{0,4},{4,0},{8,12},{12,8},{16,20},{20,16},{24,28},{28,24},{1,5},{5... | collective-permute-start | bytes 2334728 | tf_op jit(solution)/shard_map/ppermute | solution.py:24
  78.6 4.7 %copy-start.19 = (bf16[304,1280]{1,0:T(8,128)(2,1)}, bf16[304,1280]{1,0:T(8,128)(2,1)S(1)}, u32[]{:S(2)}) copy-start(bf16[304,1280]{1,0:T(8,128)(2,1)S(1)} %collective-permute-done.19.refs_19_) | copy-start | bytes 2334724
  78.6 4.7 %collective-permute-start.24 = (bf16[608,640]{1,0:T(8,128)(2,1)S(1)}, bf16[608,640]{1,0:T(8,128)(2,1)S(1)}, u32[]{:S(2)}, u32[]{:S(2)}) collective-permute-start(bf16[608,640]{1,0:T(8,128)(2,1)S(1)} %collective-permute-done.17.refs_5_), channel_id=1, source_target_pairs={{0,4},{4,0},{8,12},{12,8},{16,20},{20,16},{24,28},{28,24},{1,5},{5... | collective-permute-start | bytes 2334728 | tf_op jit(solution)/shard_map/ppermute | solution.py:24
  78.8 22.3 %collective-permute-start.25 = (bf16[736,256]{1,0:T(8,128)(2,1)S(1)}, bf16[736,256]{1,0:T(8,128)(2,1)S(1)}, u32[]{:S(2)}, u32[]{:S(2)}) collective-permute-start(bf16[736,256]{1,0:T(8,128)(2,1)S(1)} %pad_maximum_fusion.1), channel_id=1, source_target_pairs={{0,8},{4,12},{8,0},{12,4},{16,24},{20,28},{24,16},{28,20},{1,9},{5... | collective-permute-start | bytes 1130504 | tf_op jit(solution)/shard_map/ppermute | solution.py:24
  80.3 20.7 %collective-permute-start.26 = (bf16[736,256]{1,0:T(8,128)(2,1)S(1)}, bf16[736,256]{1,0:T(8,128)(2,1)S(1)}, u32[]{:S(2)}, u32[]{:S(2)}) collective-permute-start(bf16[736,256]{1,0:T(8,128)(2,1)S(1)} %pad_maximum_fusion.1), channel_id=1, source_target_pairs={{0,16},{4,20},{8,24},{12,28},{16,0},{20,4},{24,8},{28,12},{1,17},{... | collective-permute-start | bytes 1130504 | tf_op jit(solution)/shard_map/ppermute | solution.py:24
  81.4 19.6 %collective-permute-start.27 = (bf16[736,256]{1,0:T(8,128)(2,1)S(1)}, bf16[736,256]{1,0:T(8,128)(2,1)S(1)}, u32[]{:S(2)}, u32[]{:S(2)}) collective-permute-start(bf16[736,256]{1,0:T(8,128)(2,1)S(1)} %pad_maximum_fusion.1), channel_id=1, source_target_pairs={{0,24},{4,28},{8,16},{12,20},{16,8},{20,12},{24,0},{28,4},{1,25},{... | collective-permute-start | bytes 1130504 | tf_op jit(solution)/shard_map/ppermute | solution.py:24
  101.2 14.5 %collective-permute-start.33 = (bf16[2944,256]{1,0:T(8,128)(2,1)S(1)}, bf16[2944,256]{1,0:T(8,128)(2,1)S(1)}, u32[]{:S(2)}, u32[]{:S(2)}) collective-permute-start(bf16[2944,256]{1,0:T(8,128)(2,1)S(1)} %constant_dynamic-update-slice_fusion.refs_4_), channel_id=1, source_target_pairs={{0,4},{4,0},{8,12},{12,8},{16,20},{20,16},{24,28},{28,24},{1,5},{5... | collective-permute-start | bytes 4521992 | tf_op jit(solution)/shard_map/ppermute | solution.py:24
  101.3 3.7 %collective-permute-start.28 = (bf16[256,512]{1,0:T(8,128)(2,1)S(1)}, bf16[256,512]{1,0:T(8,128)(2,1)S(1)}, u32[]{:S(2)}, u32[]{:S(2)}) collective-permute-start(bf16[256,512]{1,0:T(8,128)(2,1)S(1)} %get-tuple-element.69), channel_id=1, source_target_pairs={{0,4},{4,0},{8,12},{12,8},{16,20},{20,16},{24,28},{28,24},{1,5},{5... | collective-permute-start | bytes 786440 | tf_op jit(solution)/shard_map/ppermute | solution.py:24
  101.8 9.2 %collective-permute-start.29 = (bf16[256,512]{1,0:T(8,128)(2,1)S(1)}, bf16[256,512]{1,0:T(8,128)(2,1)S(1)}, u32[]{:S(2)}, u32[]{:S(2)}) collective-permute-start(bf16[256,512]{1,0:T(8,128)(2,1)S(1)} %get-tuple-element.68), channel_id=1, source_target_pairs={{0,1},{1,0},{2,3},{3,2},{4,5},{5,4},{6,7},{7,6},{8,9},{9,8},{10,11... | collective-permute-start | bytes 786440 | tf_op jit(solution)/shard_map/ppermute | solution.py:24
  103.3 7.6 %collective-permute-start.30 = (bf16[256,512]{1,0:T(8,128)(2,1)S(1)}, bf16[256,512]{1,0:T(8,128)(2,1)S(1)}, u32[]{:S(2)}, u32[]{:S(2)}) collective-permute-start(bf16[256,512]{1,0:T(8,128)(2,1)S(1)} %get-tuple-element.68), channel_id=1, source_target_pairs={{1,2},{2,1},{5,6},{6,5},{9,10},{10,9},{13,14},{14,13},{17,18},{18,... | collective-permute-start | bytes 786440 | tf_op jit(solution)/shard_map/ppermute | solution.py:85
  104.9 10.7 %collective-permute-start.31 = (bf16[256,512]{1,0:T(8,128)(2,1)S(1)}, bf16[256,512]{1,0:T(8,128)(2,1)S(1)}, u32[]{:S(2)}, u32[]{:S(2)}) collective-permute-start(bf16[256,512]{1,0:T(8,128)(2,1)S(1)} %collective-permute-done.28), channel_id=1, source_target_pairs={{0,1},{1,0},{2,3},{3,2},{4,5},{5,4},{6,7},{7,6},{8,9},{9,8},{10,11... | collective-permute-start | bytes 786440 | tf_op jit(solution)/shard_map/ppermute | solution.py:24
  106.9 8.7 %collective-permute-start.32 = (bf16[256,512]{1,0:T(8,128)(2,1)S(1)}, bf16[256,512]{1,0:T(8,128)(2,1)S(1)}, u32[]{:S(2)}, u32[]{:S(2)}) collective-permute-start(bf16[256,512]{1,0:T(8,128)(2,1)S(1)} %collective-permute-done.28), channel_id=1, source_target_pairs={{1,2},{2,1},{5,6},{6,5},{9,10},{10,9},{13,14},{14,13},{17,18},{18,... | collective-permute-start | bytes 786440 | tf_op jit(solution)/shard_map/ppermute | solution.py:85
  115.7 15.9 %collective-permute-start.34 = (bf16[512,512]{1,0:T(8,128)(2,1)S(1)}, bf16[512,512]{1,0:T(8,128)(2,1)S(1)}, u32[]{:S(2)}, u32[]{:S(2)}) collective-permute-start(bf16[512,512]{1,0:T(8,128)(2,1)S(1)} %constant_dynamic-update-slice_fusion.7.refs_2_), channel_id=1, source_target_pairs={{1,0},{2,3},{5,4},{6,7},{9,8},{10,11},{13,12},{14,15},{17,16},{18,... | collective-permute-start | bytes 1572872 | tf_op jit(solution)/shard_map/ppermute | solution.py:85
  117.1 14.6 %collective-permute-start.35 = (bf16[512,512]{1,0:T(8,128)(2,1)S(1)}, bf16[512,512]{1,0:T(8,128)(2,1)S(1)}, u32[]{:S(2)}, u32[]{:S(2)}) collective-permute-start(bf16[512,512]{1,0:T(8,128)(2,1)S(1)} %constant_dynamic-update-slice_fusion.5.refs_1_), channel_id=1, source_target_pairs={{1,2},{2,1},{5,6},{6,5},{9,10},{10,9},{13,14},{14,13},{17,18},{18,... | collective-permute-start | bytes 1572872 | tf_op jit(solution)/shard_map/ppermute | solution.py:85
  131.6 15.1 %collective-permute-start.36 = (bf16[512,512]{1,0:T(8,128)(2,1)S(1)}, bf16[512,512]{1,0:T(8,128)(2,1)S(1)}, u32[]{:S(2)}, u32[]{:S(2)}) collective-permute-start(bf16[512,512]{1,0:T(8,128)(2,1)S(1)} %collective-permute-done.35.refs_0_), channel_id=1, source_target_pairs={{1,0},{2,3},{5,4},{6,7},{9,8},{10,11},{13,12},{14,15},{17,16},{18,... | collective-permute-start | bytes 1572872 | tf_op jit(solution)/shard_map/ppermute | solution.py:85
  146.7 8.1 %copy-start.20 = (s32[4]{0:T(128)S(1)}, s32[4]{0:T(128)}, u32[]{:S(2)}) copy-start(s32[4]{0:T(128)} %param.16) | copy-start | bytes 52
  146.7 13.5 %copy-start.11 = (f32[512,64]{0,1:T(8,128)S(1)}, f32[512,64]{0,1:T(8,128)}, u32[]{:S(2)}) copy-start(f32[512,64]{0,1:T(8,128)} %param.17) | copy-start | bytes 393220
  147.8 5.4 %collective-permute-start.37 = (f32[72,512]{1,0:T(8,128)S(1)}, f32[72,512]{1,0:T(8,128)S(1)}, u32[]{:S(2)}, u32[]{:S(2)}) collective-permute-start(f32[72,512]{1,0:T(8,128)S(1)} %shard_map.146), channel_id=1, source_target_pairs={{0,1},{1,0},{2,3},{3,2},{4,5},{5,4},{6,7},{7,6},{8,9},{9,8},{10,11... | collective-permute-start | bytes 442376 | tf_op jit(solution)/shard_map/ppermute | solution.py:24
  153.3 6.9 %collective-permute-start.38 = (f32[72,512]{1,0:T(8,128)S(1)}, f32[72,512]{1,0:T(8,128)S(1)}, u32[]{:S(2)}, u32[]{:S(2)}) collective-permute-start(f32[72,512]{1,0:T(8,128)S(1)} %add.70), channel_id=1, source_target_pairs={{0,2},{1,3},{2,0},{3,1},{4,6},{5,7},{6,4},{7,5},{8,10},{9,11},{10,... | collective-permute-start | bytes 442376 | tf_op jit(solution)/shard_map/ppermute | solution.py:24

commit v10 on v9

--- a/solution.py
+++ b/solution.py
@@ -247,7 +247,7 @@
         for k in range(width // head)
     ]
     lane = lax.broadcasted_iota(jnp.int32, (1, width), 1) // head
-    step = 256 if img % 256 == 0 else img
+    step = 512 if img % 512 == 0 else img
 
     def scores_of(k, low):
         query = jnp.where(lane == k, queries[low : low + step], 0.0).astype(BF16)

time: 161 us -> 161 us (level)
  Pallas kernels: 25 us -> 22.4 us
    pallas_call x1, Pallas kernels: 17.7 us -> 15.2 us  [per_device(): call(functools.partial(project_kernel, routes, masks, img, head), (heads_...]
  transfers between devices with their start and end apart: 39 -> 39, of which waited for: 15 -> 16; matrix products, arithmetic and copies ran while one was open for 0% -> 0% of each run, Pallas kernels for 14% -> 12%
where the time goes in v10:
time: 161 us; the launch traced here: 160 us
  waiting for transfers between devices  94.7 us (59%)
  starting transfers between devices  36.6 us (23%)
  Pallas kernels  22.4 us (14%)
  local copies, waits for them, and re-layouts  3.14 us (2%)
  between operations  2.55 us (2%)
    ppermute x30, waiting for transfers between devices, swap(): return lax.ppermute(block, axis, [(i, i ^ mask) for i in range(count)])  38.9 us
    ppermute x4, waiting for transfers between devices, gather_both(): send = lambda held, route: lax.ppermute(held, 'col', route)  30.5 us
    ppermute x30, starting transfers between devices, swap(): return lax.ppermute(block, axis, [(i, i ^ mask) for i in range(count)])  28 us
    ppermute x5, waiting for transfers between devices, gather_heads(): send = lambda held, route: lax.ppermute(held, 'col', route)  25.4 us
    pallas_call x1, Pallas kernels, per_device(): call(functools.partial(project_kernel, routes, masks, img, head), (heads_...  15.2 us
    ppermute x5, starting transfers between devices, gather_heads(): send = lambda held, route: lax.ppermute(held, 'col', route)  4.6 us
    ppermute x4, starting transfers between devices, gather_both(): send = lambda held, route: lax.ppermute(held, 'col', route)  3.99 us
  transfers between devices with their start and end apart: 39, of which 16 were waited for; matrix products, arithmetic and copies ran while one was open for 0% of the time, Pallas kernels for 12%

profile of v10, /device:TPU:0, one launch (start us, length us, event | category | flops | bytes accessed | tf_op | source)
XLA Modules:
  0.0 160.4 jit_solution(16531129683636883536)
XLA Ops:
  0.6 1.2 copy-done.1
  1.8 1.1 copy-done.3
  2.9 1.9 %shard_map.140 = (bf16[304,1280]{1,0:T(8,128)(2,1)S(1)}, bf16[304,1280]{1,0:T(8,128)(2,1)S(1)}) custom-call(bf16[3,304,512]{2,1,0:T(8,128)(2,1)S(1)} %bitcast.44, bf16[304,2,512]{2,1,0:T(2,128)(2,1)S(1)} %copy-done.3), custom_call_target="tpu_custom_call" | custom-call | flops 2300000000 | tf_op jit(solution)/shard_map/pallas_call | solution.py:508
  4.8 0.5 collective-permute-start
  5.3 0.5 shard_map.141
  5.8 2.6 %collective-permute-start.1 = (f32[8,640]{1,0:T(8,128)S(1)}, f32[8,640]{1,0:T(8,128)S(1)}, u32[]{:S(2)}, u32[]{:S(2)}) collective-permute-start(f32[8,640]{1,0:T(8,128)S(1)} %get-tuple-element.90), channel_id=1, source_target_pairs={{0,8},{4,12},{8,0},{12,4},{16,24},{20,28},{24,16},{28,20},{1,9},{5... | collective-permute-start | bytes 61448 | tf_op jit(solution)/shard_map/ppermute | solution.py:24
  8.4 1.5 collective-permute-start.2
  9.9 0.0 collective-permute-start.3
  10.0 0.2 shard_map.142
  10.2 2.1 %collective-permute-start.5 = (f32[8,640]{1,0:T(8,128)S(1)}, f32[8,640]{1,0:T(8,128)S(1)}, u32[]{:S(2)}, u32[]{:S(2)}) collective-permute-start(f32[8,640]{1,0:T(8,128)S(1)} %shard_map.142), channel_id=1, source_target_pairs={{0,1},{1,0},{2,3},{3,2},{4,5},{5,4},{6,7},{7,6},{8,9},{9,8},{10,11... | collective-permute-start | bytes 61448 | tf_op jit(solution)/shard_map/ppermute | solution.py:24
  12.3 2.6 %collective-permute-start.6 = (f32[8,640]{1,0:T(8,128)S(1)}, f32[8,640]{1,0:T(8,128)S(1)}, u32[]{:S(2)}, u32[]{:S(2)}) collective-permute-start(f32[8,640]{1,0:T(8,128)S(1)} %shard_map.142), channel_id=1, source_target_pairs={{0,2},{1,3},{2,0},{3,1},{4,6},{5,7},{6,4},{7,5},{8,10},{9,11},{10,... | collective-permute-start | bytes 61448 | tf_op jit(solution)/shard_map/ppermute | solution.py:24
  14.9 1.0 collective-permute-start.7
  15.8 0.1 collective-permute-start.4
  15.9 1.1 collective-permute-done.6
  17.1 3.4 %collective-permute-done.7 = f32[8,640]{1,0:T(8,128)S(1)} collective-permute-done((f32[8,640]{1,0:T(8,128)S(1)}, f32[8,640]{1,0:T(8,128)S(1)}, u32[]{:S(2)}, u32[]{:S(2)}) %collective-permute-start.7) | collective-permute-done | bytes 20512 | tf_op jit(solution)/shard_map/ppermute | solution.py:24
  20.4 1.6 collective-permute-start.10
  22.0 1.5 collective-permute-start.11
  23.6 0.7 shard_map.143.refs_0_
  24.3 0.1 collective-permute-start.8
  24.4 0.7 collective-permute-start.9
  25.1 0.1 collective-permute-start.16
  25.2 12.6 %collective-permute-done.10.refs_14_ = bf16[304,1280]{1,0:T(8,128)(2,1)S(1)} collective-permute-done((bf16[304,1280]{1,0:T(8,128)(2,1)S(1)}, bf16[304,1280]{1,0:T(8,128)(2,1)S(1)}, u32[]{:S(2)}, u32[]{:S(2)}) %collective-permute-start.10) | collective-permute-done | bytes 778272 | tf_op jit(solution)/shard_map/ppermute | solution.py:24
  37.8 1.2 collective-permute-done.11.refs_17_
  39.1 2.1 %collective-permute-done.8.refs_1_ = bf16[608,640]{1,0:T(8,128)(2,1)S(1)} collective-permute-done((bf16[608,640]{1,0:T(8,128)(2,1)S(1)}, bf16[608,640]{1,0:T(8,128)(2,1)S(1)}, u32[]{:S(2)}, u32[]{:S(2)}) %collective-permute-start.8) | collective-permute-done | bytes 778272 | tf_op jit(solution)/shard_map/ppermute | solution.py:24
  41.1 1.3 collective-permute-start.12
  42.4 0.7 collective-permute-start.13
  43.2 0.6 collective-permute-start.14
  43.8 0.5 collective-permute-start.15
  44.3 15.5 %collective-permute-done.12.refs_3_ = bf16[608,640]{1,0:T(8,128)(2,1)S(1)} collective-permute-done((bf16[608,640]{1,0:T(8,128)(2,1)S(1)}, bf16[608,640]{1,0:T(8,128)(2,1)S(1)}, u32[]{:S(2)}, u32[]{:S(2)}) %collective-permute-start.12) | collective-permute-done | bytes 778272 | tf_op jit(solution)/shard_map/ppermute | solution.py:99
  59.8 1.3 collective-permute-start.17
  61.1 1.0 collective-permute-start.18
  62.1 0.5 collective-permute-start.19
  62.6 0.5 collective-permute-start.20
  63.2 14.9 %collective-permute-done.17.refs_5_ = bf16[608,640]{1,0:T(8,128)(2,1)S(1)} collective-permute-done((bf16[608,640]{1,0:T(8,128)(2,1)S(1)}, bf16[608,640]{1,0:T(8,128)(2,1)S(1)}, u32[]{:S(2)}, u32[]{:S(2)}) %collective-permute-start.17) | collective-permute-done | bytes 778272 | tf_op jit(solution)/shard_map/ppermute | solution.py:99
  78.1 0.5 collective-permute-start.22
  78.6 0.1 collective-permute-start.24
  78.8 1.5 collective-permute-start.25
  80.3 0.5 collective-permute-start.26
  80.8 0.6 collective-permute-done.22.refs_9_
  81.4 1.8 %collective-permute-start.27 = (bf16[736,256]{1,0:T(8,128)(2,1)S(1)}, bf16[736,256]{1,0:T(8,128)(2,1)S(1)}, u32[]{:S(2)}, u32[]{:S(2)}) collective-permute-start(bf16[736,256]{1,0:T(8,128)(2,1)S(1)} %pad_maximum_fusion.1), channel_id=1, source_target_pairs={{0,24},{4,28},{8,16},{12,20},{16,8},{20,12},{24,0},{28,4},{1,25},{... | collective-permute-start | bytes 1130504 | tf_op jit(solution)/shard_map/ppermute | solution.py:24
  83.3 15.2 %shard_map.144 = (bf16[256,512]{1,0:T(8,128)(2,1)S(1)}, bf16[256,512]{1,0:T(8,128)(2,1)S(1)}) custom-call(s32[4]{0:T(128)S(1)} %copy-done.8, f32[1,64]{1,0:T(1,128)S(1)} %bitcast.48, f32[2,64]{1,0:T(2,128)S(1)} %copy-done.7, bf16[608,640]{1,0:T(8,128)(2,1)S(1)} %shard_map.143.refs_0_, bf16[608,640]{1,0:T(8,128)(2,1)S(1)} %collective-permute-done.8.refs_1_, ...), custom_call_target="tpu_custom_call" | custom-call | flops 23000000512 | tf_op jit(solution)/shard_map/pallas_call | solution.py:542
  98.5 0.7 collective-permute-done.26
  99.3 0.1 collective-permute-start.33
  99.4 0.5 collective-permute-start.28
  99.9 2.3 %collective-permute-start.29 = (bf16[256,512]{1,0:T(8,128)(2,1)S(1)}, bf16[256,512]{1,0:T(8,128)(2,1)S(1)}, u32[]{:S(2)}, u32[]{:S(2)}) collective-permute-start(bf16[256,512]{1,0:T(8,128)(2,1)S(1)} %get-tuple-element.68), channel_id=1, source_target_pairs={{0,1},{1,0},{2,3},{3,2},{4,5},{5,4},{6,7},{7,6},{8,9},{9,8},{10,11... | collective-permute-start | bytes 786440 | tf_op jit(solution)/shard_map/ppermute | solution.py:24
  102.2 0.7 collective-permute-start.30
  102.9 0.2 collective-permute-done.28
  103.1 2.5 %collective-permute-start.31 = (bf16[256,512]{1,0:T(8,128)(2,1)S(1)}, bf16[256,512]{1,0:T(8,128)(2,1)S(1)}, u32[]{:S(2)}, u32[]{:S(2)}) collective-permute-start(bf16[256,512]{1,0:T(8,128)(2,1)S(1)} %collective-permute-done.28), channel_id=1, source_target_pairs={{0,1},{1,0},{2,3},{3,2},{4,5},{5,4},{6,7},{7,6},{8,9},{9,8},{10,11... | collective-permute-start | bytes 786440 | tf_op jit(solution)/shard_map/ppermute | solution.py:24
  105.6 0.7 collective-permute-start.32
  106.3 3.0 %collective-permute-done.29 = bf16[256,512]{1,0:T(8,128)(2,1)S(1)} collective-permute-done((bf16[256,512]{1,0:T(8,128)(2,1)S(1)}, bf16[256,512]{1,0:T(8,128)(2,1)S(1)}, u32[]{:S(2)}, u32[]{:S(2)}) %collective-permute-start.29) | collective-permute-done | bytes 262176 | tf_op jit(solution)/shard_map/ppermute | solution.py:24
  109.3 5.1 %collective-permute-done.31 = bf16[256,512]{1,0:T(8,128)(2,1)S(1)} collective-permute-done((bf16[256,512]{1,0:T(8,128)(2,1)S(1)}, bf16[256,512]{1,0:T(8,128)(2,1)S(1)}, u32[]{:S(2)}, u32[]{:S(2)}) %collective-permute-start.31) | collective-permute-done | bytes 262176 | tf_op jit(solution)/shard_map/ppermute | solution.py:24
  114.4 1.3 collective-permute-start.34
  115.8 0.7 collective-permute-start.35
  116.5 14.1 %collective-permute-done.34.refs_3_ = bf16[512,512]{1,0:T(8,128)(2,1)S(1)} collective-permute-done((bf16[512,512]{1,0:T(8,128)(2,1)S(1)}, bf16[512,512]{1,0:T(8,128)(2,1)S(1)}, u32[]{:S(2)}, u32[]{:S(2)}) %collective-permute-start.34) | collective-permute-done | bytes 524320 | tf_op jit(solution)/shard_map/ppermute | solution.py:85
  130.6 1.3 collective-permute-start.36
  131.9 2.9 %shard_map.145 = (f32[608,512]{1,0:T(8,128)S(1)}, bf16[608,512]{1,0:T(8,128)(2,1)S(1)}, bf16[192,608]{1,0:T(8,128)(2,1)S(1)}, f32[8,512]{1,0:T(8,128)S(1)}) custom-call(f32[8,640]{1,0:T(8,128)S(1)} %add.66.mod_ref, bf16[512,512]{1,0:T(8,128)(2,1)S(1)} %pad_maximum_fusion.refs_0_, bf16[512,512]{1,0:T(8,128)(2,1)S(1)} %constant_dynamic-update-slice_fusion.5.refs_1_, ...), custom_call_target="tpu_custom_call" | custom-call | flops 5750000128 | tf_op jit(solution)/shard_map/pallas_call | solution.py:579
  134.8 11.2 %collective-permute-done.36.refs_1_ = bf16[512,512]{1,0:T(8,128)(2,1)S(1)} collective-permute-done((bf16[512,512]{1,0:T(8,128)(2,1)S(1)}, bf16[512,512]{1,0:T(8,128)(2,1)S(1)}, u32[]{:S(2)}, u32[]{:S(2)}) %collective-permute-start.36) | collective-permute-done | bytes 524320 | tf_op jit(solution)/shard_map/ppermute | solution.py:85
  146.1 1.1 shard_map.146
  147.2 0.1 collective-permute-start.37
  147.3 5.1 %collective-permute-done.37 = f32[72,512]{1,0:T(8,128)S(1)} collective-permute-done((f32[72,512]{1,0:T(8,128)S(1)}, f32[72,512]{1,0:T(8,128)S(1)}, u32[]{:S(2)}, u32[]{:S(2)}) %collective-permute-start.37) | collective-permute-done | bytes 147488 | tf_op jit(solution)/shard_map/ppermute | solution.py:24
  152.4 1.4 collective-permute-start.38
  153.9 0.6 dynamic_slice.4
  155.8 3.7 %collective-permute-done.38 = f32[72,512]{1,0:T(8,128)S(1)} collective-permute-done((f32[72,512]{1,0:T(8,128)S(1)}, f32[72,512]{1,0:T(8,128)S(1)}, u32[]{:S(2)}, u32[]{:S(2)}) %collective-permute-start.38) | collective-permute-done | bytes 147488 | tf_op jit(solution)/shard_map/ppermute | solution.py:24
  159.6 0.8 fusion.2
  (86 shorter events, 0.5 us)
Async XLA Ops:
  0.6 1.2 copy-start.1
  1.8 1.1 copy-start.3
  2.9 2.4 %copy-start = (bf16[304,7,608]{2,0,1:T(8,128)(2,1)S(1)}, bf16[304,7,608]{2,0,1:T(8,128)(2,1)}, u32[]{:S(2)}) copy-start(bf16[304,7,608]{2,0,1:T(8,128)(2,1)} %param.19) | copy-start | bytes 7762948
  2.9 2.4 %copy-start.6 = (f32[4,304]{1,0:T(4,128)S(1)}, f32[4,304]{1,0:T(4,128)}, u32[]{:S(2)}) copy-start(f32[4,304]{1,0:T(4,128)} %cond_ref.1) | copy-start | bytes 14596
  4.8 38.4 %copy-start.2 = (bf16[304,1280]{1,0:T(8,128)(2,1)}, bf16[304,1280]{1,0:T(8,128)(2,1)S(1)}, u32[]{:S(2)}) copy-start(bf16[304,1280]{1,0:T(8,128)(2,1)S(1)} %get-tuple-element.50.refs_12_) | copy-start | bytes 2334724
  4.8 11.1 %collective-permute-start = (bf16[304,1280]{1,0:T(8,128)(2,1)S(1)}, bf16[304,1280]{1,0:T(8,128)(2,1)S(1)}, u32[]{:S(2)}, u32[]{:S(2)}) collective-permute-start(bf16[304,1280]{1,0:T(8,128)(2,1)S(1)} %get-tuple-element.44), channel_id=1, source_target_pairs={{0,4},{4,0},{8,12},{12,8},{16,20},{20,16},{24,28},{28,24},{1,5},{5... | collective-permute-start | bytes 2334728 | tf_op jit(solution)/shard_map/ppermute | solution.py:24
  5.3 4.7 %copy-start.4 = (bf16[512,608]{0,1:T(8,128)(2,1)S(1)}, bf16[512,608]{0,1:T(8,128)(2,1)}, u32[]{:S(2)}) copy-start(bf16[512,608]{0,1:T(8,128)(2,1)} %param.13) | copy-start | bytes 1867780
  5.3 4.7 %copy-start.5 = (bf16[96,608]{1,0:T(8,128)(2,1)S(1)}, bf16[96,608]{1,0:T(8,128)(2,1)}, u32[]{:S(2)}) copy-start(bf16[96,608]{1,0:T(8,128)(2,1)} %txt_ref.3) | copy-start | bytes 350212
  5.8 6.4 %collective-permute-start.1 = (f32[8,640]{1,0:T(8,128)S(1)}, f32[8,640]{1,0:T(8,128)S(1)}, u32[]{:S(2)}, u32[]{:S(2)}) collective-permute-start(f32[8,640]{1,0:T(8,128)S(1)} %get-tuple-element.90), channel_id=1, source_target_pairs={{0,8},{4,12},{8,0},{12,4},{16,24},{20,28},{24,16},{28,20},{1,9},{5... | collective-permute-start | bytes 61448 | tf_op jit(solution)/shard_map/ppermute | solution.py:24
  8.4 6.4 %collective-permute-start.2 = (f32[8,640]{1,0:T(8,128)S(1)}, f32[8,640]{1,0:T(8,128)S(1)}, u32[]{:S(2)}, u32[]{:S(2)}) collective-permute-start(f32[8,640]{1,0:T(8,128)S(1)} %get-tuple-element.92), channel_id=1, source_target_pairs={{0,16},{4,20},{8,24},{12,28},{16,0},{20,4},{24,8},{28,12},{1,17},{... | collective-permute-start | bytes 61448 | tf_op jit(solution)/shard_map/ppermute | solution.py:24
  9.9 5.9 %collective-permute-start.3 = (f32[8,640]{1,0:T(8,128)S(1)}, f32[8,640]{1,0:T(8,128)S(1)}, u32[]{:S(2)}, u32[]{:S(2)}) collective-permute-start(f32[8,640]{1,0:T(8,128)S(1)} %get-tuple-element.91), channel_id=1, source_target_pairs={{0,24},{4,28},{8,16},{12,20},{16,8},{20,12},{24,0},{28,4},{1,25},{... | collective-permute-start | bytes 61448 | tf_op jit(solution)/shard_map/ppermute | solution.py:24
  10.2 5.8 %collective-permute-start.5 = (f32[8,640]{1,0:T(8,128)S(1)}, f32[8,640]{1,0:T(8,128)S(1)}, u32[]{:S(2)}, u32[]{:S(2)}) collective-permute-start(f32[8,640]{1,0:T(8,128)S(1)} %shard_map.142), channel_id=1, source_target_pairs={{0,1},{1,0},{2,3},{3,2},{4,5},{5,4},{6,7},{7,6},{8,9},{9,8},{10,11... | collective-permute-start | bytes 61448 | tf_op jit(solution)/shard_map/ppermute | solution.py:24
  12.3 4.8 %collective-permute-start.6 = (f32[8,640]{1,0:T(8,128)S(1)}, f32[8,640]{1,0:T(8,128)S(1)}, u32[]{:S(2)}, u32[]{:S(2)}) collective-permute-start(f32[8,640]{1,0:T(8,128)S(1)} %shard_map.142), channel_id=1, source_target_pairs={{0,2},{1,3},{2,0},{3,1},{4,6},{5,7},{6,4},{7,5},{8,10},{9,11},{10,... | collective-permute-start | bytes 61448 | tf_op jit(solution)/shard_map/ppermute | solution.py:24
  14.9 5.6 %collective-permute-start.7 = (f32[8,640]{1,0:T(8,128)S(1)}, f32[8,640]{1,0:T(8,128)S(1)}, u32[]{:S(2)}, u32[]{:S(2)}) collective-permute-start(f32[8,640]{1,0:T(8,128)S(1)} %shard_map.142), channel_id=1, source_target_pairs={{0,3},{1,2},{2,1},{3,0},{4,7},{5,6},{6,5},{7,4},{8,11},{9,10},{10,... | collective-permute-start | bytes 61448 | tf_op jit(solution)/shard_map/ppermute | solution.py:24
  15.8 27.9 %copy-start.13 = (bf16[304,1280]{1,0:T(8,128)(2,1)}, bf16[304,1280]{1,0:T(8,128)(2,1)S(1)}, u32[]{:S(2)}) copy-start(bf16[304,1280]{1,0:T(8,128)(2,1)S(1)} %collective-permute-done.refs_16_) | copy-start | bytes 2334724
  15.8 7.7 %collective-permute-start.4 = (f32[8,640]{1,0:T(8,128)S(1)}, f32[8,640]{1,0:T(8,128)S(1)}, u32[]{:S(2)}, u32[]{:S(2)}) collective-permute-start(f32[8,640]{1,0:T(8,128)S(1)} %fusion.6), channel_id=1, source_target_pairs={{0,4},{4,0},{8,12},{12,8},{16,20},{20,16},{24,28},{28,24},{1,5},{5... | collective-permute-start | bytes 61448 | tf_op jit(solution)/shard_map/ppermute | solution.py:24
  20.4 17.4 %collective-permute-start.10 = (bf16[304,1280]{1,0:T(8,128)(2,1)S(1)}, bf16[304,1280]{1,0:T(8,128)(2,1)S(1)}, u32[]{:S(2)}, u32[]{:S(2)}) collective-permute-start(bf16[304,1280]{1,0:T(8,128)(2,1)S(1)} %get-tuple-element.50.refs_12_), channel_id=1, source_target_pairs={{0,16},{4,20},{8,24},{12,28},{16,0},{20,4},{24,8},{28,12},{1,17},{... | collective-permute-start | bytes 2334728 | tf_op jit(solution)/shard_map/ppermute | solution.py:24
  22.0 17.0 %collective-permute-start.11 = (bf16[304,1280]{1,0:T(8,128)(2,1)S(1)}, bf16[304,1280]{1,0:T(8,128)(2,1)S(1)}, u32[]{:S(2)}, u32[]{:S(2)}) collective-permute-start(bf16[304,1280]{1,0:T(8,128)(2,1)S(1)} %collective-permute-done.refs_16_), channel_id=1, source_target_pairs={{0,8},{4,12},{8,0},{12,4},{16,24},{20,28},{24,16},{28,20},{1,9},{5... | collective-permute-start | bytes 2334728 | tf_op jit(solution)/shard_map/ppermute | solution.py:24
  23.5 55.1 %copy-start.12 = (bf16[304,64]{0,1:T(8,128)(2,1)S(1)}, bf16[304,64]{0,1:T(8,128)(2,1)}, u32[]{:S(2)}) copy-start(bf16[304,64]{0,1:T(8,128)(2,1)} %param.25) | copy-start | bytes 116740
  23.5 55.2 %copy-start.10 = (bf16[256,608]{0,1:T(8,128)(2,1)S(1)}, bf16[256,608]{0,1:T(8,128)(2,1)}, u32[]{:S(2)}) copy-start(bf16[256,608]{0,1:T(8,128)(2,1)} %param.24) | copy-start | bytes 933892
  24.3 59.0 %copy-start.7 = (f32[2,64]{1,0:T(2,128)S(1)}, f32[2,64]{1,0:T(2,128)}, u32[]{:S(2)}) copy-start(f32[2,64]{1,0:T(2,128)} %k_gain_ref.1) | copy-start | bytes 1540
  24.3 59.0 %copy-start.8 = (s32[4]{0:T(128)S(1)}, s32[4]{0:T(128)}, u32[]{:S(2)}) copy-start(s32[4]{0:T(128)} %length_ref.1) | copy-start | bytes 52
  24.3 59.0 %copy-start.9 = (f32[64]{0:T(128)S(1)}, f32[64]{0:T(128)}, u32[]{:S(2)}) copy-start(f32[64]{0:T(128)} %param.22) | copy-start | bytes 772
  24.3 16.8 %collective-permute-start.8 = (bf16[608,640]{1,0:T(8,128)(2,1)S(1)}, bf16[608,640]{1,0:T(8,128)(2,1)S(1)}, u32[]{:S(2)}, u32[]{:S(2)}) collective-permute-start(bf16[608,640]{1,0:T(8,128)(2,1)S(1)} %shard_map.143.refs_0_), channel_id=1, source_target_pairs={{0,1},{1,0},{2,3},{3,2},{4,5},{5,4},{6,7},{7,6},{8,9},{9,8},{10,11... | collective-permute-start | bytes 2334728 | tf_op jit(solution)/shard_map/ppermute | solution.py:24
  24.4 16.7 %collective-permute-start.9 = (bf16[608,640]{1,0:T(8,128)(2,1)S(1)}, bf16[608,640]{1,0:T(8,128)(2,1)S(1)}, u32[]{:S(2)}, u32[]{:S(2)}) collective-permute-start(bf16[608,640]{1,0:T(8,128)(2,1)S(1)} %shard_map.143.refs_0_), channel_id=1, source_target_pairs={{1,2},{2,1},{5,6},{6,5},{9,10},{10,9},{13,14},{14,13},{17,18},{18,... | collective-permute-start | bytes 2334728 | tf_op jit(solution)/shard_map/ppermute | solution.py:99
  25.1 19.1 %collective-permute-start.16 = (bf16[608,640]{1,0:T(8,128)(2,1)S(1)}, bf16[608,640]{1,0:T(8,128)(2,1)S(1)}, u32[]{:S(2)}, u32[]{:S(2)}) collective-permute-start(bf16[608,640]{1,0:T(8,128)(2,1)S(1)} %shard_map.143.refs_0_), channel_id=1, source_target_pairs={{0,4},{4,0},{8,12},{12,8},{16,20},{20,16},{24,28},{28,24},{1,5},{5... | collective-permute-start | bytes 2334728 | tf_op jit(solution)/shard_map/ppermute | solution.py:24
  37.8 45.5 %copy-start.14 = (bf16[304,1280]{1,0:T(8,128)(2,1)}, bf16[304,1280]{1,0:T(8,128)(2,1)S(1)}, u32[]{:S(2)}) copy-start(bf16[304,1280]{1,0:T(8,128)(2,1)S(1)} %collective-permute-done.10.refs_14_) | copy-start | bytes 2334724
  39.0 44.2 %copy-start.15 = (bf16[304,1280]{1,0:T(8,128)(2,1)}, bf16[304,1280]{1,0:T(8,128)(2,1)S(1)}, u32[]{:S(2)}) copy-start(bf16[304,1280]{1,0:T(8,128)(2,1)S(1)} %collective-permute-done.11.refs_17_) | copy-start | bytes 2334724
  41.1 18.7 %collective-permute-start.12 = (bf16[608,640]{1,0:T(8,128)(2,1)S(1)}, bf16[608,640]{1,0:T(8,128)(2,1)S(1)}, u32[]{:S(2)}, u32[]{:S(2)}) collective-permute-start(bf16[608,640]{1,0:T(8,128)(2,1)S(1)} %collective-permute-done.9.refs_2_), channel_id=1, source_target_pairs={{1,0},{2,3},{5,4},{6,7},{9,8},{10,11},{13,12},{14,15},{17,16},{18,... | collective-permute-start | bytes 2334728 | tf_op jit(solution)/shard_map/ppermute | solution.py:99
  42.4 17.4 %collective-permute-start.13 = (bf16[608,640]{1,0:T(8,128)(2,1)S(1)}, bf16[608,640]{1,0:T(8,128)(2,1)S(1)}, u32[]{:S(2)}, u32[]{:S(2)}) collective-permute-start(bf16[608,640]{1,0:T(8,128)(2,1)S(1)} %collective-permute-done.8.refs_1_), channel_id=1, source_target_pairs={{1,2},{2,1},{5,6},{6,5},{9,10},{10,9},{13,14},{14,13},{17,18},{18,... | collective-permute-start | bytes 2334728 | tf_op jit(solution)/shard_map/ppermute | solution.py:99
  43.2 16.7 %collective-permute-start.14 = (bf16[304,1280]{1,0:T(8,128)(2,1)S(1)}, bf16[304,1280]{1,0:T(8,128)(2,1)S(1)}, u32[]{:S(2)}, u32[]{:S(2)}) collective-permute-start(bf16[304,1280]{1,0:T(8,128)(2,1)S(1)} %get-tuple-element.50.refs_12_), channel_id=1, source_target_pairs={{0,8},{4,12},{8,0},{12,4},{16,24},{20,28},{24,16},{28,20},{1,9},{5... | collective-permute-start | bytes 2334728 | tf_op jit(solution)/shard_map/ppermute | solution.py:24
  43.8 16.1 %collective-permute-start.15 = (bf16[304,1280]{1,0:T(8,128)(2,1)S(1)}, bf16[304,1280]{1,0:T(8,128)(2,1)S(1)}, u32[]{:S(2)}, u32[]{:S(2)}) collective-permute-start(bf16[304,1280]{1,0:T(8,128)(2,1)S(1)} %collective-permute-done.refs_16_), channel_id=1, source_target_pairs={{0,16},{4,20},{8,24},{12,28},{16,0},{20,4},{24,8},{28,12},{1,17},{... | collective-permute-start | bytes 2334728 | tf_op jit(solution)/shard_map/ppermute | solution.py:24
  59.8 23.5 %copy-start.16 = (bf16[304,1280]{1,0:T(8,128)(2,1)}, bf16[304,1280]{1,0:T(8,128)(2,1)S(1)}, u32[]{:S(2)}) copy-start(bf16[304,1280]{1,0:T(8,128)(2,1)S(1)} %collective-permute-done.14.refs_13_) | copy-start | bytes 2334724
  59.8 23.5 %copy-start.17 = (bf16[304,1280]{1,0:T(8,128)(2,1)}, bf16[304,1280]{1,0:T(8,128)(2,1)S(1)}, u32[]{:S(2)}) copy-start(bf16[304,1280]{1,0:T(8,128)(2,1)S(1)} %collective-permute-done.15.refs_18_) | copy-start | bytes 2334724
  59.8 18.2 %collective-permute-start.17 = (bf16[608,640]{1,0:T(8,128)(2,1)S(1)}, bf16[608,640]{1,0:T(8,128)(2,1)S(1)}, u32[]{:S(2)}, u32[]{:S(2)}) collective-permute-start(bf16[608,640]{1,0:T(8,128)(2,1)S(1)} %collective-permute-done.13.refs_4_), channel_id=1, source_target_pairs={{1,0},{2,3},{5,4},{6,7},{9,8},{10,11},{13,12},{14,15},{17,16},{18,... | collective-permute-start | bytes 2334728 | tf_op jit(solution)/shard_map/ppermute | solution.py:99
  61.1 16.9 %collective-permute-start.18 = (bf16[304,1280]{1,0:T(8,128)(2,1)S(1)}, bf16[304,1280]{1,0:T(8,128)(2,1)S(1)}, u32[]{:S(2)}, u32[]{:S(2)}) collective-permute-start(bf16[304,1280]{1,0:T(8,128)(2,1)S(1)} %collective-permute-done.10.refs_14_), channel_id=1, source_target_pairs={{0,8},{4,12},{8,0},{12,4},{16,24},{20,28},{24,16},{28,20},{1,9},{5... | collective-permute-start | bytes 2334728 | tf_op jit(solution)/shard_map/ppermute | solution.py:24
  62.1 16.4 %collective-permute-start.19 = (bf16[304,1280]{1,0:T(8,128)(2,1)S(1)}, bf16[304,1280]{1,0:T(8,128)(2,1)S(1)}, u32[]{:S(2)}, u32[]{:S(2)}) collective-permute-start(bf16[304,1280]{1,0:T(8,128)(2,1)S(1)} %collective-permute-done.11.refs_17_), channel_id=1, source_target_pairs={{0,16},{4,20},{8,24},{12,28},{16,0},{20,4},{24,8},{28,12},{1,17},{... | collective-permute-start | bytes 2334728 | tf_op jit(solution)/shard_map/ppermute | solution.py:24
  62.6 20.6 %collective-permute-start.23 = (bf16[608,640]{1,0:T(8,128)(2,1)S(1)}, bf16[608,640]{1,0:T(8,128)(2,1)S(1)}, u32[]{:S(2)}, u32[]{:S(2)}) collective-permute-start(bf16[608,640]{1,0:T(8,128)(2,1)S(1)} %collective-permute-done.13.refs_4_), channel_id=1, source_target_pairs={{0,4},{4,0},{8,12},{12,8},{16,20},{20,16},{24,28},{28,24},{1,5},{5... | collective-permute-start | bytes 2334728 | tf_op jit(solution)/shard_map/ppermute | solution.py:24
  62.6 16.1 %collective-permute-start.20 = (bf16[608,640]{1,0:T(8,128)(2,1)S(1)}, bf16[608,640]{1,0:T(8,128)(2,1)S(1)}, u32[]{:S(2)}, u32[]{:S(2)}) collective-permute-start(bf16[608,640]{1,0:T(8,128)(2,1)S(1)} %collective-permute-done.8.refs_1_), channel_id=1, source_target_pairs={{0,4},{4,0},{8,12},{12,8},{16,20},{20,16},{24,28},{28,24},{1,5},{5... | collective-permute-start | bytes 2334728 | tf_op jit(solution)/shard_map/ppermute | solution.py:24
  78.1 2.3 %collective-permute-start.21 = (bf16[608,640]{1,0:T(8,128)(2,1)S(1)}, bf16[608,640]{1,0:T(8,128)(2,1)S(1)}, u32[]{:S(2)}, u32[]{:S(2)}) collective-permute-start(bf16[608,640]{1,0:T(8,128)(2,1)S(1)} %collective-permute-done.9.refs_2_), channel_id=1, source_target_pairs={{0,4},{4,0},{8,12},{12,8},{16,20},{20,16},{24,28},{28,24},{1,5},{5... | collective-permute-start | bytes 2334728 | tf_op jit(solution)/shard_map/ppermute | solution.py:24
  78.1 5.2 %copy-start.18 = (bf16[304,1280]{1,0:T(8,128)(2,1)}, bf16[304,1280]{1,0:T(8,128)(2,1)S(1)}, u32[]{:S(2)}) copy-start(bf16[304,1280]{1,0:T(8,128)(2,1)S(1)} %collective-permute-done.18.refs_15_) | copy-start | bytes 2334724
  78.1 3.4 %collective-permute-start.22 = (bf16[608,640]{1,0:T(8,128)(2,1)S(1)}, bf16[608,640]{1,0:T(8,128)(2,1)S(1)}, u32[]{:S(2)}, u32[]{:S(2)}) collective-permute-start(bf16[608,640]{1,0:T(8,128)(2,1)S(1)} %collective-permute-done.12.refs_3_), channel_id=1, source_target_pairs={{0,4},{4,0},{8,12},{12,8},{16,20},{20,16},{24,28},{28,24},{1,5},{5... | collective-permute-start | bytes 2334728 | tf_op jit(solution)/shard_map/ppermute | solution.py:24
  78.6 4.7 %copy-start.19 = (bf16[304,1280]{1,0:T(8,128)(2,1)}, bf16[304,1280]{1,0:T(8,128)(2,1)S(1)}, u32[]{:S(2)}) copy-start(bf16[304,1280]{1,0:T(8,128)(2,1)S(1)} %collective-permute-done.19.refs_19_) | copy-start | bytes 2334724
  78.6 4.7 %collective-permute-start.24 = (bf16[608,640]{1,0:T(8,128)(2,1)S(1)}, bf16[608,640]{1,0:T(8,128)(2,1)S(1)}, u32[]{:S(2)}, u32[]{:S(2)}) collective-permute-start(bf16[608,640]{1,0:T(8,128)(2,1)S(1)} %collective-permute-done.17.refs_5_), channel_id=1, source_target_pairs={{0,4},{4,0},{8,12},{12,8},{16,20},{20,16},{24,28},{28,24},{1,5},{5... | collective-permute-start | bytes 2334728 | tf_op jit(solution)/shard_map/ppermute | solution.py:24
  78.8 19.7 %collective-permute-start.25 = (bf16[736,256]{1,0:T(8,128)(2,1)S(1)}, bf16[736,256]{1,0:T(8,128)(2,1)S(1)}, u32[]{:S(2)}, u32[]{:S(2)}) collective-permute-start(bf16[736,256]{1,0:T(8,128)(2,1)S(1)} %pad_maximum_fusion.1), channel_id=1, source_target_pairs={{0,8},{4,12},{8,0},{12,4},{16,24},{20,28},{24,16},{28,20},{1,9},{5... | collective-permute-start | bytes 1130504 | tf_op jit(solution)/shard_map/ppermute | solution.py:24
  80.3 18.9 %collective-permute-start.26 = (bf16[736,256]{1,0:T(8,128)(2,1)S(1)}, bf16[736,256]{1,0:T(8,128)(2,1)S(1)}, u32[]{:S(2)}, u32[]{:S(2)}) collective-permute-start(bf16[736,256]{1,0:T(8,128)(2,1)S(1)} %pad_maximum_fusion.1), channel_id=1, source_target_pairs={{0,16},{4,20},{8,24},{12,28},{16,0},{20,4},{24,8},{28,12},{1,17},{... | collective-permute-start | bytes 1130504 | tf_op jit(solution)/shard_map/ppermute | solution.py:24
  81.4 17.8 %collective-permute-start.27 = (bf16[736,256]{1,0:T(8,128)(2,1)S(1)}, bf16[736,256]{1,0:T(8,128)(2,1)S(1)}, u32[]{:S(2)}, u32[]{:S(2)}) collective-permute-start(bf16[736,256]{1,0:T(8,128)(2,1)S(1)} %pad_maximum_fusion.1), channel_id=1, source_target_pairs={{0,24},{4,28},{8,16},{12,20},{16,8},{20,12},{24,0},{28,4},{1,25},{... | collective-permute-start | bytes 1130504 | tf_op jit(solution)/shard_map/ppermute | solution.py:24
  99.3 15.0 %collective-permute-start.33 = (bf16[2944,256]{1,0:T(8,128)(2,1)S(1)}, bf16[2944,256]{1,0:T(8,128)(2,1)S(1)}, u32[]{:S(2)}, u32[]{:S(2)}) collective-permute-start(bf16[2944,256]{1,0:T(8,128)(2,1)S(1)} %constant_dynamic-update-slice_fusion.refs_4_), channel_id=1, source_target_pairs={{0,4},{4,0},{8,12},{12,8},{16,20},{20,16},{24,28},{28,24},{1,5},{5... | collective-permute-start | bytes 4521992 | tf_op jit(solution)/shard_map/ppermute | solution.py:24
  99.4 3.7 %collective-permute-start.28 = (bf16[256,512]{1,0:T(8,128)(2,1)S(1)}, bf16[256,512]{1,0:T(8,128)(2,1)S(1)}, u32[]{:S(2)}, u32[]{:S(2)}) collective-permute-start(bf16[256,512]{1,0:T(8,128)(2,1)S(1)} %get-tuple-element.69), channel_id=1, source_target_pairs={{0,4},{4,0},{8,12},{12,8},{16,20},{20,16},{24,28},{28,24},{1,5},{5... | collective-permute-start | bytes 786440 | tf_op jit(solution)/shard_map/ppermute | solution.py:24
  99.9 9.4 %collective-permute-start.29 = (bf16[256,512]{1,0:T(8,128)(2,1)S(1)}, bf16[256,512]{1,0:T(8,128)(2,1)S(1)}, u32[]{:S(2)}, u32[]{:S(2)}) collective-permute-start(bf16[256,512]{1,0:T(8,128)(2,1)S(1)} %get-tuple-element.68), channel_id=1, source_target_pairs={{0,1},{1,0},{2,3},{3,2},{4,5},{5,4},{6,7},{7,6},{8,9},{9,8},{10,11... | collective-permute-start | bytes 786440 | tf_op jit(solution)/shard_map/ppermute | solution.py:24
  102.2 7.1 %collective-permute-start.30 = (bf16[256,512]{1,0:T(8,128)(2,1)S(1)}, bf16[256,512]{1,0:T(8,128)(2,1)S(1)}, u32[]{:S(2)}, u32[]{:S(2)}) collective-permute-start(bf16[256,512]{1,0:T(8,128)(2,1)S(1)} %get-tuple-element.68), channel_id=1, source_target_pairs={{1,2},{2,1},{5,6},{6,5},{9,10},{10,9},{13,14},{14,13},{17,18},{18,... | collective-permute-start | bytes 786440 | tf_op jit(solution)/shard_map/ppermute | solution.py:85
  103.1 11.3 %collective-permute-start.31 = (bf16[256,512]{1,0:T(8,128)(2,1)S(1)}, bf16[256,512]{1,0:T(8,128)(2,1)S(1)}, u32[]{:S(2)}, u32[]{:S(2)}) collective-permute-start(bf16[256,512]{1,0:T(8,128)(2,1)S(1)} %collective-permute-done.28), channel_id=1, source_target_pairs={{0,1},{1,0},{2,3},{3,2},{4,5},{5,4},{6,7},{7,6},{8,9},{9,8},{10,11... | collective-permute-start | bytes 786440 | tf_op jit(solution)/shard_map/ppermute | solution.py:24
  105.6 8.7 %collective-permute-start.32 = (bf16[256,512]{1,0:T(8,128)(2,1)S(1)}, bf16[256,512]{1,0:T(8,128)(2,1)S(1)}, u32[]{:S(2)}, u32[]{:S(2)}) collective-permute-start(bf16[256,512]{1,0:T(8,128)(2,1)S(1)} %collective-permute-done.28), channel_id=1, source_target_pairs={{1,2},{2,1},{5,6},{6,5},{9,10},{10,9},{13,14},{14,13},{17,18},{18,... | collective-permute-start | bytes 786440 | tf_op jit(solution)/shard_map/ppermute | solution.py:85
  114.4 16.2 %collective-permute-start.34 = (bf16[512,512]{1,0:T(8,128)(2,1)S(1)}, bf16[512,512]{1,0:T(8,128)(2,1)S(1)}, u32[]{:S(2)}, u32[]{:S(2)}) collective-permute-start(bf16[512,512]{1,0:T(8,128)(2,1)S(1)} %constant_dynamic-update-slice_fusion.7.refs_2_), channel_id=1, source_target_pairs={{1,0},{2,3},{5,4},{6,7},{9,8},{10,11},{13,12},{14,15},{17,16},{18,... | collective-permute-start | bytes 1572872 | tf_op jit(solution)/shard_map/ppermute | solution.py:85
  115.8 14.9 %collective-permute-start.35 = (bf16[512,512]{1,0:T(8,128)(2,1)S(1)}, bf16[512,512]{1,0:T(8,128)(2,1)S(1)}, u32[]{:S(2)}, u32[]{:S(2)}) collective-permute-start(bf16[512,512]{1,0:T(8,128)(2,1)S(1)} %constant_dynamic-update-slice_fusion.5.refs_1_), channel_id=1, source_target_pairs={{1,2},{2,1},{5,6},{6,5},{9,10},{10,9},{13,14},{14,13},{17,18},{18,... | collective-permute-start | bytes 1572872 | tf_op jit(solution)/shard_map/ppermute | solution.py:85
  130.6 15.4 %collective-permute-start.36 = (bf16[512,512]{1,0:T(8,128)(2,1)S(1)}, bf16[512,512]{1,0:T(8,128)(2,1)S(1)}, u32[]{:S(2)}, u32[]{:S(2)}) collective-permute-start(bf16[512,512]{1,0:T(8,128)(2,1)S(1)} %collective-permute-done.35.refs_0_), channel_id=1, source_target_pairs={{1,0},{2,3},{5,4},{6,7},{9,8},{10,11},{13,12},{14,15},{17,16},{18,... | collective-permute-start | bytes 1572872 | tf_op jit(solution)/shard_map/ppermute | solution.py:85
  146.1 7.8 %copy-start.20 = (s32[4]{0:T(128)S(1)}, s32[4]{0:T(128)}, u32[]{:S(2)}) copy-start(s32[4]{0:T(128)} %param.16) | copy-start | bytes 52
  146.1 13.5 %copy-start.11 = (f32[512,64]{0,1:T(8,128)S(1)}, f32[512,64]{0,1:T(8,128)}, u32[]{:S(2)}) copy-start(f32[512,64]{0,1:T(8,128)} %param.17) | copy-start | bytes 393220
  147.2 5.2 %collective-permute-start.37 = (f32[72,512]{1,0:T(8,128)S(1)}, f32[72,512]{1,0:T(8,128)S(1)}, u32[]{:S(2)}, u32[]{:S(2)}) collective-permute-start(f32[72,512]{1,0:T(8,128)S(1)} %shard_map.146), channel_id=1, source_target_pairs={{0,1},{1,0},{2,3},{3,2},{4,5},{5,4},{6,7},{7,6},{8,9},{9,8},{10,11... | collective-permute-start | bytes 442376 | tf_op jit(solution)/shard_map/ppermute | solution.py:24
  152.4 7.1 %collective-permute-start.38 = (f32[72,512]{1,0:T(8,128)S(1)}, f32[72,512]{1,0:T(8,128)S(1)}, u32[]{:S(2)}, u32[]{:S(2)}) collective-permute-start(f32[72,512]{1,0:T(8,128)S(1)} %add.70), channel_id=1, source_target_pairs={{0,2},{1,3},{2,0},{3,1},{4,6},{5,7},{6,4},{7,5},{8,10},{9,11},{10,... | collective-permute-start | bytes 442376 | tf_op jit(solution)/shard_map/ppermute | solution.py:24
